TPU v7x, 32 devices: a whole 2x2x4 slice. The times are simulated.
32 devices in a mesh: dp: 8 (over y, x, core), mp: 4 (over z).
Axes of the slice: x: 2, y: 2, z: 4, core: 2. Of those that a mesh axis runs over, the one named last changes fastest.
Arguments:
- tokens: bfloat16 [8, 2048, 512], P('dp', 'mp'), may hold values from -6 to 6
- gain_mix: float32 [512], replicated, may hold values from 0.5 to 1.5
- w_mix: bfloat16 [512, 3, 1024], replicated, may hold values from -0.25 to 0.25
- bias_forget: float32 [1024], replicated, may hold values from 1 to 6
- bias_input: float32 [1024], replicated, may hold values from -7 to -1
- w_out: bfloat16 [1024, 512], replicated, may hold values from -0.5 to 0.5
- gain_mlp: float32 [512], replicated, may hold values from 0.5 to 1.5
- w_up: bfloat16 [512, 2048], P(None, 'mp'), may hold values from -0.25 to 0.25
- b_up: float32 [2048], P('mp'), may hold values from -1 to 1
- w_down: bfloat16 [2048, 512], P('mp'), may hold values from -0.125 to 0.125
- resets: int32 [8, 3], P('dp'), may hold values from 1 to 2047, as said below
- cotangent: bfloat16 [8, 2048, 512], P('dp', 'mp'), may hold values from -6 to 6
Outputs:
- mixed: bfloat16 [8, 2048, 512], P('dp', 'mp')
- grad_tokens: bfloat16 [8, 2048, 512], P('dp', 'mp')
- grad_gain_mix: float32 [512], P('mp')
- grad_w_mix: float32 [512, 3, 1024], P('mp')
- grad_bias_forget: float32 [1024], P('mp')
- grad_bias_input: float32 [1024], P('mp')
- grad_w_out: float32 [1024, 512], P('mp')
- grad_gain_mlp: float32 [512], P('mp')
- grad_w_up: float32 [512, 2048], P(None, 'mp')
- grad_b_up: float32 [2048], P('mp')
- grad_w_down: float32 [2048, 512], P('mp')
Inputs may be any that keep to these rules, and one draw needn't show every extreme that they name: `resets`: in each packed row the first two positions are below 256 and the third is 1792 or later; equal positions may repeat.
All inputs are finite; a program needn't handle non-finite values.
Results may differ from a plain program's by a relative error of at most 0.007.
Values may be sent and summed in bfloat16 or wider, within the bound.
No kernel may reach another device: no remote copies, remote signals or barrier semaphores. Data moves between devices by JAX's collectives and lax.ppermute only.
A program may use at most 128 MiB of HBM per device.

v0:
```python
from functools import partial

import jax
import jax.numpy as jnp
from jax import lax
from jax.sharding import PartitionSpec as P

norm_eps = 1e-06
block_len = 8


def carried_in(shard, axis, combine, identity, reverse):
    size, index = (lax.axis_size(axis), lax.axis_index(axis))
    everything = jax.tree.map(lambda part: lax.all_gather(part, axis), shard)
    start = jax.tree.map(
        lambda part, zero: jnp.broadcast_to(jnp.asarray(zero, part.dtype), part.shape),
        shard,
        identity,
    )

    def turn(k, before):
        at = size - 1 - k if reverse else k
        reached = at > index if reverse else at < index
        new = combine(before, jax.tree.map(lambda part: part[at], everything))
        return jax.tree.map(lambda a, b: jnp.where(reached, a, b), new, before)

    return lax.fori_loop(0, size, turn, start)


def rms_norm(values, gain):
    return values * lax.rsqrt(jnp.mean(values * values, axis=-1, keepdims=True) + norm_eps) * gain


def combine(first, second):
    return (first[0] * second[0], second[0] * first[1] + second[1])


def gate_pair(projected, bias_forget, bias_input, reset_mask):
    forget = jax.nn.sigmoid(projected[:, :, 0] + bias_forget)
    admit = jax.nn.sigmoid(projected[:, :, 1] + bias_input)
    total = forget + admit
    decay = jnp.where(reset_mask[:, :, None], 0.0, forget / total)
    inject = admit / total * projected[:, :, 2]
    return (decay, inject)


def dense_scan(coeffs, terms, backward_dir):
    length = coeffs.shape[-2]
    place_t = jnp.arange(length, dtype=jnp.int32)[:, None]
    place_s = jnp.arange(length, dtype=jnp.int32)[None, :]
    if backward_dir:
        strict = place_t < place_s
    else:
        strict = place_t > place_s
    reach = jnp.logical_or(strict, place_t == place_s)
    factors = jnp.where(strict[:, :, None], coeffs[..., :, None, :], 1.0)
    spans = lax.cumprod(factors, axis=coeffs.ndim - 2, reverse=backward_dir)
    spans = jnp.where(reach[:, :, None], spans, 0.0)
    results = jnp.sum(spans * terms[..., None, :, :], axis=coeffs.ndim - 1)
    products = lax.cumprod(coeffs, axis=coeffs.ndim - 2, reverse=backward_dir)
    return (products, results)


def blocked_scan(coeffs, terms, backward_dir):
    batch_rows, length, units = coeffs.shape
    if length <= block_len or length % block_len != 0:
        return dense_scan(coeffs, terms, backward_dir)
    blocks = length // block_len
    products, results = dense_scan(
        coeffs.reshape(batch_rows, blocks, block_len, units),
        terms.reshape(batch_rows, blocks, block_len, units),
        backward_dir,
    )
    edge = 0 if backward_dir else block_len - 1
    outer_prod, outer_res = blocked_scan(products[:, :, edge], results[:, :, edge], backward_dir)
    unity = jnp.ones((batch_rows, 1, units), jnp.float32)
    nothing = jnp.zeros((batch_rows, 1, units), jnp.float32)
    if backward_dir:
        enter_prod = jnp.concatenate([outer_prod[:, 1:], unity], axis=1)
        enter_res = jnp.concatenate([outer_res[:, 1:], nothing], axis=1)
    else:
        enter_prod = jnp.concatenate([unity, outer_prod[:, :-1]], axis=1)
        enter_res = jnp.concatenate([nothing, outer_res[:, :-1]], axis=1)
    whole_prod = products * enter_prod[:, :, None, :]
    whole_res = results + products * enter_res[:, :, None, :]
    return (
        whole_prod.reshape(batch_rows, length, units),
        whole_res.reshape(batch_rows, length, units),
    )


def on_device(
    tokens,
    gain_mix,
    w_mix,
    bias_forget,
    bias_input,
    w_out,
    gain_mlp,
    w_up,
    b_up,
    w_down,
    resets,
    cotangent,
):
    batch_rows, span_len, width = tokens.shape
    hidden_units = w_out.shape[0]
    row_total = batch_rows * span_len
    inputs = tokens.astype(jnp.float32)
    positions = lax.axis_index("mp") * span_len + jnp.arange(span_len, dtype=jnp.int32)
    reset_mask = jnp.any(resets[:, :, None] == positions[None, None, :], axis=1)
    gates_fn = partial(gate_pair, reset_mask=reset_mask)
    normed_mix = rms_norm(inputs, gain_mix).astype(jnp.bfloat16)
    projected = jnp.einsum("rtd,dkh->rtkh", normed_mix, w_mix, preferred_element_type=jnp.float32)
    decay, inject = gates_fn(projected, bias_forget, bias_input)
    cum_decay, local_states = blocked_scan(decay, inject, False)
    unity = jnp.ones((batch_rows, hidden_units), jnp.float32)
    nothing = jnp.zeros((batch_rows, hidden_units), jnp.float32)
    carry_in = carried_in(
        (cum_decay[:, -1], local_states[:, -1]), "mp", combine, (unity, nothing), False
    )
    state_in = carry_in[1]
    states = local_states + cum_decay * state_in[:, None, :]
    states_low = states.astype(jnp.bfloat16)
    middle = inputs + jnp.einsum(
        "rth,hd->rtd", states_low, w_out, preferred_element_type=jnp.float32
    )
    normed_mlp = rms_norm(middle, gain_mlp).astype(jnp.bfloat16)
    rows_all = lax.all_gather(normed_mlp.reshape(row_total, width), "mp", axis=0, tiled=True)
    pre_act = jnp.dot(rows_all, w_up, preferred_element_type=jnp.float32) + b_up
    hidden_act = jax.nn.gelu(pre_act).astype(jnp.bfloat16)
    piece = hidden_act
    mlp_terms = lax.psum_scatter(
        jnp.dot(piece, w_down, preferred_element_type=jnp.float32),
        "mp",
        scatter_dimension=0,
        tiled=True,
    )
    mixed = (middle + mlp_terms.reshape(batch_rows, span_len, width)).astype(jnp.bfloat16)
    cot_all = lax.all_gather(cotangent.reshape(row_total, width), "mp", axis=0, tiled=True)
    grad_act = jnp.einsum("nd,fd->nf", cot_all, w_down, preferred_element_type=jnp.float32)
    unused, gelu_back = jax.vjp(jax.nn.gelu, pre_act)
    grad_pre = gelu_back(grad_act)[0]
    grad_b_up = jnp.sum(grad_pre, axis=0)
    grad_pre_low = grad_pre.astype(jnp.bfloat16)
    grad_w_down = jnp.einsum("nf,nd->fd", hidden_act, cot_all, preferred_element_type=jnp.float32)
    grad_w_up = jnp.einsum("nd,nf->df", rows_all, grad_pre_low, preferred_element_type=jnp.float32)
    piece = grad_pre_low
    grad_normed = lax.psum_scatter(
        jnp.einsum("nf,df->nd", piece, w_up, preferred_element_type=jnp.float32),
        "mp",
        scatter_dimension=0,
        tiled=True,
    ).reshape(batch_rows, span_len, width)
    unused, norm_back = jax.vjp(rms_norm, middle, gain_mlp)
    grad_mid_norm, grad_gain_mlp = norm_back(grad_normed)
    grad_middle = cotangent.astype(jnp.float32) + grad_mid_norm
    mlp_sums = lax.psum((grad_w_up, grad_b_up, grad_w_down), "dp")
    grad_middle_low = grad_middle.astype(jnp.bfloat16)
    grad_w_out = jnp.einsum(
        "rth,rtd->hd", states_low, grad_middle_low, preferred_element_type=jnp.float32
    )
    grad_states = jnp.einsum(
        "rtd,hd->rth", grad_middle_low, w_out, preferred_element_type=jnp.float32
    )
    tail_decay, local_flow = blocked_scan(decay, decay * grad_states, True)
    outgoing = (tail_decay[:, 0], local_flow[:, 0])
    carry_back = carried_in(outgoing, "mp", combine, (unity, nothing), True)
    incoming = carry_back[1]
    flow = local_flow + tail_decay * incoming[:, None, :]
    carried = grad_states + jnp.concatenate([flow[:, 1:], incoming[:, None, :]], axis=1)
    states_before = jnp.concatenate([state_in[:, None, :], states[:, :-1]], axis=1)
    unused, gate_back = jax.vjp(gates_fn, projected, bias_forget, bias_input)
    grad_projected, grad_bias_forget, grad_bias_input = gate_back(
        (carried * states_before, carried)
    )
    grad_proj_low = grad_projected.astype(jnp.bfloat16)
    grad_w_mix = jnp.einsum(
        "rtd,rtkh->dkh", normed_mix, grad_proj_low, preferred_element_type=jnp.float32
    )
    grad_normed_mix = jnp.einsum(
        "rtkh,dkh->rtd", grad_proj_low, w_mix, preferred_element_type=jnp.float32
    )
    unused, mix_back = jax.vjp(rms_norm, inputs, gain_mix)
    grad_in_norm, grad_gain_mix = mix_back(grad_normed_mix)
    grad_tokens = (grad_middle + grad_in_norm).astype(jnp.bfloat16)
    local_grads_all = (
        grad_gain_mix,
        grad_w_mix,
        grad_bias_forget,
        grad_bias_input,
        grad_w_out,
        grad_gain_mlp,
    )
    shares = (
        lax.psum_scatter(local_grads_all[0], "mp", scatter_dimension=0, tiled=True),
        lax.psum_scatter(local_grads_all[1], "mp", scatter_dimension=0, tiled=True),
        lax.psum_scatter(local_grads_all[2], "mp", scatter_dimension=0, tiled=True),
        lax.psum_scatter(local_grads_all[3], "mp", scatter_dimension=0, tiled=True),
        lax.psum_scatter(local_grads_all[4], "mp", scatter_dimension=0, tiled=True),
        lax.psum_scatter(local_grads_all[5], "mp", scatter_dimension=0, tiled=True),
    )
    totals = lax.psum((shares[0], shares[1], shares[2], shares[3], shares[4], shares[5]), "dp")
    return (
        mixed,
        grad_tokens,
        totals[0],
        totals[1],
        totals[2],
        totals[3],
        totals[4],
        totals[5],
        mlp_sums[0],
        mlp_sums[1],
        mlp_sums[2],
    )


def solution(mesh):
    return jax.shard_map(
        on_device,
        mesh=mesh,
        in_specs=(
            P("dp", "mp", None),
            P(),
            P(),
            P(),
            P(),
            P(),
            P(),
            P(None, "mp"),
            P("mp"),
            P("mp", None),
            P("dp", None),
            P("dp", "mp", None),
        ),
        out_specs=(
            P("dp", "mp", None),
            P("dp", "mp", None),
            P("mp"),
            P("mp", None, None),
            P("mp"),
            P("mp"),
            P("mp", None),
            P("mp"),
            P(None, "mp"),
            P("mp"),
            P("mp", None),
        ),
        check_vma=False,
    )
```

profile of v0, /device:TPU:1, one launch (start us, length us, event | category | flops | bytes accessed | tf_op | source)
XLA Modules:
  0.0 647.3 jit_solution(14233261566302300091)
XLA Ops:
  11.6 3.0 convolution_bitcast_fusion
  20.0 10.9 %reduce_window.109 = f32[1,64,8,1024]{3,2,1,0:T(8,128)} reduce-window(f32[1,64,8,1024]{3,2,1,0:T(8,128)} %fusion.66, f32[]{:T(128)} %constant.119.clone.1), window={size=1x1x8x1 pad=0_0x0_0x7_0x0_0}, to_apply=%region_4.5 | reduce-window | flops 3670016 | bytes 4194308 | tf_op jit(solution)/shard_map/dense_scan/reduce_window | solution.py:60
  33.7 5.0 bitcast_multiply_fusion.11
  38.8 19.8 %multiply_reduce_fusion.1 = f32[64,8,1024]{2,1,0:T(8,128)S(1)} fusion(f32[64,8,1024]{2,1,0:T(8,128)} %get-tuple-element.364, pred[8,8]{1,0:T(8,128)(4,1)S(1)} %get-tuple-element.382, f32[64,8,1024]{2,1,0:T(8,128)} %get-tuple-element.365, pred[8,8]{1,0:T(8,128)(4,1)S(1)} %get-tuple-element.381), kind=kOutput, calls=%fused_computation.11 | output fusion | flops 45613056 | bytes 6291584 | tf_op jit(solution)/shard_map/dense_scan/reduce_window | solution.py:57
  63.9 11.3 %all_gather.18 = f32[4,1,1024]{2,1,0:T(1,128)S(1)} all-gather(f32[1,1,1024]{2,1,0:T(1,128)S(1)} %slice.117), channel_id=1, replica_groups=mesh['dp'=8,'mp'=4] {'mp'}, dimensions={0}, use_global_device_ids=true | all-gather | bytes 20480 | tf_op jit(solution)/shard_map/all_gather | solution.py:14
  75.1 10.2 %all_gather.19 = f32[4,1,1024]{2,1,0:T(1,128)S(1)} all-gather(f32[1,1,1024]{2,1,0:T(1,128)S(1)} %slice.118), channel_id=1, replica_groups=mesh['dp'=8,'mp'=4] {'mp'}, dimensions={0}, use_global_device_ids=true | all-gather | bytes 20480 | tf_op jit(solution)/shard_map/all_gather | solution.py:14
  85.8 3.5 multiply_reduce_fusion.4
  92.1 52.1 %all-gather.5.cloned.1.call-done = bf16[1,2048,512]{1,2,0:T(8,128)(2,1)} async-done(((bf16[1,512,512]{1,2,0:T(8,128)(2,1)}), bf16[1,2048,512]{1,2,0:T(8,128)(2,1)}) %all-gather.5.cloned.1.call-update) | async-done | bytes 2097168 | tf_op jit(solution)/shard_map/all_gather | solution.py:129
  144.1 5.0 fusion.39
  149.1 41.3 %all-gather.7.cloned.1.call-done = bf16[1,2048,512]{2,1,0:T(8,128)(2,1)} async-done(((bf16[1,512,512]{2,1,0:T(8,128)(2,1)}), bf16[1,2048,512]{2,1,0:T(8,128)(2,1)}) %all-gather.7.cloned.1.call-update) | async-done | bytes 2097168 | tf_op jit(solution)/shard_map/all_gather | solution.py:140
  190.4 6.9 %fusion.149 = (f32[512]{0:T(512)S(1)}, bf16[2048,512]{1,0:T(8,128)(2,1)S(1)}) fusion(f32[2048,512]{1,0:T(8,128)} %fusion.39, f32[512]{0:T(512)S(1)} %copy-done.41, bf16[512,512]{1,0:T(8,128)(2,1)} %param.25, bf16[1,2048,512]{2,1,0:T(8,128)(2,1)} %all-gather.7.cloned.1.call-done), kind=kOutput, calls=%fused_computation.236 | convolution fusion | flops 1096809984 | bytes 8916992 | tf_op jit(solution)/shard_map/nd,fd->nf/dot_general | solution.py:141
  198.7 3.4 fusion.92
  202.1 6.4 fusion.141
  210.7 12.7 %reduce_window.118 = f32[1,64,8,1024]{3,2,1,0:T(8,128)} reduce-window(f32[1,64,8,1024]{3,2,1,0:T(8,128)} %fusion.66, f32[]{:T(128)} %constant.119.clone.1), window={size=1x1x8x1 pad=0_0x0_0x0_7x0_0}, to_apply=%region_19.20 | reduce-window | flops 3670016 | bytes 4194308 | tf_op jit(solution)/shard_map/dense_scan/reduce_window | solution.py:60
  227.9 3.3 fusion.19
  231.2 46.5 %reduce-scatter.7.cloned.1.call-done = f32[512,512]{0,1:T(8,128)} async-done(((f32[2048,512]{0,1:T(8,128)}), f32[512,512]{0,1:T(8,128)}) %reduce-scatter.7.cloned.1.call-update) | async-done | bytes 1048592 | tf_op jit(solution)/shard_map/reduce_scatter | solution.py:149
  279.6 77.7 %reduce-scatter.5.cloned.1.call-done = f32[512,512]{0,1:T(8,128)} async-done(((f32[2048,512]{0,1:T(8,128)}), f32[512,512]{0,1:T(8,128)}) %reduce-scatter.5.cloned.1.call-update) | async-done | bytes 1048592 | tf_op jit(solution)/shard_map/reduce_scatter | solution.py:133
  357.3 3.3 fusion.77
  363.9 3.6 fusion.106
  367.6 5.1 multiply_bitcast_fusion.1
  372.7 10.5 %multiply_reduce_fusion = f32[64,8,1024]{2,1,0:T(8,128)} fusion(f32[64,8,1024]{2,1,0:T(8,128)} %get-tuple-element.361, pred[8,8]{1,0:T(8,128)(4,1)S(1)} %get-tuple-element.383, f32[64,8,1024]{2,1,0:T(8,128)} %get-tuple-element.365, pred[8,8]{1,0:T(8,128)(4,1)S(1)} %get-tuple-element.384), kind=kOutput, calls=%fused_computation.8 | output fusion | flops 45613056 | bytes 6291584 | tf_op jit(solution)/shard_map/dense_scan/reduce_window | solution.py:57
  390.4 12.6 %all_gather.22 = f32[4,1,1024]{2,1,0:T(1,128)S(1)} all-gather(f32[1,1,1024]{2,1,0:T(1,128)S(1)} %slice.130), channel_id=1, replica_groups=mesh['dp'=8,'mp'=4] {'mp'}, dimensions={0}, use_global_device_ids=true | all-gather | bytes 20480 | tf_op jit(solution)/shard_map/all_gather | solution.py:14
  402.9 10.9 %all_gather.23 = f32[4,1,1024]{2,1,0:T(1,128)S(1)} all-gather(f32[1,1,1024]{2,1,0:T(1,128)S(1)} %slice.131), channel_id=1, replica_groups=mesh['dp'=8,'mp'=4] {'mp'}, dimensions={0}, use_global_device_ids=true | all-gather | bytes 20480 | tf_op jit(solution)/shard_map/all_gather | solution.py:14
  414.3 2.9 fusion.20
  417.2 6.1 fusion.142
  428.3 4.5 fusion.112
  432.9 4.6 fusion.37
  440.4 107.1 %reduce-scatter.9.cloned.1.call-done = f32[128,3,1024]{2,0,1:T(8,128)} async-done(((f32[512,3,1024]{2,0,1:T(8,128)}), f32[128,3,1024]{2,0,1:T(8,128)}) %reduce-scatter.9.cloned.1.call-update) | async-done | bytes 1572880 | tf_op jit(solution)/shard_map/reduce_scatter | solution.py:197
  552.1 5.0 fusion.76
  560.4 14.2 %all-reduce.17 = (f32[512]{0:T(512)S(1)}, f32[1024]{0:T(1024)S(1)}, f32[1024]{0:T(1024)S(1)}, f32[512]{0:T(512)S(1)}) all-reduce(f32[512]{0:T(512)S(1)} %get-tuple-element.321, f32[1024]{0:T(1024)S(1)} %get-tuple-element.359, f32[1024]{0:T(1024)S(1)} %get-tuple-element.356, ...), channel_id=6, replica_groups=mesh['dp'=8,'mp'=4] {'mp'}, use_global_device_ids=true, to_apply=%region_30.31.clone | all-reduce | flops 3072 | bytes 24576
  574.9 16.5 %all-reduce.15 = (f32[128]{0:T(128)}, f32[256]{0:T(256)}, f32[256]{0:T(256)}, f32[128]{0:T(128)}, f32[512]{0:T(512)}) all-reduce(f32[128]{0:T(128)S(1)} %dynamic-slice.1, f32[256]{0:T(256)S(1)} %dynamic-slice.3, f32[256]{0:T(256)S(1)} %dynamic-slice.5, f32[128]{0:T(128)S(1)} %dynamic-slice.7, ...), channel_id=1, replica_groups=mesh['dp'=8,'mp'=4] {'dp'}, use_global_device_ids=true, to_apply=%region_31.32 | all-reduce | flops 1280 | bytes 10240 | tf_op jit(solution)/shard_map/psum | solution.py:203
  591.4 43.2 %all-reduce.20.cloned.1.call-done = (f32[128,3,1024]{2,0,1:T(8,128)}, f32[256,512]{1,0:T(8,128)}, f32[512,512]{1,0:T(8,128)}, f32[512,512]{1,0:T(8,128)}) async-done(((f32[128,3,1024]{2,0,1:T(8,128)}, f32[256,512]{1,0:T(8,128)}, f32[512,512]{1,0:T(8,128)}, f32[512,512]{1,0:T(8,128)}), (f32[128,3,1024]{2,0,1:T(8,128)}, f32[256,512]{1,0:T(8,128)}, f32[512,512]{1,0:T(8,128)}, ...) | async-done | bytes 4194320 | tf_op jit(solution)/shard_map/psum | solution.py:203
  (199 shorter events, 61.9 us)
Async XLA Ops:
  7.2 4.4 copy-start
  7.2 136.9 %all-gather.5.cloned.1.call-start = ((), (), s32[]{:S(2)}) async-start(), calls=%async_computation.8 | async-start | bytes 2621440 | tf_op jit(solution)/shard_map/all_gather | solution.py:129
  11.5 5.7 copy-start.36
  11.5 5.7 copy-start.37
  85.8 4.5 copy-start.38
  91.2 99.2 %all-gather.7.cloned.1.call-start = ((), (), s32[]{:S(2)}) async-start(), calls=%async_computation.9 | async-start | bytes 2621440 | tf_op jit(solution)/shard_map/all_gather | solution.py:140
  92.0 98.4 %copy-start.41 = (f32[512]{0:T(512)S(1)}, f32[512]{0:T(512)}, u32[]{:S(2)}) copy-start(f32[512]{0:T(512)} %param.24) | copy-start | bytes 6148
  92.0 185.7 %reduce-scatter.7.cloned.1.call-start = ((), (), s32[]{:S(2)}) async-start(), calls=%async_computation.5 | async-start | bytes 5242880 | tf_op jit(solution)/shard_map/reduce_scatter | solution.py:149
  190.4 8.3 %copy-start.25 = (bf16[512,512]{1,0:T(8,128)(2,1)S(1)}, bf16[512,512]{1,0:T(8,128)(2,1)}, u32[]{:S(2)}) copy-start(bf16[512,512]{1,0:T(8,128)(2,1)} %param.23) | copy-start | bytes 1572868
  202.1 155.2 %reduce-scatter.5.cloned.1.call-start = ((), (), s32[]{:S(2)}) async-start(), calls=%async_computation.4 | async-start | bytes 5242880 | tf_op jit(solution)/shard_map/reduce_scatter | solution.py:133
  208.6 231.8 %reduce-scatter.11.cloned.1.call-start = ((), (), s32[]{:S(2)}) async-start(), calls=%async_computation.7 | async-start | bytes 2621440 | tf_op jit(solution)/shard_map/reduce_scatter | solution.py:200
  223.4 4.5 copy-start.17
  357.3 4.3 copy-start.3
  357.3 4.3 copy-start.5
  357.3 4.3 copy-start.23
  367.6 179.9 %reduce-scatter.9.cloned.1.call-start = ((), (), s32[]{:S(2)}) async-start(), calls=%async_computation.6 | async-start | bytes 7864320 | tf_op jit(solution)/shard_map/reduce_scatter | solution.py:197
  372.7 12.4 %copy-start.29 = (f32[1,64,1,1024]{3,1,2,0:T(8,128)S(1)}, f32[1,64,1,1024]{3,1,2,0:T(8,128)}, u32[]{:S(2)}) copy-start(f32[1,64,1,1024]{3,1,2,0:T(8,128)} %copy.101) | copy-start | bytes 786436
  383.2 3.2 copy-start.32
  383.2 3.2 copy-start.34
  414.3 9.0 %slice-start = ((s8[6291456]{0:T(1024)(128)(4,1)}), s8[4194304]{0:T(1024)(128)(4,1)S(1)}, s32[]{:S(2)}) async-start(s8[6291456]{0:T(1024)(128)(4,1)} %bitcast.371), calls=%async_computation.11 | async-start | bytes 8388608
  417.2 6.1 slice-start.1
  417.2 6.1 copy-start.7
  417.2 6.3 copy-start.8
  423.3 3.0 copy-start.26
  423.5 4.8 copy-start.12
  423.5 4.8 copy-start.39
  432.8 201.8 %all-reduce.20.cloned.1.call-start = ((), (), s32[]{:S(2)}) async-start(), calls=%async_computation.10 | async-start | bytes 8388608 | tf_op jit(solution)/shard_map/psum | solution.py:203
  432.9 4.6 copy-start.21
  432.9 4.6 copy-start.40
  552.1 5.0 copy-start.10
  552.1 5.0 copy-start.13
  634.6 3.6 copy-start.31
  (20 other events, 34.2 us)
Sparse Core Ops, SparseCore 0:
  91.4 52.6 all-gather.4
  145.7 44.6 all-gather.6
  202.2 75.4 reduce-scatter.6
  280.0 77.2 reduce-scatter.4
  367.7 44.3 reduce-scatter.10
  433.0 114.4 reduce-scatter.8
  552.6 81.9 all-reduce.19
where the time goes:
time: 652 us; the launch traced here: 647 us
  waiting for transfers between devices  369 us (57%)
  other arithmetic  96.1 us (15%)
  blocking collectives  75.6 us (12%)
  matrix products  51.2 us (8%)
  local copies, waits for them, and re-layouts  38.3 us (6%)
  between operations  16.4 us (3%)
    reduce_scatter x1, waiting for transfers between devices, on_device(): lax.psum_scatter(local_grads_all[1], 'mp', scatter_dimension=0, tiled=True)  107 us
    reduce_scatter x1, waiting for transfers between devices, on_device(): lax.psum_scatter(jnp.dot(piece, w_down, preferred_element_type=jnp.float3...  77.7 us
    all_gather x1, waiting for transfers between devices, on_device(): lax.all_gather(normed_mlp.reshape(row_total, width), 'mp', axis=0, tiled=...  52.1 us
    reduce_scatter x1, waiting for transfers between devices, on_device(): lax.psum_scatter(jnp.einsum('nf,df->nd', piece, w_up, preferred_element_t...  46.5 us
    all_gather x4, blocking collectives, carried_in(): everything = jax.tree.map(lambda part: lax.all_gather(part, axis), shard)  45 us
    psum x1, waiting for transfers between devices, on_device(): lax.psum((shares[0], shares[1], shares[2], shares[3], shares[4], shares[5...  43.2 us
    all_gather x1, waiting for transfers between devices, on_device(): lax.all_gather(cotangent.reshape(row_total, width), 'mp', axis=0, tiled=T...  41.3 us
    another operation x6, other arithmetic, dense_scan(): spans = lax.cumprod(factors, axis=coeffs.ndim - 2, reverse=backward_dir)  32.6 us
  transfers between devices with their start and end apart: 7, of which 6 were waited for; matrix products, arithmetic and copies ran while one was open for 14% of the time, Pallas kernels for 0%

commit v1 on v0

v1 whole, which is shorter than its diff:
```python
from functools import partial

import jax
import jax.numpy as jnp
from jax import lax
from jax.experimental import pallas as pl
from jax.experimental.pallas import tpu as pltpu
from jax.sharding import PartitionSpec as P

norm_eps = 1e-06
gelu_k = 0.7978845608028654
gelu_c = 0.044715
chunks = 8
f32 = jnp.float32
bf16 = jnp.bfloat16
VMEM = pl.BlockSpec(memory_space=pltpu.VMEM)
SMEM = pl.BlockSpec(memory_space=pltpu.SMEM)


def dot(a, b):
    return jnp.dot(a, b, preferred_element_type=f32)


def dot_nt(a, b):
    return lax.dot_general(a, b, (((1,), (1,)), ((), ())), preferred_element_type=f32)


def shape_of(dtype, *shape):
    return jax.ShapeDtypeStruct(shape, dtype)


def call(body, name, operands, outs, scratch=(), smem=1, flops=0, moved=0):
    return pl.pallas_call(
        body,
        out_shape=outs,
        in_specs=[SMEM] * smem + [VMEM] * (len(operands) - smem),
        out_specs=[VMEM] * len(outs),
        scratch_shapes=list(scratch),
        compiler_params=pltpu.CompilerParams(vmem_limit_bytes=48 << 20),
        cost_estimate=pl.CostEstimate(flops=flops, bytes_accessed=moved, transcendentals=0),
        name=name,
    )(*operands)


def to_chunked(src, split, put):
    length, width = src.shape
    steps = length // chunks
    for g in range(width // 128):
        cols = slice(g * 128, (g + 1) * 128)
        split[g] = src[:, cols].astype(f32)
        for s in range(steps):
            put(pl.ds(s * chunks, chunks), cols, split[g, pl.ds(s, chunks, stride=steps), :])


def from_chunked(values, split, out):
    length, width = out.shape
    steps = length // chunks
    for g in range(width // 128):
        cols = slice(g * 128, (g + 1) * 128)
        for s in range(steps):
            split[g, pl.ds(s, chunks, stride=steps), :] = values[s * chunks : (s + 1) * chunks, cols]
        out[:, cols] = split[g].astype(bf16)


def keep_mask(idx, resets, length):
    row = lax.broadcasted_iota(jnp.int32, (length, 1), 0)
    pos = idx[2] * length + (row % chunks) * (length // chunks) + row // chunks
    keep = jnp.ones((length, 1), f32)
    for i in range(3):
        keep = jnp.where(pos == resets[i], 0.0, keep)
    return keep


def mixer_in(idx, resets, tok, gain, w, bias_f, bias_i, b_up, decay, share, cand, du, dv, nmt, x, prods, ends, payload, split):
    length, width = tok.shape
    units = bias_f.shape[1]
    steps = length // chunks

    def put(rows, cols, values):
        x[rows, cols] = values

    to_chunked(tok, split, put)
    v = x[...]
    r = lax.rsqrt(jnp.mean(v * v, axis=-1, keepdims=True) + norm_eps)
    nm = (v * r * gain[...]).astype(bf16)
    nmt[...] = nm.T
    keep = keep_mask(idx, resets, length)
    block = 256
    for h in range(0, units, block):
        sl = pl.ds(h, block)
        a = jnp.exp(jnp.minimum(-(dot(nm, w[0, :, sl]) + bias_f[:, sl]), 88.0))
        b = jnp.exp(jnp.minimum(-(dot(nm, w[1, :, sl]) + bias_i[:, sl]), 88.0))
        t = 1.0 / (2.0 + a + b)
        p = (1.0 + b) * t
        q = (1.0 + a) * t
        decay[:, sl] = p * keep
        share[:, sl] = q
        cand[:, sl] = dot(nm, w[2, :, sl])
        du[:, sl] = p * (a * t)
        dv[:, sl] = q * (b * t)

    def step(s, carry):
        prod, end = carry
        rows = pl.ds(pl.multiple_of(s * chunks, chunks), chunks)
        d = decay[rows, :]
        return prod * d, end * d + share[rows, :] * cand[rows, :]

    prod, end = lax.fori_loop(
        0, steps, step, (jnp.ones((chunks, units), f32), jnp.zeros((chunks, units), f32)), unroll=8
    )
    prods[...] = prod
    ends[...] = end
    total, state = prod[0:1], end[0:1]
    for k in range(1, chunks):
        total = total * prod[k : k + 1]
        state = state * prod[k : k + 1] + end[k : k + 1]
    payload[...] = jnp.zeros_like(payload)
    payload[0:1, :] = total
    payload[1:2, :] = state
    payload[2:3, 0 : b_up.shape[1]] = b_up[...]


def feed_forward(nm, cot, wu, wd, bu):
    pre = dot(nm, wu) + bu
    grad_act = dot_nt(cot, wd)
    sq = pre * pre
    t = jnp.tanh(pre * (gelu_k + gelu_k * gelu_c * sq))
    half = 0.5 + 0.5 * t
    h = pre * half
    slope = half + h * (1.0 - t) * (gelu_k + 3.0 * gelu_k * gelu_c * sq)
    grad_pre = grad_act * slope
    return h.astype(bf16), grad_pre.astype(bf16), jnp.sum(grad_pre, axis=0, keepdims=True)


def store_pieces(ref, slot, base, rows, values):
    for p in range(4):
        ref[p, slot, base : base + rows, :] = values[p * rows : (p + 1) * rows].astype(bf16)


def ffn_block(slot, core, nm, nmt, cot, wu, wd, bu, mix, gn, keep, send, hT):
    h, g, bsum = feed_forward(nm, cot, wu, wd, bu)
    hT[...] = h.T
    half = nm.shape[1] // 2
    for ref, which in ((send, 1 - core), (keep, core)):
        rows = pl.ds(pl.multiple_of(which * half, half), half)
        store_pieces(ref, slot, 0, half // 4, dot(nmt[rows, :], g))
        store_pieces(ref, slot, half // 4, half // 4, dot(hT[rows, :], cot))
    mix[...] += dot(h, wd)
    gn[...] += dot_nt(g, wu)
    return bsum


def block_mid(idx, own, r1, r2, r3, prods, ends, decay, share, cand, x, cot, w_out, gain, wu, wd, bu,
              st, stT, middle, nm2, nm2t, cotp, mix, gn, bsum, keep, send, split, others, hT, carry8):
    length = x.shape[0]
    steps = length // chunks
    units = decay.shape[1]
    core, z = idx[0], idx[2]
    for j, ref in enumerate((own, r1, r2, r3)):
        others[j] = ref[...]
    state = jnp.zeros((1, units), f32)
    for k in range(4):
        part = others[k ^ z]
        state = jnp.where(k < z, state * part[0:1] + part[1:2], state)
    for k in range(chunks):
        carry8[k : k + 1, :] = state
        state = state * prods[k : k + 1, :] + ends[k : k + 1, :]
    st[0:chunks, :] = carry8[...]

    def step(s, state):
        rows = pl.ds(pl.multiple_of(s * chunks, chunks), chunks)
        state = state * decay[rows, :] + share[rows, :] * cand[rows, :]
        st[pl.ds(pl.multiple_of(s * chunks + chunks, chunks), chunks), :] = state
        return state

    lax.fori_loop(0, steps, step, carry8[...], unroll=8)
    low = st[chunks:, :].astype(bf16)
    stT[...] = low.T
    mid = x[...] + dot(low, w_out[...])
    middle[...] = mid
    r = lax.rsqrt(jnp.mean(mid * mid, axis=-1, keepdims=True) + norm_eps)
    nm = (mid * r * gain[...]).astype(bf16)
    nm2[...] = nm
    nm2t[...] = nm.T

    def put(rows, cols, values):
        gn[rows, cols] = values

    to_chunked(cot, split, put)
    cotp[...] = gn[...].astype(bf16)
    gn[...] = jnp.zeros_like(gn)
    mix[...] = mid
    bsum[...] = ffn_block(0, core, nm, nm2t, cotp[...], wu[...], wd[...], bu[...], mix, gn, keep, send, hT)


def block_mlp(idx, a0, a1, a2, a3, b0, b1, b2, b3, r1, r2, r3, mix0, gn0, bsum0, keep0, send0, nm2, nm2t, cotp, middle, gain,
              stT, w_out, decay,
              mixed, keep, send, grad_mid, grad_states, payload, small, mix, gn, hT, wu, wd, split):
    core, plane, z = idx[0], idx[1], idx[2]
    length, units = decay.shape
    steps = length // chunks
    mix[...] = mix0[...]
    gn[...] = gn0[...]
    small[...] = jnp.zeros_like(small)
    rows8 = wu.shape[0] // 8
    for p in range(4):
        keep[p, 0, 0 : 2 * rows8, :] = keep0[p, 0]
        send[p, 0, 0 : 2 * rows8, :] = send0[p, 0]
    small[pl.ds(6 + z, 1), :] = bsum0[...]
    for j, bias in ((1, r1), (2, r2), (3, r3)):
        for which, pieces in ((core, (a0, a1, a2, a3)), (1 - core, (b0, b1, b2, b3))):
            for k, piece in enumerate(pieces):
                at = pl.ds(pl.multiple_of((which * 4 + (plane ^ k)) * rows8, rows8), rows8)
                top = (j - 1) * 2 * rows8
                wu[at, :] = piece[top : top + rows8, :]
                wd[at, :] = piece[top + rows8 : top + 2 * rows8, :]
        bu = bias[2:3, 0 : wu.shape[1]]
        small[pl.ds(6 + (z ^ j), 1), :] = ffn_block(
            j, core, nm2[...], nm2t, cotp[...], wu[...], wd[...], bu, mix, gn, keep, send, hT
        )
    from_chunked(mix, split, mixed)
    mid = middle[...]
    r = lax.rsqrt(jnp.mean(mid * mid, axis=-1, keepdims=True) + norm_eps)
    scaled = mid * r
    g = gn[...]
    small[5:6, :] = jnp.sum(g * scaled, axis=0, keepdims=True)
    gg = g * gain[...]
    gm = cotp[...].astype(f32) + r * (gg - scaled * jnp.mean(gg * scaled, axis=-1, keepdims=True))
    grad_mid[...] = gm
    low = gm.astype(bf16)
    part = units // 8
    for k in range(4):
        for ref, which in ((send, 1 - core), (keep, core)):
            got = dot(stT[pl.ds(pl.multiple_of((2 * k + which) * part, part), part), :], low)
            for p in range(4):
                ref[p, k ^ z, 2 * rows8 :, :] = got[p * (part // 4) : (p + 1) * (part // 4)].astype(bf16)
    grad_states[...] = dot_nt(low, w_out[...])

    def step(i, carry):
        prod, flow = carry
        rows = pl.ds(pl.multiple_of((steps - 1 - i) * chunks, chunks), chunks)
        d = decay[rows, :]
        return prod * d, (flow + grad_states[rows, :]) * d

    prod, flow = lax.fori_loop(
        0, steps, step, (jnp.ones((chunks, units), f32), jnp.zeros((chunks, units), f32)), unroll=8
    )
    total, out = prod[chunks - 1 :], flow[chunks - 1 :]
    for k in range(chunks - 2, -1, -1):
        total = total * prod[k : k + 1]
        out = out * prod[k : k + 1] + flow[k : k + 1]
    payload[...] = jnp.zeros_like(payload)
    payload[0:1, :] = total
    payload[1:2, :] = out
    payload[8:16, :] = prod
    payload[16:24, :] = flow


def gate_grads(which, keep, carried, st, share, cand, du, dv, w, nmt, z, out, gnm, small):
    length, units = carried.shape
    half = units // 2
    cols = pl.ds(pl.multiple_of(which * half, half), half)
    cf = carried[:, cols]
    q = share[:, cols]
    s = cf * (st[0:length, cols] * keep - cand[:, cols])
    ga = s * du[:, cols]
    gb = -(s * dv[:, cols])
    small[pl.ds(which, 1), :] = jnp.sum(ga, axis=0, keepdims=True)
    small[pl.ds(2 + which, 1), :] = jnp.sum(gb, axis=0, keepdims=True)
    part = nmt.shape[0] // 4
    for k, g in enumerate((ga, gb, cf * q)):
        low = g.astype(bf16)
        got = dot(nmt[...], low)
        for zz in range(4):
            for p in range(4):
                top = zz * part + p * (part // 4)
                out[p, zz ^ z, k * (part // 4) : (k + 1) * (part // 4), :] = got[top : top + part // 4].astype(bf16)
        gnm[...] += dot_nt(low, w[k, :, cols])


def mixer_back(idx, resets, own, r1, r2, r3, decay, share, cand, du, dv, st, grad_states, nmt, w,
               carried, send, gnm, small, others, carry8):
    length, units = decay.shape
    steps = length // chunks
    core, z = idx[0], idx[2]
    for j, ref in enumerate((own, r1, r2, r3)):
        others[j] = ref[0:8, :]
    flow = jnp.zeros((1, units), f32)
    for k in range(3, -1, -1):
        part = others[k ^ z]
        flow = jnp.where(k > z, flow * part[0:1] + part[1:2], flow)
    for k in range(chunks - 1, -1, -1):
        carry8[k : k + 1, :] = flow
        flow = flow * own[8 + k : 9 + k, :] + own[16 + k : 17 + k, :]

    def step(i, flow):
        rows = pl.ds(pl.multiple_of((steps - 1 - i) * chunks, chunks), chunks)
        got = grad_states[rows, :] + flow
        carried[rows, :] = got
        return got * decay[rows, :]

    lax.fori_loop(0, steps, step, carry8[...], unroll=8)
    gnm[...] = jnp.zeros_like(gnm)
    small[...] = jnp.zeros_like(small)
    gate_grads(1 - core, keep_mask(idx, resets, length), carried, st, share, cand, du, dv, w, nmt, z, send, gnm, small)


def mixer_out(idx, resets, carried, share, cand, du, dv, st, nmt, w, gnm0, small0, small1, x, gain, grad_mid,
              keep, grad_tok, small, gnm, split):
    length, units = carried.shape
    core, z = idx[0], idx[2]
    gnm[...] = gnm0[...]
    small[...] = small0[...] + small1[...]
    gate_grads(core, keep_mask(idx, resets, length), carried, st, share, cand, du, dv, w, nmt, z, keep, gnm, small)
    v = x[...]
    r = lax.rsqrt(jnp.mean(v * v, axis=-1, keepdims=True) + norm_eps)
    scaled = v * r
    g = gnm[...]
    small[4:5, :] = jnp.sum(g * scaled, axis=0, keepdims=True)
    gg = g * gain[...]
    gnm[...] = grad_mid[...] + r * (gg - scaled * jnp.mean(gg * scaled, axis=-1, keepdims=True))
    from_chunked(gnm, split, grad_tok)


def pick_piece(idx, wu, wd, out):
    rows = wu.shape[0] // 8
    at = pl.ds(pl.multiple_of((idx[0] * 4 + idx[1]) * rows, rows), rows)
    out[0:rows, :] = wu[at, :]
    out[rows:, :] = wd[at, :]


def join3(a, b, c, out):
    n = a.shape[0]
    out[0:n, :] = a[...]
    out[n : 2 * n, :] = b[...]
    out[2 * n :, :] = c[...]


def two_terms(v):
    high = v.astype(bf16)
    return high, (v - high.astype(f32)).astype(bf16)


def add_plane(idx, keep, got, s1, s2, s3, own):
    plane = idx[1]
    for k, ref in ((1, s1), (2, s2), (3, s3)):
        at = plane ^ k
        ref[...] = (keep[at].astype(f32) + got[at].astype(f32)).astype(bf16)
    own[...] = keep[plane].astype(f32) + got[plane].astype(f32)


def add_depth(own, g1, g2, g3, s1, s2, s3, out):
    rows = out.shape[0]
    for k, ref in enumerate((out, s1, s2, s3)):
        at = pl.ds(k * rows, rows)
        total = (own[at, :] + g1[at, :].astype(f32)) + (g2[at, :].astype(f32) + g3[at, :].astype(f32))
        ref[...] = total.astype(ref.dtype)


def add_last(own, g1, g2, g3, out):
    total = (own[...] + g1[...].astype(f32)) + (g2[...].astype(f32) + g3[...].astype(f32))
    out[...] = total.astype(out.dtype)


def add_plane_small(idx, keep, got, small, small_got, s1, s2, s3, own, small_out):
    plane = idx[1]
    rows, n = own.shape[0], small.shape[0]
    high, low = two_terms(small[...] + small_got[...])
    small_out[0:n, :] = high
    small_out[n:, :] = low
    for k, ref in ((1, s1), (2, s2), (3, s3)):
        at = plane ^ k
        ref[0:rows, :] = (keep[at].astype(f32) + got[at].astype(f32)).astype(bf16)
        ref[rows : rows + n, :] = high
        ref[rows + n :, :] = low
    own[...] = keep[plane].astype(f32) + got[plane].astype(f32)


def add_depth_small(idx, own, small, g1, g2, g3, s1, s2, s3, out, small_out, parts):
    plane = idx[1]
    total_rows, n, rows = own.shape[0], small_out.shape[0], out.shape[0]
    parts[plane] = small[0:n, :].astype(f32) + small[n:, :].astype(f32)
    for k, ref in ((1, g1), (2, g2), (3, g3)):
        parts[plane ^ k] = ref[total_rows : total_rows + n, :].astype(f32) + ref[total_rows + n :, :].astype(f32)
    tiny = (parts[0] + parts[1]) + (parts[2] + parts[3])
    small_out[...] = tiny
    high, low = two_terms(tiny)
    for k, ref in enumerate((out, s1, s2, s3)):
        at = pl.ds(k * rows, rows)
        total = (own[at, :] + g1[at, :].astype(f32)) + (g2[at, :].astype(f32) + g3[at, :].astype(f32))
        ref[0:rows, :] = total.astype(ref.dtype)
        if k:
            ref[rows : rows + n, :] = high
            ref[rows + n :, :] = low


def add_last_small(own, small, g1, g2, g3, out, small_out):
    rows, n = own.shape[0], small.shape[0]
    total = own[...]
    tiny = small[...]
    for ref in (g1, g2, g3):
        total = total + ref[0:rows, :].astype(f32)
        tiny = tiny + (ref[rows : rows + n, :].astype(f32) + ref[rows + n :, :].astype(f32))
    out[...] = total.astype(out.dtype)
    small_out[...] = tiny


def spread_mlp(idx, a0, a1, a2, a3, b0, b1, b2, b3, up, down, w_out):
    core, plane = idx[0], idx[1]
    rows = up.shape[0] // 8
    rows_out = w_out.shape[0] // 8
    for which, pieces in ((core, (a0, a1, a2, a3)), (1 - core, (b0, b1, b2, b3))):
        for k, piece in enumerate(pieces):
            spot = which * 4 + (plane ^ k)
            at = pl.ds(pl.multiple_of(spot * rows, rows), rows)
            up[at, :] = piece[0:rows, :].astype(f32)
            down[at, :] = piece[rows : 2 * rows, :].astype(f32)
            w_out[pl.ds(pl.multiple_of(spot * rows_out, rows_out), rows_out), :] = piece[2 * rows :, :].astype(f32)


def spread_mix(idx, small, a0, a1, a2, a3, b0, b1, b2, b3, out, bias_f, bias_i, gain_mix, gain_mlp, b_up):
    core, plane, z = idx[0], idx[1], idx[2]
    rows, half = out.shape[1] // 4, out.shape[2] // 2
    for which, pieces in ((core, (a0, a1, a2, a3)), (1 - core, (b0, b1, b2, b3))):
        for k, piece in enumerate(pieces):
            at = pl.ds(pl.multiple_of((plane ^ k) * rows, rows), rows)
            cols = pl.ds(pl.multiple_of(which * half, half), half)
            for i in range(3):
                out[i, at, cols] = piece[i * rows : (i + 1) * rows, :].astype(f32)
    n = bias_f.shape[1]
    cols = pl.ds(pl.multiple_of((z % 2) * n, n), n)
    bias_f[...] = small[pl.ds(z // 2, 1), cols]
    bias_i[...] = small[pl.ds(2 + z // 2, 1), cols]
    n = gain_mix.shape[1]
    cols = pl.ds(pl.multiple_of(z * n, n), n)
    gain_mix[...] = small[4:5, cols]
    gain_mlp[...] = small[5:6, cols]
    b_up[...] = small[pl.ds(6 + z, 1), :]


def swap(value, axis, bit):
    size = lax.axis_size(axis)
    return lax.ppermute(value, axis, [(i, i ^ bit) for i in range(size)])


def on_device(tokens, gain_mix, w_mix, bias_forget, bias_input, w_out, gain_mlp, w_up, b_up, w_down, resets, cotangent):
    length, width = tokens.shape[1:]
    units = w_out.shape[0]
    ff = w_up.shape[1]
    dp, mp = lax.axis_size("dp"), lax.axis_size("mp")
    assert mp == 4 and dp % 8 == 0 and tokens.shape[0] == 1
    place = lax.axis_index("dp")
    idx = jnp.stack([place & 1, (place >> 1) & 3, lax.axis_index("mp")]).astype(jnp.int32)
    tok, cot, res = tokens[0], cotangent[0], resets[0]
    w3 = w_mix.transpose(1, 0, 2)
    row = lambda v: v.reshape(1, -1)
    lanes = width // 128

    (piece,) = call(pick_piece, "pick_piece", (idx, w_up, w_down), [shape_of(bf16, width // 4, ff)])
    depth = [swap(piece, "mp", j) for j in (1, 2, 3)]
    (cat,) = call(join3, "join3", depth, [shape_of(bf16, 3 * width // 4, ff)], smem=0)
    near = [cat] + [swap(cat, "dp", 2 * k) for k in (1, 2, 3)]
    far = [swap(v, "dp", 1) for v in near]

    wide = shape_of(f32, length, units)
    square = shape_of(f32, length, width)
    square16 = shape_of(bf16, length, width)
    edge = shape_of(f32, chunks, units)
    decay, share, cand, du, dv, nmt, x, prods, ends, payload = call(
        mixer_in, "mixer_in",
        (idx, res, tok, row(gain_mix), w3, row(bias_forget), row(bias_input), row(b_up)),
        [wide] * 5 + [shape_of(bf16, width, length), square, edge, edge, edge],
        [pltpu.VMEM((lanes, length, 128), f32)], smem=2, flops=6 * length * width * units, moved=16 << 20,
    )
    ahead = [swap(payload, "mp", j) for j in (1, 2, 3)]
    quarter = width // 8
    st, stT, middle, nm2, nm2t, cotp, mix, gn, bsum, keep0, send0 = call(
        block_mid, "block_mid",
        (idx, payload, *ahead, prods, ends, decay, share, cand, x, cot, w_out, row(gain_mlp), w_up, w_down, row(b_up)),
        [shape_of(f32, length + chunks, units), shape_of(bf16, units, length), square, square16, shape_of(bf16, width, length),
         square16, square, square, shape_of(f32, 1, ff)] + [shape_of(bf16, 4, 1, 2 * quarter, width)] * 2,
        [pltpu.VMEM((lanes, length, 128), f32), pltpu.VMEM((4, chunks, units), f32), pltpu.VMEM((ff, length), bf16),
         pltpu.VMEM((chunks, units), f32)],
        flops=16 * length * width * width, moved=16 << 20,
    )
    rows_f = 2 * quarter + units // 32
    mixed, keep, send, grad_mid, grad_states, payload, small = call(
        block_mlp, "block_mlp",
        (idx, *near, *far, *ahead, mix, gn, bsum, keep0, send0, nm2, nm2t, cotp, middle, row(gain_mlp), stT, w_out, decay),
        [square16] + [shape_of(bf16, 4, 4, rows_f, width)] * 2 + [square, wide, shape_of(f32, 24, units), shape_of(f32, 16, width)],
        [pltpu.VMEM((length, width), f32)] * 2 + [pltpu.VMEM((ff, length), bf16), pltpu.VMEM((width, ff), bf16),
         pltpu.VMEM((ff, width), bf16), pltpu.VMEM((lanes, length, 128), f32)],
        flops=44 * length * width * width, moved=24 << 20,
    )
    behind = [swap(payload, "mp", j) for j in (1, 2, 3)]

    flat = lambda v: v.reshape(4, -1, width)
    got = swap(send, "dp", 1)
    s1, s2, s3, own = call(add_plane, "add_plane", (idx, flat(keep), flat(got)),
                           [shape_of(bf16, 4 * rows_f, width)] * 3 + [shape_of(f32, 4 * rows_f, width)], moved=8 << 20)
    got = [swap(v, "dp", 2 * k) for k, v in ((1, s1), (2, s2), (3, s3))]
    s1, s2, s3, own = call(add_depth, "add_depth", (own, *got),
                           [shape_of(bf16, rows_f, width)] * 3 + [shape_of(f32, rows_f, width)], smem=0, moved=4 << 20)
    got = [swap(v, "mp", j) for j, v in ((1, s1), (2, s2), (3, s3))]
    across = [[g * 8 + i for g in range(dp // 8)] for i in range(8)]

    def last(fn, name, operands, outs):
        if dp == 8:
            return call(fn, name, operands, outs, smem=0, moved=1 << 20)
        done = call(fn, name, operands, [shape_of(f32, *o.shape) for o in outs], smem=0, moved=1 << 20)
        return [lax.psum(v, "dp", axis_index_groups=across).astype(o.dtype) for v, o in zip(done, outs)]

    (part,) = last(add_last, "add_last", (own, *got), [shape_of(bf16, rows_f, width)])
    near = [part] + [swap(part, "dp", 2 * k) for k in (1, 2, 3)]
    far = [swap(v, "dp", 1) for v in near]
    grad_up, grad_down, grad_out = call(
        spread_mlp, "spread_mlp", (idx, *near, *far),
        [shape_of(f32, width, ff), shape_of(f32, ff, width), shape_of(f32, units // 4, width)], moved=6 << 20,
    )

    rows_m = 3 * width // 16
    carried, send, gnm, small_a = call(
        mixer_back, "mixer_back",
        (idx, res, payload, *behind, decay, share, cand, du, dv, st, grad_states, nmt, w3),
        [wide, shape_of(bf16, 4, 4, rows_m, units // 2), square, shape_of(f32, 16, width)],
        [pltpu.VMEM((4, chunks, units), f32), pltpu.VMEM((chunks, units), f32)],
        smem=2, flops=6 * length * width * units, moved=16 << 20,
    )
    got = swap(send, "dp", 1)
    keep, grad_tok, small = call(
        mixer_out, "mixer_out",
        (idx, res, carried, share, cand, du, dv, st, nmt, w3, gnm, small_a, small, x, row(gain_mix), grad_mid),
        [shape_of(bf16, 4, 4, rows_m, units // 2), square16, shape_of(f32, 16, width)],
        [pltpu.VMEM((length, width), f32), pltpu.VMEM((lanes, length, 128), f32)],
        smem=2, flops=6 * length * width * units, moved=16 << 20,
    )
    small_got = swap(small, "dp", 1)
    s1, s2, s3, own, small = call(
        add_plane_small, "add_plane_small", (idx, flat(keep), flat(got), small, small_got),
        [shape_of(bf16, 4 * rows_m + 32, width)] * 3 + [shape_of(f32, 4 * rows_m, width), shape_of(bf16, 32, width)], moved=6 << 20,
    )
    got = [swap(v, "dp", 2 * k) for k, v in ((1, s1), (2, s2), (3, s3))]
    s1, s2, s3, own, small = call(
        add_depth_small, "add_depth_small", (idx, own, small, *got),
        [shape_of(bf16, rows_m + 32, width)] * 3 + [shape_of(f32, rows_m, width), shape_of(f32, 16, width)],
        [pltpu.VMEM((4, 16, width), f32)], moved=2 << 20,
    )
    got = [swap(v, "mp", j) for j, v in ((1, s1), (2, s2), (3, s3))]
    part, small = last(add_last_small, "add_last_small", (own, small, *got),
                       [shape_of(bf16, rows_m, width), shape_of(f32, 16, width)])
    near = [part] + [swap(part, "dp", 2 * k) for k in (1, 2, 3)]
    far = [swap(v, "dp", 1) for v in near]
    grad_mix, g_bf, g_bi, g_gain_mix, g_gain_mlp, g_bu = call(
        spread_mix, "spread_mix", (idx, small, *near, *far),
        [shape_of(f32, 3, width // 4, units), shape_of(f32, 1, units // 4), shape_of(f32, 1, units // 4),
         shape_of(f32, 1, width // 4), shape_of(f32, 1, width // 4), shape_of(f32, 1, ff)], moved=3 << 20,
    )
    return (
        mixed[None], grad_tok[None], g_gain_mix[0], grad_mix.transpose(1, 0, 2), g_bf[0], g_bi[0],
        grad_out, g_gain_mlp[0], grad_up, g_bu[0], grad_down,
    )


def solution(mesh):
    return jax.shard_map(
        on_device,
        mesh=mesh,
        in_specs=(P("dp", "mp", None), P(), P(), P(), P(), P(), P(), P(None, "mp"), P("mp"), P("mp", None), P("dp", None), P("dp", "mp", None)),
        out_specs=(P("dp", "mp", None), P("dp", "mp", None), P("mp"), P("mp", None, None), P("mp"), P("mp"), P("mp", None), P("mp"), P(None, "mp"), P("mp"), P("mp", None)),
        check_vma=False,
    )
```

time: 652 us -> 229 us (0.35)
  waiting for transfers between devices: 369 us -> 92.9 us
  other arithmetic: 96.1 us -> 0.08 us
  blocking collectives: 75.6 us -> 0 us
  Pallas kernels: 0 us -> 61.7 us
  starting transfers between devices: 0.28 us -> 59.2 us
  matrix products: 51.2 us -> 0 us
  local copies, waits for them, and re-layouts: 38.3 us -> 12.7 us
  between operations: 16.4 us -> 0.84 us
    reduce_scatter x4 -> x0, waiting for transfers between devices: 231 us -> none  [the longest x1 107 us: on_device(): lax.psum_scatter(local_grads_all[1], 'mp', scatter_dimension=0, tiled=True)]
    all_gather x2 -> x0, waiting for transfers between devices: 93.3 us -> none  [the longest x1 52.1 us: on_device(): lax.all_gather(normed_mlp.reshape(row_total, width), 'mp', axis=0, tiled=...]
    ppermute x0 -> x45, waiting for transfers between devices: none -> 92.9 us  [swap(): return lax.ppermute(value, axis, [(i, i ^ bit) for i in range(size)])]
    pallas_call x0 -> x15, Pallas kernels: none -> 61.7 us  [call(): pl.pallas_call(body, out_shape=outs, in_specs=[SMEM] * smem + [VMEM] * (l...]
    ppermute x0 -> x45, starting transfers between devices: none -> 59.2 us  [swap(): return lax.ppermute(value, axis, [(i, i ^ bit) for i in range(size)])]
    another operation x12 -> x1, other arithmetic: 56.7 us -> 0.08 us  [on_device(): jnp.stack([place & 1, place >> 1 & 3, lax.axis_index('mp')])]
    dot_general x12 -> x0, matrix products: 51.2 us -> none  [the longest x1 6.92 us: on_device(): jnp.einsum('nd,fd->nf', cot_all, w_down, preferred_element_type=jnp.float32)]
    all_gather x4 -> x0, blocking collectives: 45 us -> none  [carried_in(): everything = jax.tree.map(lambda part: lax.all_gather(part, axis), shard)]
  transfers between devices with their start and end apart: 7 -> 45, of which waited for: 6 -> 16; matrix products, arithmetic and copies ran while one was open for 14% -> 0% of each run, Pallas kernels for 0% -> 19%
where the time goes in v1:
time: 229 us; the launch traced here: 227 us
  waiting for transfers between devices  92.9 us (41%)
  Pallas kernels  61.7 us (27%)
  starting transfers between devices  59.2 us (26%)
  local copies, waits for them, and re-layouts  12.7 us (6%)
    ppermute x45, waiting for transfers between devices, swap(): return lax.ppermute(value, axis, [(i, i ^ bit) for i in range(size)])  92.9 us
    pallas_call x15, Pallas kernels, call(): pl.pallas_call(body, out_shape=outs, in_specs=[SMEM] * smem + [VMEM] * (l...  61.7 us
    ppermute x45, starting transfers between devices, swap(): return lax.ppermute(value, axis, [(i, i ^ bit) for i in range(size)])  59.2 us
    unnamed x42, local copies, waits for them, and re-layouts  12.7 us
  transfers between devices with their start and end apart: 45, of which 16 were waited for; matrix products, arithmetic and copies ran while one was open for 0% of the time, Pallas kernels for 19%

profile of v1, /device:TPU:1, one launch (start us, length us, event | category | flops | bytes accessed | tf_op | source)
XLA Modules:
  0.0 227.3 jit_solution(12698153961877533004)
XLA Ops:
  3.4 4.2 %collective-permute-start.2 = (bf16[128,512]{1,0:T(8,128)(2,1)S(1)}, bf16[128,512]{1,0:T(8,128)(2,1)S(1)}, u32[]{:S(2)}, u32[]{:S(2)}) collective-permute-start(bf16[128,512]{1,0:T(8,128)(2,1)S(1)} %pick_piece.1), channel_id=1, source_target_pairs={{0,3},{1,2},{2,1},{3,0},{4,7},{5,6},{6,5},{7,4},{8,11},{9,10},{10,... | collective-permute-start | bytes 393224 | tf_op jit(solution)/shard_map/ppermute | solution.py:443
  8.0 2.9 %collective-permute-done.2.c = bf16[128,512]{1,0:T(8,128)(2,1)S(1)} collective-permute-done((bf16[128,512]{1,0:T(8,128)(2,1)S(1)}, bf16[128,512]{1,0:T(8,128)(2,1)S(1)}, u32[]{:S(2)}, u32[]{:S(2)}) %collective-permute-start.2) | collective-permute-done | bytes 131104 | tf_op jit(solution)/shard_map/ppermute | solution.py:443
  10.9 7.4 %collective-permute-done.1.b = bf16[128,512]{1,0:T(8,128)(2,1)S(1)} collective-permute-done((bf16[128,512]{1,0:T(8,128)(2,1)S(1)}, bf16[128,512]{1,0:T(8,128)(2,1)S(1)}, u32[]{:S(2)}, u32[]{:S(2)}) %collective-permute-start.1) | collective-permute-done | bytes 131104 | tf_op jit(solution)/shard_map/ppermute | solution.py:443
  18.3 2.2 collective-permute-start.5
  21.0 2.2 collective-permute-start.6
  23.2 5.3 %collective-permute-done.5.a3 = bf16[384,512]{1,0:T(8,128)(2,1)S(1)} collective-permute-done((bf16[384,512]{1,0:T(8,128)(2,1)S(1)}, bf16[384,512]{1,0:T(8,128)(2,1)S(1)}, u32[]{:S(2)}, u32[]{:S(2)}) %collective-permute-start.5) | collective-permute-done | bytes 393248 | tf_op jit(solution)/shard_map/ppermute | solution.py:443
  28.5 4.2 %collective-permute-start.9 = (bf16[384,512]{1,0:T(8,128)(2,1)S(1)}, bf16[384,512]{1,0:T(8,128)(2,1)S(1)}, u32[]{:S(2)}, u32[]{:S(2)}) collective-permute-start(bf16[384,512]{1,0:T(8,128)(2,1)S(1)} %collective-permute-done.5.a3), channel_id=1, source_target_pairs={{0,4},{4,0},{8,12},{12,8},{16,20},{20,16},{24,28},{28,24},{1,5},{5... | collective-permute-start | bytes 1179656 | tf_op jit(solution)/shard_map/ppermute | solution.py:443
  32.7 6.0 %collective-permute-done.4.a2 = bf16[384,512]{1,0:T(8,128)(2,1)S(1)} collective-permute-done((bf16[384,512]{1,0:T(8,128)(2,1)S(1)}, bf16[384,512]{1,0:T(8,128)(2,1)S(1)}, u32[]{:S(2)}, u32[]{:S(2)}) %collective-permute-start.4) | collective-permute-done | bytes 393248 | tf_op jit(solution)/shard_map/ppermute | solution.py:443
  43.8 9.2 %mixer_in.1 = (f32[512,1024]{1,0:T(8,128)S(1)}, f32[512,1024]{1,0:T(8,128)}, f32[512,1024]{1,0:T(8,128)}, f32[512,1024]{1,0:T(8,128)}, f32[512,1024]{1,0:T(8,128...) custom-call(s32[3]{0:T(128)S(1)} %pad_add_fusion.idx, ...), custom_call_target="tpu_custom_call" | custom-call | flops 1610612736 | bytes 16777216 | tf_op jit(solution)/shard_map/mixer_in/pallas_call | solution.py:33
  55.2 2.0 collective-permute-start.12
  57.3 2.6 %collective-permute-done.12.r3 = f32[8,1024]{1,0:T(8,128)S(1)} collective-permute-done((f32[8,1024]{1,0:T(8,128)S(1)}, f32[8,1024]{1,0:T(8,128)S(1)}, u32[]{:S(2)}, u32[]{:S(2)}) %collective-permute-start.12) | collective-permute-done | bytes 32800 | tf_op jit(solution)/shard_map/ppermute | solution.py:443
  59.8 3.7 %collective-permute-done.11.r2 = f32[8,1024]{1,0:T(8,128)S(1)} collective-permute-done((f32[8,1024]{1,0:T(8,128)S(1)}, f32[8,1024]{1,0:T(8,128)S(1)}, u32[]{:S(2)}, u32[]{:S(2)}) %collective-permute-start.11) | collective-permute-done | bytes 32800 | tf_op jit(solution)/shard_map/ppermute | solution.py:443
  63.5 2.8 %collective-permute-done.10.r1 = f32[8,1024]{1,0:T(8,128)S(1)} collective-permute-done((f32[8,1024]{1,0:T(8,128)S(1)}, f32[8,1024]{1,0:T(8,128)S(1)}, u32[]{:S(2)}, u32[]{:S(2)}) %collective-permute-start.10) | collective-permute-done | bytes 32800 | tf_op jit(solution)/shard_map/ppermute | solution.py:443
  66.3 8.8 %block_mid.1 = (f32[520,1024]{1,0:T(8,128)}, bf16[1024,512]{1,0:T(8,128)(2,1)S(1)}, f32[512,512]{1,0:T(8,128)}, bf16[512,512]{1,0:T(8,128)(2,1)S(1)}, bf16[512,5...) custom-call(s32[3]{0:T(128)S(1)} %pad_add_fusion.idx, ...), custom_call_target="tpu_custom_call" | custom-call | flops 2147483648 | bytes 16777216 | tf_op jit(solution)/shard_map/block_mid/pallas_call | solution.py:33
  76.1 16.1 %block_mlp.1 = (bf16[512,512]{1,0:T(8,128)(2,1)}, bf16[4,4,160,512]{3,2,1,0:T(8,128)(2,1)}, bf16[4,4,160,512]{3,2,1,0:T(8,128)(2,1)}, f32[512,512]{1,0:T(8,128)}...) custom-call(s32[3]{0:T(128)S(1)} %pad_add_fusion.idx, bf16[384,512]{1,0:T(8,128)(2,1)S(1)} %join3.1.a0, ...), custom_call_target="tpu_custom_call" | custom-call | flops 5905580032 | bytes 25165824 | tf_op jit(solution)/shard_map/block_mlp/pallas_call | solution.py:33
  92.2 3.8 %collective-permute-start.31 = (bf16[4,4,160,512]{3,2,1,0:T(8,128)(2,1)}, bf16[4,4,160,512]{3,2,1,0:T(8,128)(2,1)S(1)}, u32[]{:S(2)}, u32[]{:S(2)}) collective-permute-start(bf16[4,4,160,512]{3,2,1,0:T(8,128)(2,1)} %get-tuple-element.125), channel_id=1, source_target_pairs={{0,4},{4,0},{8,12},{12,8},{16,20},{20,16},{24,28},{28,24},{1,5},{5... | collective-permute-start | bytes 7864328 | tf_op jit(solution)/shard_map/ppermute | solution.py:443
  96.0 2.0 collective-permute-start.15
  99.6 2.7 %collective-permute-done.15.r3 = f32[24,1024]{1,0:T(8,128)S(1)} collective-permute-done((f32[24,1024]{1,0:T(8,128)S(1)}, f32[24,1024]{1,0:T(8,128)S(1)}, u32[]{:S(2)}, u32[]{:S(2)}) %collective-permute-start.15) | collective-permute-done | bytes 98336 | tf_op jit(solution)/shard_map/ppermute | solution.py:443
  102.3 4.5 %collective-permute-done.14.r2 = f32[24,1024]{1,0:T(8,128)S(1)} collective-permute-done((f32[24,1024]{1,0:T(8,128)S(1)}, f32[24,1024]{1,0:T(8,128)S(1)}, u32[]{:S(2)}, u32[]{:S(2)}) %collective-permute-start.14) | collective-permute-done | bytes 98336 | tf_op jit(solution)/shard_map/ppermute | solution.py:443
  106.8 8.9 %mixer_back.1 = (f32[512,1024]{1,0:T(8,128)S(1)}, bf16[4,4,96,512]{3,2,1,0:T(8,128)(2,1)S(1)}, f32[512,512]{1,0:T(8,128)S(1)}, f32[16,512]{1,0:T(8,128)S(1)}) custom-call(s32[3]{0:T(128)S(1)} %pad_add_fusion.idx, s32[3]{0:T(128)S(1)} %bitcast.29, f32[24,1024]{1,0:T(8,128)S(1)} %get-tuple-element.93.own, f32[24,1024]{1,0:T(8,128)S(1)} %collective-permute-done.13.r1, ...), custom_call_target="tpu_custom_call" | custom-call | flops 1610612736 | bytes 16777216 | tf_op jit(solution)/shard_map/mixer_back/pallas_call | solution.py:33
  117.6 9.7 %mixer_out.1 = (bf16[4,4,96,512]{3,2,1,0:T(8,128)(2,1)S(1)}, bf16[512,512]{1,0:T(8,128)(2,1)}, f32[16,512]{1,0:T(8,128)S(1)}) custom-call(s32[3]{0:T(128)S(1)} %pad_add_fusion.idx, s32[3]{0:T(128)S(1)} %bitcast.30, f32[512,1024]{1,0:T(8,128)} %copy-done.8, f32[512,1024]{1,0:T(8,128)} %get-tuple-element.79.share, f32[512,1024]{1,0:T(8,128)} %get-tuple-element.80.cand, ...), custom_call_target="tpu_custom_call" | custom-call | flops 1610612736 | bytes 16777216 | tf_op jit(solution)/shard_map/mixer_out/pallas_call | solution.py:33
  132.2 2.3 %add_plane.1 = (bf16[640,512]{1,0:T(8,128)(2,1)S(1)}, bf16[640,512]{1,0:T(8,128)(2,1)S(1)}, bf16[640,512]{1,0:T(8,128)(2,1)S(1)}, f32[640,512]{1,0:T(8,128)S(1)}) custom-call(s32[3]{0:T(128)S(1)} %pad_add_fusion.idx, bf16[4,640,512]{2,1,0:T(8,128)(2,1)S(1)} %bitcast.24, bf16[4,640,512]{2,1,0:T(8,128)(2,1)} %bitcast.43), custom_call_target="tpu_custom_call" | custom-call | bytes 8388608 | tf_op jit(solution)/shard_map/add_plane/pallas_call | solution.py:33
  137.8 3.0 %collective-permute-done.18.g1 = bf16[416,512]{1,0:T(8,128)(2,1)S(1)} collective-permute-done((bf16[416,512]{1,0:T(8,128)(2,1)S(1)}, bf16[416,512]{1,0:T(8,128)(2,1)S(1)}, u32[]{:S(2)}, u32[]{:S(2)}) %collective-permute-start.18) | collective-permute-done | bytes 426016 | tf_op jit(solution)/shard_map/ppermute | solution.py:443
  142.2 40.5 %collective-permute-done.19.g2 = bf16[416,512]{1,0:T(8,128)(2,1)S(1)} collective-permute-done((bf16[416,512]{1,0:T(8,128)(2,1)S(1)}, bf16[416,512]{1,0:T(8,128)(2,1)S(1)}, u32[]{:S(2)}, u32[]{:S(2)}) %collective-permute-start.19) | collective-permute-done | bytes 426016 | tf_op jit(solution)/shard_map/ppermute | solution.py:443
  183.8 2.1 collective-permute-start.22
  187.4 2.3 %collective-permute-start.36 = (bf16[160,512]{1,0:T(8,128)(2,1)S(1)}, bf16[160,512]{1,0:T(8,128)(2,1)S(1)}, u32[]{:S(2)}, u32[]{:S(2)}) collective-permute-start(bf16[160,512]{1,0:T(8,128)(2,1)S(1)} %get-tuple-element.132), channel_id=1, source_target_pairs={{0,2},{1,3},{2,0},{3,1},{4,6},{5,7},{6,4},{7,5},{8,10},{9,11},{10,... | collective-permute-start | bytes 491528 | tf_op jit(solution)/shard_map/ppermute | solution.py:443
  191.3 2.1 collective-permute-done.23.g3
  193.5 4.6 %collective-permute-start.27 = (bf16[96,512]{1,0:T(8,128)(2,1)S(1)}, bf16[96,512]{1,0:T(8,128)(2,1)S(1)}, u32[]{:S(2)}, u32[]{:S(2)}) collective-permute-start(bf16[96,512]{1,0:T(8,128)(2,1)S(1)} %get-tuple-element.119.a0), channel_id=1, source_target_pairs={{0,4},{4,0},{8,12},{12,8},{16,20},{20,16},{24,28},{28,24},{1,5},{5... | collective-permute-start | bytes 294920 | tf_op jit(solution)/shard_map/ppermute | solution.py:443
  200.5 7.1 %collective-permute-done.36.g2 = bf16[160,512]{1,0:T(8,128)(2,1)S(1)} collective-permute-done((bf16[160,512]{1,0:T(8,128)(2,1)S(1)}, bf16[160,512]{1,0:T(8,128)(2,1)S(1)}, u32[]{:S(2)}, u32[]{:S(2)}) %collective-permute-start.36) | collective-permute-done | bytes 163872 | tf_op jit(solution)/shard_map/ppermute | solution.py:443
  211.6 4.7 %collective-permute-start.30 = (bf16[96,512]{1,0:T(8,128)(2,1)S(1)}, bf16[96,512]{1,0:T(8,128)(2,1)S(1)}, u32[]{:S(2)}, u32[]{:S(2)}) collective-permute-start(bf16[96,512]{1,0:T(8,128)(2,1)S(1)} %collective-permute-done.26.a3), channel_id=1, source_target_pairs={{0,4},{4,0},{8,12},{12,8},{16,20},{20,16},{24,28},{28,24},{1,5},{5... | collective-permute-start | bytes 294920 | tf_op jit(solution)/shard_map/ppermute | solution.py:443
  216.5 4.5 %collective-permute-start.29 = (bf16[96,512]{1,0:T(8,128)(2,1)S(1)}, bf16[96,512]{1,0:T(8,128)(2,1)S(1)}, u32[]{:S(2)}, u32[]{:S(2)}) collective-permute-start(bf16[96,512]{1,0:T(8,128)(2,1)S(1)} %collective-permute-done.25.a2), channel_id=1, source_target_pairs={{0,4},{4,0},{8,12},{12,8},{16,20},{20,16},{24,28},{28,24},{1,5},{5... | collective-permute-start | bytes 294920 | tf_op jit(solution)/shard_map/ppermute | solution.py:443
  225.2 2.2 spread_mlp.1
  (116 shorter events, 40.0 us)
Async XLA Ops:
  3.4 7.5 %collective-permute-start.2 = (bf16[128,512]{1,0:T(8,128)(2,1)S(1)}, bf16[128,512]{1,0:T(8,128)(2,1)S(1)}, u32[]{:S(2)}, u32[]{:S(2)}) collective-permute-start(bf16[128,512]{1,0:T(8,128)(2,1)S(1)} %pick_piece.1), channel_id=1, source_target_pairs={{0,3},{1,2},{2,1},{3,0},{4,7},{5,6},{6,5},{7,4},{8,11},{9,10},{10,... | collective-permute-start | bytes 393224 | tf_op jit(solution)/shard_map/ppermute | solution.py:443
  7.6 10.7 %collective-permute-start.1 = (bf16[128,512]{1,0:T(8,128)(2,1)S(1)}, bf16[128,512]{1,0:T(8,128)(2,1)S(1)}, u32[]{:S(2)}, u32[]{:S(2)}) collective-permute-start(bf16[128,512]{1,0:T(8,128)(2,1)S(1)} %pick_piece.1), channel_id=1, source_target_pairs={{0,2},{1,3},{2,0},{3,1},{4,6},{5,7},{6,4},{7,5},{8,10},{9,11},{10,... | collective-permute-start | bytes 393224 | tf_op jit(solution)/shard_map/ppermute | solution.py:443
  7.6 10.7 %collective-permute-start = (bf16[128,512]{1,0:T(8,128)(2,1)S(1)}, bf16[128,512]{1,0:T(8,128)(2,1)S(1)}, u32[]{:S(2)}, u32[]{:S(2)}) collective-permute-start(bf16[128,512]{1,0:T(8,128)(2,1)S(1)} %pick_piece.1), channel_id=1, source_target_pairs={{0,1},{1,0},{2,3},{3,2},{4,5},{5,4},{6,7},{7,6},{8,9},{9,8},{10,11... | collective-permute-start | bytes 393224 | tf_op jit(solution)/shard_map/ppermute | solution.py:443
  18.3 10.3 %collective-permute-start.5 = (bf16[384,512]{1,0:T(8,128)(2,1)S(1)}, bf16[384,512]{1,0:T(8,128)(2,1)S(1)}, u32[]{:S(2)}, u32[]{:S(2)}) collective-permute-start(bf16[384,512]{1,0:T(8,128)(2,1)S(1)} %join3.1.a0), channel_id=1, source_target_pairs={{0,24},{4,28},{8,16},{12,20},{16,8},{20,12},{24,0},{28,4},{1,25},{... | collective-permute-start | bytes 1179656 | tf_op jit(solution)/shard_map/ppermute | solution.py:443
  20.5 18.2 %collective-permute-start.4 = (bf16[384,512]{1,0:T(8,128)(2,1)S(1)}, bf16[384,512]{1,0:T(8,128)(2,1)S(1)}, u32[]{:S(2)}, u32[]{:S(2)}) collective-permute-start(bf16[384,512]{1,0:T(8,128)(2,1)S(1)} %join3.1.a0), channel_id=1, source_target_pairs={{0,16},{4,20},{8,24},{12,28},{16,0},{20,4},{24,8},{28,12},{1,17},{... | collective-permute-start | bytes 1179656 | tf_op jit(solution)/shard_map/ppermute | solution.py:443
  20.8 18.5 %collective-permute-start.3 = (bf16[384,512]{1,0:T(8,128)(2,1)S(1)}, bf16[384,512]{1,0:T(8,128)(2,1)S(1)}, u32[]{:S(2)}, u32[]{:S(2)}) collective-permute-start(bf16[384,512]{1,0:T(8,128)(2,1)S(1)} %join3.1.a0), channel_id=1, source_target_pairs={{0,8},{4,12},{8,0},{12,4},{16,24},{20,28},{24,16},{28,20},{1,9},{5... | collective-permute-start | bytes 1179656 | tf_op jit(solution)/shard_map/ppermute | solution.py:443
  21.0 55.1 %collective-permute-start.6 = (bf16[384,512]{1,0:T(8,128)(2,1)S(1)}, bf16[384,512]{1,0:T(8,128)(2,1)S(1)}, u32[]{:S(2)}, u32[]{:S(2)}) collective-permute-start(bf16[384,512]{1,0:T(8,128)(2,1)S(1)} %join3.1.a0), channel_id=1, source_target_pairs={{0,4},{4,0},{8,12},{12,8},{16,20},{20,16},{24,28},{28,24},{1,5},{5... | collective-permute-start | bytes 1179656 | tf_op jit(solution)/shard_map/ppermute | solution.py:443
  28.5 47.5 %collective-permute-start.9 = (bf16[384,512]{1,0:T(8,128)(2,1)S(1)}, bf16[384,512]{1,0:T(8,128)(2,1)S(1)}, u32[]{:S(2)}, u32[]{:S(2)}) collective-permute-start(bf16[384,512]{1,0:T(8,128)(2,1)S(1)} %collective-permute-done.5.a3), channel_id=1, source_target_pairs={{0,4},{4,0},{8,12},{12,8},{16,20},{20,16},{24,28},{28,24},{1,5},{5... | collective-permute-start | bytes 1179656 | tf_op jit(solution)/shard_map/ppermute | solution.py:443
  38.7 37.4 %collective-permute-start.8 = (bf16[384,512]{1,0:T(8,128)(2,1)S(1)}, bf16[384,512]{1,0:T(8,128)(2,1)S(1)}, u32[]{:S(2)}, u32[]{:S(2)}) collective-permute-start(bf16[384,512]{1,0:T(8,128)(2,1)S(1)} %collective-permute-done.4.a2), channel_id=1, source_target_pairs={{0,4},{4,0},{8,12},{12,8},{16,20},{20,16},{24,28},{28,24},{1,5},{5... | collective-permute-start | bytes 1179656 | tf_op jit(solution)/shard_map/ppermute | solution.py:443
  39.2 36.9 %collective-permute-start.7 = (bf16[384,512]{1,0:T(8,128)(2,1)S(1)}, bf16[384,512]{1,0:T(8,128)(2,1)S(1)}, u32[]{:S(2)}, u32[]{:S(2)}) collective-permute-start(bf16[384,512]{1,0:T(8,128)(2,1)S(1)} %collective-permute-done.3.a1), channel_id=1, source_target_pairs={{0,4},{4,0},{8,12},{12,8},{16,20},{20,16},{24,28},{28,24},{1,5},{5... | collective-permute-start | bytes 1179656 | tf_op jit(solution)/shard_map/ppermute | solution.py:443
  92.2 38.5 %collective-permute-start.31 = (bf16[4,4,160,512]{3,2,1,0:T(8,128)(2,1)}, bf16[4,4,160,512]{3,2,1,0:T(8,128)(2,1)S(1)}, u32[]{:S(2)}, u32[]{:S(2)}) collective-permute-start(bf16[4,4,160,512]{3,2,1,0:T(8,128)(2,1)} %get-tuple-element.125), channel_id=1, source_target_pairs={{0,4},{4,0},{8,12},{12,8},{16,20},{20,16},{24,28},{28,24},{1,5},{5... | collective-permute-start | bytes 7864328 | tf_op jit(solution)/shard_map/ppermute | solution.py:443
  98.0 8.7 %collective-permute-start.14 = (f32[24,1024]{1,0:T(8,128)S(1)}, f32[24,1024]{1,0:T(8,128)S(1)}, u32[]{:S(2)}, u32[]{:S(2)}) collective-permute-start(f32[24,1024]{1,0:T(8,128)S(1)} %get-tuple-element.93.own), channel_id=1, source_target_pairs={{0,2},{1,3},{2,0},{3,1},{4,6},{5,7},{6,4},{7,5},{8,10},{9,11},{10,... | collective-permute-start | bytes 294920 | tf_op jit(solution)/shard_map/ppermute | solution.py:443
  98.0 8.7 %collective-permute-start.13 = (f32[24,1024]{1,0:T(8,128)S(1)}, f32[24,1024]{1,0:T(8,128)S(1)}, u32[]{:S(2)}, u32[]{:S(2)}) collective-permute-start(f32[24,1024]{1,0:T(8,128)S(1)} %get-tuple-element.93.own), channel_id=1, source_target_pairs={{0,1},{1,0},{2,3},{3,2},{4,5},{5,4},{6,7},{7,6},{8,9},{9,8},{10,11... | collective-permute-start | bytes 294920 | tf_op jit(solution)/shard_map/ppermute | solution.py:443
  117.1 11.4 %collective-permute-start.16 = (bf16[4,4,96,512]{3,2,1,0:T(8,128)(2,1)S(1)}, bf16[4,4,96,512]{3,2,1,0:T(8,128)(2,1)S(1)}, u32[]{:S(2)}, u32[]{:S(2)}) collective-permute-start(bf16[4,4,96,512]{3,2,1,0:T(8,128)(2,1)S(1)} %get-tuple-element.106), channel_id=1, source_target_pairs={{0,4},{4,0},{8,12},{12,8},{16,20},{20,16},{24,28},{28,24},{1,5},{5... | collective-permute-start | bytes 4718600 | tf_op jit(solution)/shard_map/ppermute | solution.py:443
  129.4 11.3 %collective-permute-start.18 = (bf16[416,512]{1,0:T(8,128)(2,1)S(1)}, bf16[416,512]{1,0:T(8,128)(2,1)S(1)}, u32[]{:S(2)}, u32[]{:S(2)}) collective-permute-start(bf16[416,512]{1,0:T(8,128)(2,1)S(1)} %get-tuple-element.110), channel_id=1, source_target_pairs={{0,8},{4,12},{8,0},{12,4},{16,24},{20,28},{24,16},{28,20},{1,9},{5... | collective-permute-start | bytes 1277960 | tf_op jit(solution)/shard_map/ppermute | solution.py:443
  134.5 51.3 %collective-permute-start.32 = (bf16[640,512]{1,0:T(8,128)(2,1)S(1)}, bf16[640,512]{1,0:T(8,128)(2,1)S(1)}, u32[]{:S(2)}, u32[]{:S(2)}) collective-permute-start(bf16[640,512]{1,0:T(8,128)(2,1)S(1)} %get-tuple-element.127), channel_id=1, source_target_pairs={{0,8},{4,12},{8,0},{12,4},{16,24},{20,28},{24,16},{28,20},{1,9},{5... | collective-permute-start | bytes 1966088 | tf_op jit(solution)/shard_map/ppermute | solution.py:443
  134.8 52.3 %collective-permute-start.33 = (bf16[640,512]{1,0:T(8,128)(2,1)S(1)}, bf16[640,512]{1,0:T(8,128)(2,1)S(1)}, u32[]{:S(2)}, u32[]{:S(2)}) collective-permute-start(bf16[640,512]{1,0:T(8,128)(2,1)S(1)} %get-tuple-element.128), channel_id=1, source_target_pairs={{0,16},{4,20},{8,24},{12,28},{16,0},{20,4},{24,8},{28,12},{1,17},{... | collective-permute-start | bytes 1966088 | tf_op jit(solution)/shard_map/ppermute | solution.py:443
  136.1 51.0 %collective-permute-start.34 = (bf16[640,512]{1,0:T(8,128)(2,1)S(1)}, bf16[640,512]{1,0:T(8,128)(2,1)S(1)}, u32[]{:S(2)}, u32[]{:S(2)}) collective-permute-start(bf16[640,512]{1,0:T(8,128)(2,1)S(1)} %get-tuple-element.129), channel_id=1, source_target_pairs={{0,24},{4,28},{8,16},{12,20},{16,8},{20,12},{24,0},{28,4},{1,25},{... | collective-permute-start | bytes 1966088 | tf_op jit(solution)/shard_map/ppermute | solution.py:443
  137.2 45.4 %collective-permute-start.19 = (bf16[416,512]{1,0:T(8,128)(2,1)S(1)}, bf16[416,512]{1,0:T(8,128)(2,1)S(1)}, u32[]{:S(2)}, u32[]{:S(2)}) collective-permute-start(bf16[416,512]{1,0:T(8,128)(2,1)S(1)} %get-tuple-element.111), channel_id=1, source_target_pairs={{0,16},{4,20},{8,24},{12,28},{16,0},{20,4},{24,8},{28,12},{1,17},{... | collective-permute-start | bytes 1277960 | tf_op jit(solution)/shard_map/ppermute | solution.py:443
  140.7 41.9 %collective-permute-start.20 = (bf16[416,512]{1,0:T(8,128)(2,1)S(1)}, bf16[416,512]{1,0:T(8,128)(2,1)S(1)}, u32[]{:S(2)}, u32[]{:S(2)}) collective-permute-start(bf16[416,512]{1,0:T(8,128)(2,1)S(1)} %get-tuple-element.112), channel_id=1, source_target_pairs={{0,24},{4,28},{8,16},{12,20},{16,8},{20,12},{24,0},{28,4},{1,25},{... | collective-permute-start | bytes 1277960 | tf_op jit(solution)/shard_map/ppermute | solution.py:443
  183.8 7.5 %collective-permute-start.22 = (bf16[128,512]{1,0:T(8,128)(2,1)S(1)}, bf16[128,512]{1,0:T(8,128)(2,1)S(1)}, u32[]{:S(2)}, u32[]{:S(2)}) collective-permute-start(bf16[128,512]{1,0:T(8,128)(2,1)S(1)} %get-tuple-element.116), channel_id=1, source_target_pairs={{0,2},{1,3},{2,0},{3,1},{4,6},{5,7},{6,4},{7,5},{8,10},{9,11},{10,... | collective-permute-start | bytes 393224 | tf_op jit(solution)/shard_map/ppermute | solution.py:443
  185.8 7.6 %collective-permute-start.23 = (bf16[128,512]{1,0:T(8,128)(2,1)S(1)}, bf16[128,512]{1,0:T(8,128)(2,1)S(1)}, u32[]{:S(2)}, u32[]{:S(2)}) collective-permute-start(bf16[128,512]{1,0:T(8,128)(2,1)S(1)} %get-tuple-element.117), channel_id=1, source_target_pairs={{0,3},{1,2},{2,1},{3,0},{4,7},{5,6},{6,5},{7,4},{8,11},{9,10},{10,... | collective-permute-start | bytes 393224 | tf_op jit(solution)/shard_map/ppermute | solution.py:443
  187.4 12.2 %collective-permute-start.35 = (bf16[160,512]{1,0:T(8,128)(2,1)S(1)}, bf16[160,512]{1,0:T(8,128)(2,1)S(1)}, u32[]{:S(2)}, u32[]{:S(2)}) collective-permute-start(bf16[160,512]{1,0:T(8,128)(2,1)S(1)} %get-tuple-element.131), channel_id=1, source_target_pairs={{0,1},{1,0},{2,3},{3,2},{4,5},{5,4},{6,7},{7,6},{8,9},{9,8},{10,11... | collective-permute-start | bytes 491528 | tf_op jit(solution)/shard_map/ppermute | solution.py:443
  187.4 20.1 %collective-permute-start.36 = (bf16[160,512]{1,0:T(8,128)(2,1)S(1)}, bf16[160,512]{1,0:T(8,128)(2,1)S(1)}, u32[]{:S(2)}, u32[]{:S(2)}) collective-permute-start(bf16[160,512]{1,0:T(8,128)(2,1)S(1)} %get-tuple-element.132), channel_id=1, source_target_pairs={{0,2},{1,3},{2,0},{3,1},{4,6},{5,7},{6,4},{7,5},{8,10},{9,11},{10,... | collective-permute-start | bytes 491528 | tf_op jit(solution)/shard_map/ppermute | solution.py:443
  189.7 17.8 %collective-permute-start.37 = (bf16[160,512]{1,0:T(8,128)(2,1)S(1)}, bf16[160,512]{1,0:T(8,128)(2,1)S(1)}, u32[]{:S(2)}, u32[]{:S(2)}) collective-permute-start(bf16[160,512]{1,0:T(8,128)(2,1)S(1)} %get-tuple-element.133), channel_id=1, source_target_pairs={{0,3},{1,2},{2,1},{3,0},{4,7},{5,6},{6,5},{7,4},{8,11},{9,10},{10,... | collective-permute-start | bytes 491528 | tf_op jit(solution)/shard_map/ppermute | solution.py:443
  193.5 16.7 %collective-permute-start.27 = (bf16[96,512]{1,0:T(8,128)(2,1)S(1)}, bf16[96,512]{1,0:T(8,128)(2,1)S(1)}, u32[]{:S(2)}, u32[]{:S(2)}) collective-permute-start(bf16[96,512]{1,0:T(8,128)(2,1)S(1)} %get-tuple-element.119.a0), channel_id=1, source_target_pairs={{0,4},{4,0},{8,12},{12,8},{16,20},{20,16},{24,28},{28,24},{1,5},{5... | collective-permute-start | bytes 294920 | tf_op jit(solution)/shard_map/ppermute | solution.py:443
  198.1 12.3 %collective-permute-start.26 = (bf16[96,512]{1,0:T(8,128)(2,1)S(1)}, bf16[96,512]{1,0:T(8,128)(2,1)S(1)}, u32[]{:S(2)}, u32[]{:S(2)}) collective-permute-start(bf16[96,512]{1,0:T(8,128)(2,1)S(1)} %get-tuple-element.119.a0), channel_id=1, source_target_pairs={{0,24},{4,28},{8,16},{12,20},{16,8},{20,12},{24,0},{28,4},{1,25},{... | collective-permute-start | bytes 294920 | tf_op jit(solution)/shard_map/ppermute | solution.py:443
  199.6 12.0 %collective-permute-start.25 = (bf16[96,512]{1,0:T(8,128)(2,1)S(1)}, bf16[96,512]{1,0:T(8,128)(2,1)S(1)}, u32[]{:S(2)}, u32[]{:S(2)}) collective-permute-start(bf16[96,512]{1,0:T(8,128)(2,1)S(1)} %get-tuple-element.119.a0), channel_id=1, source_target_pairs={{0,16},{4,20},{8,24},{12,28},{16,0},{20,4},{24,8},{28,12},{1,17},{... | collective-permute-start | bytes 294920 | tf_op jit(solution)/shard_map/ppermute | solution.py:443
  207.7 13.3 %collective-permute-start.40 = (bf16[160,512]{1,0:T(8,128)(2,1)S(1)}, bf16[160,512]{1,0:T(8,128)(2,1)S(1)}, u32[]{:S(2)}, u32[]{:S(2)}) collective-permute-start(bf16[160,512]{1,0:T(8,128)(2,1)S(1)} %add_last.1.a0), channel_id=1, source_target_pairs={{0,24},{4,28},{8,16},{12,20},{16,8},{20,12},{24,0},{28,4},{1,25},{... | collective-permute-start | bytes 491528 | tf_op jit(solution)/shard_map/ppermute | solution.py:443
  209.2 12.3 %collective-permute-start.39 = (bf16[160,512]{1,0:T(8,128)(2,1)S(1)}, bf16[160,512]{1,0:T(8,128)(2,1)S(1)}, u32[]{:S(2)}, u32[]{:S(2)}) collective-permute-start(bf16[160,512]{1,0:T(8,128)(2,1)S(1)} %add_last.1.a0), channel_id=1, source_target_pairs={{0,16},{4,20},{8,24},{12,28},{16,0},{20,4},{24,8},{28,12},{1,17},{... | collective-permute-start | bytes 491528 | tf_op jit(solution)/shard_map/ppermute | solution.py:443
  210.1 11.4 %collective-permute-start.38 = (bf16[160,512]{1,0:T(8,128)(2,1)S(1)}, bf16[160,512]{1,0:T(8,128)(2,1)S(1)}, u32[]{:S(2)}, u32[]{:S(2)}) collective-permute-start(bf16[160,512]{1,0:T(8,128)(2,1)S(1)} %add_last.1.a0), channel_id=1, source_target_pairs={{0,8},{4,12},{8,0},{12,4},{16,24},{20,28},{24,16},{28,20},{1,9},{5... | collective-permute-start | bytes 491528 | tf_op jit(solution)/shard_map/ppermute | solution.py:443
  211.6 9.4 %collective-permute-start.30 = (bf16[96,512]{1,0:T(8,128)(2,1)S(1)}, bf16[96,512]{1,0:T(8,128)(2,1)S(1)}, u32[]{:S(2)}, u32[]{:S(2)}) collective-permute-start(bf16[96,512]{1,0:T(8,128)(2,1)S(1)} %collective-permute-done.26.a3), channel_id=1, source_target_pairs={{0,4},{4,0},{8,12},{12,8},{16,20},{20,16},{24,28},{28,24},{1,5},{5... | collective-permute-start | bytes 294920 | tf_op jit(solution)/shard_map/ppermute | solution.py:443
  (34 other events, 192.9 us)

commit v2 on v1

--- a/solution.py
+++ b/solution.py
@@ -29,17 +29,22 @@
     return jax.ShapeDtypeStruct(shape, dtype)
 
 
-def call(body, name, operands, outs, scratch=(), smem=1, flops=0, moved=0):
+def call(body, name, operands, outs, scratch=(), smem=1, flops=0, moved=0, limit=16, after=()):
+    n, extra = len(operands), len(after)
+
+    def run(*refs):
+        body(*refs[:n], *refs[n + extra :])
+
     return pl.pallas_call(
-        body,
+        run,
         out_shape=outs,
-        in_specs=[SMEM] * smem + [VMEM] * (len(operands) - smem),
+        in_specs=[SMEM] * smem + [VMEM] * (n - smem) + [pl.BlockSpec(memory_space=pl.ANY)] * extra,
         out_specs=[VMEM] * len(outs),
         scratch_shapes=list(scratch),
-        compiler_params=pltpu.CompilerParams(vmem_limit_bytes=48 << 20),
+        compiler_params=pltpu.CompilerParams(vmem_limit_bytes=limit << 20),
         cost_estimate=pl.CostEstimate(flops=flops, bytes_accessed=moved, transcendentals=0),
         name=name,
-    )(*operands)
+    )(*operands, *after)
 
 
 def to_chunked(src, split, put):
@@ -323,10 +328,24 @@
 
 
 def pick_piece(idx, wu, wd, out):
-    rows = wu.shape[0] // 8
-    at = pl.ds(pl.multiple_of((idx[0] * 4 + idx[1]) * rows, rows), rows)
-    out[0:rows, :] = wu[at, :]
-    out[rows:, :] = wd[at, :]
+    rows = wu.shape[0]
+    out[0:rows, :] = wu[...]
+    out[rows:, :] = wd[...]
+
+
+def own_piece(idx, w_up, w_down):
+    rows, width = w_up.shape[0] // 8, w_up.shape[1]
+    eighth = pl.BlockSpec((rows, width), lambda i, idx: (idx[0] * 4 + idx[1], 0))
+    return pl.pallas_call(
+        pick_piece,
+        out_shape=shape_of(bf16, 2 * rows, width),
+        grid_spec=pltpu.PrefetchScalarGridSpec(
+            num_scalar_prefetch=1, grid=(1,), in_specs=[eighth, eighth],
+            out_specs=pl.BlockSpec((2 * rows, width), lambda i, idx: (0, 0)),
+        ),
+        compiler_params=pltpu.CompilerParams(vmem_limit_bytes=2 << 20),
+        name="pick_piece",
+    )(idx, w_up, w_down)
 
 
 def join3(a, b, c, out):
@@ -456,11 +475,8 @@
     row = lambda v: v.reshape(1, -1)
     lanes = width // 128
 
-    (piece,) = call(pick_piece, "pick_piece", (idx, w_up, w_down), [shape_of(bf16, width // 4, ff)])
+    piece = own_piece(idx, w_up, w_down)
     depth = [swap(piece, "mp", j) for j in (1, 2, 3)]
-    (cat,) = call(join3, "join3", depth, [shape_of(bf16, 3 * width // 4, ff)], smem=0)
-    near = [cat] + [swap(cat, "dp", 2 * k) for k in (1, 2, 3)]
-    far = [swap(v, "dp", 1) for v in near]
 
     wide = shape_of(f32, length, units)
     square = shape_of(f32, length, width)
@@ -470,9 +486,12 @@
         mixer_in, "mixer_in",
         (idx, res, tok, row(gain_mix), w3, row(bias_forget), row(bias_input), row(b_up)),
         [wide] * 5 + [shape_of(bf16, width, length), square, edge, edge, edge],
-        [pltpu.VMEM((lanes, length, 128), f32)], smem=2, flops=6 * length * width * units, moved=16 << 20,
+        [pltpu.VMEM((lanes, length, 128), f32)], smem=2, flops=6 * length * width * units, moved=16 << 20, after=(piece,),
     )
     ahead = [swap(payload, "mp", j) for j in (1, 2, 3)]
+    (cat,) = call(join3, "join3", depth, [shape_of(bf16, 3 * width // 4, ff)], smem=0, after=(payload,))
+    near = [cat] + [swap(cat, "dp", 2 * k) for k in (1, 2, 3)]
+    far = [swap(v, "dp", 1) for v in near]
     quarter = width // 8
     st, stT, middle, nm2, nm2t, cotp, mix, gn, bsum, keep0, send0 = call(
         block_mid, "block_mid",
@@ -496,10 +515,10 @@
 
     flat = lambda v: v.reshape(4, -1, width)
     got = swap(send, "dp", 1)
-    s1, s2, s3, own = call(add_plane, "add_plane", (idx, flat(keep), flat(got)),
+    s1, s2, s3, own_mlp = call(add_plane, "add_plane", (idx, flat(keep), flat(got)),
                            [shape_of(bf16, 4 * rows_f, width)] * 3 + [shape_of(f32, 4 * rows_f, width)], moved=8 << 20)
     got = [swap(v, "dp", 2 * k) for k, v in ((1, s1), (2, s2), (3, s3))]
-    s1, s2, s3, own = call(add_depth, "add_depth", (own, *got),
+    s1, s2, s3, own = call(add_depth, "add_depth", (own_mlp, *got),
                            [shape_of(bf16, rows_f, width)] * 3 + [shape_of(f32, rows_f, width)], smem=0, moved=4 << 20)
     got = [swap(v, "mp", j) for j, v in ((1, s1), (2, s2), (3, s3))]
     across = [[g * 8 + i for g in range(dp // 8)] for i in range(8)]
@@ -524,7 +543,7 @@
         (idx, res, payload, *behind, decay, share, cand, du, dv, st, grad_states, nmt, w3),
         [wide, shape_of(bf16, 4, 4, rows_m, units // 2), square, shape_of(f32, 16, width)],
         [pltpu.VMEM((4, chunks, units), f32), pltpu.VMEM((chunks, units), f32)],
-        smem=2, flops=6 * length * width * units, moved=16 << 20,
+        smem=2, flops=6 * length * width * units, moved=16 << 20, after=(own_mlp,),
     )
     got = swap(send, "dp", 1)
     keep, grad_tok, small = call(

time: 229 us -> 164 us (0.72)
  waiting for transfers between devices: 92.9 us -> 55.7 us
  Pallas kernels: 61.7 us -> 35.9 us
  local copies, waits for them, and re-layouts: 12.7 us -> 8.44 us
  starting transfers between devices: 59.2 us -> 62 us
    ppermute x45, waiting for transfers between devices: 92.9 us -> 55.7 us  [swap(): return lax.ppermute(value, axis, [(i, i ^ bit) for i in range(size)])]
    pallas_call x15, Pallas kernels: 61.7 us -> 35.9 us  [the longest x14 35.3 us: call(): pl.pallas_call(run, out_shape=outs, in_specs=[SMEM] * smem + [VMEM] * (n...]
    unnamed x42 -> x36, local copies, waits for them, and re-layouts: 12.7 us -> 8.44 us
    ppermute x45, starting transfers between devices: 59.2 us -> 62 us  [swap(): return lax.ppermute(value, axis, [(i, i ^ bit) for i in range(size)])]
  transfers between devices with their start and end apart: 45 -> 45, of which waited for: 16 -> 17; matrix products, arithmetic and copies ran while one was open for 0% -> 0% of each run, Pallas kernels for 19% -> 12%
where the time goes in v2:
time: 164 us; the launch traced here: 163 us
  starting transfers between devices  62 us (38%)
  waiting for transfers between devices  55.7 us (34%)
  Pallas kernels  35.9 us (22%)
  local copies, waits for them, and re-layouts  8.44 us (5%)
    ppermute x45, starting transfers between devices, swap(): return lax.ppermute(value, axis, [(i, i ^ bit) for i in range(size)])  62 us
    ppermute x45, waiting for transfers between devices, swap(): return lax.ppermute(value, axis, [(i, i ^ bit) for i in range(size)])  55.7 us
    pallas_call x14, Pallas kernels, call(): pl.pallas_call(run, out_shape=outs, in_specs=[SMEM] * smem + [VMEM] * (n...  35.3 us
    unnamed x36, local copies, waits for them, and re-layouts  8.44 us
  transfers between devices with their start and end apart: 45, of which 17 were waited for; matrix products, arithmetic and copies ran while one was open for 0% of the time, Pallas kernels for 12%

profile of v2, /device:TPU:1, one launch (start us, length us, event | category | flops | bytes accessed | tf_op | source)
XLA Modules:
  0.0 163.0 jit_solution(4596196517060985399)
XLA Ops:
  3.4 4.2 %collective-permute-start.2 = (bf16[128,512]{1,0:T(8,128)(2,1)S(1)}, bf16[128,512]{1,0:T(8,128)(2,1)S(1)}, u32[]{:S(2)}, u32[]{:S(2)}) collective-permute-start(bf16[128,512]{1,0:T(8,128)(2,1)S(1)} %pick_piece.1.refs_8_), channel_id=1, source_target_pairs={{0,3},{1,2},{2,1},{3,0},{4,7},{5,6},{6,5},{7,4},{8,11},{9,10},{10,... | collective-permute-start | bytes 393224 | tf_op jit(solution)/shard_map/ppermute | solution.py:462
  8.0 1.9 %copy-done = bf16[512,3,1024]{2,0,1:T(8,128)(2,1)S(1)} copy-done((bf16[512,3,1024]{2,0,1:T(8,128)(2,1)S(1)}, bf16[512,3,1024]{2,0,1:T(8,128)(2,1)}, u32[]{:S(2)}) %copy-start) | copy-done | bytes 3145752
  14.3 4.6 %mixer_in.1 = (f32[512,1024]{1,0:T(8,128)S(1)}, f32[512,1024]{1,0:T(8,128)S(1)}, f32[512,1024]{1,0:T(8,128)S(1)}, f32[512,1024]{1,0:T(8,128)S(1)}, f32[512,1024]...) custom-call(s32[3]{0:T(128)S(1)} %pad_add_fusion.idx.refs_0_, ...), custom_call_target="tpu_custom_call" | custom-call | flops 1610612736 | bytes 16777216 | tf_op jit(solution)/shard_map/mixer_in/pallas_call | solution.py:38
  19.0 2.2 %collective-permute-start.5 = (bf16[384,512]{1,0:T(8,128)(2,1)S(1)}, bf16[384,512]{1,0:T(8,128)(2,1)S(1)}, u32[]{:S(2)}, u32[]{:S(2)}) collective-permute-start(bf16[384,512]{1,0:T(8,128)(2,1)S(1)} %join3.1.refs_1_), channel_id=1, source_target_pairs={{0,24},{4,28},{8,16},{12,20},{16,8},{20,12},{24,0},{28,4},{1,25},{... | collective-permute-start | bytes 1179656 | tf_op jit(solution)/shard_map/ppermute | solution.py:462
  21.7 2.1 %collective-permute-start.6 = (bf16[384,512]{1,0:T(8,128)(2,1)S(1)}, bf16[384,512]{1,0:T(8,128)(2,1)S(1)}, u32[]{:S(2)}, u32[]{:S(2)}) collective-permute-start(bf16[384,512]{1,0:T(8,128)(2,1)S(1)} %join3.1.refs_1_), channel_id=1, source_target_pairs={{0,4},{4,0},{8,12},{12,8},{16,20},{20,16},{24,28},{28,24},{1,5},{5... | collective-permute-start | bytes 1179656 | tf_op jit(solution)/shard_map/ppermute | solution.py:462
  23.8 5.6 %collective-permute-done.5.refs_4_ = bf16[384,512]{1,0:T(8,128)(2,1)S(1)} collective-permute-done((bf16[384,512]{1,0:T(8,128)(2,1)S(1)}, bf16[384,512]{1,0:T(8,128)(2,1)S(1)}, u32[]{:S(2)}, u32[]{:S(2)}) %collective-permute-start.5) | collective-permute-done | bytes 393248 | tf_op jit(solution)/shard_map/ppermute | solution.py:462
  29.4 3.9 %collective-permute-start.9 = (bf16[384,512]{1,0:T(8,128)(2,1)S(1)}, bf16[384,512]{1,0:T(8,128)(2,1)S(1)}, u32[]{:S(2)}, u32[]{:S(2)}) collective-permute-start(bf16[384,512]{1,0:T(8,128)(2,1)S(1)} %collective-permute-done.5.refs_4_), channel_id=1, source_target_pairs={{0,4},{4,0},{8,12},{12,8},{16,20},{20,16},{24,28},{28,24},{1,5},{5... | collective-permute-start | bytes 1179656 | tf_op jit(solution)/shard_map/ppermute | solution.py:462
  33.3 6.1 %collective-permute-done.4.refs_3_ = bf16[384,512]{1,0:T(8,128)(2,1)S(1)} collective-permute-done((bf16[384,512]{1,0:T(8,128)(2,1)S(1)}, bf16[384,512]{1,0:T(8,128)(2,1)S(1)}, u32[]{:S(2)}, u32[]{:S(2)}) %collective-permute-start.4) | collective-permute-done | bytes 393248 | tf_op jit(solution)/shard_map/ppermute | solution.py:462
  40.1 3.2 %collective-permute-start.12 = (f32[8,1024]{1,0:T(8,128)S(1)}, f32[8,1024]{1,0:T(8,128)S(1)}, u32[]{:S(2)}, u32[]{:S(2)}) collective-permute-start(f32[8,1024]{1,0:T(8,128)S(1)} %get-tuple-element.75.refs_3_.refs_1_), channel_id=1, source_target_pairs={{0,3},{1,2},{2,1},{3,0},{4,7},{5,6},{6,5},{7,4},{8,11},{9,10},{10,... | collective-permute-start | bytes 98312 | tf_op jit(solution)/shard_map/ppermute | solution.py:462
  44.8 3.6 %collective-permute-done.11.refs_3_.refs_10_ = f32[8,1024]{1,0:T(8,128)S(1)} collective-permute-done((f32[8,1024]{1,0:T(8,128)S(1)}, f32[8,1024]{1,0:T(8,128)S(1)}, u32[]{:S(2)}, u32[]{:S(2)}) %collective-permute-start.11) | collective-permute-done | bytes 32800 | tf_op jit(solution)/shard_map/ppermute | solution.py:462
  49.4 1.8 %collective-permute-done.10.refs_2_.refs_9_ = f32[8,1024]{1,0:T(8,128)S(1)} collective-permute-done((f32[8,1024]{1,0:T(8,128)S(1)}, f32[8,1024]{1,0:T(8,128)S(1)}, u32[]{:S(2)}, u32[]{:S(2)}) %collective-permute-start.10) | collective-permute-done | bytes 32800 | tf_op jit(solution)/shard_map/ppermute | solution.py:462
  51.2 4.7 %block_mid.1 = (f32[520,1024]{1,0:T(8,128)S(1)}, bf16[1024,512]{1,0:T(8,128)(2,1)S(1)}, f32[512,512]{1,0:T(8,128)S(1)}, bf16[512,512]{1,0:T(8,128)(2,1)S(1)}, bf...) custom-call(s32[3]{0:T(128)S(1)} %pad_add_fusion.idx.refs_0_, ...), custom_call_target="tpu_custom_call" | custom-call | flops 2147483648 | bytes 16777216 | tf_op jit(solution)/shard_map/block_mid/pallas_call | solution.py:38
  56.0 10.9 %block_mlp.1 = (bf16[512,512]{1,0:T(8,128)(2,1)}, bf16[4,4,160,512]{3,2,1,0:T(8,128)(2,1)S(1)}, bf16[4,4,160,512]{3,2,1,0:T(8,128)(2,1)S(1)}, f32[512,512]{1,0:T...) custom-call(s32[3]{0:T(128)S(1)} %pad_add_fusion.idx.refs_0_, ...), custom_call_target="tpu_custom_call" | custom-call | flops 5905580032 | bytes 25165824 | tf_op jit(solution)/shard_map/block_mlp/pallas_call | solution.py:38
  66.8 3.8 %collective-permute-start.16 = (bf16[4,4,160,512]{3,2,1,0:T(8,128)(2,1)S(1)}, bf16[4,4,160,512]{3,2,1,0:T(8,128)(2,1)S(1)}, u32[]{:S(2)}, u32[]{:S(2)}) collective-permute-start(bf16[4,4,160,512]{3,2,1,0:T(8,128)(2,1)S(1)} %get-tuple-element.100), channel_id=1, source_target_pairs={{0,4},{4,0},{8,12},{12,8},{16,20},{20,16},{24,28},{28,24},{1,5},{5... | collective-permute-start | bytes 7864328 | tf_op jit(solution)/shard_map/ppermute | solution.py:462
  70.6 3.2 %collective-permute-start.15 = (f32[24,1024]{1,0:T(8,128)S(1)}, f32[24,1024]{1,0:T(8,128)S(1)}, u32[]{:S(2)}, u32[]{:S(2)}) collective-permute-start(f32[24,1024]{1,0:T(8,128)S(1)} %get-tuple-element.93.refs_2_), channel_id=1, source_target_pairs={{0,3},{1,2},{2,1},{3,0},{4,7},{5,6},{6,5},{7,4},{8,11},{9,10},{10,... | collective-permute-start | bytes 294920 | tf_op jit(solution)/shard_map/ppermute | solution.py:462
  76.9 5.0 %collective-permute-done.14.refs_4_ = f32[24,1024]{1,0:T(8,128)S(1)} collective-permute-done((f32[24,1024]{1,0:T(8,128)S(1)}, f32[24,1024]{1,0:T(8,128)S(1)}, u32[]{:S(2)}, u32[]{:S(2)}) %collective-permute-start.14) | collective-permute-done | bytes 98336 | tf_op jit(solution)/shard_map/ppermute | solution.py:462
  81.9 3.0 %mixer_back.1 = (f32[512,1024]{1,0:T(8,128)S(1)}, bf16[4,4,96,512]{3,2,1,0:T(8,128)(2,1)S(1)}, f32[512,512]{1,0:T(8,128)S(1)}, f32[16,512]{1,0:T(8,128)S(1)}) custom-call(s32[3]{0:T(128)S(1)} %pad_add_fusion.idx.refs_0_, s32[3]{0:T(128)S(1)} %bitcast.33, f32[24,1024]{1,0:T(8,128)S(1)} %get-tuple-element.93.refs_2_, ...), custom_call_target="tpu_custom_call" | custom-call | flops 1610612736 | bytes 16777216 | tf_op jit(solution)/shard_map/mixer_back/pallas_call | solution.py:38
  88.4 4.8 %mixer_out.1 = (bf16[4,4,96,512]{3,2,1,0:T(8,128)(2,1)S(1)}, bf16[512,512]{1,0:T(8,128)(2,1)}, f32[16,512]{1,0:T(8,128)S(1)}) custom-call(s32[3]{0:T(128)S(1)} %pad_add_fusion.idx.refs_0_, s32[3]{0:T(128)S(1)} %bitcast.34, f32[512,1024]{1,0:T(8,128)S(1)} %get-tuple-element.102.refs_2_, f32[512,1024]{1,0:T(8,128)S(1)} %get-tuple-element.79.refs_8_.refs_7_.refs_3_, ...), custom_call_target="tpu_custom_call" | custom-call | flops 1610612736 | bytes 16777216 | tf_op jit(solution)/shard_map/mixer_out/pallas_call | solution.py:38
  97.7 4.3 %collective-permute-done.32.refs_1_ = bf16[640,512]{1,0:T(8,128)(2,1)S(1)} collective-permute-done((bf16[640,512]{1,0:T(8,128)(2,1)S(1)}, bf16[640,512]{1,0:T(8,128)(2,1)S(1)}, u32[]{:S(2)}, u32[]{:S(2)}) %collective-permute-start.32) | collective-permute-done | bytes 655392 | tf_op jit(solution)/shard_map/ppermute | solution.py:462
  103.5 13.6 %collective-permute-done.34.refs_3_ = bf16[640,512]{1,0:T(8,128)(2,1)S(1)} collective-permute-done((bf16[640,512]{1,0:T(8,128)(2,1)S(1)}, bf16[640,512]{1,0:T(8,128)(2,1)S(1)}, u32[]{:S(2)}, u32[]{:S(2)}) %collective-permute-start.34) | collective-permute-done | bytes 655392 | tf_op jit(solution)/shard_map/ppermute | solution.py:462
  118.1 1.8 %collective-permute-start.36 = (bf16[160,512]{1,0:T(8,128)(2,1)S(1)}, bf16[160,512]{1,0:T(8,128)(2,1)S(1)}, u32[]{:S(2)}, u32[]{:S(2)}) collective-permute-start(bf16[160,512]{1,0:T(8,128)(2,1)S(1)} %get-tuple-element.132), channel_id=1, source_target_pairs={{0,2},{1,3},{2,0},{3,1},{4,6},{5,7},{6,4},{7,5},{8,10},{9,11},{10,... | collective-permute-start | bytes 491528 | tf_op jit(solution)/shard_map/ppermute | solution.py:462
  119.9 3.2 %collective-permute-done.35.refs_1_ = bf16[160,512]{1,0:T(8,128)(2,1)S(1)} collective-permute-done((bf16[160,512]{1,0:T(8,128)(2,1)S(1)}, bf16[160,512]{1,0:T(8,128)(2,1)S(1)}, u32[]{:S(2)}, u32[]{:S(2)}) %collective-permute-start.35) | collective-permute-done | bytes 163872 | tf_op jit(solution)/shard_map/ppermute | solution.py:462
  123.1 3.4 %collective-permute-start.37 = (bf16[160,512]{1,0:T(8,128)(2,1)S(1)}, bf16[160,512]{1,0:T(8,128)(2,1)S(1)}, u32[]{:S(2)}, u32[]{:S(2)}) collective-permute-start(bf16[160,512]{1,0:T(8,128)(2,1)S(1)} %get-tuple-element.133), channel_id=1, source_target_pairs={{0,3},{1,2},{2,1},{3,0},{4,7},{5,6},{6,5},{7,4},{8,11},{9,10},{10,... | collective-permute-start | bytes 491528 | tf_op jit(solution)/shard_map/ppermute | solution.py:462
  126.5 2.8 %collective-permute-done.37.refs_3_ = bf16[160,512]{1,0:T(8,128)(2,1)S(1)} collective-permute-done((bf16[160,512]{1,0:T(8,128)(2,1)S(1)}, bf16[160,512]{1,0:T(8,128)(2,1)S(1)}, u32[]{:S(2)}, u32[]{:S(2)}) %collective-permute-start.37) | collective-permute-done | bytes 163872 | tf_op jit(solution)/shard_map/ppermute | solution.py:462
  131.4 4.0 %collective-permute-done.21.refs_5_ = bf16[416,512]{1,0:T(8,128)(2,1)S(1)} collective-permute-done((bf16[416,512]{1,0:T(8,128)(2,1)S(1)}, bf16[416,512]{1,0:T(8,128)(2,1)S(1)}, u32[]{:S(2)}, u32[]{:S(2)}) %collective-permute-start.21) | collective-permute-done | bytes 426016 | tf_op jit(solution)/shard_map/ppermute | solution.py:462
  138.6 3.6 %collective-permute-start.41 = (bf16[160,512]{1,0:T(8,128)(2,1)S(1)}, bf16[160,512]{1,0:T(8,128)(2,1)S(1)}, u32[]{:S(2)}, u32[]{:S(2)}) collective-permute-start(bf16[160,512]{1,0:T(8,128)(2,1)S(1)} %add_last.1.refs_1_), channel_id=1, source_target_pairs={{0,4},{4,0},{8,12},{12,8},{16,20},{20,16},{24,28},{28,24},{1,5},{5... | collective-permute-start | bytes 491528 | tf_op jit(solution)/shard_map/ppermute | solution.py:462
  142.5 2.0 %collective-permute-start.24 = (bf16[128,512]{1,0:T(8,128)(2,1)S(1)}, bf16[128,512]{1,0:T(8,128)(2,1)S(1)}, u32[]{:S(2)}, u32[]{:S(2)}) collective-permute-start(bf16[128,512]{1,0:T(8,128)(2,1)S(1)} %get-tuple-element.120), channel_id=1, source_target_pairs={{0,3},{1,2},{2,1},{3,0},{4,7},{5,6},{6,5},{7,4},{8,11},{9,10},{10,... | collective-permute-start | bytes 393224 | tf_op jit(solution)/shard_map/ppermute | solution.py:462
  148.2 4.4 %collective-permute-start.27 = (bf16[96,512]{1,0:T(8,128)(2,1)S(1)}, bf16[96,512]{1,0:T(8,128)(2,1)S(1)}, u32[]{:S(2)}, u32[]{:S(2)}) collective-permute-start(bf16[96,512]{1,0:T(8,128)(2,1)S(1)} %get-tuple-element.122.refs_2_), channel_id=1, source_target_pairs={{0,24},{4,28},{8,16},{12,20},{16,8},{20,12},{24,0},{28,4},{1,25},{... | collective-permute-start | bytes 294920 | tf_op jit(solution)/shard_map/ppermute | solution.py:462
  153.1 1.6 %collective-permute-start.42 = (bf16[160,512]{1,0:T(8,128)(2,1)S(1)}, bf16[160,512]{1,0:T(8,128)(2,1)S(1)}, u32[]{:S(2)}, u32[]{:S(2)}) collective-permute-start(bf16[160,512]{1,0:T(8,128)(2,1)S(1)} %collective-permute-done.38.refs_2_), channel_id=1, source_target_pairs={{0,4},{4,0},{8,12},{12,8},{16,20},{20,16},{24,28},{28,24},{1,5},{5... | collective-permute-start | bytes 491528 | tf_op jit(solution)/shard_map/ppermute | solution.py:462
  154.8 2.0 %collective-permute-start.31 = (bf16[96,512]{1,0:T(8,128)(2,1)S(1)}, bf16[96,512]{1,0:T(8,128)(2,1)S(1)}, u32[]{:S(2)}, u32[]{:S(2)}) collective-permute-start(bf16[96,512]{1,0:T(8,128)(2,1)S(1)} %collective-permute-done.27.refs_5_), channel_id=1, source_target_pairs={{0,4},{4,0},{8,12},{12,8},{16,20},{20,16},{24,28},{28,24},{1,5},{5... | collective-permute-start | bytes 294920 | tf_op jit(solution)/shard_map/ppermute | solution.py:462
  159.0 2.2 %spread_mlp.1 = (f32[512,512]{1,0:T(8,128)}, f32[512,512]{1,0:T(8,128)}, f32[256,512]{1,0:T(8,128)}) custom-call(s32[3]{0:T(128)S(1)} %pad_add_fusion.idx.refs_0_, bf16[160,512]{1,0:T(8,128)(2,1)S(1)} %add_last.1.refs_1_, bf16[160,512]{1,0:T(8,128)(2,1)S(1)} %collective-permute-done.38.refs_2_, bf16[160,512]{1,0:T(8,128)(2,1)S(1)} %collective-permute-done.39.refs_3_, ...), custom_call_target="tpu_custom_call" | custom-call | bytes 6291456 | tf_op jit(solution)/shard_map/spread_mlp/pallas_call | solution.py:38
  161.2 1.8 %spread_mix.1 = (f32[3,128,1024]{2,1,0:T(8,128)}, f32[1,256]{1,0:T(1,128)}, f32[1,256]{1,0:T(1,128)}, f32[1,128]{1,0:T(1,128)}, f32[1,128]{1,0:T(1,128)}, /*index=5*/f32[1,512]{1,0:T(1,128)}) custom-call(s32[3]{0:T(128)S(1)} %pad_add_fusion.idx.refs_0_, f32[16,512]{1,0:T(8,128)S(1)} %get-tuple-element.121.refs_1_, ...), custom_call_target="tpu_custom_call" | custom-call | bytes 3145728 | tf_op jit(solution)/shard_map/spread_mix/pallas_call | solution.py:38
  (110 shorter events, 36.8 us)
Async XLA Ops:
  3.4 15.6 %collective-permute-start.2 = (bf16[128,512]{1,0:T(8,128)(2,1)S(1)}, bf16[128,512]{1,0:T(8,128)(2,1)S(1)}, u32[]{:S(2)}, u32[]{:S(2)}) collective-permute-start(bf16[128,512]{1,0:T(8,128)(2,1)S(1)} %pick_piece.1.refs_8_), channel_id=1, source_target_pairs={{0,3},{1,2},{2,1},{3,0},{4,7},{5,6},{6,5},{7,4},{8,11},{9,10},{10,... | collective-permute-start | bytes 393224 | tf_op jit(solution)/shard_map/ppermute | solution.py:462
  7.6 11.4 %collective-permute-start.1 = (bf16[128,512]{1,0:T(8,128)(2,1)S(1)}, bf16[128,512]{1,0:T(8,128)(2,1)S(1)}, u32[]{:S(2)}, u32[]{:S(2)}) collective-permute-start(bf16[128,512]{1,0:T(8,128)(2,1)S(1)} %pick_piece.1.refs_8_), channel_id=1, source_target_pairs={{0,2},{1,3},{2,0},{3,1},{4,6},{5,7},{6,4},{7,5},{8,10},{9,11},{10,... | collective-permute-start | bytes 393224 | tf_op jit(solution)/shard_map/ppermute | solution.py:462
  7.6 11.4 %collective-permute-start = (bf16[128,512]{1,0:T(8,128)(2,1)S(1)}, bf16[128,512]{1,0:T(8,128)(2,1)S(1)}, u32[]{:S(2)}, u32[]{:S(2)}) collective-permute-start(bf16[128,512]{1,0:T(8,128)(2,1)S(1)} %pick_piece.1.refs_8_), channel_id=1, source_target_pairs={{0,1},{1,0},{2,3},{3,2},{4,5},{5,4},{6,7},{7,6},{8,9},{9,8},{10,11... | collective-permute-start | bytes 393224 | tf_op jit(solution)/shard_map/ppermute | solution.py:462
  19.0 10.4 %collective-permute-start.5 = (bf16[384,512]{1,0:T(8,128)(2,1)S(1)}, bf16[384,512]{1,0:T(8,128)(2,1)S(1)}, u32[]{:S(2)}, u32[]{:S(2)}) collective-permute-start(bf16[384,512]{1,0:T(8,128)(2,1)S(1)} %join3.1.refs_1_), channel_id=1, source_target_pairs={{0,24},{4,28},{8,16},{12,20},{16,8},{20,12},{24,0},{28,4},{1,25},{... | collective-permute-start | bytes 1179656 | tf_op jit(solution)/shard_map/ppermute | solution.py:462
  21.3 18.2 %collective-permute-start.4 = (bf16[384,512]{1,0:T(8,128)(2,1)S(1)}, bf16[384,512]{1,0:T(8,128)(2,1)S(1)}, u32[]{:S(2)}, u32[]{:S(2)}) collective-permute-start(bf16[384,512]{1,0:T(8,128)(2,1)S(1)} %join3.1.refs_1_), channel_id=1, source_target_pairs={{0,16},{4,20},{8,24},{12,28},{16,0},{20,4},{24,8},{28,12},{1,17},{... | collective-permute-start | bytes 1179656 | tf_op jit(solution)/shard_map/ppermute | solution.py:462
  21.5 18.5 %collective-permute-start.3 = (bf16[384,512]{1,0:T(8,128)(2,1)S(1)}, bf16[384,512]{1,0:T(8,128)(2,1)S(1)}, u32[]{:S(2)}, u32[]{:S(2)}) collective-permute-start(bf16[384,512]{1,0:T(8,128)(2,1)S(1)} %join3.1.refs_1_), channel_id=1, source_target_pairs={{0,8},{4,12},{8,0},{12,4},{16,24},{20,28},{24,16},{28,20},{1,9},{5... | collective-permute-start | bytes 1179656 | tf_op jit(solution)/shard_map/ppermute | solution.py:462
  21.7 34.2 %collective-permute-start.6 = (bf16[384,512]{1,0:T(8,128)(2,1)S(1)}, bf16[384,512]{1,0:T(8,128)(2,1)S(1)}, u32[]{:S(2)}, u32[]{:S(2)}) collective-permute-start(bf16[384,512]{1,0:T(8,128)(2,1)S(1)} %join3.1.refs_1_), channel_id=1, source_target_pairs={{0,4},{4,0},{8,12},{12,8},{16,20},{20,16},{24,28},{28,24},{1,5},{5... | collective-permute-start | bytes 1179656 | tf_op jit(solution)/shard_map/ppermute | solution.py:462
  29.4 26.5 %collective-permute-start.9 = (bf16[384,512]{1,0:T(8,128)(2,1)S(1)}, bf16[384,512]{1,0:T(8,128)(2,1)S(1)}, u32[]{:S(2)}, u32[]{:S(2)}) collective-permute-start(bf16[384,512]{1,0:T(8,128)(2,1)S(1)} %collective-permute-done.5.refs_4_), channel_id=1, source_target_pairs={{0,4},{4,0},{8,12},{12,8},{16,20},{20,16},{24,28},{28,24},{1,5},{5... | collective-permute-start | bytes 1179656 | tf_op jit(solution)/shard_map/ppermute | solution.py:462
  39.5 16.5 %collective-permute-start.8 = (bf16[384,512]{1,0:T(8,128)(2,1)S(1)}, bf16[384,512]{1,0:T(8,128)(2,1)S(1)}, u32[]{:S(2)}, u32[]{:S(2)}) collective-permute-start(bf16[384,512]{1,0:T(8,128)(2,1)S(1)} %collective-permute-done.4.refs_3_), channel_id=1, source_target_pairs={{0,4},{4,0},{8,12},{12,8},{16,20},{20,16},{24,28},{28,24},{1,5},{5... | collective-permute-start | bytes 1179656 | tf_op jit(solution)/shard_map/ppermute | solution.py:462
  40.0 16.0 %collective-permute-start.7 = (bf16[384,512]{1,0:T(8,128)(2,1)S(1)}, bf16[384,512]{1,0:T(8,128)(2,1)S(1)}, u32[]{:S(2)}, u32[]{:S(2)}) collective-permute-start(bf16[384,512]{1,0:T(8,128)(2,1)S(1)} %collective-permute-done.3.refs_2_), channel_id=1, source_target_pairs={{0,4},{4,0},{8,12},{12,8},{16,20},{20,16},{24,28},{28,24},{1,5},{5... | collective-permute-start | bytes 1179656 | tf_op jit(solution)/shard_map/ppermute | solution.py:462
  66.8 8.3 %collective-permute-start.16 = (bf16[4,4,160,512]{3,2,1,0:T(8,128)(2,1)S(1)}, bf16[4,4,160,512]{3,2,1,0:T(8,128)(2,1)S(1)}, u32[]{:S(2)}, u32[]{:S(2)}) collective-permute-start(bf16[4,4,160,512]{3,2,1,0:T(8,128)(2,1)S(1)} %get-tuple-element.100), channel_id=1, source_target_pairs={{0,4},{4,0},{8,12},{12,8},{16,20},{20,16},{24,28},{28,24},{1,5},{5... | collective-permute-start | bytes 7864328 | tf_op jit(solution)/shard_map/ppermute | solution.py:462
  73.8 8.1 %collective-permute-start.14 = (f32[24,1024]{1,0:T(8,128)S(1)}, f32[24,1024]{1,0:T(8,128)S(1)}, u32[]{:S(2)}, u32[]{:S(2)}) collective-permute-start(f32[24,1024]{1,0:T(8,128)S(1)} %get-tuple-element.93.refs_2_), channel_id=1, source_target_pairs={{0,2},{1,3},{2,0},{3,1},{4,6},{5,7},{6,4},{7,5},{8,10},{9,11},{10,... | collective-permute-start | bytes 294920 | tf_op jit(solution)/shard_map/ppermute | solution.py:462
  73.8 8.1 %collective-permute-start.13 = (f32[24,1024]{1,0:T(8,128)S(1)}, f32[24,1024]{1,0:T(8,128)S(1)}, u32[]{:S(2)}, u32[]{:S(2)}) collective-permute-start(f32[24,1024]{1,0:T(8,128)S(1)} %get-tuple-element.93.refs_2_), channel_id=1, source_target_pairs={{0,1},{1,0},{2,3},{3,2},{4,5},{5,4},{6,7},{7,6},{8,9},{9,8},{10,11... | collective-permute-start | bytes 294920 | tf_op jit(solution)/shard_map/ppermute | solution.py:462
  84.9 10.1 %collective-permute-start.17 = (bf16[4,4,96,512]{3,2,1,0:T(8,128)(2,1)S(1)}, bf16[4,4,96,512]{3,2,1,0:T(8,128)(2,1)S(1)}, u32[]{:S(2)}, u32[]{:S(2)}) collective-permute-start(bf16[4,4,96,512]{3,2,1,0:T(8,128)(2,1)S(1)} %get-tuple-element.109), channel_id=1, source_target_pairs={{0,4},{4,0},{8,12},{12,8},{16,20},{20,16},{24,28},{28,24},{1,5},{5... | collective-permute-start | bytes 4718600 | tf_op jit(solution)/shard_map/ppermute | solution.py:462
  85.8 16.3 %collective-permute-start.32 = (bf16[640,512]{1,0:T(8,128)(2,1)S(1)}, bf16[640,512]{1,0:T(8,128)(2,1)S(1)}, u32[]{:S(2)}, u32[]{:S(2)}) collective-permute-start(bf16[640,512]{1,0:T(8,128)(2,1)S(1)} %get-tuple-element.127), channel_id=1, source_target_pairs={{0,8},{4,12},{8,0},{12,4},{16,24},{20,28},{24,16},{28,20},{1,9},{5... | collective-permute-start | bytes 1966088 | tf_op jit(solution)/shard_map/ppermute | solution.py:462
  87.0 16.6 %collective-permute-start.33 = (bf16[640,512]{1,0:T(8,128)(2,1)S(1)}, bf16[640,512]{1,0:T(8,128)(2,1)S(1)}, u32[]{:S(2)}, u32[]{:S(2)}) collective-permute-start(bf16[640,512]{1,0:T(8,128)(2,1)S(1)} %get-tuple-element.128), channel_id=1, source_target_pairs={{0,16},{4,20},{8,24},{12,28},{16,0},{20,4},{24,8},{28,12},{1,17},{... | collective-permute-start | bytes 1966088 | tf_op jit(solution)/shard_map/ppermute | solution.py:462
  87.5 29.6 %collective-permute-start.34 = (bf16[640,512]{1,0:T(8,128)(2,1)S(1)}, bf16[640,512]{1,0:T(8,128)(2,1)S(1)}, u32[]{:S(2)}, u32[]{:S(2)}) collective-permute-start(bf16[640,512]{1,0:T(8,128)(2,1)S(1)} %get-tuple-element.129), channel_id=1, source_target_pairs={{0,24},{4,28},{8,16},{12,20},{16,8},{20,12},{24,0},{28,4},{1,25},{... | collective-permute-start | bytes 1966088 | tf_op jit(solution)/shard_map/ppermute | solution.py:462
  95.9 35.5 %collective-permute-start.19 = (bf16[416,512]{1,0:T(8,128)(2,1)S(1)}, bf16[416,512]{1,0:T(8,128)(2,1)S(1)}, u32[]{:S(2)}, u32[]{:S(2)}) collective-permute-start(bf16[416,512]{1,0:T(8,128)(2,1)S(1)} %get-tuple-element.113), channel_id=1, source_target_pairs={{0,8},{4,12},{8,0},{12,4},{16,24},{20,28},{24,16},{28,20},{1,9},{5... | collective-permute-start | bytes 1277960 | tf_op jit(solution)/shard_map/ppermute | solution.py:462
  97.2 34.2 %collective-permute-start.20 = (bf16[416,512]{1,0:T(8,128)(2,1)S(1)}, bf16[416,512]{1,0:T(8,128)(2,1)S(1)}, u32[]{:S(2)}, u32[]{:S(2)}) collective-permute-start(bf16[416,512]{1,0:T(8,128)(2,1)S(1)} %get-tuple-element.114), channel_id=1, source_target_pairs={{0,16},{4,20},{8,24},{12,28},{16,0},{20,4},{24,8},{28,12},{1,17},{... | collective-permute-start | bytes 1277960 | tf_op jit(solution)/shard_map/ppermute | solution.py:462
  102.1 33.3 %collective-permute-start.21 = (bf16[416,512]{1,0:T(8,128)(2,1)S(1)}, bf16[416,512]{1,0:T(8,128)(2,1)S(1)}, u32[]{:S(2)}, u32[]{:S(2)}) collective-permute-start(bf16[416,512]{1,0:T(8,128)(2,1)S(1)} %get-tuple-element.115), channel_id=1, source_target_pairs={{0,24},{4,28},{8,16},{12,20},{16,8},{20,12},{24,0},{28,4},{1,25},{... | collective-permute-start | bytes 1277960 | tf_op jit(solution)/shard_map/ppermute | solution.py:462
  118.1 8.5 %collective-permute-start.36 = (bf16[160,512]{1,0:T(8,128)(2,1)S(1)}, bf16[160,512]{1,0:T(8,128)(2,1)S(1)}, u32[]{:S(2)}, u32[]{:S(2)}) collective-permute-start(bf16[160,512]{1,0:T(8,128)(2,1)S(1)} %get-tuple-element.132), channel_id=1, source_target_pairs={{0,2},{1,3},{2,0},{3,1},{4,6},{5,7},{6,4},{7,5},{8,10},{9,11},{10,... | collective-permute-start | bytes 491528 | tf_op jit(solution)/shard_map/ppermute | solution.py:462
  129.4 12.9 %collective-permute-start.40 = (bf16[160,512]{1,0:T(8,128)(2,1)S(1)}, bf16[160,512]{1,0:T(8,128)(2,1)S(1)}, u32[]{:S(2)}, u32[]{:S(2)}) collective-permute-start(bf16[160,512]{1,0:T(8,128)(2,1)S(1)} %add_last.1.refs_1_), channel_id=1, source_target_pairs={{0,24},{4,28},{8,16},{12,20},{16,8},{20,12},{24,0},{28,4},{1,25},{... | collective-permute-start | bytes 491528 | tf_op jit(solution)/shard_map/ppermute | solution.py:462
  130.6 11.8 %collective-permute-start.39 = (bf16[160,512]{1,0:T(8,128)(2,1)S(1)}, bf16[160,512]{1,0:T(8,128)(2,1)S(1)}, u32[]{:S(2)}, u32[]{:S(2)}) collective-permute-start(bf16[160,512]{1,0:T(8,128)(2,1)S(1)} %add_last.1.refs_1_), channel_id=1, source_target_pairs={{0,16},{4,20},{8,24},{12,28},{16,0},{20,4},{24,8},{28,12},{1,17},{... | collective-permute-start | bytes 491528 | tf_op jit(solution)/shard_map/ppermute | solution.py:462
  136.2 8.2 %collective-permute-start.22 = (bf16[128,512]{1,0:T(8,128)(2,1)S(1)}, bf16[128,512]{1,0:T(8,128)(2,1)S(1)}, u32[]{:S(2)}, u32[]{:S(2)}) collective-permute-start(bf16[128,512]{1,0:T(8,128)(2,1)S(1)} %get-tuple-element.118), channel_id=1, source_target_pairs={{0,1},{1,0},{2,3},{3,2},{4,5},{5,4},{6,7},{7,6},{8,9},{9,8},{10,11... | collective-permute-start | bytes 393224 | tf_op jit(solution)/shard_map/ppermute | solution.py:462
  137.7 8.1 %collective-permute-start.23 = (bf16[128,512]{1,0:T(8,128)(2,1)S(1)}, bf16[128,512]{1,0:T(8,128)(2,1)S(1)}, u32[]{:S(2)}, u32[]{:S(2)}) collective-permute-start(bf16[128,512]{1,0:T(8,128)(2,1)S(1)} %get-tuple-element.119), channel_id=1, source_target_pairs={{0,2},{1,3},{2,0},{3,1},{4,6},{5,7},{6,4},{7,5},{8,10},{9,11},{10,... | collective-permute-start | bytes 393224 | tf_op jit(solution)/shard_map/ppermute | solution.py:462
  138.6 14.0 %collective-permute-start.41 = (bf16[160,512]{1,0:T(8,128)(2,1)S(1)}, bf16[160,512]{1,0:T(8,128)(2,1)S(1)}, u32[]{:S(2)}, u32[]{:S(2)}) collective-permute-start(bf16[160,512]{1,0:T(8,128)(2,1)S(1)} %add_last.1.refs_1_), channel_id=1, source_target_pairs={{0,4},{4,0},{8,12},{12,8},{16,20},{20,16},{24,28},{28,24},{1,5},{5... | collective-permute-start | bytes 491528 | tf_op jit(solution)/shard_map/ppermute | solution.py:462
  142.3 10.3 %collective-permute-start.38 = (bf16[160,512]{1,0:T(8,128)(2,1)S(1)}, bf16[160,512]{1,0:T(8,128)(2,1)S(1)}, u32[]{:S(2)}, u32[]{:S(2)}) collective-permute-start(bf16[160,512]{1,0:T(8,128)(2,1)S(1)} %add_last.1.refs_1_), channel_id=1, source_target_pairs={{0,8},{4,12},{8,0},{12,4},{16,24},{20,28},{24,16},{28,20},{1,9},{5... | collective-permute-start | bytes 491528 | tf_op jit(solution)/shard_map/ppermute | solution.py:462
  144.4 8.6 %collective-permute-start.44 = (bf16[160,512]{1,0:T(8,128)(2,1)S(1)}, bf16[160,512]{1,0:T(8,128)(2,1)S(1)}, u32[]{:S(2)}, u32[]{:S(2)}) collective-permute-start(bf16[160,512]{1,0:T(8,128)(2,1)S(1)} %collective-permute-done.40.refs_4_), channel_id=1, source_target_pairs={{0,4},{4,0},{8,12},{12,8},{16,20},{20,16},{24,28},{28,24},{1,5},{5... | collective-permute-start | bytes 491528 | tf_op jit(solution)/shard_map/ppermute | solution.py:462
  145.8 8.9 %collective-permute-start.43 = (bf16[160,512]{1,0:T(8,128)(2,1)S(1)}, bf16[160,512]{1,0:T(8,128)(2,1)S(1)}, u32[]{:S(2)}, u32[]{:S(2)}) collective-permute-start(bf16[160,512]{1,0:T(8,128)(2,1)S(1)} %collective-permute-done.39.refs_3_), channel_id=1, source_target_pairs={{0,4},{4,0},{8,12},{12,8},{16,20},{20,16},{24,28},{28,24},{1,5},{5... | collective-permute-start | bytes 491528 | tf_op jit(solution)/shard_map/ppermute | solution.py:462
  148.2 6.5 %collective-permute-start.27 = (bf16[96,512]{1,0:T(8,128)(2,1)S(1)}, bf16[96,512]{1,0:T(8,128)(2,1)S(1)}, u32[]{:S(2)}, u32[]{:S(2)}) collective-permute-start(bf16[96,512]{1,0:T(8,128)(2,1)S(1)} %get-tuple-element.122.refs_2_), channel_id=1, source_target_pairs={{0,24},{4,28},{8,16},{12,20},{16,8},{20,12},{24,0},{28,4},{1,25},{... | collective-permute-start | bytes 294920 | tf_op jit(solution)/shard_map/ppermute | solution.py:462
  154.7 6.4 %collective-permute-start.28 = (bf16[96,512]{1,0:T(8,128)(2,1)S(1)}, bf16[96,512]{1,0:T(8,128)(2,1)S(1)}, u32[]{:S(2)}, u32[]{:S(2)}) collective-permute-start(bf16[96,512]{1,0:T(8,128)(2,1)S(1)} %get-tuple-element.122.refs_2_), channel_id=1, source_target_pairs={{0,4},{4,0},{8,12},{12,8},{16,20},{20,16},{24,28},{28,24},{1,5},{5... | collective-permute-start | bytes 294920 | tf_op jit(solution)/shard_map/ppermute | solution.py:462
  154.8 6.4 %collective-permute-start.31 = (bf16[96,512]{1,0:T(8,128)(2,1)S(1)}, bf16[96,512]{1,0:T(8,128)(2,1)S(1)}, u32[]{:S(2)}, u32[]{:S(2)}) collective-permute-start(bf16[96,512]{1,0:T(8,128)(2,1)S(1)} %collective-permute-done.27.refs_5_), channel_id=1, source_target_pairs={{0,4},{4,0},{8,12},{12,8},{16,20},{20,16},{24,28},{28,24},{1,5},{5... | collective-permute-start | bytes 294920 | tf_op jit(solution)/shard_map/ppermute | solution.py:462
  (31 other events, 309.4 us)

commit v3 on v1

v3 whole, which is shorter than its diff:
```python
from functools import partial

import jax
import jax.numpy as jnp
from jax import lax
from jax.experimental import pallas as pl
from jax.experimental.pallas import tpu as pltpu
from jax.sharding import PartitionSpec as P

norm_eps = 1e-06
gelu_k = 0.7978845608028654
gelu_c = 0.044715
chunks = 8
f32 = jnp.float32
bf16 = jnp.bfloat16
VMEM = pl.BlockSpec(memory_space=pltpu.VMEM)
SMEM = pl.BlockSpec(memory_space=pltpu.SMEM)
HBM = pl.BlockSpec(memory_space=pltpu.HBM)


weight = {
    "pick_piece": 16, "mixer_in": 32, "join_depth": 8, "block_mid": 16, "join_one": 32, "mlp_one": 8, "join_two": 1,
    "mlp_two": 16, "mid_back": 32, "add_core": 32, "mixer_back": 32, "mixer_out": 16, "add_core_small": 0, "add_cross": 0,
    "mixed_out": 1, "tokens_out": 2, "add_cross_small": 2, "add_depth": 16, "add_depth_small": 32, "add_far": 16,
    "add_far_small": 1, "add_last": 0, "add_last_small": 4, "join_mlp": 2, "join_mix": 32, "spread_mlp": 16, "spread_mix": 8,
}


def dot(a, b):
    return jnp.dot(a, b, preferred_element_type=f32)


def dot_nt(a, b):
    return lax.dot_general(a, b, (((1,), (1,)), ((), ())), preferred_element_type=f32)


def shape_of(dtype, *shape):
    return jax.ShapeDtypeStruct(shape, dtype)


def call(body, name, operands, outs, scratch=(), smem=1, limit=16, after=(), hbm=0):
    n, extra, cost = len(operands), len(after), weight[name]
    operands = [pltpu.with_memory_space_constraint(v, pltpu.HBM) if smem <= i < smem + hbm else v for i, v in enumerate(operands)]

    def run(*refs):
        body(*refs[:n], *refs[n + extra :])

    return pl.pallas_call(
        run,
        out_shape=outs,
        in_specs=[SMEM] * smem + [HBM] * hbm + [VMEM] * (n - smem - hbm) + [pl.BlockSpec(memory_space=pl.ANY)] * extra,
        out_specs=[VMEM] * len(outs),
        scratch_shapes=list(scratch),
        compiler_params=pltpu.CompilerParams(vmem_limit_bytes=limit << 20),
        cost_estimate=pl.CostEstimate(flops=cost << 30, bytes_accessed=cost << 22, transcendentals=0),
        name=name,
    )(*operands, *after)


def to_chunked(src, split, put):
    length, width = src.shape
    steps = length // chunks
    for g in range(width // 128):
        cols = slice(g * 128, (g + 1) * 128)
        split[g] = src[:, cols].astype(f32)
        for s in range(steps):
            put(pl.ds(s * chunks, chunks), cols, split[g, pl.ds(s, chunks, stride=steps), :])


def from_chunked(values, split, out):
    length, width = out.shape
    steps = length // chunks
    for g in range(width // 128):
        cols = slice(g * 128, (g + 1) * 128)
        for s in range(steps):
            split[g, pl.ds(s, chunks, stride=steps), :] = values[s * chunks : (s + 1) * chunks, cols]
        out[:, cols] = split[g].astype(bf16)


def keep_mask(idx, length):
    row = lax.broadcasted_iota(jnp.int32, (length, 1), 0)
    pos = idx[2] * length + (row % chunks) * (length // chunks) + row // chunks
    keep = jnp.ones((length, 1), f32)
    for i in range(3):
        keep = jnp.where(pos == idx[3 + i], 0.0, keep)
    return keep


def fetch(pairs, sems):
    copies = [pltpu.make_async_copy(src, dst, sems.at[i]) for i, (src, dst) in enumerate(pairs)]
    for copy in copies:
        copy.start()
    return copies


def mixer_in(idx, tok_hbm, gain_hbm, bias_f_hbm, bias_i_hbm, b_up_hbm, w_hbm, decay, share, cand, du, dv, nmt, x, prods, ends, payload,
             split, tok, gain, bias_f, bias_i, b_up, w, sems):
    length, width = tok.shape
    units = bias_f.shape[1]
    steps = length // chunks
    block = 256
    pairs = [(tok_hbm, tok), (gain_hbm, gain), (bias_f_hbm, bias_f), (bias_i_hbm, bias_i), (b_up_hbm, b_up)]
    for h in range(0, units, block):
        sl = pl.ds(h, block)
        pairs.append((w_hbm.at[:, :, sl], w.at[:, :, sl]))
    copies = fetch(pairs, sems)
    for copy in copies[:5]:
        copy.wait()

    def put(rows, cols, values):
        x[rows, cols] = values

    to_chunked(tok, split, put)
    v = x[...]
    r = lax.rsqrt(jnp.mean(v * v, axis=-1, keepdims=True) + norm_eps)
    nm = (v * r * gain[...]).astype(bf16)
    nmt[...] = nm.T
    keep = keep_mask(idx, length)
    for i, h in enumerate(range(0, units, block)):
        sl = pl.ds(h, block)
        copies[5 + i].wait()
        a = jnp.exp(jnp.minimum(-(dot(nm, w[0, :, sl]) + bias_f[:, sl]), 88.0))
        b = jnp.exp(jnp.minimum(-(dot(nm, w[1, :, sl]) + bias_i[:, sl]), 88.0))
        t = 1.0 / (2.0 + a + b)
        p = (1.0 + b) * t
        q = (1.0 + a) * t
        decay[:, sl] = p * keep
        share[:, sl] = q
        cand[:, sl] = dot(nm, w[2, :, sl])
        du[:, sl] = p * (a * t)
        dv[:, sl] = q * (b * t)

    def step(s, carry):
        prod, end = carry
        rows = pl.ds(pl.multiple_of(s * chunks, chunks), chunks)
        d = decay[rows, :]
        return prod * d, end * d + share[rows, :] * cand[rows, :]

    prod, end = lax.fori_loop(
        0, steps, step, (jnp.ones((chunks, units), f32), jnp.zeros((chunks, units), f32)), unroll=8
    )
    prods[...] = prod
    ends[...] = end
    total, state = prod[0:1], end[0:1]
    for k in range(1, chunks):
        total = total * prod[k : k + 1]
        state = state * prod[k : k + 1] + end[k : k + 1]
    payload[...] = jnp.zeros_like(payload)
    payload[0:1, :] = total
    payload[1:2, :] = state
    payload[2:3, 0 : b_up.shape[1]] = b_up[...]


def feed_forward(nm, cot, wu, wd, bu):
    pre = dot(nm, wu) + bu
    grad_act = dot_nt(cot, wd)
    sq = pre * pre
    t = jnp.tanh(pre * (gelu_k + gelu_k * gelu_c * sq))
    half = 0.5 + 0.5 * t
    h = pre * half
    slope = half + h * (1.0 - t) * (gelu_k + 3.0 * gelu_k * gelu_c * sq)
    grad_pre = grad_act * slope
    return h.astype(bf16), grad_pre.astype(bf16), jnp.sum(grad_pre, axis=0, keepdims=True)


def store_pieces(ref, base, rows, values):
    for p in range(4):
        ref[p, base : base + rows, :] = values[p * rows : (p + 1) * rows].astype(bf16)


def ffn_block(slot, core, nm, nmt, cot, wu, wd, bu, mix, gn, keep, send, hT):
    h, g, bsum = feed_forward(nm, cot, wu, wd, bu)
    hT[...] = h.T
    half = nm.shape[1] // 2
    for ref, which in ((send, 1 - core), (keep, core)):
        rows = pl.ds(pl.multiple_of(which * half, half), half)
        store_pieces(ref, slot * (half // 2), half // 4, dot(nmt[rows, :], g))
        store_pieces(ref, slot * (half // 2) + half // 4, half // 4, dot(hT[rows, :], cot))
    mix[...] += dot(h, wd)
    gn[...] += dot_nt(g, wu)
    return bsum


def block_mid(idx, own, r1, r2, r3, prods, ends, decay, share, cand, x, cot, w_out, gain, wu, wd, bu,
              st, stT, middle, nm2, nm2t, cotp, mix, gn, bsum, keep, send, split, others, hT, carry8):
    length = x.shape[0]
    steps = length // chunks
    units = decay.shape[1]
    core, z = idx[0], idx[2]
    for j, ref in enumerate((own, r1, r2, r3)):
        others[j] = ref[...]
    state = jnp.zeros((1, units), f32)
    for k in range(4):
        part = others[k ^ z]
        state = jnp.where(k < z, state * part[0:1] + part[1:2], state)
    for k in range(chunks):
        carry8[k : k + 1, :] = state
        state = state * prods[k : k + 1, :] + ends[k : k + 1, :]
    st[0:chunks, :] = carry8[...]

    def step(s, state):
        rows = pl.ds(pl.multiple_of(s * chunks, chunks), chunks)
        state = state * decay[rows, :] + share[rows, :] * cand[rows, :]
        st[pl.ds(pl.multiple_of(s * chunks + chunks, chunks), chunks), :] = state
        return state

    lax.fori_loop(0, steps, step, carry8[...], unroll=8)
    low = st[chunks:, :].astype(bf16)
    stT[...] = low.T
    mid = x[...] + dot(low, w_out[...])
    middle[...] = mid
    r = lax.rsqrt(jnp.mean(mid * mid, axis=-1, keepdims=True) + norm_eps)
    nm = (mid * r * gain[...]).astype(bf16)
    nm2[...] = nm
    nm2t[...] = nm.T

    def put(rows, cols, values):
        gn[rows, cols] = values

    to_chunked(cot, split, put)
    cotp[...] = gn[...].astype(bf16)
    gn[...] = jnp.zeros_like(gn)
    mix[...] = mid
    bsum[...] = ffn_block(0, core, nm, nm2t, cotp[...], wu[...], wd[...], bu[...], mix, gn, keep, send, hT)


def lay_out(idx, near, far, at, wu, wd):
    rows = wu.shape[0] // 8
    for which, pieces in ((idx[0], near), (1 - idx[0], far)):
        for k in range(4):
            spot = pl.ds(pl.multiple_of((which * 4 + (idx[1] ^ k)) * rows, rows), rows)
            wu[spot, :] = pieces[k, at : at + rows, :]
            wd[spot, :] = pieces[k, at + rows : at + 2 * rows, :]


def mlp_one(idx, near, far, bias, mix0, gn0, bsum0, nm2, nm2t, cotp, keep0, send0,
            mix, gn, keep, send, small, hT, wu, wd):
    z = idx[2]
    block = keep0.shape[1]
    mix[...] = mix0[...]
    gn[...] = gn0[...]
    keep[:, 0:block, :] = keep0[...]
    send[:, 0:block, :] = send0[...]
    small[...] = jnp.zeros_like(small)
    small[pl.ds(4 * z + 2, 1), :] = bsum0[...]
    lay_out(idx, near, far, 0, wu, wd)
    small[pl.ds(4 * (z ^ 1) + 2, 1), :] = ffn_block(
        1, idx[0], nm2[...], nm2t, cotp[...], wu[...], wd[...], bias[2:3, 0 : wu.shape[1]], mix, gn, keep, send, hT
    )


def mlp_two(idx, near, far, bias2, bias3, mix0, gn0, small0, nm2, nm2t, cotp, mix, gn, keep, send, small, hT, wu, wd):
    mix[...] = mix0[...]
    gn[...] = gn0[...]
    small[...] = small0[...]
    for slot, bias in enumerate((bias2, bias3)):
        lay_out(idx, near, far, slot * wu.shape[0] // 4, wu, wd)
        small[pl.ds(4 * (idx[2] ^ (2 + slot)) + 2, 1), :] = ffn_block(
            slot, idx[0], nm2[...], nm2t, cotp[...], wu[...], wd[...], bias[2:3, 0 : wu.shape[1]], mix, gn, keep, send, hT
        )


def mid_back(idx, gn, cotp, middle, gain, stT, w_out, decay,
             keep, send, grad_mid, grad_states, payload, prods, flows, gain_row):
    core, z = idx[0], idx[2]
    length, units = decay.shape
    steps = length // chunks
    mid = middle[...]
    r = lax.rsqrt(jnp.mean(mid * mid, axis=-1, keepdims=True) + norm_eps)
    scaled = mid * r
    g = gn[...]
    gain_row[...] = jnp.sum(g * scaled, axis=0, keepdims=True)
    gg = g * gain[...]
    gm = cotp[...].astype(f32) + r * (gg - scaled * jnp.mean(gg * scaled, axis=-1, keepdims=True))
    grad_mid[...] = gm
    low = gm.astype(bf16)
    grad_states[...] = dot_nt(low, w_out[...])
    part = units // 8
    for k in range(4):
        for ref, which in ((send, 1 - core), (keep, core)):
            got = dot(stT[pl.ds(pl.multiple_of((2 * k + which) * part, part), part), :], low)
            at = pl.ds(pl.multiple_of((k ^ z) * (part // 4), part // 4), part // 4)
            for p in range(4):
                ref[p, at, :] = got[p * (part // 4) : (p + 1) * (part // 4)].astype(bf16)

    def step(i, carry):
        prod, flow = carry
        rows = pl.ds(pl.multiple_of((steps - 1 - i) * chunks, chunks), chunks)
        d = decay[rows, :]
        return prod * d, (flow + grad_states[rows, :]) * d

    prod, flow = lax.fori_loop(
        0, steps, step, (jnp.ones((chunks, units), f32), jnp.zeros((chunks, units), f32)), unroll=8
    )
    total, out = prod[chunks - 1 :], flow[chunks - 1 :]
    for k in range(chunks - 2, -1, -1):
        total = total * prod[k : k + 1]
        out = out * prod[k : k + 1] + flow[k : k + 1]
    payload[0:1, :] = total
    payload[1:2, :] = out
    prods[...] = prod
    flows[...] = flow


def mixed_out(mix, mixed, done, split):
    from_chunked(mix, split, mixed)
    done[...] = jnp.zeros_like(done)


def gate_grads(which, keep, carried, st, share, cand, du, dv, w, nmt, z, out, gnm, small):
    length, units = carried.shape
    half = units // 2
    cols = pl.ds(pl.multiple_of(which * half, half), half)
    cf = carried[:, cols]
    q = share[:, cols]
    s = cf * (st[0:length, cols] * keep - cand[:, cols])
    ga = s * du[:, cols]
    gb = -(s * dv[:, cols])
    quarter = half // 2
    sum_a, sum_b = jnp.sum(ga, axis=0, keepdims=True), jnp.sum(gb, axis=0, keepdims=True)
    for i in range(2):
        at = pl.ds(4 * (2 * which + i), 1)
        small[at, 0:quarter] = sum_a[:, i * quarter : (i + 1) * quarter]
        small[at, quarter:] = sum_b[:, i * quarter : (i + 1) * quarter]
    part = nmt.shape[0] // 4
    for k, g in enumerate((ga, gb, cf * q)):
        low = g.astype(bf16)
        got = dot(nmt[...], low)
        for zz in range(4):
            for p in range(4):
                top = zz * part + p * (part // 4)
                out[p, zz ^ z, k * (part // 4) : (k + 1) * (part // 4), :] = got[top : top + part // 4].astype(bf16)
        gnm[...] += dot_nt(low, w[k, :, cols])


def mixer_back(idx, own, r1, r2, r3, prods, flows, decay, share, cand, du, dv, st, grad_states, nmt, w,
               carried, send, gnm, small, others, carry8):
    length, units = decay.shape
    steps = length // chunks
    core, z = idx[0], idx[2]
    for j, ref in enumerate((own, r1, r2, r3)):
        others[j] = ref[...]
    flow = jnp.zeros((1, units), f32)
    for k in range(3, -1, -1):
        part = others[k ^ z]
        flow = jnp.where(k > z, flow * part[0:1] + part[1:2], flow)
    for k in range(chunks - 1, -1, -1):
        carry8[k : k + 1, :] = flow
        flow = flow * prods[k : k + 1, :] + flows[k : k + 1, :]

    def step(i, flow):
        rows = pl.ds(pl.multiple_of((steps - 1 - i) * chunks, chunks), chunks)
        got = grad_states[rows, :] + flow
        carried[rows, :] = got
        return got * decay[rows, :]

    lax.fori_loop(0, steps, step, carry8[...], unroll=8)
    gnm[...] = jnp.zeros_like(gnm)
    small[...] = jnp.zeros_like(small)
    gate_grads(1 - core, keep_mask(idx, length), carried, st, share, cand, du, dv, w, nmt, z, send, gnm, small)


def mixer_out(idx, carried, share, cand, du, dv, st, nmt, w, gnm0, small0, small1, gain_row, x,
              keep, gnm, small):
    length, units = carried.shape
    core, z = idx[0], idx[2]
    gnm[...] = gnm0[...]
    small[...] = small0[...] + small1[...]
    gate_grads(core, keep_mask(idx, length), carried, st, share, cand, du, dv, w, nmt, z, keep, gnm, small)
    v = x[...]
    r = lax.rsqrt(jnp.mean(v * v, axis=-1, keepdims=True) + norm_eps)
    gains = jnp.sum(gnm[...] * (v * r), axis=0, keepdims=True)
    n = gains.shape[1] // 4
    for k in range(4):
        small[4 * k + 1 : 4 * k + 2, 0:n] = gains[:, k * n : (k + 1) * n]
        small[4 * k + 1 : 4 * k + 2, n : 2 * n] = gain_row[:, k * n : (k + 1) * n]


def tokens_out(gnm, x, gain, grad_mid, grad_tok, done, total, split):
    v = x[...]
    r = lax.rsqrt(jnp.mean(v * v, axis=-1, keepdims=True) + norm_eps)
    scaled = v * r
    gg = gnm[...] * gain[...]
    total[...] = grad_mid[...] + r * (gg - scaled * jnp.mean(gg * scaled, axis=-1, keepdims=True))
    from_chunked(total, split, grad_tok)
    done[...] = jnp.zeros_like(done)


def pick_piece(idx, wu, wd, out, sems):
    rows = wu.shape[0] // 8
    at = pl.ds(pl.multiple_of((idx[0] * 4 + idx[1]) * rows, rows), rows)
    for copy in fetch([(wu.at[at, :], out.at[pl.ds(0, rows), :]), (wd.at[at, :], out.at[pl.ds(rows, rows), :])], sems):
        copy.wait()


def gate(value, after):
    any_space = pl.BlockSpec(memory_space=pl.ANY)
    return pl.pallas_call(
        lambda *refs: None,
        out_shape=jax.ShapeDtypeStruct(value.shape, value.dtype),
        in_specs=[any_space, any_space],
        out_specs=any_space,
        input_output_aliases={0: 0},
        compiler_params=pltpu.CompilerParams(vmem_limit_bytes=1 << 20),
        name="gate",
    )(value, after)


def join(*refs):
    out, rows = refs[-1], refs[0].shape[0]
    for k, ref in enumerate(refs[:-1]):
        if len(out.shape) == 3:
            out[k] = ref[...]
        else:
            out[k * rows : (k + 1) * rows, :] = ref[...]


def two_terms(v):
    high = v.astype(bf16)
    return high, (v - high.astype(f32)).astype(bf16)


def add_core(idx, keep_a, got_a, keep_b, got_b, keep_c, got_c, send_x, send_y, own_x, own_y):
    x, y = idx[1] % 2, idx[1] // 2
    half = send_x.shape[1]

    def put(ref, k, p, first):
        top = 0
        for keep, got in ((keep_a, got_a), (keep_b, got_b), (keep_c, got_c)):
            low, high = max(first, top), min(first + half, top + keep.shape[1])
            if low < high:
                rows = slice(low - top, high - top)
                ref[k, low - first : high - first, :] = (
                    keep[p, rows, :].astype(f32) + got[p, rows, :].astype(f32)
                ).astype(ref.dtype)
            top += keep.shape[1]

    for k in range(2):
        put(send_x, k, 2 * k + 1 - x, 0)
        put(own_x, k, 2 * k + x, 0)
        put(send_y, k, 2 * (1 - y) + k, half)
        put(own_y, k, 2 * y + k, half)


def add_cross(idx, own_x, got_x, own_y, got_y, send_y, send_x, out_x, out_y):
    x, y = idx[1] % 2, idx[1] // 2
    send_y[...] = (own_x[1 - y] + got_x[1 - y].astype(f32)).astype(bf16)
    out_x[...] = own_x[y] + got_x[y].astype(f32)
    send_x[...] = (own_y[1 - x] + got_y[1 - x].astype(f32)).astype(bf16)
    out_y[...] = own_y[x] + got_y[x].astype(f32)


def add_depth(own_x, got_x, own_y, got_y, send, own, total):
    rows = send.shape[0] // 2
    part = rows // 5
    block = 4 * part
    half = own_x.shape[0]
    total[0:half, :] = own_x[...] + got_x[...].astype(f32)
    total[half:, :] = own_y[...] + got_y[...].astype(f32)
    for j, ref, base in ((1, send, 0), (2, own, rows), (3, send, rows), (0, own, 0)):
        at = j * block
        ref[base : base + block, :] = total[at : at + block, :].astype(ref.dtype)
        at = 4 * block + j * part
        ref[base + block : base + rows, :] = total[at : at + part, :].astype(ref.dtype)


def add_far(own, got, send, out):
    rows = out.shape[0]
    out[...] = own[0:rows, :] + got[0:rows, :].astype(f32)
    send[...] = (own[rows:, :] + got[rows:, :].astype(f32)).astype(bf16)


def add_last(own, got, out):
    out[...] = (own[...] + got[...].astype(f32)).astype(out.dtype)


def add_core_small(idx, keep, got, small, send_x, send_y, own_x, own_y, tiny):
    x, y = idx[1] % 2, idx[1] // 2
    half, n = own_x.shape[1], small.shape[0]
    high, low = two_terms(small[...])
    tiny[0:n, :] = high
    tiny[n:, :] = low
    send_x[2 * half : 2 * half + n, :] = high
    send_x[2 * half + n :, :] = low
    for k in range(2):
        at = slice(k * half, (k + 1) * half)
        p = 2 * k + 1 - x
        send_x[at, :] = (keep[p, 0:half, :].astype(f32) + got[p, 0:half, :].astype(f32)).astype(bf16)
        p = 2 * k + x
        own_x[k] = keep[p, 0:half, :].astype(f32) + got[p, 0:half, :].astype(f32)
        p = 2 * (1 - y) + k
        send_y[at, :] = (keep[p, half:, :].astype(f32) + got[p, half:, :].astype(f32)).astype(bf16)
        p = 2 * y + k
        own_y[k] = keep[p, half:, :].astype(f32) + got[p, half:, :].astype(f32)


def add_tiny(tiny, got, at):
    n = tiny.shape[0] // 2
    return (tiny[0:n, :].astype(f32) + tiny[n:, :].astype(f32)) + (
        got[at : at + n, :].astype(f32) + got[at + n : at + 2 * n, :].astype(f32)
    )


def add_cross_small(idx, own_x, got_x, own_y, got_y, tiny, send_y, send_x, out_x, out_y, tiny_out):
    x, y = idx[1] % 2, idx[1] // 2
    half, n = out_x.shape[0], tiny.shape[0] // 2
    high, low = two_terms(add_tiny(tiny, got_x, 2 * half))
    tiny_out[0:n, :] = high
    tiny_out[n:, :] = low
    send_y[half : half + n, :] = high
    send_y[half + n :, :] = low
    side = pl.ds(pl.multiple_of((1 - y) * half, half), half)
    send_y[0:half, :] = (own_x[1 - y] + got_x[side, :].astype(f32)).astype(bf16)
    side = pl.ds(pl.multiple_of(y * half, half), half)
    out_x[...] = own_x[y] + got_x[side, :].astype(f32)
    side = pl.ds(pl.multiple_of((1 - x) * half, half), half)
    send_x[...] = (own_y[1 - x] + got_y[side, :].astype(f32)).astype(bf16)
    side = pl.ds(pl.multiple_of(x * half, half), half)
    out_y[...] = own_y[x] + got_y[side, :].astype(f32)


def add_depth_small(idx, own_x, got_x, own_y, got_y, tiny, send, own, small):
    half, z = own_x.shape[0], idx[2]
    rows = half // 2
    total = add_tiny(tiny, got_x, half)
    n = total.shape[0] // 4
    small[...] = jnp.zeros_like(small)
    for k in range(4):
        small[k, 0:n, :] = total[k * n : (k + 1) * n]
    for j in range(4):
        own_ref, got = ((own_x, got_x), (own_y, got_y))[j // 2]
        at = slice((j % 2) * rows, (j % 2 + 1) * rows)
        value = own_ref[at, :] + got[at, :].astype(f32)
        base = (j // 2) * (rows + 16)
        if j % 2:
            send[base : base + rows, :] = value.astype(bf16)
            high, low = two_terms(small[z ^ j])
            send[base + rows : base + rows + 16, :] = jnp.concatenate([high, low], axis=0)
        else:
            own[(j // 2) * rows : (j // 2 + 1) * rows, :] = value


def add_far_small(idx, own, got, small, send, out, tiny_out):
    z = idx[2]
    rows, n = out.shape[0], tiny_out.shape[0]
    tiny = []
    for k in range(2):
        base = k * (rows + 16)
        mine = small[z ^ (2 * k)]
        other = got[base + rows : base + rows + 16, :].astype(f32)
        tiny.append(mine + (other[0:n] + other[n : 2 * n]))
    out[...] = own[0:rows, :] + got[0:rows, :].astype(f32)
    tiny_out[...] = tiny[0]
    send[0:rows, :] = (own[rows:, :] + got[rows + 16 : 2 * rows + 16, :].astype(f32)).astype(bf16)
    high, low = two_terms(tiny[1])
    send[rows:, :] = jnp.concatenate([high, low], axis=0)


def add_last_small(own, tiny, got, out, tiny_out):
    rows, n = own.shape[0], tiny.shape[0]
    out[...] = (own[...] + got[0:rows, :].astype(f32)).astype(out.dtype)
    other = got[rows:, :].astype(f32)
    tiny_out[...] = tiny[...] + (other[0:n] + other[n : 2 * n])


def spread_mlp(idx, near, far, up, down, w_out, done):
    rows = up.shape[0] // 8
    rows_out = w_out.shape[0] // 8
    for which, pieces in ((idx[0], near), (1 - idx[0], far)):
        for k in range(4):
            spot = which * 4 + (idx[1] ^ k)
            at = pl.ds(pl.multiple_of(spot * rows, rows), rows)
            up[at, :] = pieces[k, 0:rows, :].astype(f32)
            down[at, :] = pieces[k, rows : 2 * rows, :].astype(f32)
            w_out[pl.ds(pl.multiple_of(spot * rows_out, rows_out), rows_out), :] = pieces[k, 2 * rows :, :].astype(f32)
    done[...] = jnp.zeros_like(done)


def spread_mix(idx, tiny, tiny_far, near, far, out, bias_f, bias_i, gain_mix, gain_mlp, b_up):
    rows, half = out.shape[1] // 4, out.shape[2] // 2
    for which, pieces in ((idx[0], near), (1 - idx[0], far)):
        cols = pl.ds(pl.multiple_of(which * half, half), half)
        for k in range(4):
            at = pl.ds(pl.multiple_of((idx[1] ^ k) * rows, rows), rows)
            for i in range(3):
                out[i, at, cols] = pieces[k, i * rows : (i + 1) * rows, :].astype(f32)
    small = tiny[...] + tiny_far[...]
    n = bias_f.shape[1]
    bias_f[...] = small[0:1, 0:n]
    bias_i[...] = small[0:1, n:]
    n = gain_mix.shape[1]
    gain_mix[...] = small[1:2, 0:n]
    gain_mlp[...] = small[1:2, n : 2 * n]
    b_up[...] = small[2:3, :]


def swap(value, axis, bit):
    size = lax.axis_size(axis)
    return lax.ppermute(value, axis, [(i, i ^ bit) for i in range(size)])


def on_device(tokens, gain_mix, w_mix, bias_forget, bias_input, w_out, gain_mlp, w_up, b_up, w_down, resets, cotangent):
    length, width = tokens.shape[1:]
    units = w_out.shape[0]
    ff = w_up.shape[1]
    dp, mp = lax.axis_size("dp"), lax.axis_size("mp")
    assert mp == 4 and dp % 8 == 0 and tokens.shape[0] == 1
    place = lax.axis_index("dp")
    here = jnp.stack([place & 1, (place >> 1) & 3, lax.axis_index("mp")]).astype(jnp.int32)
    idx = jnp.concatenate([here, resets[0]])
    tok, cot = tokens[0], cotangent[0]
    w3 = w_mix.transpose(1, 0, 2)
    row = lambda v: v.reshape(1, -1)
    lanes = width // 128

    (piece,) = call(pick_piece, "pick_piece", (idx, w_up, w_down), [shape_of(bf16, width // 4, ff)],
                    [pltpu.SemaphoreType.DMA((2,))], hbm=2, limit=2)
    depth = [swap(piece, "mp", j) for j in (1, 2, 3)]

    wide = shape_of(f32, length, units)
    square = shape_of(f32, length, width)
    square16 = shape_of(bf16, length, width)
    edge = shape_of(f32, chunks, units)
    decay, share, cand, du, dv, nmt, x, prods, ends, payload = call(
        mixer_in, "mixer_in",
        (idx, tok, row(gain_mix), row(bias_forget), row(bias_input), row(b_up), w3),
        [wide] * 5 + [shape_of(bf16, width, length), square, edge, edge, shape_of(f32, 4, units)],
        [pltpu.VMEM((lanes, length, 128), f32), pltpu.VMEM((length, width), bf16), pltpu.VMEM((1, width), f32)]
        + [pltpu.VMEM((1, units), f32)] * 2 + [pltpu.VMEM((1, ff), f32), pltpu.VMEM((3, width, units), bf16),
                                              pltpu.SemaphoreType.DMA((5 + units // 256,))],
        hbm=6, after=(piece,),
    )
    ahead = [swap(payload, "mp", j) for j in (1, 2, 3)]
    around = lambda v: [v] + [swap(v, "dp", 2 * k) for k in (1, 2, 3)]
    near_one = around(gate(depth[0], payload))
    (pair,) = call(join, "join_depth", depth[1:], [shape_of(bf16, width // 2, ff)], smem=0, after=(payload,))
    near_two = around(pair)
    (near_one,) = call(join, "join_one", near_one, [shape_of(bf16, 4, width // 4, ff)], smem=0)
    far_one = swap(near_one, "dp", 1)
    quarter = width // 8
    st, stT, middle, nm2, nm2t, cotp, mix, gn, bsum, keep0, send0 = call(
        block_mid, "block_mid",
        (idx, payload, *ahead, prods, ends, decay, share, cand, x, cot, w_out, row(gain_mlp), w_up, w_down, row(b_up)),
        [shape_of(f32, length + chunks, units), shape_of(bf16, units, length), square, square16, shape_of(bf16, width, length),
         square16, square, square, shape_of(f32, 1, ff)] + [shape_of(bf16, 4, 2 * quarter, width)] * 2,
        [pltpu.VMEM((lanes, length, 128), f32), pltpu.VMEM((4, 4, units), f32), pltpu.VMEM((ff, length), bf16),
         pltpu.VMEM((chunks, units), f32)], after=(pair,),
    )
    block = 2 * quarter
    pair = lambda dtype, rows: shape_of(dtype, 2, rows, width)
    weights = [pltpu.VMEM((ff, length), bf16), pltpu.VMEM((width, ff), bf16), pltpu.VMEM((ff, width), bf16)]
    mix, gn, keep_a, send_a, small_mlp = call(
        mlp_one, "mlp_one",
        (idx, near_one, far_one, ahead[0], mix, gn, bsum, nm2, nm2t, cotp, keep0, send0),
        [square] * 2 + [shape_of(bf16, 4, 2 * block, width)] * 2 + [shape_of(f32, 16, width)], weights,
    )
    (near_two,) = call(join, "join_two", near_two, [shape_of(bf16, 4, width // 2, ff)], smem=0, after=(gn,))
    mix, gn, keep, send, small_mlp = call(
        mlp_two, "mlp_two",
        (idx, near_two, swap(near_two, "dp", 1), ahead[1], ahead[2], mix, gn, small_mlp, nm2, nm2t, cotp),
        [square] * 2 + [shape_of(bf16, 4, 2 * block, width)] * 2 + [shape_of(f32, 16, width)], weights,
    )
    got_a, got = swap(send_a, "dp", 1), swap(send, "dp", 1)
    out_rows = units // 8
    keep_out, send_out, grad_mid, grad_states, payload, prods, flows, gain_row = call(
        mid_back, "mid_back",
        (idx, gn, cotp, middle, row(gain_mlp), stT, w_out, decay),
        [shape_of(bf16, 4, out_rows, width)] * 2 + [square, wide, shape_of(f32, 2, units), edge, edge, shape_of(f32, 1, width)],
    )
    behind = [swap(payload, "mp", j) for j in (1, 2, 3)]

    half = (4 * block + out_rows) // 2
    send_x, send_y, own_x, own_y = call(add_core, "add_core", (idx, keep_a, got_a, keep, got, keep_out, swap(send_out, "dp", 1)),
                                        [pair(bf16, half)] * 2 + [pair(f32, half)] * 2)
    got_x, got_y = swap(send_x, "dp", 2), swap(send_y, "dp", 4)

    rows_m = 3 * width // 16
    carried, send, gnm, small = call(
        mixer_back, "mixer_back",
        (idx, payload, *behind, prods, flows, decay, share, cand, du, dv, st, grad_states, nmt, w3),
        [wide, shape_of(bf16, 4, 4, rows_m, units // 2), square, shape_of(f32, 16, width)],
        [pltpu.VMEM((4, 2, units), f32), pltpu.VMEM((chunks, units), f32)], after=(own_x,),
    )
    flat = lambda v: v.reshape(4, -1, width)
    got = swap(send, "dp", 1)
    keep, gnm, small = call(
        mixer_out, "mixer_out",
        (idx, carried, share, cand, du, dv, st, nmt, w3, gnm, small, small_mlp, gain_row, x),
        [shape_of(bf16, 4, 4, rows_m, units // 2), square, shape_of(f32, 16, width)],
    )
    half_m = 2 * rows_m
    one = lambda dtype, rows: shape_of(dtype, rows, width)
    send_mx, send_my, own_mx, own_my, tiny = call(
        add_core_small, "add_core_small", (idx, flat(keep), flat(got), small),
        [one(bf16, 2 * half_m + 32), one(bf16, 2 * half_m), pair(f32, half_m), pair(f32, half_m), one(bf16, 32)],
    )
    got_mx, got_my = swap(send_mx, "dp", 2), swap(send_my, "dp", 4)
    mark = shape_of(f32, 8, 128)
    grad_tok, done_tok = call(tokens_out, "tokens_out", (gnm, x, row(gain_mix), grad_mid), [square16, mark],
                       [pltpu.VMEM((length, width), f32), pltpu.VMEM((lanes, length, 128), f32)], smem=0, after=(own_mx,))
    mixed, done_mix = call(mixed_out, "mixed_out", (mix,), [square16, mark], [pltpu.VMEM((lanes, length, 128), f32)], smem=0, after=(own_mx,))

    send_y, send_x, own_x, own_y = call(add_cross, "add_cross", (idx, own_x, got_x, own_y, got_y),
                                        [one(bf16, half)] * 2 + [one(f32, half)] * 2, after=(own_mx,))
    got_x, got_y = swap(send_y, "dp", 4), swap(send_x, "dp", 2)
    send_my, send_mx, own_mx, own_my, tiny = call(
        add_cross_small, "add_cross_small", (idx, own_mx, got_mx, own_my, got_my, tiny),
        [one(bf16, half_m + 32), one(bf16, half_m), one(f32, half_m), one(f32, half_m), one(bf16, 32)],
        after=(own_x, done_mix, done_tok),
    )
    got_mx, got_my = swap(send_my, "dp", 4), swap(send_mx, "dp", 2)
    rows_f = block + units // 32
    send, own = call(add_depth, "add_depth", (own_x, got_x, own_y, got_y), [one(bf16, 2 * rows_f), one(f32, 2 * rows_f)],
                     [pltpu.VMEM((2 * half, width), f32)], smem=0, after=(own_mx,))
    got = swap(send, "mp", 1)
    send_m, own_m, small = call(
        add_depth_small, "add_depth_small", (idx, own_mx, got_mx, own_my, got_my, tiny),
        [one(bf16, 2 * rows_m + 32), one(f32, 2 * rows_m), shape_of(f32, 4, 8, width)], after=(own,),
    )
    got_m = swap(send_m, "mp", 1)
    send, own = call(add_far, "add_far", (own, got), [one(bf16, rows_f), one(f32, rows_f)], smem=0, after=(small,))
    got = swap(send, "mp", 2)
    send_m, own_m, tiny = call(
        add_far_small, "add_far_small", (idx, own_m, got_m, small),
        [one(bf16, rows_m + 16), one(f32, rows_m), one(f32, 8)], after=(own,),
    )
    got_m = swap(send_m, "mp", 2)
    across = [[g * 8 + i for g in range(dp // 8)] for i in range(8)]

    def last(fn, name, operands, outs, after):
        if dp == 8:
            return call(fn, name, operands, outs, smem=0, after=after)
        done = call(fn, name, operands, [shape_of(f32, *o.shape) for o in outs], smem=0, after=after)
        return [lax.psum(v, "dp", axis_index_groups=across).astype(o.dtype) for v, o in zip(done, outs)]

    (part,) = last(add_last, "add_last", (own, got), [one(bf16, rows_f)], (tiny,))
    near_f = around(part)
    part, tiny = last(add_last_small, "add_last_small", (own_m, tiny, got_m), [one(bf16, rows_m), one(f32, 8)], (part,))
    near_m = around(part)
    (near,) = call(join, "join_mlp", near_f, [shape_of(bf16, 4, rows_f, width)], smem=0, after=(part,))
    grad_up, grad_down, grad_out, done = call(
        spread_mlp, "spread_mlp", (idx, near, swap(near, "dp", 1)),
        [shape_of(f32, width, ff), shape_of(f32, ff, width), shape_of(f32, units // 4, width), mark],
    )
    (near,) = call(join, "join_mix", near_m, [shape_of(bf16, 4, rows_m, width)], smem=0)
    grad_mix, g_bf, g_bi, g_gain_mix, g_gain_mlp, g_bu = call(
        spread_mix, "spread_mix", (idx, tiny, swap(tiny, "dp", 1), near, swap(near, "dp", 1)),
        [shape_of(f32, 3, width // 4, units), shape_of(f32, 1, units // 4), shape_of(f32, 1, units // 4),
         shape_of(f32, 1, width // 4), shape_of(f32, 1, width // 4), shape_of(f32, 1, ff)],
        after=(done,),
    )
    return (
        mixed[None], grad_tok[None], g_gain_mix[0], grad_mix.transpose(1, 0, 2), g_bf[0], g_bi[0],
        grad_out, g_gain_mlp[0], grad_up, g_bu[0], grad_down,
    )


def solution(mesh):
    return jax.shard_map(
        on_device,
        mesh=mesh,
        in_specs=(P("dp", "mp", None), P(), P(), P(), P(), P(), P(), P(None, "mp"), P("mp"), P("mp", None), P("dp", None), P("dp", "mp", None)),
        out_specs=(P("dp", "mp", None), P("dp", "mp", None), P("mp"), P("mp", None, None), P("mp"), P("mp"), P("mp", None), P("mp"), P(None, "mp"), P("mp"), P("mp", None)),
        check_vma=False,
    )
```

time: 229 us -> 128 us (0.56)
  waiting for transfers between devices: 92.9 us -> 31.4 us
  Pallas kernels: 61.7 us -> 42.2 us
  local copies, waits for them, and re-layouts: 12.7 us -> 0.05 us
  starting transfers between devices: 59.2 us -> 52 us
    ppermute x45 -> x42, waiting for transfers between devices: 92.9 us -> 31.4 us  [swap(): return lax.ppermute(value, axis, [(i, i ^ bit) for i in range(size)])]
    pallas_call x15 -> x28, Pallas kernels: 61.7 us -> 42.2 us  [the longest x27 42.2 us: call(): pl.pallas_call(run, out_shape=outs, in_specs=[SMEM] * smem + [HBM] * hbm...]
    unnamed x42 -> x16, local copies, waits for them, and re-layouts: 12.7 us -> 0.05 us
    ppermute x45 -> x42, starting transfers between devices: 59.2 us -> 52 us  [swap(): return lax.ppermute(value, axis, [(i, i ^ bit) for i in range(size)])]
  transfers between devices with their start and end apart: 45 -> 42, of which waited for: 16 -> 13; matrix products, arithmetic and copies ran while one was open for 0% -> 0% of each run, Pallas kernels for 19% -> 31%
where the time goes in v3:
time: 128 us; the launch traced here: 127 us
  starting transfers between devices  52 us (41%)
  Pallas kernels  42.2 us (33%)
  waiting for transfers between devices  31.4 us (25%)
    ppermute x42, starting transfers between devices, swap(): return lax.ppermute(value, axis, [(i, i ^ bit) for i in range(size)])  52 us
    pallas_call x27, Pallas kernels, call(): pl.pallas_call(run, out_shape=outs, in_specs=[SMEM] * smem + [HBM] * hbm...  42.2 us
    ppermute x42, waiting for transfers between devices, swap(): return lax.ppermute(value, axis, [(i, i ^ bit) for i in range(size)])  31.4 us
  transfers between devices with their start and end apart: 42, of which 13 were waited for; matrix products, arithmetic and copies ran while one was open for 0% of the time, Pallas kernels for 31%

profile of v3, /device:TPU:1, one launch (start us, length us, event | category | flops | bytes accessed | tf_op | source)
XLA Modules:
  0.0 127.4 jit_solution(6346121017658388891)
XLA Ops:
  1.4 1.4 %pick_piece.1.refs_7_ = bf16[128,512]{1,0:T(8,128)(2,1)S(1)} custom-call(s32[6]{0:T(128)S(1)} %pad_add_fusion.refs_0_, bf16[512,512]{1,0:T(8,128)(2,1)} %refs_14_.1, bf16[512,512]{1,0:T(8,128)(2,1)} %refs_15_.1), custom_call_target="tpu_custom_call" | custom-call | flops 17179869184 | bytes 67108864 | tf_op jit(solution)/shard_map/pick_piece/pallas_call | solution.py:48
  2.8 2.2 %collective-permute-start.5 = (bf16[128,512]{1,0:T(8,128)(2,1)S(1)}, bf16[128,512]{1,0:T(8,128)(2,1)S(1)}, u32[]{:S(2)}, u32[]{:S(2)}) collective-permute-start(bf16[128,512]{1,0:T(8,128)(2,1)S(1)} %pick_piece.1.refs_7_), channel_id=1, source_target_pairs={{0,1},{1,0},{2,3},{3,2},{4,5},{5,4},{6,7},{7,6},{8,9},{9,8},{10,11... | collective-permute-start | bytes 393224 | tf_op jit(solution)/shard_map/ppermute | solution.py:599
  5.0 2.2 %collective-permute-start.1 = (bf16[128,512]{1,0:T(8,128)(2,1)S(1)}, bf16[128,512]{1,0:T(8,128)(2,1)S(1)}, u32[]{:S(2)}, u32[]{:S(2)}) collective-permute-start(bf16[128,512]{1,0:T(8,128)(2,1)S(1)} %pick_piece.1.refs_7_), channel_id=1, source_target_pairs={{0,3},{1,2},{2,1},{3,0},{4,7},{5,6},{6,5},{7,4},{8,11},{9,10},{10,... | collective-permute-start | bytes 393224 | tf_op jit(solution)/shard_map/ppermute | solution.py:599
  7.3 7.1 %mixer_in.1 = (f32[512,1024]{1,0:T(8,128)S(1)}, f32[512,1024]{1,0:T(8,128)S(1)}, f32[512,1024]{1,0:T(8,128)S(1)}, f32[512,1024]{1,0:T(8,128)S(1)}, f32[512,1024]...) custom-call(s32[6]{0:T(128)S(1)} %pad_add_fusion.refs_0_, ...), custom_call_target="tpu_custom_call" | custom-call | flops 34359738368 | bytes 134217728 | tf_op jit(solution)/shard_map/mixer_in/pallas_call | solution.py:48
  14.4 2.4 %collective-permute-start.12 = (f32[4,1024]{1,0:T(4,128)S(1)}, f32[4,1024]{1,0:T(4,128)S(1)}, u32[]{:S(2)}, u32[]{:S(2)}) collective-permute-start(f32[4,1024]{1,0:T(4,128)S(1)} %get-tuple-element.101.refs_2_.refs_1_), channel_id=1, source_target_pairs={{0,3},{1,2},{2,1},{3,0},{4,7},{5,6},{6,5},{7,4},{8,11},{9,10},{10,... | collective-permute-start | bytes 49160 | tf_op jit(solution)/shard_map/ppermute | solution.py:599
  16.9 2.2 %collective-permute-start.8 = (bf16[128,512]{1,0:T(8,128)(2,1)S(1)}, bf16[128,512]{1,0:T(8,128)(2,1)S(1)}, u32[]{:S(2)}, u32[]{:S(2)}) collective-permute-start(bf16[128,512]{1,0:T(8,128)(2,1)S(1)} %gate.1.refs_0_), channel_id=1, source_target_pairs={{0,24},{4,28},{8,16},{12,20},{16,8},{20,12},{24,0},{28,4},{1,25},{... | collective-permute-start | bytes 393224 | tf_op jit(solution)/shard_map/ppermute | solution.py:599
  20.2 1.4 %collective-permute-done.8.refs_3_ = bf16[128,512]{1,0:T(8,128)(2,1)S(1)} collective-permute-done((bf16[128,512]{1,0:T(8,128)(2,1)S(1)}, bf16[128,512]{1,0:T(8,128)(2,1)S(1)}, u32[]{:S(2)}, u32[]{:S(2)}) %collective-permute-start.8) | collective-permute-done | bytes 131104 | tf_op jit(solution)/shard_map/ppermute | solution.py:599
  23.6 1.6 %collective-permute-start.4 = (bf16[256,512]{1,0:T(8,128)(2,1)S(1)}, bf16[256,512]{1,0:T(8,128)(2,1)S(1)}, u32[]{:S(2)}, u32[]{:S(2)}) collective-permute-start(bf16[256,512]{1,0:T(8,128)(2,1)S(1)} %join_depth.1.refs_17_.refs_0_), channel_id=1, source_target_pairs={{0,24},{4,28},{8,16},{12,20},{16,8},{20,12},{24,0},{28,4},{1,25},{... | collective-permute-start | bytes 786440 | tf_op jit(solution)/shard_map/ppermute | solution.py:599
  26.6 4.2 %collective-permute-start.9 = (bf16[4,128,512]{2,1,0:T(8,128)(2,1)S(1)}, bf16[4,128,512]{2,1,0:T(8,128)(2,1)S(1)}, u32[]{:S(2)}, u32[]{:S(2)}) collective-permute-start(bf16[4,128,512]{2,1,0:T(8,128)(2,1)S(1)} %join_one.1.refs_1_), channel_id=1, source_target_pairs={{0,4},{4,0},{8,12},{12,8},{16,20},{20,16},{24,28},{28,24},{1,5},{5... | collective-permute-start | bytes 1572872 | tf_op jit(solution)/shard_map/ppermute | solution.py:599
  30.8 4.6 %block_mid.1 = (f32[520,1024]{1,0:T(8,128)S(1)}, bf16[1024,512]{1,0:T(8,128)(2,1)S(1)}, f32[512,512]{1,0:T(8,128)S(1)}, bf16[512,512]{1,0:T(8,128)(2,1)S(1)}, bf...) custom-call(s32[6]{0:T(128)S(1)} %pad_add_fusion.refs_0_, ...), custom_call_target="tpu_custom_call" | custom-call | flops 17179869184 | bytes 67108864 | tf_op jit(solution)/shard_map/block_mid/pallas_call | solution.py:48
  35.4 2.9 %mlp_one.1 = (f32[512,512]{1,0:T(8,128)S(1)}, f32[512,512]{1,0:T(8,128)S(1)}, bf16[4,256,512]{2,1,0:T(8,128)(2,1)S(1)}, bf16[4,256,512]{2,1,0:T(8,128)(2,1)S(1)}, f32[16,512]{1,0:T(8,128)S(1)}) custom-call(s32[6]{0:T(128)S(1)} %pad_add_fusion.refs_0_, bf16[4,128,512]{2,1,0:T(8,128)(2,1)S(1)} %join_one.1.refs_1_, ...), custom_call_target="tpu_custom_call" | custom-call | flops 8589934592 | bytes 33554432 | tf_op jit(solution)/shard_map/mlp_one/pallas_call | solution.py:48
  39.3 2.2 %collective-permute-done.13.refs_2_ = bf16[4,256,512]{2,1,0:T(8,128)(2,1)S(1)} collective-permute-done((bf16[4,256,512]{2,1,0:T(8,128)(2,1)S(1)}, bf16[4,256,512]{2,1,0:T(8,128)(2,1)S(1)}, u32[]{:S(2)}, u32[]{:S(2)}) %collective-permute-start.13) | collective-permute-done | bytes 1048608 | tf_op jit(solution)/shard_map/ppermute | solution.py:599
  41.5 4.9 %mlp_two.1 = (f32[512,512]{1,0:T(8,128)S(1)}, f32[512,512]{1,0:T(8,128)S(1)}, bf16[4,256,512]{2,1,0:T(8,128)(2,1)S(1)}, bf16[4,256,512]{2,1,0:T(8,128)(2,1)S(1)}, f32[16,512]{1,0:T(8,128)S(1)}) custom-call(s32[6]{0:T(128)S(1)} %pad_add_fusion.refs_0_, bf16[4,256,512]{2,1,0:T(8,128)(2,1)S(1)} %join_two.1.refs_1_, ...), custom_call_target="tpu_custom_call" | custom-call | flops 17179869184 | bytes 67108864 | tf_op jit(solution)/shard_map/mlp_two/pallas_call | solution.py:48
  46.9 2.8 %mid_back.1 = (bf16[4,128,512]{2,1,0:T(8,128)(2,1)S(1)}, bf16[4,128,512]{2,1,0:T(8,128)(2,1)S(1)}, f32[512,512]{1,0:T(8,128)S(1)}, f32[512,1024]{1,0:T(8,128)S(1...) custom-call(s32[6]{0:T(128)S(1)} %pad_add_fusion.refs_0_, ...), custom_call_target="tpu_custom_call" | custom-call | flops 34359738368 | bytes 134217728 | tf_op jit(solution)/shard_map/mid_back/pallas_call | solution.py:48
  49.9 2.5 %collective-permute-start.16 = (f32[2,1024]{1,0:T(2,128)S(1)}, f32[2,1024]{1,0:T(2,128)S(1)}, u32[]{:S(2)}, u32[]{:S(2)}) collective-permute-start(f32[2,1024]{1,0:T(2,128)S(1)} %get-tuple-element.123.refs_1_), channel_id=1, source_target_pairs={{0,3},{1,2},{2,1},{3,0},{4,7},{5,6},{6,5},{7,4},{8,11},{9,10},{10,... | collective-permute-start | bytes 24584 | tf_op jit(solution)/shard_map/ppermute | solution.py:599
  56.3 3.0 %mixer_back.1 = (f32[512,1024]{1,0:T(8,128)S(1)}, bf16[4,4,96,512]{3,2,1,0:T(8,128)(2,1)S(1)}, f32[512,512]{1,0:T(8,128)S(1)}, f32[16,512]{1,0:T(8,128)S(1)}) custom-call(s32[6]{0:T(128)S(1)} %pad_add_fusion.refs_0_, f32[2,1024]{1,0:T(2,128)S(1)} %get-tuple-element.123.refs_1_, f32[2,1024]{1,0:T(2,128)S(1)} %collective-permute-done.14.refs_2_, ...), custom_call_target="tpu_custom_call" | custom-call | flops 34359738368 | bytes 134217728 | tf_op jit(solution)/shard_map/mixer_back/pallas_call | solution.py:48
  59.3 1.8 %collective-permute-start.20 = (bf16[4,4,96,512]{3,2,1,0:T(8,128)(2,1)S(1)}, bf16[4,4,96,512]{3,2,1,0:T(8,128)(2,1)S(1)}, u32[]{:S(2)}, u32[]{:S(2)}) collective-permute-start(bf16[4,4,96,512]{3,2,1,0:T(8,128)(2,1)S(1)} %get-tuple-element.144), channel_id=1, source_target_pairs={{0,4},{4,0},{8,12},{12,8},{16,20},{20,16},{24,28},{28,24},{1,5},{5... | collective-permute-start | bytes 4718600 | tf_op jit(solution)/shard_map/ppermute | solution.py:599
  61.1 2.7 %mixer_out.1 = (bf16[4,4,96,512]{3,2,1,0:T(8,128)(2,1)S(1)}, f32[512,512]{1,0:T(8,128)S(1)}, f32[16,512]{1,0:T(8,128)S(1)}) custom-call(s32[6]{0:T(128)S(1)} %pad_add_fusion.refs_0_, f32[512,1024]{1,0:T(8,128)S(1)} %get-tuple-element.138.refs_1_, f32[512,1024]{1,0:T(8,128)S(1)} %get-tuple-element.105.refs_8_.refs_2_, ...), custom_call_target="tpu_custom_call" | custom-call | flops 17179869184 | bytes 67108864 | tf_op jit(solution)/shard_map/mixer_out/pallas_call | solution.py:48
  66.4 3.3 %collective-permute-done.23.refs_2_ = bf16[2,320,512]{2,1,0:T(8,128)(2,1)S(1)} collective-permute-done((bf16[2,320,512]{2,1,0:T(8,128)(2,1)S(1)}, bf16[2,320,512]{2,1,0:T(8,128)(2,1)S(1)}, u32[]{:S(2)}, u32[]{:S(2)}) %collective-permute-start.23) | collective-permute-done | bytes 655392 | tf_op jit(solution)/shard_map/ppermute | solution.py:599
  73.0 2.3 %tokens_out.1 = (bf16[512,512]{1,0:T(8,128)(2,1)}, f32[8,128]{1,0:T(8,128)S(1)}) custom-call(f32[512,512]{1,0:T(8,128)S(1)} %get-tuple-element.148.refs_0_, f32[512,512]{1,0:T(8,128)S(1)} %get-tuple-element.107.refs_10_.refs_13_.refs_1_, f32[1,512]{1,0:T(1,128)S(1)} %bitcast.33, f32[512,512]{1,0:T(8,128)S(1)} %get-tuple-element.149.refs_3_, ...), custom_call_target="tpu_custom_call" | custom-call | flops 2147483648 | bytes 8388608 | tf_op jit(solution)/shard_map/tokens_out/pallas_call | solution.py:48
  75.3 1.5 %mixed_out.1 = (bf16[512,512]{1,0:T(8,128)(2,1)}, f32[8,128]{1,0:T(8,128)S(1)}) custom-call(f32[512,512]{1,0:T(8,128)S(1)} %get-tuple-element.119.refs_0_, f32[2,192,512]{2,1,0:T(8,128)S(1)} %get-tuple-element.146.refs_1_.refs_4_.refs_5_), custom_call_target="tpu_custom_call" | custom-call | flops 1073741824 | bytes 4194304 | tf_op jit(solution)/shard_map/mixed_out/pallas_call | solution.py:48
  76.8 2.1 %collective-permute-done.22.refs_4_ = bf16[384,512]{1,0:T(8,128)(2,1)S(1)} collective-permute-done((bf16[384,512]{1,0:T(8,128)(2,1)S(1)}, bf16[384,512]{1,0:T(8,128)(2,1)S(1)}, u32[]{:S(2)}, u32[]{:S(2)}) %collective-permute-start.22) | collective-permute-done | bytes 393248 | tf_op jit(solution)/shard_map/ppermute | solution.py:599
  81.3 4.6 %collective-permute-done.27.refs_1_ = bf16[320,512]{1,0:T(8,128)(2,1)S(1)} collective-permute-done((bf16[320,512]{1,0:T(8,128)(2,1)S(1)}, bf16[320,512]{1,0:T(8,128)(2,1)S(1)}, u32[]{:S(2)}, u32[]{:S(2)}) %collective-permute-start.27) | collective-permute-done | bytes 327712 | tf_op jit(solution)/shard_map/ppermute | solution.py:599
  86.1 1.5 %collective-permute-start.30 = (bf16[320,512]{1,0:T(8,128)(2,1)S(1)}, bf16[320,512]{1,0:T(8,128)(2,1)S(1)}, u32[]{:S(2)}, u32[]{:S(2)}) collective-permute-start(bf16[320,512]{1,0:T(8,128)(2,1)S(1)} %get-tuple-element.173), channel_id=1, source_target_pairs={{0,1},{1,0},{2,3},{3,2},{4,5},{5,4},{6,7},{7,6},{8,9},{9,8},{10,11... | collective-permute-start | bytes 983048 | tf_op jit(solution)/shard_map/ppermute | solution.py:599
  87.5 2.5 %collective-permute-done.26.refs_4_ = bf16[192,512]{1,0:T(8,128)(2,1)S(1)} collective-permute-done((bf16[192,512]{1,0:T(8,128)(2,1)S(1)}, bf16[192,512]{1,0:T(8,128)(2,1)S(1)}, u32[]{:S(2)}, u32[]{:S(2)}) %collective-permute-start.26) | collective-permute-done | bytes 196640 | tf_op jit(solution)/shard_map/ppermute | solution.py:599
  91.5 1.5 %collective-permute-start.29 = (bf16[224,512]{1,0:T(8,128)(2,1)S(1)}, bf16[224,512]{1,0:T(8,128)(2,1)S(1)}, u32[]{:S(2)}, u32[]{:S(2)}) collective-permute-start(bf16[224,512]{1,0:T(8,128)(2,1)S(1)} %get-tuple-element.171), channel_id=1, source_target_pairs={{0,1},{1,0},{2,3},{3,2},{4,5},{5,4},{6,7},{7,6},{8,9},{9,8},{10,11... | collective-permute-start | bytes 688136 | tf_op jit(solution)/shard_map/ppermute | solution.py:599
  94.1 6.8 %collective-permute-done.29.refs_2_ = bf16[224,512]{1,0:T(8,128)(2,1)S(1)} collective-permute-done((bf16[224,512]{1,0:T(8,128)(2,1)S(1)}, bf16[224,512]{1,0:T(8,128)(2,1)S(1)}, u32[]{:S(2)}, u32[]{:S(2)}) %collective-permute-start.29) | collective-permute-done | bytes 229408 | tf_op jit(solution)/shard_map/ppermute | solution.py:599
  104.6 5.7 %collective-permute-done.31.refs_2_ = bf16[112,512]{1,0:T(8,128)(2,1)S(1)} collective-permute-done((bf16[112,512]{1,0:T(8,128)(2,1)S(1)}, bf16[112,512]{1,0:T(8,128)(2,1)S(1)}, u32[]{:S(2)}, u32[]{:S(2)}) %collective-permute-start.31) | collective-permute-done | bytes 114720 | tf_op jit(solution)/shard_map/ppermute | solution.py:599
  113.0 7.0 %collective-permute-start.33 = (f32[8,512]{1,0:T(8,128)S(1)}, f32[8,512]{1,0:T(8,128)S(1)}, u32[]{:S(2)}, u32[]{:S(2)}) collective-permute-start(f32[8,512]{1,0:T(8,128)S(1)} %get-tuple-element.179.refs_1_), channel_id=1, source_target_pairs={{0,4},{4,0},{8,12},{12,8},{16,20},{20,16},{24,28},{28,24},{1,5},{5... | collective-permute-start | bytes 49160 | tf_op jit(solution)/shard_map/ppermute | solution.py:599
  120.4 3.0 %collective-permute-start.37 = (bf16[4,96,512]{2,1,0:T(8,128)(2,1)S(1)}, bf16[4,96,512]{2,1,0:T(8,128)(2,1)S(1)}, u32[]{:S(2)}, u32[]{:S(2)}) collective-permute-start(bf16[4,96,512]{2,1,0:T(8,128)(2,1)S(1)} %join_mix.1.refs_3_), channel_id=1, source_target_pairs={{0,4},{4,0},{8,12},{12,8},{16,20},{20,16},{24,28},{28,24},{1,5},{5... | collective-permute-start | bytes 1179656 | tf_op jit(solution)/shard_map/ppermute | solution.py:599
  123.4 2.2 %spread_mlp.1 = (f32[512,512]{1,0:T(8,128)}, f32[512,512]{1,0:T(8,128)}, f32[256,512]{1,0:T(8,128)}, f32[8,128]{1,0:T(8,128)S(1)}) custom-call(s32[6]{0:T(128)S(1)} %pad_add_fusion.refs_0_, bf16[4,160,512]{2,1,0:T(8,128)(2,1)S(1)} %join_mlp.1.refs_1_, bf16[4,160,512]{2,1,0:T(8,128)(2,1)S(1)} %collective-permute-done.41.refs_2_), custom_call_target="tpu_custom_call" | custom-call | flops 17179869184 | bytes 67108864 | tf_op jit(solution)/shard_map/spread_mlp/pallas_call | solution.py:48
  125.6 1.8 %spread_mix.1 = (f32[3,128,1024]{2,1,0:T(8,128)}, f32[1,256]{1,0:T(1,128)}, f32[1,256]{1,0:T(1,128)}, f32[1,128]{1,0:T(1,128)}, f32[1,128]{1,0:T(1,128)}, /*index=5*/f32[1,512]{1,0:T(1,128)}) custom-call(s32[6]{0:T(128)S(1)} %pad_add_fusion.refs_0_, f32[8,512]{1,0:T(8,128)S(1)} %get-tuple-element.179.refs_1_, f32[8,512]{1,0:T(8,128)S(1)} %collective-permute-done.33.refs_2_, ...), custom_call_target="tpu_custom_call" | custom-call | flops 8589934592 | bytes 33554432 | tf_op jit(solution)/shard_map/spread_mix/pallas_call | solution.py:48
  (97 shorter events, 28.7 us)
Async XLA Ops:
  2.8 14.1 %collective-permute-start.5 = (bf16[128,512]{1,0:T(8,128)(2,1)S(1)}, bf16[128,512]{1,0:T(8,128)(2,1)S(1)}, u32[]{:S(2)}, u32[]{:S(2)}) collective-permute-start(bf16[128,512]{1,0:T(8,128)(2,1)S(1)} %pick_piece.1.refs_7_), channel_id=1, source_target_pairs={{0,1},{1,0},{2,3},{3,2},{4,5},{5,4},{6,7},{7,6},{8,9},{9,8},{10,11... | collective-permute-start | bytes 393224 | tf_op jit(solution)/shard_map/ppermute | solution.py:599
  5.0 14.0 %collective-permute-start.1 = (bf16[128,512]{1,0:T(8,128)(2,1)S(1)}, bf16[128,512]{1,0:T(8,128)(2,1)S(1)}, u32[]{:S(2)}, u32[]{:S(2)}) collective-permute-start(bf16[128,512]{1,0:T(8,128)(2,1)S(1)} %pick_piece.1.refs_7_), channel_id=1, source_target_pairs={{0,3},{1,2},{2,1},{3,0},{4,7},{5,6},{6,5},{7,4},{8,11},{9,10},{10,... | collective-permute-start | bytes 393224 | tf_op jit(solution)/shard_map/ppermute | solution.py:599
  7.2 12.1 %collective-permute-start = (bf16[128,512]{1,0:T(8,128)(2,1)S(1)}, bf16[128,512]{1,0:T(8,128)(2,1)S(1)}, u32[]{:S(2)}, u32[]{:S(2)}) collective-permute-start(bf16[128,512]{1,0:T(8,128)(2,1)S(1)} %pick_piece.1.refs_7_), channel_id=1, source_target_pairs={{0,2},{1,3},{2,0},{3,1},{4,6},{5,7},{6,4},{7,5},{8,10},{9,11},{10,... | collective-permute-start | bytes 393224 | tf_op jit(solution)/shard_map/ppermute | solution.py:599
  14.4 11.7 %collective-permute-start.12 = (f32[4,1024]{1,0:T(4,128)S(1)}, f32[4,1024]{1,0:T(4,128)S(1)}, u32[]{:S(2)}, u32[]{:S(2)}) collective-permute-start(f32[4,1024]{1,0:T(4,128)S(1)} %get-tuple-element.101.refs_2_.refs_1_), channel_id=1, source_target_pairs={{0,3},{1,2},{2,1},{3,0},{4,7},{5,6},{6,5},{7,4},{8,11},{9,10},{10,... | collective-permute-start | bytes 49160 | tf_op jit(solution)/shard_map/ppermute | solution.py:599
  16.8 9.8 %collective-permute-start.11 = (f32[4,1024]{1,0:T(4,128)S(1)}, f32[4,1024]{1,0:T(4,128)S(1)}, u32[]{:S(2)}, u32[]{:S(2)}) collective-permute-start(f32[4,1024]{1,0:T(4,128)S(1)} %get-tuple-element.101.refs_2_.refs_1_), channel_id=1, source_target_pairs={{0,2},{1,3},{2,0},{3,1},{4,6},{5,7},{6,4},{7,5},{8,10},{9,11},{10,... | collective-permute-start | bytes 49160 | tf_op jit(solution)/shard_map/ppermute | solution.py:599
  21.6 9.2 %collective-permute-start.10 = (f32[4,1024]{1,0:T(4,128)S(1)}, f32[4,1024]{1,0:T(4,128)S(1)}, u32[]{:S(2)}, u32[]{:S(2)}) collective-permute-start(f32[4,1024]{1,0:T(4,128)S(1)} %get-tuple-element.101.refs_2_.refs_1_), channel_id=1, source_target_pairs={{0,1},{1,0},{2,3},{3,2},{4,5},{5,4},{6,7},{7,6},{8,9},{9,8},{10,11... | collective-permute-start | bytes 49160 | tf_op jit(solution)/shard_map/ppermute | solution.py:599
  23.6 14.8 %collective-permute-start.4 = (bf16[256,512]{1,0:T(8,128)(2,1)S(1)}, bf16[256,512]{1,0:T(8,128)(2,1)S(1)}, u32[]{:S(2)}, u32[]{:S(2)}) collective-permute-start(bf16[256,512]{1,0:T(8,128)(2,1)S(1)} %join_depth.1.refs_17_.refs_0_), channel_id=1, source_target_pairs={{0,24},{4,28},{8,16},{12,20},{16,8},{20,12},{24,0},{28,4},{1,25},{... | collective-permute-start | bytes 786440 | tf_op jit(solution)/shard_map/ppermute | solution.py:599
  25.2 13.1 %collective-permute-start.3 = (bf16[256,512]{1,0:T(8,128)(2,1)S(1)}, bf16[256,512]{1,0:T(8,128)(2,1)S(1)}, u32[]{:S(2)}, u32[]{:S(2)}) collective-permute-start(bf16[256,512]{1,0:T(8,128)(2,1)S(1)} %join_depth.1.refs_17_.refs_0_), channel_id=1, source_target_pairs={{0,16},{4,20},{8,24},{12,28},{16,0},{20,4},{24,8},{28,12},{1,17},{... | collective-permute-start | bytes 786440 | tf_op jit(solution)/shard_map/ppermute | solution.py:599
  26.1 12.3 %collective-permute-start.2 = (bf16[256,512]{1,0:T(8,128)(2,1)S(1)}, bf16[256,512]{1,0:T(8,128)(2,1)S(1)}, u32[]{:S(2)}, u32[]{:S(2)}) collective-permute-start(bf16[256,512]{1,0:T(8,128)(2,1)S(1)} %join_depth.1.refs_17_.refs_0_), channel_id=1, source_target_pairs={{0,8},{4,12},{8,0},{12,4},{16,24},{20,28},{24,16},{28,20},{1,9},{5... | collective-permute-start | bytes 786440 | tf_op jit(solution)/shard_map/ppermute | solution.py:599
  26.6 8.8 %collective-permute-start.9 = (bf16[4,128,512]{2,1,0:T(8,128)(2,1)S(1)}, bf16[4,128,512]{2,1,0:T(8,128)(2,1)S(1)}, u32[]{:S(2)}, u32[]{:S(2)}) collective-permute-start(bf16[4,128,512]{2,1,0:T(8,128)(2,1)S(1)} %join_one.1.refs_1_), channel_id=1, source_target_pairs={{0,4},{4,0},{8,12},{12,8},{16,20},{20,16},{24,28},{28,24},{1,5},{5... | collective-permute-start | bytes 1572872 | tf_op jit(solution)/shard_map/ppermute | solution.py:599
  39.2 14.1 %collective-permute-start.17 = (bf16[4,256,512]{2,1,0:T(8,128)(2,1)S(1)}, bf16[4,256,512]{2,1,0:T(8,128)(2,1)S(1)}, u32[]{:S(2)}, u32[]{:S(2)}) collective-permute-start(bf16[4,256,512]{2,1,0:T(8,128)(2,1)S(1)} %get-tuple-element.132), channel_id=1, source_target_pairs={{0,4},{4,0},{8,12},{12,8},{16,20},{20,16},{24,28},{28,24},{1,5},{5... | collective-permute-start | bytes 3145736 | tf_op jit(solution)/shard_map/ppermute | solution.py:599
  46.4 7.0 %collective-permute-start.18 = (bf16[4,256,512]{2,1,0:T(8,128)(2,1)S(1)}, bf16[4,256,512]{2,1,0:T(8,128)(2,1)S(1)}, u32[]{:S(2)}, u32[]{:S(2)}) collective-permute-start(bf16[4,256,512]{2,1,0:T(8,128)(2,1)S(1)} %get-tuple-element.134), channel_id=1, source_target_pairs={{0,4},{4,0},{8,12},{12,8},{16,20},{20,16},{24,28},{28,24},{1,5},{5... | collective-permute-start | bytes 3145736 | tf_op jit(solution)/shard_map/ppermute | solution.py:599
  49.9 6.4 %collective-permute-start.16 = (f32[2,1024]{1,0:T(2,128)S(1)}, f32[2,1024]{1,0:T(2,128)S(1)}, u32[]{:S(2)}, u32[]{:S(2)}) collective-permute-start(f32[2,1024]{1,0:T(2,128)S(1)} %get-tuple-element.123.refs_1_), channel_id=1, source_target_pairs={{0,3},{1,2},{2,1},{3,0},{4,7},{5,6},{6,5},{7,4},{8,11},{9,10},{10,... | collective-permute-start | bytes 24584 | tf_op jit(solution)/shard_map/ppermute | solution.py:599
  54.6 15.1 %collective-permute-start.23 = (bf16[2,320,512]{2,1,0:T(8,128)(2,1)S(1)}, bf16[2,320,512]{2,1,0:T(8,128)(2,1)S(1)}, u32[]{:S(2)}, u32[]{:S(2)}) collective-permute-start(bf16[2,320,512]{2,1,0:T(8,128)(2,1)S(1)} %get-tuple-element.155), channel_id=1, source_target_pairs={{0,8},{4,12},{8,0},{12,4},{16,24},{20,28},{24,16},{28,20},{1,9},{5... | collective-permute-start | bytes 1966088 | tf_op jit(solution)/shard_map/ppermute | solution.py:599
  55.7 14.8 %collective-permute-start.24 = (bf16[2,320,512]{2,1,0:T(8,128)(2,1)S(1)}, bf16[2,320,512]{2,1,0:T(8,128)(2,1)S(1)}, u32[]{:S(2)}, u32[]{:S(2)}) collective-permute-start(bf16[2,320,512]{2,1,0:T(8,128)(2,1)S(1)} %get-tuple-element.157), channel_id=1, source_target_pairs={{0,16},{4,20},{8,24},{12,28},{16,0},{20,4},{24,8},{28,12},{1,17},{... | collective-permute-start | bytes 1966088 | tf_op jit(solution)/shard_map/ppermute | solution.py:599
  65.0 13.9 %collective-permute-start.21 = (bf16[416,512]{1,0:T(8,128)(2,1)S(1)}, bf16[416,512]{1,0:T(8,128)(2,1)S(1)}, u32[]{:S(2)}, u32[]{:S(2)}) collective-permute-start(bf16[416,512]{1,0:T(8,128)(2,1)S(1)} %get-tuple-element.151), channel_id=1, source_target_pairs={{0,8},{4,12},{8,0},{12,4},{16,24},{20,28},{24,16},{28,20},{1,9},{5... | collective-permute-start | bytes 1277960 | tf_op jit(solution)/shard_map/ppermute | solution.py:599
  66.0 12.9 %collective-permute-start.22 = (bf16[384,512]{1,0:T(8,128)(2,1)S(1)}, bf16[384,512]{1,0:T(8,128)(2,1)S(1)}, u32[]{:S(2)}, u32[]{:S(2)}) collective-permute-start(bf16[384,512]{1,0:T(8,128)(2,1)S(1)} %get-tuple-element.153), channel_id=1, source_target_pairs={{0,16},{4,20},{8,24},{12,28},{16,0},{20,4},{24,8},{28,12},{1,17},{... | collective-permute-start | bytes 1179656 | tf_op jit(solution)/shard_map/ppermute | solution.py:599
  71.2 14.7 %collective-permute-start.27 = (bf16[320,512]{1,0:T(8,128)(2,1)S(1)}, bf16[320,512]{1,0:T(8,128)(2,1)S(1)}, u32[]{:S(2)}, u32[]{:S(2)}) collective-permute-start(bf16[320,512]{1,0:T(8,128)(2,1)S(1)} %get-tuple-element.166), channel_id=1, source_target_pairs={{0,16},{4,20},{8,24},{12,28},{16,0},{20,4},{24,8},{28,12},{1,17},{... | collective-permute-start | bytes 983048 | tf_op jit(solution)/shard_map/ppermute | solution.py:599
  71.9 14.1 %collective-permute-start.28 = (bf16[320,512]{1,0:T(8,128)(2,1)S(1)}, bf16[320,512]{1,0:T(8,128)(2,1)S(1)}, u32[]{:S(2)}, u32[]{:S(2)}) collective-permute-start(bf16[320,512]{1,0:T(8,128)(2,1)S(1)} %get-tuple-element.168), channel_id=1, source_target_pairs={{0,8},{4,12},{8,0},{12,4},{16,24},{20,28},{24,16},{28,20},{1,9},{5... | collective-permute-start | bytes 983048 | tf_op jit(solution)/shard_map/ppermute | solution.py:599
  79.6 10.4 %collective-permute-start.26 = (bf16[192,512]{1,0:T(8,128)(2,1)S(1)}, bf16[192,512]{1,0:T(8,128)(2,1)S(1)}, u32[]{:S(2)}, u32[]{:S(2)}) collective-permute-start(bf16[192,512]{1,0:T(8,128)(2,1)S(1)} %get-tuple-element.164), channel_id=1, source_target_pairs={{0,8},{4,12},{8,0},{12,4},{16,24},{20,28},{24,16},{28,20},{1,9},{5... | collective-permute-start | bytes 589832 | tf_op jit(solution)/shard_map/ppermute | solution.py:599
  80.6 10.2 %collective-permute-start.25 = (bf16[224,512]{1,0:T(8,128)(2,1)S(1)}, bf16[224,512]{1,0:T(8,128)(2,1)S(1)}, u32[]{:S(2)}, u32[]{:S(2)}) collective-permute-start(bf16[224,512]{1,0:T(8,128)(2,1)S(1)} %get-tuple-element.162), channel_id=1, source_target_pairs={{0,16},{4,20},{8,24},{12,28},{16,0},{20,4},{24,8},{28,12},{1,17},{... | collective-permute-start | bytes 688136 | tf_op jit(solution)/shard_map/ppermute | solution.py:599
  86.1 6.9 %collective-permute-start.30 = (bf16[320,512]{1,0:T(8,128)(2,1)S(1)}, bf16[320,512]{1,0:T(8,128)(2,1)S(1)}, u32[]{:S(2)}, u32[]{:S(2)}) collective-permute-start(bf16[320,512]{1,0:T(8,128)(2,1)S(1)} %get-tuple-element.173), channel_id=1, source_target_pairs={{0,1},{1,0},{2,3},{3,2},{4,5},{5,4},{6,7},{7,6},{8,9},{9,8},{10,11... | collective-permute-start | bytes 983048 | tf_op jit(solution)/shard_map/ppermute | solution.py:599
  91.5 9.4 %collective-permute-start.29 = (bf16[224,512]{1,0:T(8,128)(2,1)S(1)}, bf16[224,512]{1,0:T(8,128)(2,1)S(1)}, u32[]{:S(2)}, u32[]{:S(2)}) collective-permute-start(bf16[224,512]{1,0:T(8,128)(2,1)S(1)} %get-tuple-element.171), channel_id=1, source_target_pairs={{0,1},{1,0},{2,3},{3,2},{4,5},{5,4},{6,7},{7,6},{8,9},{9,8},{10,11... | collective-permute-start | bytes 688136 | tf_op jit(solution)/shard_map/ppermute | solution.py:599
  93.0 8.8 %collective-permute-start.32 = (bf16[160,512]{1,0:T(8,128)(2,1)S(1)}, bf16[160,512]{1,0:T(8,128)(2,1)S(1)}, u32[]{:S(2)}, u32[]{:S(2)}) collective-permute-start(bf16[160,512]{1,0:T(8,128)(2,1)S(1)} %get-tuple-element.178), channel_id=1, source_target_pairs={{0,2},{1,3},{2,0},{3,1},{4,6},{5,7},{6,4},{7,5},{8,10},{9,11},{10,... | collective-permute-start | bytes 491528 | tf_op jit(solution)/shard_map/ppermute | solution.py:599
  101.5 8.8 %collective-permute-start.31 = (bf16[112,512]{1,0:T(8,128)(2,1)S(1)}, bf16[112,512]{1,0:T(8,128)(2,1)S(1)}, u32[]{:S(2)}, u32[]{:S(2)}) collective-permute-start(bf16[112,512]{1,0:T(8,128)(2,1)S(1)} %get-tuple-element.177), channel_id=1, source_target_pairs={{0,2},{1,3},{2,0},{3,1},{4,6},{5,7},{6,4},{7,5},{8,10},{9,11},{10,... | collective-permute-start | bytes 344072 | tf_op jit(solution)/shard_map/ppermute | solution.py:599
  101.8 9.8 %collective-permute-start.40 = (bf16[160,512]{1,0:T(8,128)(2,1)S(1)}, bf16[160,512]{1,0:T(8,128)(2,1)S(1)}, u32[]{:S(2)}, u32[]{:S(2)}) collective-permute-start(bf16[160,512]{1,0:T(8,128)(2,1)S(1)} %add_last.1.refs_3_.refs_0_), channel_id=1, source_target_pairs={{0,24},{4,28},{8,16},{12,20},{16,8},{20,12},{24,0},{28,4},{1,25},{... | collective-permute-start | bytes 491528 | tf_op jit(solution)/shard_map/ppermute | solution.py:599
  103.2 9.8 %collective-permute-start.39 = (bf16[160,512]{1,0:T(8,128)(2,1)S(1)}, bf16[160,512]{1,0:T(8,128)(2,1)S(1)}, u32[]{:S(2)}, u32[]{:S(2)}) collective-permute-start(bf16[160,512]{1,0:T(8,128)(2,1)S(1)} %add_last.1.refs_3_.refs_0_), channel_id=1, source_target_pairs={{0,16},{4,20},{8,24},{12,28},{16,0},{20,4},{24,8},{28,12},{1,17},{... | collective-permute-start | bytes 491528 | tf_op jit(solution)/shard_map/ppermute | solution.py:599
  104.1 15.9 %collective-permute-start.38 = (bf16[160,512]{1,0:T(8,128)(2,1)S(1)}, bf16[160,512]{1,0:T(8,128)(2,1)S(1)}, u32[]{:S(2)}, u32[]{:S(2)}) collective-permute-start(bf16[160,512]{1,0:T(8,128)(2,1)S(1)} %add_last.1.refs_3_.refs_0_), channel_id=1, source_target_pairs={{0,8},{4,12},{8,0},{12,4},{16,24},{20,28},{24,16},{28,20},{1,9},{5... | collective-permute-start | bytes 491528 | tf_op jit(solution)/shard_map/ppermute | solution.py:599
  110.2 10.1 %collective-permute-start.36 = (bf16[96,512]{1,0:T(8,128)(2,1)S(1)}, bf16[96,512]{1,0:T(8,128)(2,1)S(1)}, u32[]{:S(2)}, u32[]{:S(2)}) collective-permute-start(bf16[96,512]{1,0:T(8,128)(2,1)S(1)} %get-tuple-element.180.refs_0_.refs_4_), channel_id=1, source_target_pairs={{0,24},{4,28},{8,16},{12,20},{16,8},{20,12},{24,0},{28,4},{1,25},{... | collective-permute-start | bytes 294920 | tf_op jit(solution)/shard_map/ppermute | solution.py:599
  111.5 8.8 %collective-permute-start.35 = (bf16[96,512]{1,0:T(8,128)(2,1)S(1)}, bf16[96,512]{1,0:T(8,128)(2,1)S(1)}, u32[]{:S(2)}, u32[]{:S(2)}) collective-permute-start(bf16[96,512]{1,0:T(8,128)(2,1)S(1)} %get-tuple-element.180.refs_0_.refs_4_), channel_id=1, source_target_pairs={{0,16},{4,20},{8,24},{12,28},{16,0},{20,4},{24,8},{28,12},{1,17},{... | collective-permute-start | bytes 294920 | tf_op jit(solution)/shard_map/ppermute | solution.py:599
  111.6 8.7 %collective-permute-start.34 = (bf16[96,512]{1,0:T(8,128)(2,1)S(1)}, bf16[96,512]{1,0:T(8,128)(2,1)S(1)}, u32[]{:S(2)}, u32[]{:S(2)}) collective-permute-start(bf16[96,512]{1,0:T(8,128)(2,1)S(1)} %get-tuple-element.180.refs_0_.refs_4_), channel_id=1, source_target_pairs={{0,8},{4,12},{8,0},{12,4},{16,24},{20,28},{24,16},{28,20},{1,9},{5... | collective-permute-start | bytes 294920 | tf_op jit(solution)/shard_map/ppermute | solution.py:599
  113.0 12.6 %collective-permute-start.33 = (f32[8,512]{1,0:T(8,128)S(1)}, f32[8,512]{1,0:T(8,128)S(1)}, u32[]{:S(2)}, u32[]{:S(2)}) collective-permute-start(f32[8,512]{1,0:T(8,128)S(1)} %get-tuple-element.179.refs_1_), channel_id=1, source_target_pairs={{0,4},{4,0},{8,12},{12,8},{16,20},{20,16},{24,28},{28,24},{1,5},{5... | collective-permute-start | bytes 49160 | tf_op jit(solution)/shard_map/ppermute | solution.py:599
  (18 other events, 111.5 us)

commit v4 on v3

--- a/solution.py
+++ b/solution.py
@@ -19,10 +19,11 @@
 
 
 weight = {
-    "pick_piece": 16, "mixer_in": 32, "join_depth": 8, "block_mid": 16, "join_one": 32, "mlp_one": 8, "join_two": 1,
-    "mlp_two": 16, "mid_back": 32, "add_core": 32, "mixer_back": 32, "mixer_out": 16, "add_core_small": 0, "add_cross": 0,
-    "mixed_out": 1, "tokens_out": 2, "add_cross_small": 2, "add_depth": 16, "add_depth_small": 32, "add_far": 16,
-    "add_far_small": 1, "add_last": 0, "add_last_small": 4, "join_mlp": 2, "join_mix": 32, "spread_mlp": 16, "spread_mix": 8,
+    "pick_piece": 4, "mixer_in": 0, "join_depth": 16, "join_one": 0, "mlp_one": 0, "join_two": 0, "mlp_two": 32, "mid_back": 32,
+    "add_core": 32, "mixer_back": 0, "mixer_out": 16, "add_core_small": 4, "add_cross": 0, "mixed_out": 0, "tokens_out": 2,
+    "add_cross_small": 0, "add_depth": 0, "add_depth_small": 8, "add_far": 2, "add_far_small": 16, "add_last": 4,
+    "add_last_small": 4, "join_mlp": 2, "join_mix": 16, "spread_mlp": 8, "spread_mix": 8, "add_pair": 2, "mid_in": 0,
+    "mlp_own": 16,
 }
 
 
@@ -181,12 +182,12 @@
     return bsum
 
 
-def block_mid(idx, own, r1, r2, r3, prods, ends, decay, share, cand, x, cot, w_out, gain, wu, wd, bu,
-              st, stT, middle, nm2, nm2t, cotp, mix, gn, bsum, keep, send, split, others, hT, carry8):
+def mid_in(idx, own, r1, r2, r3, prods, ends, decay, share, cand, x, cot, w_out, gain,
+           st, stT, middle, nm2, nm2t, cotp, split, others, carry8, square):
     length = x.shape[0]
     steps = length // chunks
     units = decay.shape[1]
-    core, z = idx[0], idx[2]
+    z = idx[2]
     for j, ref in enumerate((own, r1, r2, r3)):
         others[j] = ref[...]
     state = jnp.zeros((1, units), f32)
@@ -215,46 +216,52 @@
     nm2t[...] = nm.T
 
     def put(rows, cols, values):
-        gn[rows, cols] = values
+        square[rows, cols] = values
 
     to_chunked(cot, split, put)
-    cotp[...] = gn[...].astype(bf16)
+    cotp[...] = square[...].astype(bf16)
+
+
+def pieces_of(idx, near, near_far, far, far_far):
+    for which, arrays in ((idx[0], (near, near_far)), (1 - idx[0], (far, far_far))):
+        for k in range(2):
+            for i in range(2):
+                yield which, idx[1] ^ (i * (1 + which) + k * (2 - which)), arrays[k].at[i]
+
+
+def lay_out(idx, arrays, at, wu, wd):
+    rows = wu.shape[0] // 8
+    for which, place, piece in pieces_of(idx, *arrays):
+        spot = pl.ds(pl.multiple_of((which * 4 + place) * rows, rows), rows)
+        wu[spot, :] = piece[at : at + rows, :]
+        wd[spot, :] = piece[at + rows : at + 2 * rows, :]
+
+
+def mlp_own(idx, wu, wd, bu, middle, nm2, nm2t, cotp, mix, gn, keep, send, small, hT):
+    mix[...] = middle[...]
     gn[...] = jnp.zeros_like(gn)
-    mix[...] = mid
-    bsum[...] = ffn_block(0, core, nm, nm2t, cotp[...], wu[...], wd[...], bu[...], mix, gn, keep, send, hT)
-
-
-def lay_out(idx, near, far, at, wu, wd):
-    rows = wu.shape[0] // 8
-    for which, pieces in ((idx[0], near), (1 - idx[0], far)):
-        for k in range(4):
-            spot = pl.ds(pl.multiple_of((which * 4 + (idx[1] ^ k)) * rows, rows), rows)
-            wu[spot, :] = pieces[k, at : at + rows, :]
-            wd[spot, :] = pieces[k, at + rows : at + 2 * rows, :]
-
-
-def mlp_one(idx, near, far, bias, mix0, gn0, bsum0, nm2, nm2t, cotp, keep0, send0,
-            mix, gn, keep, send, small, hT, wu, wd):
-    z = idx[2]
-    block = keep0.shape[1]
+    small[...] = jnp.zeros_like(small)
+    small[pl.ds(4 * idx[2] + 2, 1), :] = ffn_block(
+        0, idx[0], nm2[...], nm2t, cotp[...], wu[...], wd[...], bu[...], mix, gn, keep, send, hT
+    )
+
+
+def mlp_one(idx, n1, n2, f1, f2, bias, mix0, gn0, small0, nm2, nm2t, cotp, mix, gn, keep, send, small, hT, wu, wd):
     mix[...] = mix0[...]
     gn[...] = gn0[...]
-    keep[:, 0:block, :] = keep0[...]
-    send[:, 0:block, :] = send0[...]
-    small[...] = jnp.zeros_like(small)
-    small[pl.ds(4 * z + 2, 1), :] = bsum0[...]
-    lay_out(idx, near, far, 0, wu, wd)
-    small[pl.ds(4 * (z ^ 1) + 2, 1), :] = ffn_block(
-        1, idx[0], nm2[...], nm2t, cotp[...], wu[...], wd[...], bias[2:3, 0 : wu.shape[1]], mix, gn, keep, send, hT
-    )
-
-
-def mlp_two(idx, near, far, bias2, bias3, mix0, gn0, small0, nm2, nm2t, cotp, mix, gn, keep, send, small, hT, wu, wd):
+    small[...] = small0[...]
+    lay_out(idx, (n1, n2, f1, f2), 0, wu, wd)
+    small[pl.ds(4 * (idx[2] ^ 1) + 2, 1), :] = ffn_block(
+        0, idx[0], nm2[...], nm2t, cotp[...], wu[...], wd[...], bias[2:3, 0 : wu.shape[1]], mix, gn, keep, send, hT
+    )
+
+
+def mlp_two(idx, n1, n2, f1, f2, bias2, bias3, mix0, gn0, small0, nm2, nm2t, cotp, mix, gn, keep, send, small, hT, wu, wd):
     mix[...] = mix0[...]
     gn[...] = gn0[...]
     small[...] = small0[...]
     for slot, bias in enumerate((bias2, bias3)):
-        lay_out(idx, near, far, slot * wu.shape[0] // 4, wu, wd)
+        lay_out(idx, (n1, n2, f1, f2), slot * wu.shape[0] // 4, wu, wd)
         small[pl.ds(4 * (idx[2] ^ (2 + slot)) + 2, 1), :] = ffn_block(
             slot, idx[0], nm2[...], nm2t, cotp[...], wu[...], wd[...], bias[2:3, 0 : wu.shape[1]], mix, gn, keep, send, hT
         )
@@ -420,20 +427,26 @@
     return high, (v - high.astype(f32)).astype(bf16)
 
 
-def add_core(idx, keep_a, got_a, keep_b, got_b, keep_c, got_c, send_x, send_y, own_x, own_y):
+def add_pair(keep, got, out):
+    out[...] = (keep[...].astype(f32) + got[...].astype(f32)).astype(bf16)
+
+
+def add_core(idx, keep_a, got_a, more_a, keep_b, got_b, keep_c, got_c, send_x, send_y, own_x, own_y):
     x, y = idx[1] % 2, idx[1] // 2
     half = send_x.shape[1]
 
     def put(ref, k, p, first):
         top = 0
-        for keep, got in ((keep_a, got_a), (keep_b, got_b), (keep_c, got_c)):
-            low, high = max(first, top), min(first + half, top + keep.shape[1])
+        for arrays in ((keep_a, got_a, more_a), (keep_b, got_b), (keep_c, got_c)):
+            n = arrays[0].shape[1]
+            low, high = max(first, top), min(first + half, top + n)
             if low < high:
                 rows = slice(low - top, high - top)
-                ref[k, low - first : high - first, :] = (
-                    keep[p, rows, :].astype(f32) + got[p, rows, :].astype(f32)
-                ).astype(ref.dtype)
-            top += keep.shape[1]
+                total = arrays[0][p, rows, :].astype(f32)
+                for more in arrays[1:]:
+                    total = total + more[p, rows, :].astype(f32)
+                ref[k, low - first : high - first, :] = total.astype(ref.dtype)
+            top += n
 
     for k in range(2):
         put(send_x, k, 2 * k + 1 - x, 0)
@@ -451,23 +464,25 @@
 
 
 def add_depth(own_x, got_x, own_y, got_y, send, own, total):
-    rows = send.shape[0] // 2
+    half = own_x.shape[0]
+    part = send.shape[0] // 6
+    block = 4 * part
+    total[0:half, :] = own_x[...] + got_x[...].astype(f32)
+    total[half:, :] = own_y[...] + got_y[...].astype(f32)
+    out = 3 * block
+    for ref, to, at, n in ((send, 0, 2 * block, block), (send, block, out + part, part), (send, block + part, out + 3 * part, part),
+                           (own, 0, 0, block), (own, block, out, part), (own, block + part, block, block), (own, 2 * block + part, out + 2 * part, part)):
+        ref[to : to + n, :] = total[at : at + n, :].astype(ref.dtype)
+
+
+def add_far(own, got, send, out):
+    rows = out.shape[0]
     part = rows // 5
     block = 4 * part
-    half = own_x.shape[0]
-    total[0:half, :] = own_x[...] + got_x[...].astype(f32)
-    total[half:, :] = own_y[...] + got_y[...].astype(f32)
-    for j, ref, base in ((1, send, 0), (2, own, rows), (3, send, rows), (0, own, 0)):
-        at = j * block
-        ref[base : base + block, :] = total[at : at + block, :].astype(ref.dtype)
-        at = 4 * block + j * part
-        ref[base + block : base + rows, :] = total[at : at + part, :].astype(ref.dtype)
-
-
-def add_far(own, got, send, out):
-    rows = out.shape[0]
-    out[...] = own[0:rows, :] + got[0:rows, :].astype(f32)
-    send[...] = (own[rows:, :] + got[rows:, :].astype(f32)).astype(bf16)
+    out[0:block, :] = own[0:block, :]
+    out[block:, :] = own[block:rows, :] + got[block:rows, :].astype(f32)
+    send[0:block, :] = (own[rows : rows + block, :] + got[0:block, :].astype(f32)).astype(bf16)
+    send[block:, :] = (own[rows + block :, :] + got[rows:, :].astype(f32)).astype(bf16)
 
 
 def add_last(own, got, out):
@@ -599,6 +614,11 @@
     return lax.ppermute(value, axis, [(i, i ^ bit) for i in range(size)])
 
 
+def across(value, turn):
+    size = lax.axis_size("dp")
+    return lax.ppermute(value, "dp", [(i, i ^ (2 << ((i & 1) ^ turn))) for i in range(size)])
+
+
 def on_device(tokens, gain_mix, w_mix, bias_forget, bias_input, w_out, gain_mlp, w_up, b_up, w_down, resets, cotangent):
     length, width = tokens.shape[1:]
     units = w_out.shape[0]
@@ -632,45 +652,50 @@
     )
     ahead = [swap(payload, "mp", j) for j in (1, 2, 3)]
     around = lambda v: [v] + [swap(v, "dp", 2 * k) for k in (1, 2, 3)]
-    near_one = around(gate(depth[0], payload))
-    (pair,) = call(join, "join_depth", depth[1:], [shape_of(bf16, width // 2, ff)], smem=0, after=(payload,))
-    near_two = around(pair)
-    (near_one,) = call(join, "join_one", near_one, [shape_of(bf16, 4, width // 4, ff)], smem=0)
-    far_one = swap(near_one, "dp", 1)
+    mine = gate(depth[0], payload)
+    (two,) = call(join, "join_depth", depth[1:], [shape_of(bf16, width // 2, ff)], smem=0, after=(payload,))
+    (one_a,) = call(join, "join_one", (mine, across(mine, 0)), [shape_of(bf16, 2, width // 4, ff)], smem=0, after=(two,))
+    (two_a,) = call(join, "join_two", (two, across(two, 0)), [shape_of(bf16, 2, width // 2, ff)], smem=0)
+    two_b = across(two_a, 1)
     quarter = width // 8
-    st, stT, middle, nm2, nm2t, cotp, mix, gn, bsum, keep0, send0 = call(
-        block_mid, "block_mid",
-        (idx, payload, *ahead, prods, ends, decay, share, cand, x, cot, w_out, row(gain_mlp), w_up, w_down, row(b_up)),
-        [shape_of(f32, length + chunks, units), shape_of(bf16, units, length), square, square16, shape_of(bf16, width, length),
-         square16, square, square, shape_of(f32, 1, ff)] + [shape_of(bf16, 4, 2 * quarter, width)] * 2,
-        [pltpu.VMEM((lanes, length, 128), f32), pltpu.VMEM((4, 4, units), f32), pltpu.VMEM((ff, length), bf16),
-         pltpu.VMEM((chunks, units), f32)], after=(pair,),
+    st, stT, middle, nm2, nm2t, cotp = call(
+        mid_in, "mid_in",
+        (idx, payload, *ahead, prods, ends, decay, share, cand, x, cot, w_out, row(gain_mlp)),
+        [shape_of(f32, length + chunks, units), shape_of(bf16, units, length), square, square16, shape_of(bf16, width, length), square16],
+        [pltpu.VMEM((lanes, length, 128), f32), pltpu.VMEM((4, 4, units), f32), pltpu.VMEM((chunks, units), f32), pltpu.VMEM((length, width), f32)],
+        after=(two_a,),
     )
     block = 2 * quarter
     pair = lambda dtype, rows: shape_of(dtype, 2, rows, width)
     weights = [pltpu.VMEM((ff, length), bf16), pltpu.VMEM((width, ff), bf16), pltpu.VMEM((ff, width), bf16)]
+    grads = lambda rows: [square] * 2 + [shape_of(bf16, 4, rows, width)] * 2 + [shape_of(f32, 16, width)]
+    one_b = gate(across(one_a, 1), nm2)
+    mix, gn, keep0, send0, small_mlp = call(
+        mlp_own, "mlp_own", (idx, w_up, w_down, row(b_up), middle, nm2, nm2t, cotp), grads(block), weights[:1],
+    )
     mix, gn, keep_a, send_a, small_mlp = call(
         mlp_one, "mlp_one",
-        (idx, near_one, far_one, ahead[0], mix, gn, bsum, nm2, nm2t, cotp, keep0, send0),
-        [square] * 2 + [shape_of(bf16, 4, 2 * block, width)] * 2 + [shape_of(f32, 16, width)], weights,
-    )
-    (near_two,) = call(join, "join_two", near_two, [shape_of(bf16, 4, width // 2, ff)], smem=0, after=(gn,))
+        (idx, one_a, one_b, swap(one_a, "dp", 1), swap(one_b, "dp", 1), ahead[0], mix, gn, small_mlp, nm2, nm2t, cotp), grads(block), weights,
+    )
+    (pair_a,) = call(add_pair, "add_pair", (keep_a, swap(send_a, "dp", 1)), [shape_of(bf16, 4, block, width)], smem=0)
+    more_a = swap(pair_a, "mp", 1)
     mix, gn, keep, send, small_mlp = call(
         mlp_two, "mlp_two",
-        (idx, near_two, swap(near_two, "dp", 1), ahead[1], ahead[2], mix, gn, small_mlp, nm2, nm2t, cotp),
-        [square] * 2 + [shape_of(bf16, 4, 2 * block, width)] * 2 + [shape_of(f32, 16, width)], weights,
-    )
-    got_a, got = swap(send_a, "dp", 1), swap(send, "dp", 1)
+        (idx, two_a, two_b, swap(two_a, "dp", 1), swap(two_b, "dp", 1), ahead[1], ahead[2], mix, gn, small_mlp, nm2, nm2t, cotp),
+        grads(2 * block), weights, after=(pair_a,),
+    )
+    got, got0 = swap(send, "dp", 1), swap(send0, "dp", 1)
     out_rows = units // 8
     keep_out, send_out, grad_mid, grad_states, payload, prods, flows, gain_row = call(
         mid_back, "mid_back",
         (idx, gn, cotp, middle, row(gain_mlp), stT, w_out, decay),
         [shape_of(bf16, 4, out_rows, width)] * 2 + [square, wide, shape_of(f32, 2, units), edge, edge, shape_of(f32, 1, width)],
     )
+    payload = gate(payload, got)
     behind = [swap(payload, "mp", j) for j in (1, 2, 3)]
 
-    half = (4 * block + out_rows) // 2
-    send_x, send_y, own_x, own_y = call(add_core, "add_core", (idx, keep_a, got_a, keep, got, keep_out, swap(send_out, "dp", 1)),
+    half = (3 * block + out_rows) // 2
+    send_x, send_y, own_x, own_y = call(add_core, "add_core", (idx, keep0, got0, more_a, keep, got, keep_out, swap(send_out, "dp", 1)),
                                         [pair(bf16, half)] * 2 + [pair(f32, half)] * 2)
     got_x, got_y = swap(send_x, "dp", 2), swap(send_y, "dp", 4)
 
@@ -710,7 +735,7 @@
     )
     got_mx, got_my = swap(send_my, "dp", 4), swap(send_mx, "dp", 2)
     rows_f = block + units // 32
-    send, own = call(add_depth, "add_depth", (own_x, got_x, own_y, got_y), [one(bf16, 2 * rows_f), one(f32, 2 * rows_f)],
+    send, own = call(add_depth, "add_depth", (own_x, got_x, own_y, got_y), [one(bf16, block + units // 16), one(f32, 2 * rows_f)],
                      [pltpu.VMEM((2 * half, width), f32)], smem=0, after=(own_mx,))
     got = swap(send, "mp", 1)
     send_m, own_m, small = call(
@@ -725,13 +750,13 @@
         [one(bf16, rows_m + 16), one(f32, rows_m), one(f32, 8)], after=(own,),
     )
     got_m = swap(send_m, "mp", 2)
-    across = [[g * 8 + i for g in range(dp // 8)] for i in range(8)]
+    groups = [[g * 8 + i for g in range(dp // 8)] for i in range(8)]
 
     def last(fn, name, operands, outs, after):
         if dp == 8:
             return call(fn, name, operands, outs, smem=0, after=after)
         done = call(fn, name, operands, [shape_of(f32, *o.shape) for o in outs], smem=0, after=after)
-        return [lax.psum(v, "dp", axis_index_groups=across).astype(o.dtype) for v, o in zip(done, outs)]
+        return [lax.psum(v, "dp", axis_index_groups=groups).astype(o.dtype) for v, o in zip(done, outs)]
 
     (part,) = last(add_last, "add_last", (own, got), [one(bf16, rows_f)], (tiny,))
     near_f = around(part)

time: 128 us -> 120 us (0.938)
  starting transfers between devices: 52 us -> 45.1 us
    ppermute x42 -> x40, starting transfers between devices: 52 us -> 40 us  [swap(): return lax.ppermute(value, axis, [(i, i ^ bit) for i in range(size)])]
    ppermute x0 -> x4, starting transfers between devices: none -> 5.16 us  [across(): lax.ppermute(value, 'dp', [(i, i ^ 2 << (i & 1 ^ turn)) for i in range(si...]
    ppermute x42 -> x40, waiting for transfers between devices: 31.4 us -> 29.9 us  [swap(): return lax.ppermute(value, axis, [(i, i ^ bit) for i in range(size)])]
    pallas_call x27 -> x29, Pallas kernels: 42.2 us -> 42.9 us  [call(): pl.pallas_call(run, out_shape=outs, in_specs=[SMEM] * smem + [HBM] * hbm...]
  transfers between devices with their start and end apart: 42 -> 44, of which waited for: 13 -> 16; matrix products, arithmetic and copies ran while one was open for 0% -> 0% of each run, Pallas kernels for 31% -> 33%
where the time goes in v4:
time: 120 us
  starting transfers between devices  45.1 us (38%)
  Pallas kernels  42.9 us (36%)
  waiting for transfers between devices  30.3 us (25%)
    pallas_call x29, Pallas kernels, call(): pl.pallas_call(run, out_shape=outs, in_specs=[SMEM] * smem + [HBM] * hbm...  42.9 us
    ppermute x40, starting transfers between devices, swap(): return lax.ppermute(value, axis, [(i, i ^ bit) for i in range(size)])  40 us
    ppermute x40, waiting for transfers between devices, swap(): return lax.ppermute(value, axis, [(i, i ^ bit) for i in range(size)])  29.9 us
    ppermute x4, starting transfers between devices, across(): lax.ppermute(value, 'dp', [(i, i ^ 2 << (i & 1 ^ turn)) for i in range(si...  5.16 us
  transfers between devices with their start and end apart: 44, of which 16 were waited for; matrix products, arithmetic and copies ran while one was open for 0% of the time, Pallas kernels for 33%

profile of v4, /device:TPU:1, one launch (start us, length us, event | category | flops | bytes accessed | tf_op | source)
XLA Modules:
  0.0 120.1 jit_solution(6244884255898753037)
XLA Ops:
  1.4 1.4 %pick_piece.1.refs_7_ = bf16[128,512]{1,0:T(8,128)(2,1)S(1)} custom-call(s32[6]{0:T(128)S(1)} %pad_add_fusion.refs_0_, bf16[512,512]{1,0:T(8,128)(2,1)} %refs_1_.3, bf16[512,512]{1,0:T(8,128)(2,1)} %refs_2_.3), custom_call_target="tpu_custom_call" | custom-call | flops 4294967296 | bytes 16777216 | tf_op jit(solution)/shard_map/pick_piece/pallas_call | solution.py:49
  2.8 2.2 %collective-permute-start.8 = (bf16[128,512]{1,0:T(8,128)(2,1)S(1)}, bf16[128,512]{1,0:T(8,128)(2,1)S(1)}, u32[]{:S(2)}, u32[]{:S(2)}) collective-permute-start(bf16[128,512]{1,0:T(8,128)(2,1)S(1)} %pick_piece.1.refs_7_), channel_id=1, source_target_pairs={{0,1},{1,0},{2,3},{3,2},{4,5},{5,4},{6,7},{7,6},{8,9},{9,8},{10,11... | collective-permute-start | bytes 393224 | tf_op jit(solution)/shard_map/ppermute | solution.py:614
  5.0 2.2 %collective-permute-start.1 = (bf16[128,512]{1,0:T(8,128)(2,1)S(1)}, bf16[128,512]{1,0:T(8,128)(2,1)S(1)}, u32[]{:S(2)}, u32[]{:S(2)}) collective-permute-start(bf16[128,512]{1,0:T(8,128)(2,1)S(1)} %pick_piece.1.refs_7_), channel_id=1, source_target_pairs={{0,3},{1,2},{2,1},{3,0},{4,7},{5,6},{6,5},{7,4},{8,11},{9,10},{10,... | collective-permute-start | bytes 393224 | tf_op jit(solution)/shard_map/ppermute | solution.py:614
  7.3 6.9 %mixer_in.1 = (f32[512,1024]{1,0:T(8,128)S(1)}, f32[512,1024]{1,0:T(8,128)S(1)}, f32[512,1024]{1,0:T(8,128)S(1)}, f32[512,1024]{1,0:T(8,128)S(1)}, f32[512,1024]...) custom-call(s32[6]{0:T(128)S(1)} %pad_add_fusion.refs_0_, ...), custom_call_target="tpu_custom_call" | custom-call | tf_op jit(solution)/shard_map/mixer_in/pallas_call | solution.py:49
  14.2 1.3 %collective-permute-start.9 = (bf16[128,512]{1,0:T(8,128)(2,1)S(1)}, bf16[128,512]{1,0:T(8,128)(2,1)S(1)}, u32[]{:S(2)}, u32[]{:S(2)}) collective-permute-start(bf16[128,512]{1,0:T(8,128)(2,1)S(1)} %gate.3.refs_0_), channel_id=1, source_target_pairs={{0,8},{4,20},{8,0},{12,28},{16,24},{20,4},{24,16},{28,12},{1,9},{5... | collective-permute-start | bytes 393224 | tf_op jit(solution)/shard_map/ppermute | solution.py:619
  15.6 3.3 %collective-permute-done.refs_0_ = bf16[128,512]{1,0:T(8,128)(2,1)S(1)} collective-permute-done((bf16[128,512]{1,0:T(8,128)(2,1)S(1)}, bf16[128,512]{1,0:T(8,128)(2,1)S(1)}, u32[]{:S(2)}, u32[]{:S(2)}) %collective-permute-start) | collective-permute-done | bytes 131104 | tf_op jit(solution)/shard_map/ppermute | solution.py:614
  18.9 1.3 %collective-permute-start.2 = (bf16[256,512]{1,0:T(8,128)(2,1)S(1)}, bf16[256,512]{1,0:T(8,128)(2,1)S(1)}, u32[]{:S(2)}, u32[]{:S(2)}) collective-permute-start(bf16[256,512]{1,0:T(8,128)(2,1)S(1)} %join_depth.1.refs_0_.refs_2_), channel_id=1, source_target_pairs={{0,8},{4,20},{8,0},{12,28},{16,24},{20,4},{24,16},{28,12},{1,9},{5... | collective-permute-start | bytes 786440 | tf_op jit(solution)/shard_map/ppermute | solution.py:619
  21.6 2.1 %collective-permute-start.7 = (f32[4,1024]{1,0:T(4,128)S(1)}, f32[4,1024]{1,0:T(4,128)S(1)}, u32[]{:S(2)}, u32[]{:S(2)}) collective-permute-start(f32[4,1024]{1,0:T(4,128)S(1)} %get-tuple-element.101.refs_2_.refs_1_), channel_id=1, source_target_pairs={{0,3},{1,2},{2,1},{3,0},{4,7},{5,6},{6,5},{7,4},{8,11},{9,10},{10,... | collective-permute-start | bytes 49160 | tf_op jit(solution)/shard_map/ppermute | solution.py:614
  24.5 4.5 %collective-permute-start.12 = (bf16[2,128,512]{2,1,0:T(8,128)(2,1)S(1)}, bf16[2,128,512]{2,1,0:T(8,128)(2,1)S(1)}, u32[]{:S(2)}, u32[]{:S(2)}) collective-permute-start(bf16[2,128,512]{2,1,0:T(8,128)(2,1)S(1)} %join_one.1.refs_1_), channel_id=1, source_target_pairs={{0,4},{4,0},{8,12},{12,8},{16,20},{20,16},{24,28},{28,24},{1,5},{5... | collective-permute-start | bytes 786440 | tf_op jit(solution)/shard_map/ppermute | solution.py:614
  30.5 2.8 %mid_in.1 = (f32[520,1024]{1,0:T(8,128)S(1)}, bf16[1024,512]{1,0:T(8,128)(2,1)S(1)}, f32[512,512]{1,0:T(8,128)S(1)}, bf16[512,512]{1,0:T(8,128)(2,1)S(1)}, bf16[...) custom-call(s32[6]{0:T(128)S(1)} %pad_add_fusion.refs_0_, f32[4,1024]{1,0:T(4,128)S(1)} %get-tuple-element.101.refs_2_.refs_1_, ...), custom_call_target="tpu_custom_call" | custom-call | tf_op jit(solution)/shard_map/mid_in/pallas_call | solution.py:49
  34.0 2.8 %mlp_own.1 = (f32[512,512]{1,0:T(8,128)S(1)}, f32[512,512]{1,0:T(8,128)S(1)}, bf16[4,128,512]{2,1,0:T(8,128)(2,1)S(1)}, bf16[4,128,512]{2,1,0:T(8,128)(2,1)S(1)}, f32[16,512]{1,0:T(8,128)S(1)}) custom-call(s32[6]{0:T(128)S(1)} %pad_add_fusion.refs_0_, bf16[512,512]{1,0:T(8,128)(2,1)S(1)} %copy-done.6, bf16[512,512]{1,0:T(8,128)(2,1)S(1)} %copy-done.7, ...), custom_call_target="tpu_custom_call" | custom-call | flops 17179869184 | bytes 67108864 | tf_op jit(solution)/shard_map/mlp_own/pallas_call | solution.py:49
  36.8 2.8 %mlp_one.1 = (f32[512,512]{1,0:T(8,128)S(1)}, f32[512,512]{1,0:T(8,128)S(1)}, bf16[4,128,512]{2,1,0:T(8,128)(2,1)S(1)}, bf16[4,128,512]{2,1,0:T(8,128)(2,1)S(1)}, f32[16,512]{1,0:T(8,128)S(1)}) custom-call(s32[6]{0:T(128)S(1)} %pad_add_fusion.refs_0_, bf16[2,128,512]{2,1,0:T(8,128)(2,1)S(1)} %join_one.1.refs_1_, bf16[2,128,512]{2,1,0:T(8,128)(2,1)S(1)} %gate.4.refs_2_, ...), custom_call_target="tpu_custom_call" | custom-call | tf_op jit(solution)/shard_map/mlp_one/pallas_call | solution.py:49
  43.1 4.9 %mlp_two.1 = (f32[512,512]{1,0:T(8,128)S(1)}, f32[512,512]{1,0:T(8,128)S(1)}, bf16[4,256,512]{2,1,0:T(8,128)(2,1)S(1)}, bf16[4,256,512]{2,1,0:T(8,128)(2,1)S(1)}, f32[16,512]{1,0:T(8,128)S(1)}) custom-call(s32[6]{0:T(128)S(1)} %pad_add_fusion.refs_0_, bf16[2,256,512]{2,1,0:T(8,128)(2,1)S(1)} %join_two.1.refs_14_.refs_1_, ...), custom_call_target="tpu_custom_call" | custom-call | flops 34359738368 | bytes 134217728 | tf_op jit(solution)/shard_map/mlp_two/pallas_call | solution.py:49
  48.2 2.8 %mid_back.1 = (bf16[4,128,512]{2,1,0:T(8,128)(2,1)S(1)}, bf16[4,128,512]{2,1,0:T(8,128)(2,1)S(1)}, f32[512,512]{1,0:T(8,128)S(1)}, f32[512,1024]{1,0:T(8,128)S(1...) custom-call(s32[6]{0:T(128)S(1)} %pad_add_fusion.refs_0_, ...), custom_call_target="tpu_custom_call" | custom-call | flops 34359738368 | bytes 134217728 | tf_op jit(solution)/shard_map/mid_back/pallas_call | solution.py:49
  51.4 1.6 %collective-permute-start.18 = (f32[2,1024]{1,0:T(2,128)S(1)}, f32[2,1024]{1,0:T(2,128)S(1)}, u32[]{:S(2)}, u32[]{:S(2)}) collective-permute-start(f32[2,1024]{1,0:T(2,128)S(1)} %gate.5.refs_1_), channel_id=1, source_target_pairs={{0,3},{1,2},{2,1},{3,0},{4,7},{5,6},{6,5},{7,4},{8,11},{9,10},{10,... | collective-permute-start | bytes 24584 | tf_op jit(solution)/shard_map/ppermute | solution.py:614
  53.1 1.9 %collective-permute-start.16 = (f32[2,1024]{1,0:T(2,128)S(1)}, f32[2,1024]{1,0:T(2,128)S(1)}, u32[]{:S(2)}, u32[]{:S(2)}) collective-permute-start(f32[2,1024]{1,0:T(2,128)S(1)} %gate.5.refs_1_), channel_id=1, source_target_pairs={{0,1},{1,0},{2,3},{3,2},{4,5},{5,4},{6,7},{7,6},{8,9},{9,8},{10,11... | collective-permute-start | bytes 24584 | tf_op jit(solution)/shard_map/ppermute | solution.py:614
  57.8 3.0 %mixer_back.1 = (f32[512,1024]{1,0:T(8,128)S(1)}, bf16[4,4,96,512]{3,2,1,0:T(8,128)(2,1)S(1)}, f32[512,512]{1,0:T(8,128)S(1)}, f32[16,512]{1,0:T(8,128)S(1)}) custom-call(s32[6]{0:T(128)S(1)} %pad_add_fusion.refs_0_, f32[2,1024]{1,0:T(2,128)S(1)} %gate.5.refs_1_, f32[2,1024]{1,0:T(2,128)S(1)} %collective-permute-done.16.refs_2_, ...), custom_call_target="tpu_custom_call" | custom-call | tf_op jit(solution)/shard_map/mixer_back/pallas_call | solution.py:49
  60.7 1.6 %collective-permute-start.22 = (bf16[4,4,96,512]{3,2,1,0:T(8,128)(2,1)S(1)}, bf16[4,4,96,512]{3,2,1,0:T(8,128)(2,1)S(1)}, u32[]{:S(2)}, u32[]{:S(2)}) collective-permute-start(bf16[4,4,96,512]{3,2,1,0:T(8,128)(2,1)S(1)} %get-tuple-element.144), channel_id=1, source_target_pairs={{0,4},{4,0},{8,12},{12,8},{16,20},{20,16},{24,28},{28,24},{1,5},{5... | collective-permute-start | bytes 4718600 | tf_op jit(solution)/shard_map/ppermute | solution.py:614
  62.3 2.7 %mixer_out.1 = (bf16[4,4,96,512]{3,2,1,0:T(8,128)(2,1)S(1)}, f32[512,512]{1,0:T(8,128)S(1)}, f32[16,512]{1,0:T(8,128)S(1)}) custom-call(s32[6]{0:T(128)S(1)} %pad_add_fusion.refs_0_, f32[512,1024]{1,0:T(8,128)S(1)} %get-tuple-element.138.refs_1_, f32[512,1024]{1,0:T(8,128)S(1)} %get-tuple-element.105.refs_8_.refs_2_, ...), custom_call_target="tpu_custom_call" | custom-call | flops 17179869184 | bytes 67108864 | tf_op jit(solution)/shard_map/mixer_out/pallas_call | solution.py:49
  71.0 2.3 %tokens_out.1 = (bf16[512,512]{1,0:T(8,128)(2,1)}, f32[8,128]{1,0:T(8,128)S(1)}) custom-call(f32[512,512]{1,0:T(8,128)S(1)} %get-tuple-element.148.refs_0_, f32[512,512]{1,0:T(8,128)S(1)} %get-tuple-element.107.refs_10_.refs_13_.refs_1_, f32[1,512]{1,0:T(1,128)S(1)} %bitcast.29, f32[512,512]{1,0:T(8,128)S(1)} %get-tuple-element.149.refs_3_, ...), custom_call_target="tpu_custom_call" | custom-call | flops 2147483648 | bytes 8388608 | tf_op jit(solution)/shard_map/tokens_out/pallas_call | solution.py:49
  73.3 1.5 %mixed_out.1 = (bf16[512,512]{1,0:T(8,128)(2,1)}, f32[8,128]{1,0:T(8,128)S(1)}) custom-call(f32[512,512]{1,0:T(8,128)S(1)} %get-tuple-element.120.refs_0_, f32[2,192,512]{2,1,0:T(8,128)S(1)} %get-tuple-element.146.refs_1_.refs_4_.refs_5_), custom_call_target="tpu_custom_call" | custom-call | tf_op jit(solution)/shard_map/mixed_out/pallas_call | solution.py:49
  74.8 3.3 %collective-permute-done.24.refs_4_ = bf16[384,512]{1,0:T(8,128)(2,1)S(1)} collective-permute-done((bf16[384,512]{1,0:T(8,128)(2,1)S(1)}, bf16[384,512]{1,0:T(8,128)(2,1)S(1)}, u32[]{:S(2)}, u32[]{:S(2)}) %collective-permute-start.24) | collective-permute-done | bytes 393248 | tf_op jit(solution)/shard_map/ppermute | solution.py:614
  80.5 3.2 %collective-permute-done.29.refs_1_ = bf16[256,512]{1,0:T(8,128)(2,1)S(1)} collective-permute-done((bf16[256,512]{1,0:T(8,128)(2,1)S(1)}, bf16[256,512]{1,0:T(8,128)(2,1)S(1)}, u32[]{:S(2)}, u32[]{:S(2)}) %collective-permute-start.29) | collective-permute-done | bytes 262176 | tf_op jit(solution)/shard_map/ppermute | solution.py:614
  84.5 3.5 %collective-permute-done.28.refs_4_ = bf16[192,512]{1,0:T(8,128)(2,1)S(1)} collective-permute-done((bf16[192,512]{1,0:T(8,128)(2,1)S(1)}, bf16[192,512]{1,0:T(8,128)(2,1)S(1)}, u32[]{:S(2)}, u32[]{:S(2)}) %collective-permute-start.28) | collective-permute-done | bytes 196640 | tf_op jit(solution)/shard_map/ppermute | solution.py:614
  91.3 7.5 %collective-permute-done.31.refs_2_ = bf16[224,512]{1,0:T(8,128)(2,1)S(1)} collective-permute-done((bf16[224,512]{1,0:T(8,128)(2,1)S(1)}, bf16[224,512]{1,0:T(8,128)(2,1)S(1)}, u32[]{:S(2)}, u32[]{:S(2)}) %collective-permute-start.31) | collective-permute-done | bytes 229408 | tf_op jit(solution)/shard_map/ppermute | solution.py:614
  99.7 2.7 %collective-permute-start.41 = (bf16[160,512]{1,0:T(8,128)(2,1)S(1)}, bf16[160,512]{1,0:T(8,128)(2,1)S(1)}, u32[]{:S(2)}, u32[]{:S(2)}) collective-permute-start(bf16[160,512]{1,0:T(8,128)(2,1)S(1)} %add_last.1.refs_3_.refs_0_), channel_id=1, source_target_pairs={{0,16},{4,20},{8,24},{12,28},{16,0},{20,4},{24,8},{28,12},{1,17},{... | collective-permute-start | bytes 491528 | tf_op jit(solution)/shard_map/ppermute | solution.py:614
  102.3 4.1 %collective-permute-done.33.refs_2_ = bf16[112,512]{1,0:T(8,128)(2,1)S(1)} collective-permute-done((bf16[112,512]{1,0:T(8,128)(2,1)S(1)}, bf16[112,512]{1,0:T(8,128)(2,1)S(1)}, u32[]{:S(2)}, u32[]{:S(2)}) %collective-permute-start.33) | collective-permute-done | bytes 114720 | tf_op jit(solution)/shard_map/ppermute | solution.py:614
  106.5 1.9 %collective-permute-start.37 = (bf16[96,512]{1,0:T(8,128)(2,1)S(1)}, bf16[96,512]{1,0:T(8,128)(2,1)S(1)}, u32[]{:S(2)}, u32[]{:S(2)}) collective-permute-start(bf16[96,512]{1,0:T(8,128)(2,1)S(1)} %get-tuple-element.180.refs_0_.refs_4_), channel_id=1, source_target_pairs={{0,16},{4,20},{8,24},{12,28},{16,0},{20,4},{24,8},{28,12},{1,17},{... | collective-permute-start | bytes 294920 | tf_op jit(solution)/shard_map/ppermute | solution.py:614
  109.1 4.4 %collective-permute-start.35 = (f32[8,512]{1,0:T(8,128)S(1)}, f32[8,512]{1,0:T(8,128)S(1)}, u32[]{:S(2)}, u32[]{:S(2)}) collective-permute-start(f32[8,512]{1,0:T(8,128)S(1)} %get-tuple-element.179.refs_1_), channel_id=1, source_target_pairs={{0,4},{4,0},{8,12},{12,8},{16,20},{20,16},{24,28},{28,24},{1,5},{5... | collective-permute-start | bytes 49160 | tf_op jit(solution)/shard_map/ppermute | solution.py:614
  113.8 2.3 %collective-permute-start.39 = (bf16[4,96,512]{2,1,0:T(8,128)(2,1)S(1)}, bf16[4,96,512]{2,1,0:T(8,128)(2,1)S(1)}, u32[]{:S(2)}, u32[]{:S(2)}) collective-permute-start(bf16[4,96,512]{2,1,0:T(8,128)(2,1)S(1)} %join_mix.1.refs_3_), channel_id=1, source_target_pairs={{0,4},{4,0},{8,12},{12,8},{16,20},{20,16},{24,28},{28,24},{1,5},{5... | collective-permute-start | bytes 1179656 | tf_op jit(solution)/shard_map/ppermute | solution.py:614
  116.1 2.2 %spread_mlp.1 = (f32[512,512]{1,0:T(8,128)}, f32[512,512]{1,0:T(8,128)}, f32[256,512]{1,0:T(8,128)}, f32[8,128]{1,0:T(8,128)S(1)}) custom-call(s32[6]{0:T(128)S(1)} %pad_add_fusion.refs_0_, bf16[4,160,512]{2,1,0:T(8,128)(2,1)S(1)} %join_mlp.1.refs_1_, bf16[4,160,512]{2,1,0:T(8,128)(2,1)S(1)} %collective-permute-done.43.refs_2_), custom_call_target="tpu_custom_call" | custom-call | flops 8589934592 | bytes 33554432 | tf_op jit(solution)/shard_map/spread_mlp/pallas_call | solution.py:49
  118.3 1.8 %spread_mix.1 = (f32[3,128,1024]{2,1,0:T(8,128)}, f32[1,256]{1,0:T(1,128)}, f32[1,256]{1,0:T(1,128)}, f32[1,128]{1,0:T(1,128)}, f32[1,128]{1,0:T(1,128)}, /*index=5*/f32[1,512]{1,0:T(1,128)}) custom-call(s32[6]{0:T(128)S(1)} %pad_add_fusion.refs_0_, f32[8,512]{1,0:T(8,128)S(1)} %get-tuple-element.179.refs_1_, f32[8,512]{1,0:T(8,128)S(1)} %collective-permute-done.35.refs_2_, ...), custom_call_target="tpu_custom_call" | custom-call | flops 8589934592 | bytes 33554432 | tf_op jit(solution)/shard_map/spread_mix/pallas_call | solution.py:49
  (105 shorter events, 26.3 us)
Async XLA Ops:
  2.8 11.4 %collective-permute-start.8 = (bf16[128,512]{1,0:T(8,128)(2,1)S(1)}, bf16[128,512]{1,0:T(8,128)(2,1)S(1)}, u32[]{:S(2)}, u32[]{:S(2)}) collective-permute-start(bf16[128,512]{1,0:T(8,128)(2,1)S(1)} %pick_piece.1.refs_7_), channel_id=1, source_target_pairs={{0,1},{1,0},{2,3},{3,2},{4,5},{5,4},{6,7},{7,6},{8,9},{9,8},{10,11... | collective-permute-start | bytes 393224 | tf_op jit(solution)/shard_map/ppermute | solution.py:614
  5.0 10.5 %collective-permute-start.1 = (bf16[128,512]{1,0:T(8,128)(2,1)S(1)}, bf16[128,512]{1,0:T(8,128)(2,1)S(1)}, u32[]{:S(2)}, u32[]{:S(2)}) collective-permute-start(bf16[128,512]{1,0:T(8,128)(2,1)S(1)} %pick_piece.1.refs_7_), channel_id=1, source_target_pairs={{0,3},{1,2},{2,1},{3,0},{4,7},{5,6},{6,5},{7,4},{8,11},{9,10},{10,... | collective-permute-start | bytes 393224 | tf_op jit(solution)/shard_map/ppermute | solution.py:614
  7.2 11.7 %collective-permute-start = (bf16[128,512]{1,0:T(8,128)(2,1)S(1)}, bf16[128,512]{1,0:T(8,128)(2,1)S(1)}, u32[]{:S(2)}, u32[]{:S(2)}) collective-permute-start(bf16[128,512]{1,0:T(8,128)(2,1)S(1)} %pick_piece.1.refs_7_), channel_id=1, source_target_pairs={{0,2},{1,3},{2,0},{3,1},{4,6},{5,7},{6,4},{7,5},{8,10},{9,11},{10,... | collective-permute-start | bytes 393224 | tf_op jit(solution)/shard_map/ppermute | solution.py:614
  14.2 6.0 %collective-permute-start.9 = (bf16[128,512]{1,0:T(8,128)(2,1)S(1)}, bf16[128,512]{1,0:T(8,128)(2,1)S(1)}, u32[]{:S(2)}, u32[]{:S(2)}) collective-permute-start(bf16[128,512]{1,0:T(8,128)(2,1)S(1)} %gate.3.refs_0_), channel_id=1, source_target_pairs={{0,8},{4,20},{8,0},{12,28},{16,24},{20,4},{24,16},{28,12},{1,9},{5... | collective-permute-start | bytes 393224 | tf_op jit(solution)/shard_map/ppermute | solution.py:619
  18.9 5.6 %collective-permute-start.2 = (bf16[256,512]{1,0:T(8,128)(2,1)S(1)}, bf16[256,512]{1,0:T(8,128)(2,1)S(1)}, u32[]{:S(2)}, u32[]{:S(2)}) collective-permute-start(bf16[256,512]{1,0:T(8,128)(2,1)S(1)} %join_depth.1.refs_0_.refs_2_), channel_id=1, source_target_pairs={{0,8},{4,20},{8,0},{12,28},{16,24},{20,4},{24,16},{28,12},{1,9},{5... | collective-permute-start | bytes 786440 | tf_op jit(solution)/shard_map/ppermute | solution.py:619
  20.3 13.0 %collective-permute-start.10 = (bf16[2,128,512]{2,1,0:T(8,128)(2,1)S(1)}, bf16[2,128,512]{2,1,0:T(8,128)(2,1)S(1)}, u32[]{:S(2)}, u32[]{:S(2)}) collective-permute-start(bf16[2,128,512]{2,1,0:T(8,128)(2,1)S(1)} %join_one.1.refs_1_), channel_id=1, source_target_pairs={{0,16},{4,12},{8,24},{12,4},{16,0},{20,28},{24,8},{28,20},{1,17},{... | collective-permute-start | bytes 786440 | tf_op jit(solution)/shard_map/ppermute | solution.py:619
  21.6 7.6 %collective-permute-start.11 = (f32[4,1024]{1,0:T(4,128)S(1)}, f32[4,1024]{1,0:T(4,128)S(1)}, u32[]{:S(2)}, u32[]{:S(2)}) collective-permute-start(f32[4,1024]{1,0:T(4,128)S(1)} %get-tuple-element.101.refs_2_.refs_1_), channel_id=1, source_target_pairs={{0,1},{1,0},{2,3},{3,2},{4,5},{5,4},{6,7},{7,6},{8,9},{9,8},{10,11... | collective-permute-start | bytes 49160 | tf_op jit(solution)/shard_map/ppermute | solution.py:614
  21.6 8.8 %collective-permute-start.7 = (f32[4,1024]{1,0:T(4,128)S(1)}, f32[4,1024]{1,0:T(4,128)S(1)}, u32[]{:S(2)}, u32[]{:S(2)}) collective-permute-start(f32[4,1024]{1,0:T(4,128)S(1)} %get-tuple-element.101.refs_2_.refs_1_), channel_id=1, source_target_pairs={{0,3},{1,2},{2,1},{3,0},{4,7},{5,6},{6,5},{7,4},{8,11},{9,10},{10,... | collective-permute-start | bytes 49160 | tf_op jit(solution)/shard_map/ppermute | solution.py:614
  23.7 6.7 %collective-permute-start.6 = (f32[4,1024]{1,0:T(4,128)S(1)}, f32[4,1024]{1,0:T(4,128)S(1)}, u32[]{:S(2)}, u32[]{:S(2)}) collective-permute-start(f32[4,1024]{1,0:T(4,128)S(1)} %get-tuple-element.101.refs_2_.refs_1_), channel_id=1, source_target_pairs={{0,2},{1,3},{2,0},{3,1},{4,6},{5,7},{6,4},{7,5},{8,10},{9,11},{10,... | collective-permute-start | bytes 49160 | tf_op jit(solution)/shard_map/ppermute | solution.py:614
  24.5 12.2 %collective-permute-start.12 = (bf16[2,128,512]{2,1,0:T(8,128)(2,1)S(1)}, bf16[2,128,512]{2,1,0:T(8,128)(2,1)S(1)}, u32[]{:S(2)}, u32[]{:S(2)}) collective-permute-start(bf16[2,128,512]{2,1,0:T(8,128)(2,1)S(1)} %join_one.1.refs_1_), channel_id=1, source_target_pairs={{0,4},{4,0},{8,12},{12,8},{16,20},{20,16},{24,28},{28,24},{1,5},{5... | collective-permute-start | bytes 786440 | tf_op jit(solution)/shard_map/ppermute | solution.py:614
  29.1 11.1 %collective-permute-start.3 = (bf16[2,256,512]{2,1,0:T(8,128)(2,1)S(1)}, bf16[2,256,512]{2,1,0:T(8,128)(2,1)S(1)}, u32[]{:S(2)}, u32[]{:S(2)}) collective-permute-start(bf16[2,256,512]{2,1,0:T(8,128)(2,1)S(1)} %join_two.1.refs_14_.refs_1_), channel_id=1, source_target_pairs={{0,16},{4,12},{8,24},{12,4},{16,0},{20,28},{24,8},{28,20},{1,17},{... | collective-permute-start | bytes 1572872 | tf_op jit(solution)/shard_map/ppermute | solution.py:619
  40.3 12.8 %collective-permute-start.19 = (bf16[4,128,512]{2,1,0:T(8,128)(2,1)S(1)}, bf16[4,128,512]{2,1,0:T(8,128)(2,1)S(1)}, u32[]{:S(2)}, u32[]{:S(2)}) collective-permute-start(bf16[4,128,512]{2,1,0:T(8,128)(2,1)S(1)} %get-tuple-element.133), channel_id=1, source_target_pairs={{0,4},{4,0},{8,12},{12,8},{16,20},{20,16},{24,28},{28,24},{1,5},{5... | collective-permute-start | bytes 1572872 | tf_op jit(solution)/shard_map/ppermute | solution.py:614
  41.7 13.4 %collective-permute-start.20 = (bf16[4,128,512]{2,1,0:T(8,128)(2,1)S(1)}, bf16[4,128,512]{2,1,0:T(8,128)(2,1)S(1)}, u32[]{:S(2)}, u32[]{:S(2)}) collective-permute-start(bf16[4,128,512]{2,1,0:T(8,128)(2,1)S(1)} %add_pair.1.refs_13_), channel_id=1, source_target_pairs={{0,1},{1,0},{2,3},{3,2},{4,5},{5,4},{6,7},{7,6},{8,9},{9,8},{10,11... | collective-permute-start | bytes 1572872 | tf_op jit(solution)/shard_map/ppermute | solution.py:614
  51.4 6.3 %collective-permute-start.18 = (f32[2,1024]{1,0:T(2,128)S(1)}, f32[2,1024]{1,0:T(2,128)S(1)}, u32[]{:S(2)}, u32[]{:S(2)}) collective-permute-start(f32[2,1024]{1,0:T(2,128)S(1)} %gate.5.refs_1_), channel_id=1, source_target_pairs={{0,3},{1,2},{2,1},{3,0},{4,7},{5,6},{6,5},{7,4},{8,11},{9,10},{10,... | collective-permute-start | bytes 24584 | tf_op jit(solution)/shard_map/ppermute | solution.py:614
  56.2 12.5 %collective-permute-start.25 = (bf16[2,256,512]{2,1,0:T(8,128)(2,1)S(1)}, bf16[2,256,512]{2,1,0:T(8,128)(2,1)S(1)}, u32[]{:S(2)}, u32[]{:S(2)}) collective-permute-start(bf16[2,256,512]{2,1,0:T(8,128)(2,1)S(1)} %get-tuple-element.155), channel_id=1, source_target_pairs={{0,8},{4,12},{8,0},{12,4},{16,24},{20,28},{24,16},{28,20},{1,9},{5... | collective-permute-start | bytes 1572872 | tf_op jit(solution)/shard_map/ppermute | solution.py:614
  57.5 12.2 %collective-permute-start.26 = (bf16[2,256,512]{2,1,0:T(8,128)(2,1)S(1)}, bf16[2,256,512]{2,1,0:T(8,128)(2,1)S(1)}, u32[]{:S(2)}, u32[]{:S(2)}) collective-permute-start(bf16[2,256,512]{2,1,0:T(8,128)(2,1)S(1)} %get-tuple-element.157), channel_id=1, source_target_pairs={{0,16},{4,20},{8,24},{12,28},{16,0},{20,4},{24,8},{28,12},{1,17},{... | collective-permute-start | bytes 1572872 | tf_op jit(solution)/shard_map/ppermute | solution.py:614
  66.3 12.0 %collective-permute-start.23 = (bf16[416,512]{1,0:T(8,128)(2,1)S(1)}, bf16[416,512]{1,0:T(8,128)(2,1)S(1)}, u32[]{:S(2)}, u32[]{:S(2)}) collective-permute-start(bf16[416,512]{1,0:T(8,128)(2,1)S(1)} %get-tuple-element.151), channel_id=1, source_target_pairs={{0,8},{4,12},{8,0},{12,4},{16,24},{20,28},{24,16},{28,20},{1,9},{5... | collective-permute-start | bytes 1277960 | tf_op jit(solution)/shard_map/ppermute | solution.py:614
  66.6 11.5 %collective-permute-start.24 = (bf16[384,512]{1,0:T(8,128)(2,1)S(1)}, bf16[384,512]{1,0:T(8,128)(2,1)S(1)}, u32[]{:S(2)}, u32[]{:S(2)}) collective-permute-start(bf16[384,512]{1,0:T(8,128)(2,1)S(1)} %get-tuple-element.153), channel_id=1, source_target_pairs={{0,16},{4,20},{8,24},{12,28},{16,0},{20,4},{24,8},{28,12},{1,17},{... | collective-permute-start | bytes 1179656 | tf_op jit(solution)/shard_map/ppermute | solution.py:614
  70.4 13.3 %collective-permute-start.29 = (bf16[256,512]{1,0:T(8,128)(2,1)S(1)}, bf16[256,512]{1,0:T(8,128)(2,1)S(1)}, u32[]{:S(2)}, u32[]{:S(2)}) collective-permute-start(bf16[256,512]{1,0:T(8,128)(2,1)S(1)} %get-tuple-element.166), channel_id=1, source_target_pairs={{0,16},{4,20},{8,24},{12,28},{16,0},{20,4},{24,8},{28,12},{1,17},{... | collective-permute-start | bytes 786440 | tf_op jit(solution)/shard_map/ppermute | solution.py:614
  70.7 13.1 %collective-permute-start.30 = (bf16[256,512]{1,0:T(8,128)(2,1)S(1)}, bf16[256,512]{1,0:T(8,128)(2,1)S(1)}, u32[]{:S(2)}, u32[]{:S(2)}) collective-permute-start(bf16[256,512]{1,0:T(8,128)(2,1)S(1)} %get-tuple-element.168), channel_id=1, source_target_pairs={{0,8},{4,12},{8,0},{12,4},{16,24},{20,28},{24,16},{28,20},{1,9},{5... | collective-permute-start | bytes 786440 | tf_op jit(solution)/shard_map/ppermute | solution.py:614
  78.9 9.7 %collective-permute-start.27 = (bf16[224,512]{1,0:T(8,128)(2,1)S(1)}, bf16[224,512]{1,0:T(8,128)(2,1)S(1)}, u32[]{:S(2)}, u32[]{:S(2)}) collective-permute-start(bf16[224,512]{1,0:T(8,128)(2,1)S(1)} %get-tuple-element.162), channel_id=1, source_target_pairs={{0,16},{4,20},{8,24},{12,28},{16,0},{20,4},{24,8},{28,12},{1,17},{... | collective-permute-start | bytes 688136 | tf_op jit(solution)/shard_map/ppermute | solution.py:614
  79.8 8.3 %collective-permute-start.28 = (bf16[192,512]{1,0:T(8,128)(2,1)S(1)}, bf16[192,512]{1,0:T(8,128)(2,1)S(1)}, u32[]{:S(2)}, u32[]{:S(2)}) collective-permute-start(bf16[192,512]{1,0:T(8,128)(2,1)S(1)} %get-tuple-element.164), channel_id=1, source_target_pairs={{0,8},{4,12},{8,0},{12,4},{16,24},{20,28},{24,16},{28,20},{1,9},{5... | collective-permute-start | bytes 589832 | tf_op jit(solution)/shard_map/ppermute | solution.py:614
  83.9 6.1 %collective-permute-start.32 = (bf16[192,512]{1,0:T(8,128)(2,1)S(1)}, bf16[192,512]{1,0:T(8,128)(2,1)S(1)}, u32[]{:S(2)}, u32[]{:S(2)}) collective-permute-start(bf16[192,512]{1,0:T(8,128)(2,1)S(1)} %get-tuple-element.173), channel_id=1, source_target_pairs={{0,1},{1,0},{2,3},{3,2},{4,5},{5,4},{6,7},{7,6},{8,9},{9,8},{10,11... | collective-permute-start | bytes 589832 | tf_op jit(solution)/shard_map/ppermute | solution.py:614
  89.3 9.5 %collective-permute-start.31 = (bf16[224,512]{1,0:T(8,128)(2,1)S(1)}, bf16[224,512]{1,0:T(8,128)(2,1)S(1)}, u32[]{:S(2)}, u32[]{:S(2)}) collective-permute-start(bf16[224,512]{1,0:T(8,128)(2,1)S(1)} %get-tuple-element.171), channel_id=1, source_target_pairs={{0,1},{1,0},{2,3},{3,2},{4,5},{5,4},{6,7},{7,6},{8,9},{9,8},{10,11... | collective-permute-start | bytes 688136 | tf_op jit(solution)/shard_map/ppermute | solution.py:614
  90.1 9.3 %collective-permute-start.34 = (bf16[160,512]{1,0:T(8,128)(2,1)S(1)}, bf16[160,512]{1,0:T(8,128)(2,1)S(1)}, u32[]{:S(2)}, u32[]{:S(2)}) collective-permute-start(bf16[160,512]{1,0:T(8,128)(2,1)S(1)} %get-tuple-element.178), channel_id=1, source_target_pairs={{0,2},{1,3},{2,0},{3,1},{4,6},{5,7},{6,4},{7,5},{8,10},{9,11},{10,... | collective-permute-start | bytes 491528 | tf_op jit(solution)/shard_map/ppermute | solution.py:614
  99.3 7.1 %collective-permute-start.33 = (bf16[112,512]{1,0:T(8,128)(2,1)S(1)}, bf16[112,512]{1,0:T(8,128)(2,1)S(1)}, u32[]{:S(2)}, u32[]{:S(2)}) collective-permute-start(bf16[112,512]{1,0:T(8,128)(2,1)S(1)} %get-tuple-element.177), channel_id=1, source_target_pairs={{0,2},{1,3},{2,0},{3,1},{4,6},{5,7},{6,4},{7,5},{8,10},{9,11},{10,... | collective-permute-start | bytes 344072 | tf_op jit(solution)/shard_map/ppermute | solution.py:614
  99.5 9.0 %collective-permute-start.42 = (bf16[160,512]{1,0:T(8,128)(2,1)S(1)}, bf16[160,512]{1,0:T(8,128)(2,1)S(1)}, u32[]{:S(2)}, u32[]{:S(2)}) collective-permute-start(bf16[160,512]{1,0:T(8,128)(2,1)S(1)} %add_last.1.refs_3_.refs_0_), channel_id=1, source_target_pairs={{0,24},{4,28},{8,16},{12,20},{16,8},{20,12},{24,0},{28,4},{1,25},{... | collective-permute-start | bytes 491528 | tf_op jit(solution)/shard_map/ppermute | solution.py:614
  99.7 9.5 %collective-permute-start.41 = (bf16[160,512]{1,0:T(8,128)(2,1)S(1)}, bf16[160,512]{1,0:T(8,128)(2,1)S(1)}, u32[]{:S(2)}, u32[]{:S(2)}) collective-permute-start(bf16[160,512]{1,0:T(8,128)(2,1)S(1)} %add_last.1.refs_3_.refs_0_), channel_id=1, source_target_pairs={{0,16},{4,20},{8,24},{12,28},{16,0},{20,4},{24,8},{28,12},{1,17},{... | collective-permute-start | bytes 491528 | tf_op jit(solution)/shard_map/ppermute | solution.py:614
  102.3 11.3 %collective-permute-start.40 = (bf16[160,512]{1,0:T(8,128)(2,1)S(1)}, bf16[160,512]{1,0:T(8,128)(2,1)S(1)}, u32[]{:S(2)}, u32[]{:S(2)}) collective-permute-start(bf16[160,512]{1,0:T(8,128)(2,1)S(1)} %add_last.1.refs_3_.refs_0_), channel_id=1, source_target_pairs={{0,8},{4,12},{8,0},{12,4},{16,24},{20,28},{24,16},{28,20},{1,9},{5... | collective-permute-start | bytes 491528 | tf_op jit(solution)/shard_map/ppermute | solution.py:614
  106.4 7.3 %collective-permute-start.38 = (bf16[96,512]{1,0:T(8,128)(2,1)S(1)}, bf16[96,512]{1,0:T(8,128)(2,1)S(1)}, u32[]{:S(2)}, u32[]{:S(2)}) collective-permute-start(bf16[96,512]{1,0:T(8,128)(2,1)S(1)} %get-tuple-element.180.refs_0_.refs_4_), channel_id=1, source_target_pairs={{0,24},{4,28},{8,16},{12,20},{16,8},{20,12},{24,0},{28,4},{1,25},{... | collective-permute-start | bytes 294920 | tf_op jit(solution)/shard_map/ppermute | solution.py:614
  106.5 7.2 %collective-permute-start.37 = (bf16[96,512]{1,0:T(8,128)(2,1)S(1)}, bf16[96,512]{1,0:T(8,128)(2,1)S(1)}, u32[]{:S(2)}, u32[]{:S(2)}) collective-permute-start(bf16[96,512]{1,0:T(8,128)(2,1)S(1)} %get-tuple-element.180.refs_0_.refs_4_), channel_id=1, source_target_pairs={{0,16},{4,20},{8,24},{12,28},{16,0},{20,4},{24,8},{28,12},{1,17},{... | collective-permute-start | bytes 294920 | tf_op jit(solution)/shard_map/ppermute | solution.py:614
  109.1 9.1 %collective-permute-start.35 = (f32[8,512]{1,0:T(8,128)S(1)}, f32[8,512]{1,0:T(8,128)S(1)}, u32[]{:S(2)}, u32[]{:S(2)}) collective-permute-start(f32[8,512]{1,0:T(8,128)S(1)} %get-tuple-element.179.refs_1_), channel_id=1, source_target_pairs={{0,4},{4,0},{8,12},{12,8},{16,20},{20,16},{24,28},{28,24},{1,5},{5... | collective-permute-start | bytes 49160 | tf_op jit(solution)/shard_map/ppermute | solution.py:614
  (20 other events, 101.9 us)

commit v5 on v4

--- a/solution.py
+++ b/solution.py
@@ -78,12 +78,12 @@
         out[:, cols] = split[g].astype(bf16)
 
 
-def keep_mask(idx, length):
+def keep_mask(idx, resets, length):
     row = lax.broadcasted_iota(jnp.int32, (length, 1), 0)
     pos = idx[2] * length + (row % chunks) * (length // chunks) + row // chunks
     keep = jnp.ones((length, 1), f32)
     for i in range(3):
-        keep = jnp.where(pos == idx[3 + i], 0.0, keep)
+        keep = jnp.where(pos == resets[0, i], 0.0, keep)
     return keep
 
 
@@ -94,18 +94,18 @@
     return copies
 
 
-def mixer_in(idx, tok_hbm, gain_hbm, bias_f_hbm, bias_i_hbm, b_up_hbm, w_hbm, decay, share, cand, du, dv, nmt, x, prods, ends, payload,
-             split, tok, gain, bias_f, bias_i, b_up, w, sems):
+def mixer_in(idx, res_hbm, tok_hbm, gain_hbm, bias_f_hbm, bias_i_hbm, b_up_hbm, w_hbm, decay, share, cand, du, dv, nmt, x, prods, ends, payload, mask,
+             resets, split, tok, gain, bias_f, bias_i, b_up, w, sems):
     length, width = tok.shape
     units = bias_f.shape[1]
     steps = length // chunks
     block = 256
-    pairs = [(tok_hbm, tok), (gain_hbm, gain), (bias_f_hbm, bias_f), (bias_i_hbm, bias_i), (b_up_hbm, b_up)]
+    pairs = [(tok_hbm, tok), (gain_hbm, gain), (bias_f_hbm, bias_f), (bias_i_hbm, bias_i), (b_up_hbm, b_up), (res_hbm, resets)]
     for h in range(0, units, block):
         sl = pl.ds(h, block)
         pairs.append((w_hbm.at[:, :, sl], w.at[:, :, sl]))
     copies = fetch(pairs, sems)
-    for copy in copies[:5]:
+    for copy in copies[:6]:
         copy.wait()
 
     def put(rows, cols, values):
@@ -116,10 +116,11 @@
     r = lax.rsqrt(jnp.mean(v * v, axis=-1, keepdims=True) + norm_eps)
     nm = (v * r * gain[...]).astype(bf16)
     nmt[...] = nm.T
-    keep = keep_mask(idx, length)
+    keep = keep_mask(idx, resets, length)
+    mask[...] = keep
     for i, h in enumerate(range(0, units, block)):
         sl = pl.ds(h, block)
-        copies[5 + i].wait()
+        copies[6 + i].wait()
         a = jnp.exp(jnp.minimum(-(dot(nm, w[0, :, sl]) + bias_f[:, sl]), 88.0))
         b = jnp.exp(jnp.minimum(-(dot(nm, w[1, :, sl]) + bias_i[:, sl]), 88.0))
         t = 1.0 / (2.0 + a + b)
@@ -340,7 +341,7 @@
         gnm[...] += dot_nt(low, w[k, :, cols])
 
 
-def mixer_back(idx, own, r1, r2, r3, prods, flows, decay, share, cand, du, dv, st, grad_states, nmt, w,
+def mixer_back(idx, own, r1, r2, r3, prods, flows, decay, share, cand, du, dv, st, grad_states, nmt, w, mask,
                carried, send, gnm, small, others, carry8):
     length, units = decay.shape
     steps = length // chunks
@@ -364,16 +365,16 @@
     lax.fori_loop(0, steps, step, carry8[...], unroll=8)
     gnm[...] = jnp.zeros_like(gnm)
     small[...] = jnp.zeros_like(small)
-    gate_grads(1 - core, keep_mask(idx, length), carried, st, share, cand, du, dv, w, nmt, z, send, gnm, small)
-
-
-def mixer_out(idx, carried, share, cand, du, dv, st, nmt, w, gnm0, small0, small1, gain_row, x,
+    gate_grads(1 - core, mask[...], carried, st, share, cand, du, dv, w, nmt, z, send, gnm, small)
+
+
+def mixer_out(idx, carried, share, cand, du, dv, st, nmt, w, gnm0, small0, small1, gain_row, x, mask,
               keep, gnm, small):
     length, units = carried.shape
     core, z = idx[0], idx[2]
     gnm[...] = gnm0[...]
     small[...] = small0[...] + small1[...]
-    gate_grads(core, keep_mask(idx, length), carried, st, share, cand, du, dv, w, nmt, z, keep, gnm, small)
+    gate_grads(core, mask[...], carried, st, share, cand, du, dv, w, nmt, z, keep, gnm, small)
     v = x[...]
     r = lax.rsqrt(jnp.mean(v * v, axis=-1, keepdims=True) + norm_eps)
     gains = jnp.sum(gnm[...] * (v * r), axis=0, keepdims=True)
@@ -626,8 +627,7 @@
     dp, mp = lax.axis_size("dp"), lax.axis_size("mp")
     assert mp == 4 and dp % 8 == 0 and tokens.shape[0] == 1
     place = lax.axis_index("dp")
-    here = jnp.stack([place & 1, (place >> 1) & 3, lax.axis_index("mp")]).astype(jnp.int32)
-    idx = jnp.concatenate([here, resets[0]])
+    idx = jnp.stack([place & 1, (place >> 1) & 3, lax.axis_index("mp")]).astype(jnp.int32)
     tok, cot = tokens[0], cotangent[0]
     w3 = w_mix.transpose(1, 0, 2)
     row = lambda v: v.reshape(1, -1)
@@ -641,37 +641,37 @@
     square = shape_of(f32, length, width)
     square16 = shape_of(bf16, length, width)
     edge = shape_of(f32, chunks, units)
-    decay, share, cand, du, dv, nmt, x, prods, ends, payload = call(
+    decay, share, cand, du, dv, nmt, x, prods, ends, payload, mask = call(
         mixer_in, "mixer_in",
-        (idx, tok, row(gain_mix), row(bias_forget), row(bias_input), row(b_up), w3),
-        [wide] * 5 + [shape_of(bf16, width, length), square, edge, edge, shape_of(f32, 4, units)],
-        [pltpu.VMEM((lanes, length, 128), f32), pltpu.VMEM((length, width), bf16), pltpu.VMEM((1, width), f32)]
+        (idx, resets, tok, row(gain_mix), row(bias_forget), row(bias_input), row(b_up), w3),
+        [wide] * 5 + [shape_of(bf16, width, length), square, edge, edge, shape_of(f32, 4, units), shape_of(f32, length, 1)],
+        [pltpu.SMEM(resets.shape, jnp.int32), pltpu.VMEM((lanes, length, 128), f32), pltpu.VMEM((length, width), bf16), pltpu.VMEM((1, width), f32)]
         + [pltpu.VMEM((1, units), f32)] * 2 + [pltpu.VMEM((1, ff), f32), pltpu.VMEM((3, width, units), bf16),
-                                              pltpu.SemaphoreType.DMA((5 + units // 256,))],
-        hbm=6, after=(piece,),
+                                              pltpu.SemaphoreType.DMA((6 + units // 256,))],
+        hbm=7, after=(piece,),
     )
     ahead = [swap(payload, "mp", j) for j in (1, 2, 3)]
     around = lambda v: [v] + [swap(v, "dp", 2 * k) for k in (1, 2, 3)]
     mine = gate(depth[0], payload)
     (two,) = call(join, "join_depth", depth[1:], [shape_of(bf16, width // 2, ff)], smem=0, after=(payload,))
-    (one_a,) = call(join, "join_one", (mine, across(mine, 0)), [shape_of(bf16, 2, width // 4, ff)], smem=0, after=(two,))
-    (two_a,) = call(join, "join_two", (two, across(two, 0)), [shape_of(bf16, 2, width // 2, ff)], smem=0)
-    two_b = across(two_a, 1)
+    (one_a,) = call(join, "join_one", (mine, across(mine, 0)), [shape_of(bf16, 2, width // 4, ff)], smem=0, after=(two, *ahead))
+    far_two = across(two, 0)
     quarter = width // 8
     st, stT, middle, nm2, nm2t, cotp = call(
         mid_in, "mid_in",
         (idx, payload, *ahead, prods, ends, decay, share, cand, x, cot, w_out, row(gain_mlp)),
         [shape_of(f32, length + chunks, units), shape_of(bf16, units, length), square, square16, shape_of(bf16, width, length), square16],
         [pltpu.VMEM((lanes, length, 128), f32), pltpu.VMEM((4, 4, units), f32), pltpu.VMEM((chunks, units), f32), pltpu.VMEM((length, width), f32)],
-        after=(two_a,),
-    )
+    )
+    (two_a,) = call(join, "join_two", (two, far_two), [shape_of(bf16, 2, width // 2, ff)], smem=0, after=(nm2,))
+    two_b = across(two_a, 1)
     block = 2 * quarter
     pair = lambda dtype, rows: shape_of(dtype, 2, rows, width)
     weights = [pltpu.VMEM((ff, length), bf16), pltpu.VMEM((width, ff), bf16), pltpu.VMEM((ff, width), bf16)]
     grads = lambda rows: [square] * 2 + [shape_of(bf16, 4, rows, width)] * 2 + [shape_of(f32, 16, width)]
     one_b = gate(across(one_a, 1), nm2)
     mix, gn, keep0, send0, small_mlp = call(
-        mlp_own, "mlp_own", (idx, w_up, w_down, row(b_up), middle, nm2, nm2t, cotp), grads(block), weights[:1],
+        mlp_own, "mlp_own", (idx, w_up, w_down, row(b_up), middle, nm2, nm2t, cotp), grads(block), weights[:1], after=(two_a,),
     )
     mix, gn, keep_a, send_a, small_mlp = call(
         mlp_one, "mlp_one",
@@ -702,7 +702,7 @@
     rows_m = 3 * width // 16
     carried, send, gnm, small = call(
         mixer_back, "mixer_back",
-        (idx, payload, *behind, prods, flows, decay, share, cand, du, dv, st, grad_states, nmt, w3),
+        (idx, payload, *behind, prods, flows, decay, share, cand, du, dv, st, grad_states, nmt, w3, mask),
         [wide, shape_of(bf16, 4, 4, rows_m, units // 2), square, shape_of(f32, 16, width)],
         [pltpu.VMEM((4, 2, units), f32), pltpu.VMEM((chunks, units), f32)], after=(own_x,),
     )
@@ -710,7 +710,7 @@
     got = swap(send, "dp", 1)
     keep, gnm, small = call(
         mixer_out, "mixer_out",
-        (idx, carried, share, cand, du, dv, st, nmt, w3, gnm, small, small_mlp, gain_row, x),
+        (idx, carried, share, cand, du, dv, st, nmt, w3, gnm, small, small_mlp, gain_row, x, mask),
         [shape_of(bf16, 4, 4, rows_m, units // 2), square, shape_of(f32, 16, width)],
     )
     half_m = 2 * rows_m

time: 120 us -> 118 us (0.983)
  waiting for transfers between devices: 30.3 us -> 21.5 us
  starting transfers between devices: 45.1 us -> 52.1 us
    ppermute x40, waiting for transfers between devices: 29.9 us -> 20.1 us  [swap(): return lax.ppermute(value, axis, [(i, i ^ bit) for i in range(size)])]
    ppermute x40, starting transfers between devices: 40 us -> 47 us  [swap(): return lax.ppermute(value, axis, [(i, i ^ bit) for i in range(size)])]
  transfers between devices with their start and end apart: 44 -> 44, of which waited for: 16 -> 14; matrix products, arithmetic and copies ran while one was open for 0% -> 0% of each run, Pallas kernels for 33% -> 34%
where the time goes in v5:
time: 118 us
  starting transfers between devices  52.1 us (44%)
  Pallas kernels  43.1 us (37%)
  waiting for transfers between devices  21.5 us (18%)
    ppermute x40, starting transfers between devices, swap(): return lax.ppermute(value, axis, [(i, i ^ bit) for i in range(size)])  47 us
    pallas_call x29, Pallas kernels, call(): pl.pallas_call(run, out_shape=outs, in_specs=[SMEM] * smem + [HBM] * hbm...  43.1 us
    ppermute x40, waiting for transfers between devices, swap(): return lax.ppermute(value, axis, [(i, i ^ bit) for i in range(size)])  20.1 us
    ppermute x4, starting transfers between devices, across(): lax.ppermute(value, 'dp', [(i, i ^ 2 << (i & 1 ^ turn)) for i in range(si...  5.11 us
  transfers between devices with their start and end apart: 44, of which 14 were waited for; matrix products, arithmetic and copies ran while one was open for 0% of the time, Pallas kernels for 34%

profile of v5, /device:TPU:1, one launch (start us, length us, event | category | flops | bytes accessed | tf_op | source)
XLA Modules:
  0.0 117.7 jit_solution(18229348130095580901)
XLA Ops:
  0.7 1.4 %pick_piece.1.refs_8_ = bf16[128,512]{1,0:T(8,128)(2,1)S(1)} custom-call(s32[3]{0:T(128)S(1)} %pad_add_fusion.refs_0_, bf16[512,512]{1,0:T(8,128)(2,1)} %refs_1_.5, bf16[512,512]{1,0:T(8,128)(2,1)} %refs_2_.3), custom_call_target="tpu_custom_call" | custom-call | flops 4294967296 | bytes 16777216 | tf_op jit(solution)/shard_map/pick_piece/pallas_call | solution.py:49
  2.2 2.2 %collective-permute-start.9 = (bf16[128,512]{1,0:T(8,128)(2,1)S(1)}, bf16[128,512]{1,0:T(8,128)(2,1)S(1)}, u32[]{:S(2)}, u32[]{:S(2)}) collective-permute-start(bf16[128,512]{1,0:T(8,128)(2,1)S(1)} %pick_piece.1.refs_8_), channel_id=1, source_target_pairs={{0,1},{1,0},{2,3},{3,2},{4,5},{5,4},{6,7},{7,6},{8,9},{9,8},{10,11... | collective-permute-start | bytes 393224 | tf_op jit(solution)/shard_map/ppermute | solution.py:615
  4.4 2.2 %collective-permute-start.1 = (bf16[128,512]{1,0:T(8,128)(2,1)S(1)}, bf16[128,512]{1,0:T(8,128)(2,1)S(1)}, u32[]{:S(2)}, u32[]{:S(2)}) collective-permute-start(bf16[128,512]{1,0:T(8,128)(2,1)S(1)} %pick_piece.1.refs_8_), channel_id=1, source_target_pairs={{0,3},{1,2},{2,1},{3,0},{4,7},{5,6},{6,5},{7,4},{8,11},{9,10},{10,... | collective-permute-start | bytes 393224 | tf_op jit(solution)/shard_map/ppermute | solution.py:615
  6.7 6.9 %mixer_in.1 = (f32[512,1024]{1,0:T(8,128)S(1)}, f32[512,1024]{1,0:T(8,128)S(1)}, f32[512,1024]{1,0:T(8,128)S(1)}, f32[512,1024]{1,0:T(8,128)S(1)}, f32[512,1024]...) custom-call(s32[3]{0:T(128)S(1)} %pad_add_fusion.refs_0_, ...), custom_call_target="tpu_custom_call" | custom-call | tf_op jit(solution)/shard_map/mixer_in/pallas_call | solution.py:49
  13.5 2.4 %collective-permute-start.5 = (f32[4,1024]{1,0:T(4,128)S(1)}, f32[4,1024]{1,0:T(4,128)S(1)}, u32[]{:S(2)}, u32[]{:S(2)}) collective-permute-start(f32[4,1024]{1,0:T(4,128)S(1)} %get-tuple-element.102.refs_2_.refs_1_), channel_id=1, source_target_pairs={{0,3},{1,2},{2,1},{3,0},{4,7},{5,6},{6,5},{7,4},{8,11},{9,10},{10,... | collective-permute-start | bytes 49160 | tf_op jit(solution)/shard_map/ppermute | solution.py:615
  22.7 2.8 %mid_in.1 = (f32[520,1024]{1,0:T(8,128)S(1)}, bf16[1024,512]{1,0:T(8,128)(2,1)S(1)}, f32[512,512]{1,0:T(8,128)S(1)}, bf16[512,512]{1,0:T(8,128)(2,1)S(1)}, bf16[...) custom-call(s32[3]{0:T(128)S(1)} %pad_add_fusion.refs_0_, f32[4,1024]{1,0:T(4,128)S(1)} %get-tuple-element.102.refs_2_.refs_1_, ...), custom_call_target="tpu_custom_call" | custom-call | tf_op jit(solution)/shard_map/mid_in/pallas_call | solution.py:49
  25.5 3.3 %collective-permute-start.12 = (bf16[2,128,512]{2,1,0:T(8,128)(2,1)S(1)}, bf16[2,128,512]{2,1,0:T(8,128)(2,1)S(1)}, u32[]{:S(2)}, u32[]{:S(2)}) collective-permute-start(bf16[2,128,512]{2,1,0:T(8,128)(2,1)S(1)} %join_one.1.refs_1_), channel_id=1, source_target_pairs={{0,4},{4,0},{8,12},{12,8},{16,20},{20,16},{24,28},{28,24},{1,5},{5... | collective-permute-start | bytes 786440 | tf_op jit(solution)/shard_map/ppermute | solution.py:615
  30.1 1.5 %collective-permute-start.13 = (bf16[2,128,512]{2,1,0:T(8,128)(2,1)S(1)}, bf16[2,128,512]{2,1,0:T(8,128)(2,1)S(1)}, u32[]{:S(2)}, u32[]{:S(2)}) collective-permute-start(bf16[2,128,512]{2,1,0:T(8,128)(2,1)S(1)} %gate.4.refs_2_), channel_id=1, source_target_pairs={{0,4},{4,0},{8,12},{12,8},{16,20},{20,16},{24,28},{28,24},{1,5},{5... | collective-permute-start | bytes 786440 | tf_op jit(solution)/shard_map/ppermute | solution.py:615
  31.6 2.8 %mlp_own.1 = (f32[512,512]{1,0:T(8,128)S(1)}, f32[512,512]{1,0:T(8,128)S(1)}, bf16[4,128,512]{2,1,0:T(8,128)(2,1)S(1)}, bf16[4,128,512]{2,1,0:T(8,128)(2,1)S(1)}, f32[16,512]{1,0:T(8,128)S(1)}) custom-call(s32[3]{0:T(128)S(1)} %pad_add_fusion.refs_0_, bf16[512,512]{1,0:T(8,128)(2,1)S(1)} %copy-done.6, bf16[512,512]{1,0:T(8,128)(2,1)S(1)} %copy-done.7, ...), custom_call_target="tpu_custom_call" | custom-call | flops 17179869184 | bytes 67108864 | tf_op jit(solution)/shard_map/mlp_own/pallas_call | solution.py:49
  34.4 2.8 %mlp_one.1 = (f32[512,512]{1,0:T(8,128)S(1)}, f32[512,512]{1,0:T(8,128)S(1)}, bf16[4,128,512]{2,1,0:T(8,128)(2,1)S(1)}, bf16[4,128,512]{2,1,0:T(8,128)(2,1)S(1)}, f32[16,512]{1,0:T(8,128)S(1)}) custom-call(s32[3]{0:T(128)S(1)} %pad_add_fusion.refs_0_, bf16[2,128,512]{2,1,0:T(8,128)(2,1)S(1)} %join_one.1.refs_1_, bf16[2,128,512]{2,1,0:T(8,128)(2,1)S(1)} %gate.4.refs_2_, ...), custom_call_target="tpu_custom_call" | custom-call | tf_op jit(solution)/shard_map/mlp_one/pallas_call | solution.py:49
  37.8 1.4 %collective-permute-start.8 = (bf16[2,256,512]{2,1,0:T(8,128)(2,1)S(1)}, bf16[2,256,512]{2,1,0:T(8,128)(2,1)S(1)}, u32[]{:S(2)}, u32[]{:S(2)}) collective-permute-start(bf16[2,256,512]{2,1,0:T(8,128)(2,1)S(1)} %collective-permute-done.6.refs_2_), channel_id=1, source_target_pairs={{0,4},{4,0},{8,12},{12,8},{16,20},{20,16},{24,28},{28,24},{1,5},{5... | collective-permute-start | bytes 1572872 | tf_op jit(solution)/shard_map/ppermute | solution.py:615
  40.8 4.9 %mlp_two.1 = (f32[512,512]{1,0:T(8,128)S(1)}, f32[512,512]{1,0:T(8,128)S(1)}, bf16[4,256,512]{2,1,0:T(8,128)(2,1)S(1)}, bf16[4,256,512]{2,1,0:T(8,128)(2,1)S(1)}, f32[16,512]{1,0:T(8,128)S(1)}) custom-call(s32[3]{0:T(128)S(1)} %pad_add_fusion.refs_0_, bf16[2,256,512]{2,1,0:T(8,128)(2,1)S(1)} %join_two.1.refs_8_.refs_1_, ...), custom_call_target="tpu_custom_call" | custom-call | flops 34359738368 | bytes 134217728 | tf_op jit(solution)/shard_map/mlp_two/pallas_call | solution.py:49
  46.1 2.8 %mid_back.1 = (bf16[4,128,512]{2,1,0:T(8,128)(2,1)S(1)}, bf16[4,128,512]{2,1,0:T(8,128)(2,1)S(1)}, f32[512,512]{1,0:T(8,128)S(1)}, f32[512,1024]{1,0:T(8,128)S(1...) custom-call(s32[3]{0:T(128)S(1)} %pad_add_fusion.refs_0_, ...), custom_call_target="tpu_custom_call" | custom-call | flops 34359738368 | bytes 134217728 | tf_op jit(solution)/shard_map/mid_back/pallas_call | solution.py:49
  49.2 2.6 %collective-permute-start.18 = (f32[2,1024]{1,0:T(2,128)S(1)}, f32[2,1024]{1,0:T(2,128)S(1)}, u32[]{:S(2)}, u32[]{:S(2)}) collective-permute-start(f32[2,1024]{1,0:T(2,128)S(1)} %gate.5.refs_1_), channel_id=1, source_target_pairs={{0,3},{1,2},{2,1},{3,0},{4,7},{5,6},{6,5},{7,4},{8,11},{9,10},{10,... | collective-permute-start | bytes 24584 | tf_op jit(solution)/shard_map/ppermute | solution.py:615
  55.9 3.1 %mixer_back.1 = (f32[512,1024]{1,0:T(8,128)S(1)}, bf16[4,4,96,512]{3,2,1,0:T(8,128)(2,1)S(1)}, f32[512,512]{1,0:T(8,128)S(1)}, f32[16,512]{1,0:T(8,128)S(1)}) custom-call(s32[3]{0:T(128)S(1)} %pad_add_fusion.refs_0_, f32[2,1024]{1,0:T(2,128)S(1)} %gate.5.refs_1_, f32[2,1024]{1,0:T(2,128)S(1)} %collective-permute-done.16.refs_2_, ...), custom_call_target="tpu_custom_call" | custom-call | tf_op jit(solution)/shard_map/mixer_back/pallas_call | solution.py:49
  59.0 1.9 %collective-permute-start.22 = (bf16[4,4,96,512]{3,2,1,0:T(8,128)(2,1)S(1)}, bf16[4,4,96,512]{3,2,1,0:T(8,128)(2,1)S(1)}, u32[]{:S(2)}, u32[]{:S(2)}) collective-permute-start(bf16[4,4,96,512]{3,2,1,0:T(8,128)(2,1)S(1)} %get-tuple-element.146), channel_id=1, source_target_pairs={{0,4},{4,0},{8,12},{12,8},{16,20},{20,16},{24,28},{28,24},{1,5},{5... | collective-permute-start | bytes 4718600 | tf_op jit(solution)/shard_map/ppermute | solution.py:615
  60.9 2.7 %mixer_out.1 = (bf16[4,4,96,512]{3,2,1,0:T(8,128)(2,1)S(1)}, f32[512,512]{1,0:T(8,128)S(1)}, f32[16,512]{1,0:T(8,128)S(1)}) custom-call(s32[3]{0:T(128)S(1)} %pad_add_fusion.refs_0_, f32[512,1024]{1,0:T(8,128)S(1)} %get-tuple-element.140.refs_1_, f32[512,1024]{1,0:T(8,128)S(1)} %get-tuple-element.106.refs_8_.refs_2_, ...), custom_call_target="tpu_custom_call" | custom-call | flops 17179869184 | bytes 67108864 | tf_op jit(solution)/shard_map/mixer_out/pallas_call | solution.py:49
  69.3 2.3 %tokens_out.1 = (bf16[512,512]{1,0:T(8,128)(2,1)}, f32[8,128]{1,0:T(8,128)S(1)}) custom-call(f32[512,512]{1,0:T(8,128)S(1)} %get-tuple-element.150.refs_0_, f32[512,512]{1,0:T(8,128)S(1)} %get-tuple-element.108.refs_10_.refs_13_.refs_1_, f32[1,512]{1,0:T(1,128)S(1)} %bitcast.28, f32[512,512]{1,0:T(8,128)S(1)} %get-tuple-element.151.refs_3_, ...), custom_call_target="tpu_custom_call" | custom-call | flops 2147483648 | bytes 8388608 | tf_op jit(solution)/shard_map/tokens_out/pallas_call | solution.py:49
  71.6 1.5 %mixed_out.1 = (bf16[512,512]{1,0:T(8,128)(2,1)}, f32[8,128]{1,0:T(8,128)S(1)}) custom-call(f32[512,512]{1,0:T(8,128)S(1)} %get-tuple-element.121.refs_0_, f32[2,192,512]{2,1,0:T(8,128)S(1)} %get-tuple-element.148.refs_1_.refs_4_.refs_5_), custom_call_target="tpu_custom_call" | custom-call | tf_op jit(solution)/shard_map/mixed_out/pallas_call | solution.py:49
  73.1 3.1 %collective-permute-done.24.refs_4_ = bf16[384,512]{1,0:T(8,128)(2,1)S(1)} collective-permute-done((bf16[384,512]{1,0:T(8,128)(2,1)S(1)}, bf16[384,512]{1,0:T(8,128)(2,1)S(1)}, u32[]{:S(2)}, u32[]{:S(2)}) %collective-permute-start.24) | collective-permute-done | bytes 393248 | tf_op jit(solution)/shard_map/ppermute | solution.py:615
  77.0 1.5 %collective-permute-start.27 = (bf16[224,512]{1,0:T(8,128)(2,1)S(1)}, bf16[224,512]{1,0:T(8,128)(2,1)S(1)}, u32[]{:S(2)}, u32[]{:S(2)}) collective-permute-start(bf16[224,512]{1,0:T(8,128)(2,1)S(1)} %get-tuple-element.164), channel_id=1, source_target_pairs={{0,16},{4,20},{8,24},{12,28},{16,0},{20,4},{24,8},{28,12},{1,17},{... | collective-permute-start | bytes 688136 | tf_op jit(solution)/shard_map/ppermute | solution.py:615
  79.3 2.6 %collective-permute-done.29.refs_1_ = bf16[256,512]{1,0:T(8,128)(2,1)S(1)} collective-permute-done((bf16[256,512]{1,0:T(8,128)(2,1)S(1)}, bf16[256,512]{1,0:T(8,128)(2,1)S(1)}, u32[]{:S(2)}, u32[]{:S(2)}) %collective-permute-start.29) | collective-permute-done | bytes 262176 | tf_op jit(solution)/shard_map/ppermute | solution.py:615
  83.0 2.6 %collective-permute-done.28.refs_4_ = bf16[192,512]{1,0:T(8,128)(2,1)S(1)} collective-permute-done((bf16[192,512]{1,0:T(8,128)(2,1)S(1)}, bf16[192,512]{1,0:T(8,128)(2,1)S(1)}, u32[]{:S(2)}, u32[]{:S(2)}) %collective-permute-start.28) | collective-permute-done | bytes 196640 | tf_op jit(solution)/shard_map/ppermute | solution.py:615
  88.5 2.5 %collective-permute-start.34 = (bf16[160,512]{1,0:T(8,128)(2,1)S(1)}, bf16[160,512]{1,0:T(8,128)(2,1)S(1)}, u32[]{:S(2)}, u32[]{:S(2)}) collective-permute-start(bf16[160,512]{1,0:T(8,128)(2,1)S(1)} %get-tuple-element.180), channel_id=1, source_target_pairs={{0,2},{1,3},{2,0},{3,1},{4,6},{5,7},{6,4},{7,5},{8,10},{9,11},{10,... | collective-permute-start | bytes 491528 | tf_op jit(solution)/shard_map/ppermute | solution.py:615
  91.0 5.8 %collective-permute-done.31.refs_2_ = bf16[224,512]{1,0:T(8,128)(2,1)S(1)} collective-permute-done((bf16[224,512]{1,0:T(8,128)(2,1)S(1)}, bf16[224,512]{1,0:T(8,128)(2,1)S(1)}, u32[]{:S(2)}, u32[]{:S(2)}) %collective-permute-start.31) | collective-permute-done | bytes 229408 | tf_op jit(solution)/shard_map/ppermute | solution.py:615
  99.6 1.9 %collective-permute-start.40 = (bf16[160,512]{1,0:T(8,128)(2,1)S(1)}, bf16[160,512]{1,0:T(8,128)(2,1)S(1)}, u32[]{:S(2)}, u32[]{:S(2)}) collective-permute-start(bf16[160,512]{1,0:T(8,128)(2,1)S(1)} %add_last.1.refs_3_.refs_0_), channel_id=1, source_target_pairs={{0,8},{4,12},{8,0},{12,4},{16,24},{20,28},{24,16},{28,20},{1,9},{5... | collective-permute-start | bytes 491528 | tf_op jit(solution)/shard_map/ppermute | solution.py:615
  101.5 1.7 %collective-permute-done.33.refs_2_ = bf16[112,512]{1,0:T(8,128)(2,1)S(1)} collective-permute-done((bf16[112,512]{1,0:T(8,128)(2,1)S(1)}, bf16[112,512]{1,0:T(8,128)(2,1)S(1)}, u32[]{:S(2)}, u32[]{:S(2)}) %collective-permute-start.33) | collective-permute-done | bytes 114720 | tf_op jit(solution)/shard_map/ppermute | solution.py:615
  103.3 3.6 %collective-permute-start.38 = (bf16[96,512]{1,0:T(8,128)(2,1)S(1)}, bf16[96,512]{1,0:T(8,128)(2,1)S(1)}, u32[]{:S(2)}, u32[]{:S(2)}) collective-permute-start(bf16[96,512]{1,0:T(8,128)(2,1)S(1)} %get-tuple-element.182.refs_0_.refs_4_), channel_id=1, source_target_pairs={{0,24},{4,28},{8,16},{12,20},{16,8},{20,12},{24,0},{28,4},{1,25},{... | collective-permute-start | bytes 294920 | tf_op jit(solution)/shard_map/ppermute | solution.py:615
  107.3 2.9 %collective-permute-start.35 = (f32[8,512]{1,0:T(8,128)S(1)}, f32[8,512]{1,0:T(8,128)S(1)}, u32[]{:S(2)}, u32[]{:S(2)}) collective-permute-start(f32[8,512]{1,0:T(8,128)S(1)} %get-tuple-element.181.refs_1_), channel_id=1, source_target_pairs={{0,4},{4,0},{8,12},{12,8},{16,20},{20,16},{24,28},{28,24},{1,5},{5... | collective-permute-start | bytes 49160 | tf_op jit(solution)/shard_map/ppermute | solution.py:615
  111.9 1.8 %collective-permute-start.39 = (bf16[4,96,512]{2,1,0:T(8,128)(2,1)S(1)}, bf16[4,96,512]{2,1,0:T(8,128)(2,1)S(1)}, u32[]{:S(2)}, u32[]{:S(2)}) collective-permute-start(bf16[4,96,512]{2,1,0:T(8,128)(2,1)S(1)} %join_mix.1.refs_3_), channel_id=1, source_target_pairs={{0,4},{4,0},{8,12},{12,8},{16,20},{20,16},{24,28},{28,24},{1,5},{5... | collective-permute-start | bytes 1179656 | tf_op jit(solution)/shard_map/ppermute | solution.py:615
  113.7 2.2 %spread_mlp.1 = (f32[512,512]{1,0:T(8,128)}, f32[512,512]{1,0:T(8,128)}, f32[256,512]{1,0:T(8,128)}, f32[8,128]{1,0:T(8,128)S(1)}) custom-call(s32[3]{0:T(128)S(1)} %pad_add_fusion.refs_0_, bf16[4,160,512]{2,1,0:T(8,128)(2,1)S(1)} %join_mlp.1.refs_1_, bf16[4,160,512]{2,1,0:T(8,128)(2,1)S(1)} %collective-permute-done.43.refs_2_), custom_call_target="tpu_custom_call" | custom-call | flops 8589934592 | bytes 33554432 | tf_op jit(solution)/shard_map/spread_mlp/pallas_call | solution.py:49
  115.9 1.8 %spread_mix.1 = (f32[3,128,1024]{2,1,0:T(8,128)}, f32[1,256]{1,0:T(1,128)}, f32[1,256]{1,0:T(1,128)}, f32[1,128]{1,0:T(1,128)}, f32[1,128]{1,0:T(1,128)}, /*index=5*/f32[1,512]{1,0:T(1,128)}) custom-call(s32[3]{0:T(128)S(1)} %pad_add_fusion.refs_0_, f32[8,512]{1,0:T(8,128)S(1)} %get-tuple-element.181.refs_1_, f32[8,512]{1,0:T(8,128)S(1)} %collective-permute-done.35.refs_2_, ...), custom_call_target="tpu_custom_call" | custom-call | flops 8589934592 | bytes 33554432 | tf_op jit(solution)/shard_map/spread_mix/pallas_call | solution.py:49
  (105 shorter events, 31.4 us)
Async XLA Ops:
  2.2 13.9 %collective-permute-start.9 = (bf16[128,512]{1,0:T(8,128)(2,1)S(1)}, bf16[128,512]{1,0:T(8,128)(2,1)S(1)}, u32[]{:S(2)}, u32[]{:S(2)}) collective-permute-start(bf16[128,512]{1,0:T(8,128)(2,1)S(1)} %pick_piece.1.refs_8_), channel_id=1, source_target_pairs={{0,1},{1,0},{2,3},{3,2},{4,5},{5,4},{6,7},{7,6},{8,9},{9,8},{10,11... | collective-permute-start | bytes 393224 | tf_op jit(solution)/shard_map/ppermute | solution.py:615
  4.4 12.8 %collective-permute-start.1 = (bf16[128,512]{1,0:T(8,128)(2,1)S(1)}, bf16[128,512]{1,0:T(8,128)(2,1)S(1)}, u32[]{:S(2)}, u32[]{:S(2)}) collective-permute-start(bf16[128,512]{1,0:T(8,128)(2,1)S(1)} %pick_piece.1.refs_8_), channel_id=1, source_target_pairs={{0,3},{1,2},{2,1},{3,0},{4,7},{5,6},{6,5},{7,4},{8,11},{9,10},{10,... | collective-permute-start | bytes 393224 | tf_op jit(solution)/shard_map/ppermute | solution.py:615
  6.6 11.9 %collective-permute-start = (bf16[128,512]{1,0:T(8,128)(2,1)S(1)}, bf16[128,512]{1,0:T(8,128)(2,1)S(1)}, u32[]{:S(2)}, u32[]{:S(2)}) collective-permute-start(bf16[128,512]{1,0:T(8,128)(2,1)S(1)} %pick_piece.1.refs_8_), channel_id=1, source_target_pairs={{0,2},{1,3},{2,0},{3,1},{4,6},{5,7},{6,4},{7,5},{8,10},{9,11},{10,... | collective-permute-start | bytes 393224 | tf_op jit(solution)/shard_map/ppermute | solution.py:615
  13.5 6.2 %collective-permute-start.5 = (f32[4,1024]{1,0:T(4,128)S(1)}, f32[4,1024]{1,0:T(4,128)S(1)}, u32[]{:S(2)}, u32[]{:S(2)}) collective-permute-start(f32[4,1024]{1,0:T(4,128)S(1)} %get-tuple-element.102.refs_2_.refs_1_), channel_id=1, source_target_pairs={{0,3},{1,2},{2,1},{3,0},{4,7},{5,6},{6,5},{7,4},{8,11},{9,10},{10,... | collective-permute-start | bytes 49160 | tf_op jit(solution)/shard_map/ppermute | solution.py:615
  18.5 10.3 %collective-permute-start.2 = (bf16[256,512]{1,0:T(8,128)(2,1)S(1)}, bf16[256,512]{1,0:T(8,128)(2,1)S(1)}, u32[]{:S(2)}, u32[]{:S(2)}) collective-permute-start(bf16[256,512]{1,0:T(8,128)(2,1)S(1)} %join_depth.1.refs_0_.refs_2_), channel_id=1, source_target_pairs={{0,8},{4,20},{8,0},{12,28},{16,24},{20,4},{24,16},{28,12},{1,9},{5... | collective-permute-start | bytes 786440 | tf_op jit(solution)/shard_map/ppermute | solution.py:620
  21.4 8.7 %collective-permute-start.11 = (bf16[2,128,512]{2,1,0:T(8,128)(2,1)S(1)}, bf16[2,128,512]{2,1,0:T(8,128)(2,1)S(1)}, u32[]{:S(2)}, u32[]{:S(2)}) collective-permute-start(bf16[2,128,512]{2,1,0:T(8,128)(2,1)S(1)} %join_one.1.refs_1_), channel_id=1, source_target_pairs={{0,16},{4,12},{8,24},{12,4},{16,0},{20,28},{24,8},{28,20},{1,17},{... | collective-permute-start | bytes 786440 | tf_op jit(solution)/shard_map/ppermute | solution.py:620
  25.5 8.9 %collective-permute-start.12 = (bf16[2,128,512]{2,1,0:T(8,128)(2,1)S(1)}, bf16[2,128,512]{2,1,0:T(8,128)(2,1)S(1)}, u32[]{:S(2)}, u32[]{:S(2)}) collective-permute-start(bf16[2,128,512]{2,1,0:T(8,128)(2,1)S(1)} %join_one.1.refs_1_), channel_id=1, source_target_pairs={{0,4},{4,0},{8,12},{12,8},{16,20},{20,16},{24,28},{28,24},{1,5},{5... | collective-permute-start | bytes 786440 | tf_op jit(solution)/shard_map/ppermute | solution.py:615
  28.8 9.0 %collective-permute-start.6 = (bf16[2,256,512]{2,1,0:T(8,128)(2,1)S(1)}, bf16[2,256,512]{2,1,0:T(8,128)(2,1)S(1)}, u32[]{:S(2)}, u32[]{:S(2)}) collective-permute-start(bf16[2,256,512]{2,1,0:T(8,128)(2,1)S(1)} %join_two.1.refs_8_.refs_1_), channel_id=1, source_target_pairs={{0,16},{4,12},{8,24},{12,4},{16,0},{20,28},{24,8},{28,20},{1,17},{... | collective-permute-start | bytes 1572872 | tf_op jit(solution)/shard_map/ppermute | solution.py:620
  30.1 4.3 %collective-permute-start.13 = (bf16[2,128,512]{2,1,0:T(8,128)(2,1)S(1)}, bf16[2,128,512]{2,1,0:T(8,128)(2,1)S(1)}, u32[]{:S(2)}, u32[]{:S(2)}) collective-permute-start(bf16[2,128,512]{2,1,0:T(8,128)(2,1)S(1)} %gate.4.refs_2_), channel_id=1, source_target_pairs={{0,4},{4,0},{8,12},{12,8},{16,20},{20,16},{24,28},{28,24},{1,5},{5... | collective-permute-start | bytes 786440 | tf_op jit(solution)/shard_map/ppermute | solution.py:615
  39.3 12.4 %collective-permute-start.19 = (bf16[4,128,512]{2,1,0:T(8,128)(2,1)S(1)}, bf16[4,128,512]{2,1,0:T(8,128)(2,1)S(1)}, u32[]{:S(2)}, u32[]{:S(2)}) collective-permute-start(bf16[4,128,512]{2,1,0:T(8,128)(2,1)S(1)} %get-tuple-element.135), channel_id=1, source_target_pairs={{0,4},{4,0},{8,12},{12,8},{16,20},{20,16},{24,28},{28,24},{1,5},{5... | collective-permute-start | bytes 1572872 | tf_op jit(solution)/shard_map/ppermute | solution.py:615
  39.4 13.3 %collective-permute-start.20 = (bf16[4,128,512]{2,1,0:T(8,128)(2,1)S(1)}, bf16[4,128,512]{2,1,0:T(8,128)(2,1)S(1)}, u32[]{:S(2)}, u32[]{:S(2)}) collective-permute-start(bf16[4,128,512]{2,1,0:T(8,128)(2,1)S(1)} %add_pair.1.refs_13_), channel_id=1, source_target_pairs={{0,1},{1,0},{2,3},{3,2},{4,5},{5,4},{6,7},{7,6},{8,9},{9,8},{10,11... | collective-permute-start | bytes 1572872 | tf_op jit(solution)/shard_map/ppermute | solution.py:615
  49.2 6.7 %collective-permute-start.18 = (f32[2,1024]{1,0:T(2,128)S(1)}, f32[2,1024]{1,0:T(2,128)S(1)}, u32[]{:S(2)}, u32[]{:S(2)}) collective-permute-start(f32[2,1024]{1,0:T(2,128)S(1)} %gate.5.refs_1_), channel_id=1, source_target_pairs={{0,3},{1,2},{2,1},{3,0},{4,7},{5,6},{6,5},{7,4},{8,11},{9,10},{10,... | collective-permute-start | bytes 24584 | tf_op jit(solution)/shard_map/ppermute | solution.py:615
  53.8 12.8 %collective-permute-start.25 = (bf16[2,256,512]{2,1,0:T(8,128)(2,1)S(1)}, bf16[2,256,512]{2,1,0:T(8,128)(2,1)S(1)}, u32[]{:S(2)}, u32[]{:S(2)}) collective-permute-start(bf16[2,256,512]{2,1,0:T(8,128)(2,1)S(1)} %get-tuple-element.157), channel_id=1, source_target_pairs={{0,8},{4,12},{8,0},{12,4},{16,24},{20,28},{24,16},{28,20},{1,9},{5... | collective-permute-start | bytes 1572872 | tf_op jit(solution)/shard_map/ppermute | solution.py:615
  54.7 11.9 %collective-permute-start.26 = (bf16[2,256,512]{2,1,0:T(8,128)(2,1)S(1)}, bf16[2,256,512]{2,1,0:T(8,128)(2,1)S(1)}, u32[]{:S(2)}, u32[]{:S(2)}) collective-permute-start(bf16[2,256,512]{2,1,0:T(8,128)(2,1)S(1)} %get-tuple-element.159), channel_id=1, source_target_pairs={{0,16},{4,20},{8,24},{12,28},{16,0},{20,4},{24,8},{28,12},{1,17},{... | collective-permute-start | bytes 1572872 | tf_op jit(solution)/shard_map/ppermute | solution.py:615
  59.0 4.9 %collective-permute-start.22 = (bf16[4,4,96,512]{3,2,1,0:T(8,128)(2,1)S(1)}, bf16[4,4,96,512]{3,2,1,0:T(8,128)(2,1)S(1)}, u32[]{:S(2)}, u32[]{:S(2)}) collective-permute-start(bf16[4,4,96,512]{3,2,1,0:T(8,128)(2,1)S(1)} %get-tuple-element.146), channel_id=1, source_target_pairs={{0,4},{4,0},{8,12},{12,8},{16,20},{20,16},{24,28},{28,24},{1,5},{5... | collective-permute-start | bytes 4718600 | tf_op jit(solution)/shard_map/ppermute | solution.py:615
  64.9 11.4 %collective-permute-start.23 = (bf16[416,512]{1,0:T(8,128)(2,1)S(1)}, bf16[416,512]{1,0:T(8,128)(2,1)S(1)}, u32[]{:S(2)}, u32[]{:S(2)}) collective-permute-start(bf16[416,512]{1,0:T(8,128)(2,1)S(1)} %get-tuple-element.153), channel_id=1, source_target_pairs={{0,8},{4,12},{8,0},{12,4},{16,24},{20,28},{24,16},{28,20},{1,9},{5... | collective-permute-start | bytes 1277960 | tf_op jit(solution)/shard_map/ppermute | solution.py:615
  65.6 10.6 %collective-permute-start.24 = (bf16[384,512]{1,0:T(8,128)(2,1)S(1)}, bf16[384,512]{1,0:T(8,128)(2,1)S(1)}, u32[]{:S(2)}, u32[]{:S(2)}) collective-permute-start(bf16[384,512]{1,0:T(8,128)(2,1)S(1)} %get-tuple-element.155), channel_id=1, source_target_pairs={{0,16},{4,20},{8,24},{12,28},{16,0},{20,4},{24,8},{28,12},{1,17},{... | collective-permute-start | bytes 1179656 | tf_op jit(solution)/shard_map/ppermute | solution.py:615
  67.4 14.5 %collective-permute-start.29 = (bf16[256,512]{1,0:T(8,128)(2,1)S(1)}, bf16[256,512]{1,0:T(8,128)(2,1)S(1)}, u32[]{:S(2)}, u32[]{:S(2)}) collective-permute-start(bf16[256,512]{1,0:T(8,128)(2,1)S(1)} %get-tuple-element.168), channel_id=1, source_target_pairs={{0,16},{4,20},{8,24},{12,28},{16,0},{20,4},{24,8},{28,12},{1,17},{... | collective-permute-start | bytes 786440 | tf_op jit(solution)/shard_map/ppermute | solution.py:615
  68.6 13.3 %collective-permute-start.30 = (bf16[256,512]{1,0:T(8,128)(2,1)S(1)}, bf16[256,512]{1,0:T(8,128)(2,1)S(1)}, u32[]{:S(2)}, u32[]{:S(2)}) collective-permute-start(bf16[256,512]{1,0:T(8,128)(2,1)S(1)} %get-tuple-element.170), channel_id=1, source_target_pairs={{0,8},{4,12},{8,0},{12,4},{16,24},{20,28},{24,16},{28,20},{1,9},{5... | collective-permute-start | bytes 786440 | tf_op jit(solution)/shard_map/ppermute | solution.py:615
  77.0 9.8 %collective-permute-start.27 = (bf16[224,512]{1,0:T(8,128)(2,1)S(1)}, bf16[224,512]{1,0:T(8,128)(2,1)S(1)}, u32[]{:S(2)}, u32[]{:S(2)}) collective-permute-start(bf16[224,512]{1,0:T(8,128)(2,1)S(1)} %get-tuple-element.164), channel_id=1, source_target_pairs={{0,16},{4,20},{8,24},{12,28},{16,0},{20,4},{24,8},{28,12},{1,17},{... | collective-permute-start | bytes 688136 | tf_op jit(solution)/shard_map/ppermute | solution.py:615
  78.4 7.2 %collective-permute-start.28 = (bf16[192,512]{1,0:T(8,128)(2,1)S(1)}, bf16[192,512]{1,0:T(8,128)(2,1)S(1)}, u32[]{:S(2)}, u32[]{:S(2)}) collective-permute-start(bf16[192,512]{1,0:T(8,128)(2,1)S(1)} %get-tuple-element.166), channel_id=1, source_target_pairs={{0,8},{4,12},{8,0},{12,4},{16,24},{20,28},{24,16},{28,20},{1,9},{5... | collective-permute-start | bytes 589832 | tf_op jit(solution)/shard_map/ppermute | solution.py:615
  82.0 6.5 %collective-permute-start.32 = (bf16[192,512]{1,0:T(8,128)(2,1)S(1)}, bf16[192,512]{1,0:T(8,128)(2,1)S(1)}, u32[]{:S(2)}, u32[]{:S(2)}) collective-permute-start(bf16[192,512]{1,0:T(8,128)(2,1)S(1)} %get-tuple-element.175), channel_id=1, source_target_pairs={{0,1},{1,0},{2,3},{3,2},{4,5},{5,4},{6,7},{7,6},{8,9},{9,8},{10,11... | collective-permute-start | bytes 589832 | tf_op jit(solution)/shard_map/ppermute | solution.py:615
  87.4 9.5 %collective-permute-start.31 = (bf16[224,512]{1,0:T(8,128)(2,1)S(1)}, bf16[224,512]{1,0:T(8,128)(2,1)S(1)}, u32[]{:S(2)}, u32[]{:S(2)}) collective-permute-start(bf16[224,512]{1,0:T(8,128)(2,1)S(1)} %get-tuple-element.173), channel_id=1, source_target_pairs={{0,1},{1,0},{2,3},{3,2},{4,5},{5,4},{6,7},{7,6},{8,9},{9,8},{10,11... | collective-permute-start | bytes 688136 | tf_op jit(solution)/shard_map/ppermute | solution.py:615
  88.5 10.3 %collective-permute-start.34 = (bf16[160,512]{1,0:T(8,128)(2,1)S(1)}, bf16[160,512]{1,0:T(8,128)(2,1)S(1)}, u32[]{:S(2)}, u32[]{:S(2)}) collective-permute-start(bf16[160,512]{1,0:T(8,128)(2,1)S(1)} %get-tuple-element.180), channel_id=1, source_target_pairs={{0,2},{1,3},{2,0},{3,1},{4,6},{5,7},{6,4},{7,5},{8,10},{9,11},{10,... | collective-permute-start | bytes 491528 | tf_op jit(solution)/shard_map/ppermute | solution.py:615
  97.4 5.8 %collective-permute-start.33 = (bf16[112,512]{1,0:T(8,128)(2,1)S(1)}, bf16[112,512]{1,0:T(8,128)(2,1)S(1)}, u32[]{:S(2)}, u32[]{:S(2)}) collective-permute-start(bf16[112,512]{1,0:T(8,128)(2,1)S(1)} %get-tuple-element.179), channel_id=1, source_target_pairs={{0,2},{1,3},{2,0},{3,1},{4,6},{5,7},{6,4},{7,5},{8,10},{9,11},{10,... | collective-permute-start | bytes 344072 | tf_op jit(solution)/shard_map/ppermute | solution.py:615
  98.8 8.1 %collective-permute-start.42 = (bf16[160,512]{1,0:T(8,128)(2,1)S(1)}, bf16[160,512]{1,0:T(8,128)(2,1)S(1)}, u32[]{:S(2)}, u32[]{:S(2)}) collective-permute-start(bf16[160,512]{1,0:T(8,128)(2,1)S(1)} %add_last.1.refs_3_.refs_0_), channel_id=1, source_target_pairs={{0,24},{4,28},{8,16},{12,20},{16,8},{20,12},{24,0},{28,4},{1,25},{... | collective-permute-start | bytes 491528 | tf_op jit(solution)/shard_map/ppermute | solution.py:615
  99.3 8.0 %collective-permute-start.41 = (bf16[160,512]{1,0:T(8,128)(2,1)S(1)}, bf16[160,512]{1,0:T(8,128)(2,1)S(1)}, u32[]{:S(2)}, u32[]{:S(2)}) collective-permute-start(bf16[160,512]{1,0:T(8,128)(2,1)S(1)} %add_last.1.refs_3_.refs_0_), channel_id=1, source_target_pairs={{0,16},{4,20},{8,24},{12,28},{16,0},{20,4},{24,8},{28,12},{1,17},{... | collective-permute-start | bytes 491528 | tf_op jit(solution)/shard_map/ppermute | solution.py:615
  99.6 10.6 %collective-permute-start.40 = (bf16[160,512]{1,0:T(8,128)(2,1)S(1)}, bf16[160,512]{1,0:T(8,128)(2,1)S(1)}, u32[]{:S(2)}, u32[]{:S(2)}) collective-permute-start(bf16[160,512]{1,0:T(8,128)(2,1)S(1)} %add_last.1.refs_3_.refs_0_), channel_id=1, source_target_pairs={{0,8},{4,12},{8,0},{12,4},{16,24},{20,28},{24,16},{28,20},{1,9},{5... | collective-permute-start | bytes 491528 | tf_op jit(solution)/shard_map/ppermute | solution.py:615
  103.3 7.0 %collective-permute-start.38 = (bf16[96,512]{1,0:T(8,128)(2,1)S(1)}, bf16[96,512]{1,0:T(8,128)(2,1)S(1)}, u32[]{:S(2)}, u32[]{:S(2)}) collective-permute-start(bf16[96,512]{1,0:T(8,128)(2,1)S(1)} %get-tuple-element.182.refs_0_.refs_4_), channel_id=1, source_target_pairs={{0,24},{4,28},{8,16},{12,20},{16,8},{20,12},{24,0},{28,4},{1,25},{... | collective-permute-start | bytes 294920 | tf_op jit(solution)/shard_map/ppermute | solution.py:615
  106.9 4.7 %collective-permute-start.37 = (bf16[96,512]{1,0:T(8,128)(2,1)S(1)}, bf16[96,512]{1,0:T(8,128)(2,1)S(1)}, u32[]{:S(2)}, u32[]{:S(2)}) collective-permute-start(bf16[96,512]{1,0:T(8,128)(2,1)S(1)} %get-tuple-element.182.refs_0_.refs_4_), channel_id=1, source_target_pairs={{0,16},{4,20},{8,24},{12,28},{16,0},{20,4},{24,8},{28,12},{1,17},{... | collective-permute-start | bytes 294920 | tf_op jit(solution)/shard_map/ppermute | solution.py:615
  106.9 5.0 %collective-permute-start.36 = (bf16[96,512]{1,0:T(8,128)(2,1)S(1)}, bf16[96,512]{1,0:T(8,128)(2,1)S(1)}, u32[]{:S(2)}, u32[]{:S(2)}) collective-permute-start(bf16[96,512]{1,0:T(8,128)(2,1)S(1)} %get-tuple-element.182.refs_0_.refs_4_), channel_id=1, source_target_pairs={{0,8},{4,12},{8,0},{12,4},{16,24},{20,28},{24,16},{28,20},{1,9},{5... | collective-permute-start | bytes 294920 | tf_op jit(solution)/shard_map/ppermute | solution.py:615
  107.3 8.6 %collective-permute-start.35 = (f32[8,512]{1,0:T(8,128)S(1)}, f32[8,512]{1,0:T(8,128)S(1)}, u32[]{:S(2)}, u32[]{:S(2)}) collective-permute-start(f32[8,512]{1,0:T(8,128)S(1)} %get-tuple-element.181.refs_1_), channel_id=1, source_target_pairs={{0,4},{4,0},{8,12},{12,8},{16,20},{20,16},{24,28},{28,24},{1,5},{5... | collective-permute-start | bytes 49160 | tf_op jit(solution)/shard_map/ppermute | solution.py:615
  (20 other events, 85.5 us)

commit v6 on v5

--- a/solution.py
+++ b/solution.py
@@ -14,16 +14,15 @@
 f32 = jnp.float32
 bf16 = jnp.bfloat16
 VMEM = pl.BlockSpec(memory_space=pltpu.VMEM)
-SMEM = pl.BlockSpec(memory_space=pltpu.SMEM)
 HBM = pl.BlockSpec(memory_space=pltpu.HBM)
 
 
 weight = {
-    "pick_piece": 4, "mixer_in": 0, "join_depth": 16, "join_one": 0, "mlp_one": 0, "join_two": 0, "mlp_two": 32, "mid_back": 32,
-    "add_core": 32, "mixer_back": 0, "mixer_out": 16, "add_core_small": 4, "add_cross": 0, "mixed_out": 0, "tokens_out": 2,
-    "add_cross_small": 0, "add_depth": 0, "add_depth_small": 8, "add_far": 2, "add_far_small": 16, "add_last": 4,
-    "add_last_small": 4, "join_mlp": 2, "join_mix": 16, "spread_mlp": 8, "spread_mix": 8, "add_pair": 2, "mid_in": 0,
-    "mlp_own": 16,
+    "pick_piece": 4, "mixer_in": 32, "join_depth": 32, "join_one": 4, "mlp_one": 0, "join_two": 0, "mlp_two": 8, "mid_back": 8,
+    "add_core": 32, "mixer_back": 0, "mixer_out": 0, "add_core_small": 0, "add_cross": 16, "mixed_out": 0, "tokens_out": 2,
+    "add_cross_small": 16, "add_depth": 0, "add_near_small": 8, "add_far": 16, "add_far_small": 0, "add_last": 4,
+    "add_last_small": 4, "join_mlp": 2, "join_mix": 16, "spread_mlp": 8, "spread_mix": 0, "add_pair": 8, "mid_in": 8,
+    "mlp_own": 4,
 }
 
 
@@ -39,17 +38,24 @@
     return jax.ShapeDtypeStruct(shape, dtype)
 
 
-def call(body, name, operands, outs, scratch=(), smem=1, limit=16, after=(), hbm=0):
+def place():
+    row = lax.axis_index("dp")
+    return row & 1, (row >> 1) & 3, lax.axis_index("mp")
+
+
+def call(body, name, operands, outs, scratch=(), limit=16, after=(), hbm=0):
+    placed = operands[0] is None
+    operands = operands[placed:]
     n, extra, cost = len(operands), len(after), weight[name]
-    operands = [pltpu.with_memory_space_constraint(v, pltpu.HBM) if smem <= i < smem + hbm else v for i, v in enumerate(operands)]
+    operands = [pltpu.with_memory_space_constraint(v, pltpu.HBM) if i < hbm else v for i, v in enumerate(operands)]
 
     def run(*refs):
-        body(*refs[:n], *refs[n + extra :])
+        body(*((place(),) if placed else ()), *refs[:n], *refs[n + extra :])
 
     return pl.pallas_call(
         run,
         out_shape=outs,
-        in_specs=[SMEM] * smem + [HBM] * hbm + [VMEM] * (n - smem - hbm) + [pl.BlockSpec(memory_space=pl.ANY)] * extra,
+        in_specs=[HBM] * hbm + [VMEM] * (n - hbm) + [pl.BlockSpec(memory_space=pl.ANY)] * extra,
         out_specs=[VMEM] * len(outs),
         scratch_shapes=list(scratch),
         compiler_params=pltpu.CompilerParams(vmem_limit_bytes=limit << 20),
@@ -153,34 +159,36 @@
     payload[2:3, 0 : b_up.shape[1]] = b_up[...]
 
 
-def feed_forward(nm, cot, wu, wd, bu):
-    pre = dot(nm, wu) + bu
-    grad_act = dot_nt(cot, wd)
+def store_pieces(ref, base, rows, values):
+    for p in range(4):
+        ref[p, base : base + rows, :] = values[p * rows : (p + 1) * rows].astype(bf16)
+
+
+def send_first(ref, core, values):
+    n = values.shape[0] // 2
+    ref[pl.ds(pl.multiple_of((1 - core) * n, n), n), :] = values[0:n]
+    ref[pl.ds(pl.multiple_of(core * n, n), n), :] = values[n:]
+
+
+def ffn_block(slot, core, nm, nmt, cot, wu, wd, bu, mix, gn, keep, send, hT):
+    pre = dot(nm, wu[...]) + bu
+    grad_act = dot_nt(cot, wd[...])
     sq = pre * pre
     t = jnp.tanh(pre * (gelu_k + gelu_k * gelu_c * sq))
     half = 0.5 + 0.5 * t
     h = pre * half
     slope = half + h * (1.0 - t) * (gelu_k + 3.0 * gelu_k * gelu_c * sq)
     grad_pre = grad_act * slope
-    return h.astype(bf16), grad_pre.astype(bf16), jnp.sum(grad_pre, axis=0, keepdims=True)
-
-
-def store_pieces(ref, base, rows, values):
-    for p in range(4):
-        ref[p, base : base + rows, :] = values[p * rows : (p + 1) * rows].astype(bf16)
-
-
-def ffn_block(slot, core, nm, nmt, cot, wu, wd, bu, mix, gn, keep, send, hT):
-    h, g, bsum = feed_forward(nm, cot, wu, wd, bu)
-    hT[...] = h.T
-    half = nm.shape[1] // 2
-    for ref, which in ((send, 1 - core), (keep, core)):
-        rows = pl.ds(pl.multiple_of(which * half, half), half)
-        store_pieces(ref, slot * (half // 2), half // 4, dot(nmt[rows, :], g))
-        store_pieces(ref, slot * (half // 2) + half // 4, half // 4, dot(hT[rows, :], cot))
-    mix[...] += dot(h, wd)
-    gn[...] += dot_nt(g, wu)
-    return bsum
+    total = jnp.sum(grad_pre, axis=0, keepdims=True)
+    h, g = h.astype(bf16), grad_pre.astype(bf16)
+    send_first(hT, core, h.T)
+    mix[...] += dot(h, wd[...])
+    gn[...] += dot_nt(g, wu[...])
+    n = nm.shape[1] // 2
+    for base, got in ((0, dot(nmt[...], g)), (n // 4, dot(hT[...], cot))):
+        store_pieces(send, slot * (n // 2) + base, n // 4, got[0:n])
+        store_pieces(keep, slot * (n // 2) + base, n // 4, got[n:])
+    return total
 
 
 def mid_in(idx, own, r1, r2, r3, prods, ends, decay, share, cand, x, cot, w_out, gain,
@@ -214,7 +222,7 @@
     r = lax.rsqrt(jnp.mean(mid * mid, axis=-1, keepdims=True) + norm_eps)
     nm = (mid * r * gain[...]).astype(bf16)
     nm2[...] = nm
-    nm2t[...] = nm.T
+    send_first(nm2t, idx[0], nm.T)
 
     def put(rows, cols, values):
         square[rows, cols] = values
@@ -243,7 +251,7 @@
     gn[...] = jnp.zeros_like(gn)
     small[...] = jnp.zeros_like(small)
     small[pl.ds(4 * idx[2] + 2, 1), :] = ffn_block(
-        0, idx[0], nm2[...], nm2t, cotp[...], wu[...], wd[...], bu[...], mix, gn, keep, send, hT
+        0, idx[0], nm2[...], nm2t, cotp[...], wu, wd, bu[...], mix, gn, keep, send, hT
     )
 
 
@@ -253,7 +261,7 @@
     small[...] = small0[...]
     lay_out(idx, (n1, n2, f1, f2), 0, wu, wd)
     small[pl.ds(4 * (idx[2] ^ 1) + 2, 1), :] = ffn_block(
-        0, idx[0], nm2[...], nm2t, cotp[...], wu[...], wd[...], bias[2:3, 0 : wu.shape[1]], mix, gn, keep, send, hT
+        0, idx[0], nm2[...], nm2t, cotp[...], wu, wd, bias[2:3, 0 : wu.shape[1]], mix, gn, keep, send, hT
     )
 
 
@@ -264,7 +272,7 @@
     for slot, bias in enumerate((bias2, bias3)):
         lay_out(idx, (n1, n2, f1, f2), slot * wu.shape[0] // 4, wu, wd)
         small[pl.ds(4 * (idx[2] ^ (2 + slot)) + 2, 1), :] = ffn_block(
-            slot, idx[0], nm2[...], nm2t, cotp[...], wu[...], wd[...], bias[2:3, 0 : wu.shape[1]], mix, gn, keep, send, hT
+            slot, idx[0], nm2[...], nm2t, cotp[...], wu, wd, bias[2:3, 0 : wu.shape[1]], mix, gn, keep, send, hT
         )
 
 
@@ -315,7 +323,7 @@
     done[...] = jnp.zeros_like(done)
 
 
-def gate_grads(which, keep, carried, st, share, cand, du, dv, w, nmt, z, out, gnm, small):
+def gate_grads(which, keep, carried, st, share, cand, du, dv, nmt, z, out, lows, small):
     length, units = carried.shape
     half = units // 2
     cols = pl.ds(pl.multiple_of(which * half, half), half)
@@ -332,17 +340,16 @@
         small[at, quarter:] = sum_b[:, i * quarter : (i + 1) * quarter]
     part = nmt.shape[0] // 4
     for k, g in enumerate((ga, gb, cf * q)):
-        low = g.astype(bf16)
-        got = dot(nmt[...], low)
+        lows[k] = g.astype(bf16)
+        got = dot(nmt[...], lows[k])
         for zz in range(4):
             for p in range(4):
                 top = zz * part + p * (part // 4)
                 out[p, zz ^ z, k * (part // 4) : (k + 1) * (part // 4), :] = got[top : top + part // 4].astype(bf16)
-        gnm[...] += dot_nt(low, w[k, :, cols])
-
-
-def mixer_back(idx, own, r1, r2, r3, prods, flows, decay, share, cand, du, dv, st, grad_states, nmt, w, mask,
-               carried, send, gnm, small, others, carry8):
+
+
+def mixer_back(idx, own, r1, r2, r3, prods, flows, decay, share, cand, du, dv, st, grad_states, nmt, mask,
+               carried, send, lows, small, others, carry8):
     length, units = decay.shape
     steps = length // chunks
     core, z = idx[0], idx[2]
@@ -363,18 +370,23 @@
         return got * decay[rows, :]
 
     lax.fori_loop(0, steps, step, carry8[...], unroll=8)
-    gnm[...] = jnp.zeros_like(gnm)
     small[...] = jnp.zeros_like(small)
-    gate_grads(1 - core, mask[...], carried, st, share, cand, du, dv, w, nmt, z, send, gnm, small)
-
-
-def mixer_out(idx, carried, share, cand, du, dv, st, nmt, w, gnm0, small0, small1, gain_row, x, mask,
-              keep, gnm, small):
+    gate_grads(1 - core, mask[...], carried, st, share, cand, du, dv, nmt, z, send, lows, small)
+
+
+def mixer_out(idx, carried, share, cand, du, dv, st, nmt, w, lows0, small0, small1, gain_row, x, mask,
+              keep, gnm, small, lows):
     length, units = carried.shape
     core, z = idx[0], idx[2]
-    gnm[...] = gnm0[...]
     small[...] = small0[...] + small1[...]
-    gate_grads(core, mask[...], carried, st, share, cand, du, dv, w, nmt, z, keep, gnm, small)
+    gate_grads(core, mask[...], carried, st, share, cand, du, dv, nmt, z, keep, lows, small)
+    half = units // 2
+    total = jnp.zeros(gnm.shape, f32)
+    for part, which in ((lows0, 1 - core), (lows, core)):
+        cols = pl.ds(pl.multiple_of(which * half, half), half)
+        for k in range(3):
+            total = total + dot_nt(part[k], w[k, :, cols])
+    gnm[...] = total
     v = x[...]
     r = lax.rsqrt(jnp.mean(v * v, axis=-1, keepdims=True) + norm_eps)
     gains = jnp.sum(gnm[...] * (v * r), axis=0, keepdims=True)
@@ -490,24 +502,50 @@
     out[...] = (own[...] + got[...].astype(f32)).astype(out.dtype)
 
 
-def add_core_small(idx, keep, got, small, send_x, send_y, own_x, own_y, tiny):
+def add_core_small(idx, keep, got, small, send, own, tiny, slots):
+    z = idx[2]
+    rows = keep.shape[1] // 4
+    n = small.shape[0] // 4
+    slots[...] = jnp.zeros_like(slots)
+    for k in range(4):
+        slots[k, 0:n, :] = small[k * n : (k + 1) * n, :]
+    for p in range(4):
+        for j in range(4):
+            at = slice(j * rows, (j + 1) * rows)
+            total = keep[p, at, :].astype(f32) + got[p, at, :].astype(f32)
+            base = j // 2 * rows
+            if j % 2:
+                send[p * 2 * rows + base : p * 2 * rows + base + rows, :] = total.astype(bf16)
+            else:
+                own[p, base : base + rows, :] = total
+    for k in range(2):
+        base = 8 * rows + 16 * k
+        high, low = two_terms(slots[z ^ (2 * k + 1)])
+        send[base : base + 16, :] = jnp.concatenate([high, low], axis=0)
+        tiny[8 * k : 8 * k + 8, :] = slots[z ^ (2 * k)]
+
+
+def add_near_small(idx, own, got, tiny, send_x, send_y, own_x, own_y, tiny_out):
     x, y = idx[1] % 2, idx[1] // 2
-    half, n = own_x.shape[1], small.shape[0]
-    high, low = two_terms(small[...])
-    tiny[0:n, :] = high
-    tiny[n:, :] = low
-    send_x[2 * half : 2 * half + n, :] = high
-    send_x[2 * half + n :, :] = low
+    rows = own.shape[1] // 2
     for k in range(2):
-        at = slice(k * half, (k + 1) * half)
-        p = 2 * k + 1 - x
-        send_x[at, :] = (keep[p, 0:half, :].astype(f32) + got[p, 0:half, :].astype(f32)).astype(bf16)
-        p = 2 * k + x
-        own_x[k] = keep[p, 0:half, :].astype(f32) + got[p, 0:half, :].astype(f32)
-        p = 2 * (1 - y) + k
-        send_y[at, :] = (keep[p, half:, :].astype(f32) + got[p, half:, :].astype(f32)).astype(bf16)
-        p = 2 * y + k
-        own_y[k] = keep[p, half:, :].astype(f32) + got[p, half:, :].astype(f32)
+        base = 8 * rows + 16 * k
+        other = got[base : base + 16, :].astype(f32)
+        high, low = two_terms(tiny[8 * k : 8 * k + 8, :] + (other[0:8] + other[8:16]))
+        for ref, top in ((tiny_out, 0), (send_x, 2 * rows)):
+            ref[top + 8 * k : top + 8 * k + 8, :] = high
+            ref[top + 16 + 8 * k : top + 24 + 8 * k, :] = low
+
+    def total(p, slot):
+        at = pl.ds(pl.multiple_of(p * 2 * rows + slot * rows, 16), rows)
+        return own[p, slot * rows : (slot + 1) * rows, :] + got[at, :].astype(f32)
+
+    for k in range(2):
+        at = slice(k * rows, (k + 1) * rows)
+        send_x[at, :] = total(2 * k + 1 - x, 0).astype(bf16)
+        own_x[k] = total(2 * k + x, 0)
+        send_y[at, :] = total(2 * (1 - y) + k, 1).astype(bf16)
+        own_y[k] = total(2 * y + k, 1)
 
 
 def add_tiny(tiny, got, at):
@@ -535,40 +573,13 @@
     out_y[...] = own_y[x] + got_y[side, :].astype(f32)
 
 
-def add_depth_small(idx, own_x, got_x, own_y, got_y, tiny, send, own, small):
-    half, z = own_x.shape[0], idx[2]
-    rows = half // 2
-    total = add_tiny(tiny, got_x, half)
-    n = total.shape[0] // 4
-    small[...] = jnp.zeros_like(small)
-    for k in range(4):
-        small[k, 0:n, :] = total[k * n : (k + 1) * n]
-    for j in range(4):
-        own_ref, got = ((own_x, got_x), (own_y, got_y))[j // 2]
-        at = slice((j % 2) * rows, (j % 2 + 1) * rows)
-        value = own_ref[at, :] + got[at, :].astype(f32)
-        base = (j // 2) * (rows + 16)
-        if j % 2:
-            send[base : base + rows, :] = value.astype(bf16)
-            high, low = two_terms(small[z ^ j])
-            send[base + rows : base + rows + 16, :] = jnp.concatenate([high, low], axis=0)
-        else:
-            own[(j // 2) * rows : (j // 2 + 1) * rows, :] = value
-
-
-def add_far_small(idx, own, got, small, send, out, tiny_out):
-    z = idx[2]
-    rows, n = out.shape[0], tiny_out.shape[0]
-    tiny = []
-    for k in range(2):
-        base = k * (rows + 16)
-        mine = small[z ^ (2 * k)]
-        other = got[base + rows : base + rows + 16, :].astype(f32)
-        tiny.append(mine + (other[0:n] + other[n : 2 * n]))
-    out[...] = own[0:rows, :] + got[0:rows, :].astype(f32)
-    tiny_out[...] = tiny[0]
-    send[0:rows, :] = (own[rows:, :] + got[rows + 16 : 2 * rows + 16, :].astype(f32)).astype(bf16)
-    high, low = two_terms(tiny[1])
+def add_far_small(own_x, got_x, own_y, got_y, tiny, send, out, tiny_out):
+    rows = out.shape[0]
+    total = add_tiny(tiny, got_x, rows)
+    out[...] = own_x[...] + got_x[0:rows, :].astype(f32)
+    tiny_out[...] = total[0:8]
+    send[0:rows, :] = (own_y[...] + got_y[...].astype(f32)).astype(bf16)
+    high, low = two_terms(total[8:16])
     send[rows:, :] = jnp.concatenate([high, low], axis=0)
 
 
@@ -626,8 +637,7 @@
     ff = w_up.shape[1]
     dp, mp = lax.axis_size("dp"), lax.axis_size("mp")
     assert mp == 4 and dp % 8 == 0 and tokens.shape[0] == 1
-    place = lax.axis_index("dp")
-    idx = jnp.stack([place & 1, (place >> 1) & 3, lax.axis_index("mp")]).astype(jnp.int32)
+    idx = None
     tok, cot = tokens[0], cotangent[0]
     w3 = w_mix.transpose(1, 0, 2)
     row = lambda v: v.reshape(1, -1)
@@ -653,8 +663,8 @@
     ahead = [swap(payload, "mp", j) for j in (1, 2, 3)]
     around = lambda v: [v] + [swap(v, "dp", 2 * k) for k in (1, 2, 3)]
     mine = gate(depth[0], payload)
-    (two,) = call(join, "join_depth", depth[1:], [shape_of(bf16, width // 2, ff)], smem=0, after=(payload,))
-    (one_a,) = call(join, "join_one", (mine, across(mine, 0)), [shape_of(bf16, 2, width // 4, ff)], smem=0, after=(two, *ahead))
+    (two,) = call(join, "join_depth", depth[1:], [shape_of(bf16, width // 2, ff)], after=(payload,))
+    (one_a,) = call(join, "join_one", (mine, across(mine, 0)), [shape_of(bf16, 2, width // 4, ff)], after=(two, *ahead))
     far_two = across(two, 0)
     quarter = width // 8
     st, stT, middle, nm2, nm2t, cotp = call(
@@ -663,7 +673,7 @@
         [shape_of(f32, length + chunks, units), shape_of(bf16, units, length), square, square16, shape_of(bf16, width, length), square16],
         [pltpu.VMEM((lanes, length, 128), f32), pltpu.VMEM((4, 4, units), f32), pltpu.VMEM((chunks, units), f32), pltpu.VMEM((length, width), f32)],
     )
-    (two_a,) = call(join, "join_two", (two, far_two), [shape_of(bf16, 2, width // 2, ff)], smem=0, after=(nm2,))
+    (two_a,) = call(join, "join_two", (two, far_two), [shape_of(bf16, 2, width // 2, ff)], after=(nm2,))
     two_b = across(two_a, 1)
     block = 2 * quarter
     pair = lambda dtype, rows: shape_of(dtype, 2, rows, width)
@@ -677,7 +687,7 @@
         mlp_one, "mlp_one",
         (idx, one_a, one_b, swap(one_a, "dp", 1), swap(one_b, "dp", 1), ahead[0], mix, gn, small_mlp, nm2, nm2t, cotp), grads(block), weights,
     )
-    (pair_a,) = call(add_pair, "add_pair", (keep_a, swap(send_a, "dp", 1)), [shape_of(bf16, 4, block, width)], smem=0)
+    (pair_a,) = call(add_pair, "add_pair", (keep_a, swap(send_a, "dp", 1)), [shape_of(bf16, 4, block, width)])
     more_a = swap(pair_a, "mp", 1)
     mix, gn, keep, send, small_mlp = call(
         mlp_two, "mlp_two",
@@ -700,74 +710,73 @@
     got_x, got_y = swap(send_x, "dp", 2), swap(send_y, "dp", 4)
 
     rows_m = 3 * width // 16
-    carried, send, gnm, small = call(
+    carried, send, lows, small = call(
         mixer_back, "mixer_back",
-        (idx, payload, *behind, prods, flows, decay, share, cand, du, dv, st, grad_states, nmt, w3, mask),
-        [wide, shape_of(bf16, 4, 4, rows_m, units // 2), square, shape_of(f32, 16, width)],
+        (idx, payload, *behind, prods, flows, decay, share, cand, du, dv, st, grad_states, nmt, mask),
+        [wide, shape_of(bf16, 4, 4, rows_m, units // 2), shape_of(bf16, 3, length, units // 2), shape_of(f32, 16, width)],
         [pltpu.VMEM((4, 2, units), f32), pltpu.VMEM((chunks, units), f32)], after=(own_x,),
     )
     flat = lambda v: v.reshape(4, -1, width)
     got = swap(send, "dp", 1)
     keep, gnm, small = call(
         mixer_out, "mixer_out",
-        (idx, carried, share, cand, du, dv, st, nmt, w3, gnm, small, small_mlp, gain_row, x, mask),
+        (idx, carried, share, cand, du, dv, st, nmt, w3, lows, small, small_mlp, gain_row, x, mask),
         [shape_of(bf16, 4, 4, rows_m, units // 2), square, shape_of(f32, 16, width)],
-    )
-    half_m = 2 * rows_m
+        [pltpu.VMEM((3, length, units // 2), bf16)],
+    )
     one = lambda dtype, rows: shape_of(dtype, rows, width)
-    send_mx, send_my, own_mx, own_my, tiny = call(
+    send_m, own_m, tiny = call(
         add_core_small, "add_core_small", (idx, flat(keep), flat(got), small),
-        [one(bf16, 2 * half_m + 32), one(bf16, 2 * half_m), pair(f32, half_m), pair(f32, half_m), one(bf16, 32)],
-    )
-    got_mx, got_my = swap(send_mx, "dp", 2), swap(send_my, "dp", 4)
+        [one(bf16, 8 * rows_m + 32), shape_of(f32, 4, 2 * rows_m, width), one(f32, 16)], [pltpu.VMEM((4, 8, width), f32)],
+    )
+    got_m = swap(send_m, "mp", 1)
     mark = shape_of(f32, 8, 128)
     grad_tok, done_tok = call(tokens_out, "tokens_out", (gnm, x, row(gain_mix), grad_mid), [square16, mark],
-                       [pltpu.VMEM((length, width), f32), pltpu.VMEM((lanes, length, 128), f32)], smem=0, after=(own_mx,))
-    mixed, done_mix = call(mixed_out, "mixed_out", (mix,), [square16, mark], [pltpu.VMEM((lanes, length, 128), f32)], smem=0, after=(own_mx,))
+                       [pltpu.VMEM((length, width), f32), pltpu.VMEM((lanes, length, 128), f32)], after=(own_m,))
+    mixed, done_mix = call(mixed_out, "mixed_out", (mix,), [square16, mark], [pltpu.VMEM((lanes, length, 128), f32)], after=(own_m,))
 
     send_y, send_x, own_x, own_y = call(add_cross, "add_cross", (idx, own_x, got_x, own_y, got_y),
-                                        [one(bf16, half)] * 2 + [one(f32, half)] * 2, after=(own_mx,))
+                                        [one(bf16, half)] * 2 + [one(f32, half)] * 2, after=(own_m,))
     got_x, got_y = swap(send_y, "dp", 4), swap(send_x, "dp", 2)
+    rows_f = block + units // 32
+    send, own = call(add_depth, "add_depth", (own_x, got_x, own_y, got_y), [one(bf16, block + units // 16), one(f32, 2 * rows_f)],
+                     [pltpu.VMEM((2 * half, width), f32)])
+    got = swap(send, "mp", 1)
+    send_mx, send_my, own_mx, own_my, tiny = call(
+        add_near_small, "add_near_small", (idx, own_m, got_m, tiny),
+        [one(bf16, 2 * rows_m + 32), one(bf16, 2 * rows_m), pair(f32, rows_m), pair(f32, rows_m), one(bf16, 32)],
+        after=(own, done_mix, done_tok),
+    )
+    got_mx, got_my = swap(send_mx, "dp", 2), swap(send_my, "dp", 4)
+    send, own = call(add_far, "add_far", (own, got), [one(bf16, rows_f), one(f32, rows_f)], after=(tiny,))
+    got = swap(send, "mp", 2)
     send_my, send_mx, own_mx, own_my, tiny = call(
         add_cross_small, "add_cross_small", (idx, own_mx, got_mx, own_my, got_my, tiny),
-        [one(bf16, half_m + 32), one(bf16, half_m), one(f32, half_m), one(f32, half_m), one(bf16, 32)],
-        after=(own_x, done_mix, done_tok),
+        [one(bf16, rows_m + 32), one(bf16, rows_m), one(f32, rows_m), one(f32, rows_m), one(bf16, 32)], after=(own,),
     )
     got_mx, got_my = swap(send_my, "dp", 4), swap(send_mx, "dp", 2)
-    rows_f = block + units // 32
-    send, own = call(add_depth, "add_depth", (own_x, got_x, own_y, got_y), [one(bf16, block + units // 16), one(f32, 2 * rows_f)],
-                     [pltpu.VMEM((2 * half, width), f32)], smem=0, after=(own_mx,))
-    got = swap(send, "mp", 1)
-    send_m, own_m, small = call(
-        add_depth_small, "add_depth_small", (idx, own_mx, got_mx, own_my, got_my, tiny),
-        [one(bf16, 2 * rows_m + 32), one(f32, 2 * rows_m), shape_of(f32, 4, 8, width)], after=(own,),
-    )
-    got_m = swap(send_m, "mp", 1)
-    send, own = call(add_far, "add_far", (own, got), [one(bf16, rows_f), one(f32, rows_f)], smem=0, after=(small,))
-    got = swap(send, "mp", 2)
     send_m, own_m, tiny = call(
-        add_far_small, "add_far_small", (idx, own_m, got_m, small),
-        [one(bf16, rows_m + 16), one(f32, rows_m), one(f32, 8)], after=(own,),
+        add_far_small, "add_far_small", (own_mx, got_mx, own_my, got_my, tiny), [one(bf16, rows_m + 16), one(f32, rows_m), one(f32, 8)],
     )
     got_m = swap(send_m, "mp", 2)
     groups = [[g * 8 + i for g in range(dp // 8)] for i in range(8)]
 
     def last(fn, name, operands, outs, after):
         if dp == 8:
-            return call(fn, name, operands, outs, smem=0, after=after)
-        done = call(fn, name, operands, [shape_of(f32, *o.shape) for o in outs], smem=0, after=after)
+            return call(fn, name, operands, outs, after=after)
+        done = call(fn, name, operands, [shape_of(f32, *o.shape) for o in outs], after=after)
         return [lax.psum(v, "dp", axis_index_groups=groups).astype(o.dtype) for v, o in zip(done, outs)]
 
     (part,) = last(add_last, "add_last", (own, got), [one(bf16, rows_f)], (tiny,))
     near_f = around(part)
     part, tiny = last(add_last_small, "add_last_small", (own_m, tiny, got_m), [one(bf16, rows_m), one(f32, 8)], (part,))
     near_m = around(part)
-    (near,) = call(join, "join_mlp", near_f, [shape_of(bf16, 4, rows_f, width)], smem=0, after=(part,))
+    (near,) = call(join, "join_mlp", near_f, [shape_of(bf16, 4, rows_f, width)], after=(part,))
     grad_up, grad_down, grad_out, done = call(
         spread_mlp, "spread_mlp", (idx, near, swap(near, "dp", 1)),
         [shape_of(f32, width, ff), shape_of(f32, ff, width), shape_of(f32, units // 4, width), mark],
     )
-    (near,) = call(join, "join_mix", near_m, [shape_of(bf16, 4, rows_m, width)], smem=0)
+    (near,) = call(join, "join_mix", near_m, [shape_of(bf16, 4, rows_m, width)])
     grad_mix, g_bf, g_bi, g_gain_mix, g_gain_mlp, g_bu = call(
         spread_mix, "spread_mix", (idx, tiny, swap(tiny, "dp", 1), near, swap(near, "dp", 1)),
         [shape_of(f32, 3, width // 4, units), shape_of(f32, 1, units // 4), shape_of(f32, 1, units // 4),

time: 118 us -> 114 us (0.966)
  Pallas kernels: 43.1 us -> 33 us
  waiting for transfers between devices: 21.5 us -> 25.3 us
  starting transfers between devices: 52.1 us -> 54.4 us
    pallas_call x29, Pallas kernels: 43.1 us -> 33 us  [call(): pl.pallas_call(run, out_shape=outs, in_specs=[HBM] * hbm + [VMEM] * (n -...]
    ppermute x40, waiting for transfers between devices: 20.1 us -> 23.9 us  [swap(): return lax.ppermute(value, axis, [(i, i ^ bit) for i in range(size)])]
    ppermute x40, starting transfers between devices: 47 us -> 49.3 us  [swap(): return lax.ppermute(value, axis, [(i, i ^ bit) for i in range(size)])]
  transfers between devices with their start and end apart: 44 -> 44, of which waited for: 14 -> 17; matrix products, arithmetic and copies ran while one was open for 0% -> 0% of each run, Pallas kernels for 34% -> 26%
where the time goes in v6:
time: 114 us
  starting transfers between devices  54.4 us (48%)
  Pallas kernels  33 us (29%)
  waiting for transfers between devices  25.3 us (22%)
    ppermute x40, starting transfers between devices, swap(): return lax.ppermute(value, axis, [(i, i ^ bit) for i in range(size)])  49.3 us
    pallas_call x29, Pallas kernels, call(): pl.pallas_call(run, out_shape=outs, in_specs=[HBM] * hbm + [VMEM] * (n -...  33 us
    ppermute x40, waiting for transfers between devices, swap(): return lax.ppermute(value, axis, [(i, i ^ bit) for i in range(size)])  23.9 us
    ppermute x4, starting transfers between devices, across(): lax.ppermute(value, 'dp', [(i, i ^ 2 << (i & 1 ^ turn)) for i in range(si...  5.09 us
  transfers between devices with their start and end apart: 44, of which 17 were waited for; matrix products, arithmetic and copies ran while one was open for 0% of the time, Pallas kernels for 26%

profile of v6, /device:TPU:1, one launch (start us, length us, event | category | flops | bytes accessed | tf_op | source)
XLA Modules:
  0.0 113.6 jit_solution(13206669957482840604)
XLA Ops:
  1.6 2.2 %collective-permute-start.9 = (bf16[128,512]{1,0:T(8,128)(2,1)S(1)}, bf16[128,512]{1,0:T(8,128)(2,1)S(1)}, u32[]{:S(2)}, u32[]{:S(2)}) collective-permute-start(bf16[128,512]{1,0:T(8,128)(2,1)S(1)} %pick_piece.1.refs_7_), channel_id=1, source_target_pairs={{0,1},{1,0},{2,3},{3,2},{4,5},{5,4},{6,7},{7,6},{8,9},{9,8},{10,11... | collective-permute-start | bytes 393224 | tf_op jit(solution)/shard_map/ppermute | solution.py:626
  3.7 2.2 %collective-permute-start.1 = (bf16[128,512]{1,0:T(8,128)(2,1)S(1)}, bf16[128,512]{1,0:T(8,128)(2,1)S(1)}, u32[]{:S(2)}, u32[]{:S(2)}) collective-permute-start(bf16[128,512]{1,0:T(8,128)(2,1)S(1)} %pick_piece.1.refs_7_), channel_id=1, source_target_pairs={{0,3},{1,2},{2,1},{3,0},{4,7},{5,6},{6,5},{7,4},{8,11},{9,10},{10,... | collective-permute-start | bytes 393224 | tf_op jit(solution)/shard_map/ppermute | solution.py:626
  6.1 6.5 %mixer_in.1 = (f32[512,1024]{1,0:T(8,128)S(1)}, f32[512,1024]{1,0:T(8,128)S(1)}, f32[512,1024]{1,0:T(8,128)S(1)}, f32[512,1024]{1,0:T(8,128)S(1)}, f32[512,1024]...) custom-call(s32[1,3]{1,0:T(1,128)} %refs_0_.4, ...), custom_call_target="tpu_custom_call" | custom-call | flops 34359738368 | bytes 134217728 | tf_op jit(solution)/shard_map/mixer_in/pallas_call | solution.py:55
  12.6 2.4 %collective-permute-start.5 = (f32[4,1024]{1,0:T(4,128)S(1)}, f32[4,1024]{1,0:T(4,128)S(1)}, u32[]{:S(2)}, u32[]{:S(2)}) collective-permute-start(f32[4,1024]{1,0:T(4,128)S(1)} %get-tuple-element.102.refs_2_.refs_0_.refs_1_), channel_id=1, source_target_pairs={{0,3},{1,2},{2,1},{3,0},{4,7},{5,6},{6,5},{7,4},{8,11},{9,10},{10,... | collective-permute-start | bytes 49160 | tf_op jit(solution)/shard_map/ppermute | solution.py:626
  17.9 1.3 %collective-permute-start.2 = (bf16[256,512]{1,0:T(8,128)(2,1)S(1)}, bf16[256,512]{1,0:T(8,128)(2,1)S(1)}, u32[]{:S(2)}, u32[]{:S(2)}) collective-permute-start(bf16[256,512]{1,0:T(8,128)(2,1)S(1)} %join_depth.1.refs_0_.refs_2_), channel_id=1, source_target_pairs={{0,8},{4,20},{8,0},{12,28},{16,24},{20,4},{24,16},{28,12},{1,9},{5... | collective-permute-start | bytes 786440 | tf_op jit(solution)/shard_map/ppermute | solution.py:631
  21.6 2.0 %mid_in.1 = (f32[520,1024]{1,0:T(8,128)S(1)}, bf16[1024,512]{1,0:T(8,128)(2,1)S(1)}, f32[512,512]{1,0:T(8,128)S(1)}, bf16[512,512]{1,0:T(8,128)(2,1)S(1)}, bf16[...) custom-call(f32[4,1024]{1,0:T(4,128)S(1)} %get-tuple-element.102.refs_2_.refs_0_.refs_1_, ...), custom_call_target="tpu_custom_call" | custom-call | flops 8589934592 | bytes 33554432 | tf_op jit(solution)/shard_map/mid_in/pallas_call | solution.py:55
  23.7 3.3 %collective-permute-start.12 = (bf16[2,128,512]{2,1,0:T(8,128)(2,1)S(1)}, bf16[2,128,512]{2,1,0:T(8,128)(2,1)S(1)}, u32[]{:S(2)}, u32[]{:S(2)}) collective-permute-start(bf16[2,128,512]{2,1,0:T(8,128)(2,1)S(1)} %join_one.1.refs_0_), channel_id=1, source_target_pairs={{0,4},{4,0},{8,12},{12,8},{16,20},{20,16},{24,28},{28,24},{1,5},{5... | collective-permute-start | bytes 786440 | tf_op jit(solution)/shard_map/ppermute | solution.py:626
  28.7 2.0 %collective-permute-start.13 = (bf16[2,128,512]{2,1,0:T(8,128)(2,1)S(1)}, bf16[2,128,512]{2,1,0:T(8,128)(2,1)S(1)}, u32[]{:S(2)}, u32[]{:S(2)}) collective-permute-start(bf16[2,128,512]{2,1,0:T(8,128)(2,1)S(1)} %gate.4.refs_1_), channel_id=1, source_target_pairs={{0,4},{4,0},{8,12},{12,8},{16,20},{20,16},{24,28},{28,24},{1,5},{5... | collective-permute-start | bytes 786440 | tf_op jit(solution)/shard_map/ppermute | solution.py:626
  30.7 2.1 %mlp_own.1 = (f32[512,512]{1,0:T(8,128)S(1)}, f32[512,512]{1,0:T(8,128)S(1)}, bf16[4,128,512]{2,1,0:T(8,128)(2,1)S(1)}, bf16[4,128,512]{2,1,0:T(8,128)(2,1)S(1)}, f32[16,512]{1,0:T(8,128)S(1)}) custom-call(bf16[512,512]{1,0:T(8,128)(2,1)S(1)} %copy-done.3, bf16[512,512]{1,0:T(8,128)(2,1)S(1)} %copy-done.4, f32[1,512]{1,0:T(1,128)S(1)} %bitcast.24, ...), custom_call_target="tpu_custom_call" | custom-call | flops 4294967296 | bytes 16777216 | tf_op jit(solution)/shard_map/mlp_own/pallas_call | solution.py:55
  32.9 2.2 %mlp_one.1 = (f32[512,512]{1,0:T(8,128)S(1)}, f32[512,512]{1,0:T(8,128)S(1)}, bf16[4,128,512]{2,1,0:T(8,128)(2,1)S(1)}, bf16[4,128,512]{2,1,0:T(8,128)(2,1)S(1)}, f32[16,512]{1,0:T(8,128)S(1)}) custom-call(bf16[2,128,512]{2,1,0:T(8,128)(2,1)S(1)} %join_one.1.refs_0_, bf16[2,128,512]{2,1,0:T(8,128)(2,1)S(1)} %gate.4.refs_1_, ...), custom_call_target="tpu_custom_call" | custom-call | tf_op jit(solution)/shard_map/mlp_one/pallas_call | solution.py:55
  35.7 2.7 %collective-permute-start.8 = (bf16[2,256,512]{2,1,0:T(8,128)(2,1)S(1)}, bf16[2,256,512]{2,1,0:T(8,128)(2,1)S(1)}, u32[]{:S(2)}, u32[]{:S(2)}) collective-permute-start(bf16[2,256,512]{2,1,0:T(8,128)(2,1)S(1)} %collective-permute-done.6.refs_1_), channel_id=1, source_target_pairs={{0,4},{4,0},{8,12},{12,8},{16,20},{20,16},{24,28},{28,24},{1,5},{5... | collective-permute-start | bytes 1572872 | tf_op jit(solution)/shard_map/ppermute | solution.py:626
  39.9 4.0 %mlp_two.1 = (f32[512,512]{1,0:T(8,128)S(1)}, f32[512,512]{1,0:T(8,128)S(1)}, bf16[4,256,512]{2,1,0:T(8,128)(2,1)S(1)}, bf16[4,256,512]{2,1,0:T(8,128)(2,1)S(1)}, f32[16,512]{1,0:T(8,128)S(1)}) custom-call(bf16[2,256,512]{2,1,0:T(8,128)(2,1)S(1)} %join_two.1.refs_7_.refs_0_, bf16[2,256,512]{2,1,0:T(8,128)(2,1)S(1)} %collective-permute-done.6.refs_1_, ...), custom_call_target="tpu_custom_call" | custom-call | flops 8589934592 | bytes 33554432 | tf_op jit(solution)/shard_map/mlp_two/pallas_call | solution.py:55
  44.4 2.2 %mid_back.1 = (bf16[4,128,512]{2,1,0:T(8,128)(2,1)S(1)}, bf16[4,128,512]{2,1,0:T(8,128)(2,1)S(1)}, f32[512,512]{1,0:T(8,128)S(1)}, f32[512,1024]{1,0:T(8,128)S(1...) custom-call(f32[512,512]{1,0:T(8,128)S(1)} %get-tuple-element.122.refs_0_, ...), custom_call_target="tpu_custom_call" | custom-call | flops 8589934592 | bytes 33554432 | tf_op jit(solution)/shard_map/mid_back/pallas_call | solution.py:55
  46.8 2.4 %collective-permute-start.18 = (f32[2,1024]{1,0:T(2,128)S(1)}, f32[2,1024]{1,0:T(2,128)S(1)}, u32[]{:S(2)}, u32[]{:S(2)}) collective-permute-start(f32[2,1024]{1,0:T(2,128)S(1)} %gate.5.refs_0_), channel_id=1, source_target_pairs={{0,3},{1,2},{2,1},{3,0},{4,7},{5,6},{6,5},{7,4},{8,11},{9,10},{10,... | collective-permute-start | bytes 24584 | tf_op jit(solution)/shard_map/ppermute | solution.py:626
  50.4 1.8 %collective-permute-done.20.refs_2_ = bf16[4,128,512]{2,1,0:T(8,128)(2,1)S(1)} collective-permute-done((bf16[4,128,512]{2,1,0:T(8,128)(2,1)S(1)}, bf16[4,128,512]{2,1,0:T(8,128)(2,1)S(1)}, u32[]{:S(2)}, u32[]{:S(2)}) %collective-permute-start.20) | collective-permute-done | bytes 524320 | tf_op jit(solution)/shard_map/ppermute | solution.py:626
  53.1 1.7 %mixer_back.1 = (f32[512,1024]{1,0:T(8,128)S(1)}, bf16[4,4,96,512]{3,2,1,0:T(8,128)(2,1)S(1)}, bf16[3,512,512]{2,1,0:T(8,128)(2,1)S(1)}, f32[16,512]{1,0:T(8,128)S(1)}) custom-call(f32[2,1024]{1,0:T(2,128)S(1)} %gate.5.refs_0_, f32[2,1024]{1,0:T(2,128)S(1)} %collective-permute-done.16.refs_1_, f32[2,1024]{1,0:T(2,128)S(1)} %collective-permute-done.17.refs_2_, ...), custom_call_target="tpu_custom_call" | custom-call | tf_op jit(solution)/shard_map/mixer_back/pallas_call | solution.py:55
  54.8 1.4 %collective-permute-start.22 = (bf16[4,4,96,512]{3,2,1,0:T(8,128)(2,1)S(1)}, bf16[4,4,96,512]{3,2,1,0:T(8,128)(2,1)S(1)}, u32[]{:S(2)}, u32[]{:S(2)}) collective-permute-start(bf16[4,4,96,512]{3,2,1,0:T(8,128)(2,1)S(1)} %get-tuple-element.146), channel_id=1, source_target_pairs={{0,4},{4,0},{8,12},{12,8},{16,20},{20,16},{24,28},{28,24},{1,5},{5... | collective-permute-start | bytes 4718600 | tf_op jit(solution)/shard_map/ppermute | solution.py:626
  58.7 2.8 %mixer_out.1 = (bf16[4,4,96,512]{3,2,1,0:T(8,128)(2,1)S(1)}, f32[512,512]{1,0:T(8,128)S(1)}, f32[16,512]{1,0:T(8,128)S(1)}) custom-call(f32[512,1024]{1,0:T(8,128)S(1)} %get-tuple-element.140.refs_0_, f32[512,1024]{1,0:T(8,128)S(1)} %get-tuple-element.106.refs_7_.refs_1_, f32[512,1024]{1,0:T(8,128)S(1)} %get-tuple-element.107.refs_8_.refs_2_, ...), custom_call_target="tpu_custom_call" | custom-call | tf_op jit(solution)/shard_map/mixer_out/pallas_call | solution.py:55
  62.5 7.3 %collective-permute-done.24.refs_1_ = bf16[2,256,512]{2,1,0:T(8,128)(2,1)S(1)} collective-permute-done((bf16[2,256,512]{2,1,0:T(8,128)(2,1)S(1)}, bf16[2,256,512]{2,1,0:T(8,128)(2,1)S(1)}, u32[]{:S(2)}, u32[]{:S(2)}) %collective-permute-start.24) | collective-permute-done | bytes 524320 | tf_op jit(solution)/shard_map/ppermute | solution.py:626
  72.4 1.5 %mixed_out.1 = (bf16[512,512]{1,0:T(8,128)(2,1)}, f32[8,128]{1,0:T(8,128)S(1)}) custom-call(f32[512,512]{1,0:T(8,128)S(1)} %get-tuple-element.121.refs_0_, f32[4,192,512]{2,1,0:T(8,128)S(1)} %get-tuple-element.148.refs_1_.refs_4_.refs_0_), custom_call_target="tpu_custom_call" | custom-call | tf_op jit(solution)/shard_map/mixed_out/pallas_call | solution.py:55
  74.0 2.2 %tokens_out.1 = (bf16[512,512]{1,0:T(8,128)(2,1)}, f32[8,128]{1,0:T(8,128)S(1)}) custom-call(f32[512,512]{1,0:T(8,128)S(1)} %get-tuple-element.150.refs_0_, f32[512,512]{1,0:T(8,128)S(1)} %get-tuple-element.108.refs_9_.refs_12_.refs_1_, f32[1,512]{1,0:T(1,128)S(1)} %bitcast.28, f32[512,512]{1,0:T(8,128)S(1)} %get-tuple-element.151.refs_3_, ...), custom_call_target="tpu_custom_call" | custom-call | flops 2147483648 | bytes 8388608 | tf_op jit(solution)/shard_map/tokens_out/pallas_call | solution.py:55
  76.2 1.3 %collective-permute-done.26.refs_1_ = bf16[256,512]{1,0:T(8,128)(2,1)S(1)} collective-permute-done((bf16[256,512]{1,0:T(8,128)(2,1)S(1)}, bf16[256,512]{1,0:T(8,128)(2,1)S(1)}, u32[]{:S(2)}, u32[]{:S(2)}) %collective-permute-start.26) | collective-permute-done | bytes 262176 | tf_op jit(solution)/shard_map/ppermute | solution.py:626
  79.1 2.0 %collective-permute-done.23.refs_1_ = bf16[800,512]{1,0:T(8,128)(2,1)S(1)} collective-permute-done((bf16[800,512]{1,0:T(8,128)(2,1)S(1)}, bf16[800,512]{1,0:T(8,128)(2,1)S(1)}, u32[]{:S(2)}, u32[]{:S(2)}) %collective-permute-start.23) | collective-permute-done | bytes 819232 | tf_op jit(solution)/shard_map/ppermute | solution.py:626
  81.9 2.5 %collective-permute-done.30.refs_1_ = bf16[192,512]{1,0:T(8,128)(2,1)S(1)} collective-permute-done((bf16[192,512]{1,0:T(8,128)(2,1)S(1)}, bf16[192,512]{1,0:T(8,128)(2,1)S(1)}, u32[]{:S(2)}, u32[]{:S(2)}) %collective-permute-start.30) | collective-permute-done | bytes 196640 | tf_op jit(solution)/shard_map/ppermute | solution.py:626
  84.5 1.7 %collective-permute-start.34 = (bf16[160,512]{1,0:T(8,128)(2,1)S(1)}, bf16[160,512]{1,0:T(8,128)(2,1)S(1)}, u32[]{:S(2)}, u32[]{:S(2)}) collective-permute-start(bf16[160,512]{1,0:T(8,128)(2,1)S(1)} %get-tuple-element.180), channel_id=1, source_target_pairs={{0,2},{1,3},{2,0},{3,1},{4,6},{5,7},{6,4},{7,5},{8,10},{9,11},{10,... | collective-permute-start | bytes 491528 | tf_op jit(solution)/shard_map/ppermute | solution.py:626
  86.6 1.6 %collective-permute-start.31 = (bf16[128,512]{1,0:T(8,128)(2,1)S(1)}, bf16[128,512]{1,0:T(8,128)(2,1)S(1)}, u32[]{:S(2)}, u32[]{:S(2)}) collective-permute-start(bf16[128,512]{1,0:T(8,128)(2,1)S(1)} %get-tuple-element.173), channel_id=1, source_target_pairs={{0,16},{4,20},{8,24},{12,28},{16,0},{20,4},{24,8},{28,12},{1,17},{... | collective-permute-start | bytes 393224 | tf_op jit(solution)/shard_map/ppermute | solution.py:626
  88.4 3.5 %collective-permute-done.32.refs_3_ = bf16[96,512]{1,0:T(8,128)(2,1)S(1)} collective-permute-done((bf16[96,512]{1,0:T(8,128)(2,1)S(1)}, bf16[96,512]{1,0:T(8,128)(2,1)S(1)}, u32[]{:S(2)}, u32[]{:S(2)}) %collective-permute-start.32) | collective-permute-done | bytes 98336 | tf_op jit(solution)/shard_map/ppermute | solution.py:626
  92.0 1.7 %collective-permute-start.33 = (bf16[112,512]{1,0:T(8,128)(2,1)S(1)}, bf16[112,512]{1,0:T(8,128)(2,1)S(1)}, u32[]{:S(2)}, u32[]{:S(2)}) collective-permute-start(bf16[112,512]{1,0:T(8,128)(2,1)S(1)} %get-tuple-element.179), channel_id=1, source_target_pairs={{0,2},{1,3},{2,0},{3,1},{4,6},{5,7},{6,4},{7,5},{8,10},{9,11},{10,... | collective-permute-start | bytes 344072 | tf_op jit(solution)/shard_map/ppermute | solution.py:626
  95.4 1.4 %collective-permute-start.40 = (bf16[160,512]{1,0:T(8,128)(2,1)S(1)}, bf16[160,512]{1,0:T(8,128)(2,1)S(1)}, u32[]{:S(2)}, u32[]{:S(2)}) collective-permute-start(bf16[160,512]{1,0:T(8,128)(2,1)S(1)} %add_last.1.refs_3_.refs_0_), channel_id=1, source_target_pairs={{0,8},{4,12},{8,0},{12,4},{16,24},{20,28},{24,16},{28,20},{1,9},{5... | collective-permute-start | bytes 491528 | tf_op jit(solution)/shard_map/ppermute | solution.py:626
  100.6 6.6 %collective-permute-start.35 = (f32[8,512]{1,0:T(8,128)S(1)}, f32[8,512]{1,0:T(8,128)S(1)}, u32[]{:S(2)}, u32[]{:S(2)}) collective-permute-start(f32[8,512]{1,0:T(8,128)S(1)} %get-tuple-element.181.refs_0_), channel_id=1, source_target_pairs={{0,4},{4,0},{8,12},{12,8},{16,20},{20,16},{24,28},{28,24},{1,5},{5... | collective-permute-start | bytes 49160 | tf_op jit(solution)/shard_map/ppermute | solution.py:626
  107.4 3.3 %collective-permute-start.39 = (bf16[4,96,512]{2,1,0:T(8,128)(2,1)S(1)}, bf16[4,96,512]{2,1,0:T(8,128)(2,1)S(1)}, u32[]{:S(2)}, u32[]{:S(2)}) collective-permute-start(bf16[4,96,512]{2,1,0:T(8,128)(2,1)S(1)} %join_mix.1.refs_2_), channel_id=1, source_target_pairs={{0,4},{4,0},{8,12},{12,8},{16,20},{20,16},{24,28},{28,24},{1,5},{5... | collective-permute-start | bytes 1179656 | tf_op jit(solution)/shard_map/ppermute | solution.py:626
  110.7 1.7 %spread_mlp.1 = (f32[512,512]{1,0:T(8,128)}, f32[512,512]{1,0:T(8,128)}, f32[256,512]{1,0:T(8,128)}, f32[8,128]{1,0:T(8,128)S(1)}) custom-call(bf16[4,160,512]{2,1,0:T(8,128)(2,1)S(1)} %join_mlp.1.refs_0_, bf16[4,160,512]{2,1,0:T(8,128)(2,1)S(1)} %collective-permute-done.43.refs_1_), custom_call_target="tpu_custom_call" | custom-call | flops 8589934592 | bytes 33554432 | tf_op jit(solution)/shard_map/spread_mlp/pallas_call | solution.py:55
  (104 shorter events, 29.1 us)
Async XLA Ops:
  1.6 13.5 %collective-permute-start.9 = (bf16[128,512]{1,0:T(8,128)(2,1)S(1)}, bf16[128,512]{1,0:T(8,128)(2,1)S(1)}, u32[]{:S(2)}, u32[]{:S(2)}) collective-permute-start(bf16[128,512]{1,0:T(8,128)(2,1)S(1)} %pick_piece.1.refs_7_), channel_id=1, source_target_pairs={{0,1},{1,0},{2,3},{3,2},{4,5},{5,4},{6,7},{7,6},{8,9},{9,8},{10,11... | collective-permute-start | bytes 393224 | tf_op jit(solution)/shard_map/ppermute | solution.py:626
  3.7 12.4 %collective-permute-start.1 = (bf16[128,512]{1,0:T(8,128)(2,1)S(1)}, bf16[128,512]{1,0:T(8,128)(2,1)S(1)}, u32[]{:S(2)}, u32[]{:S(2)}) collective-permute-start(bf16[128,512]{1,0:T(8,128)(2,1)S(1)} %pick_piece.1.refs_7_), channel_id=1, source_target_pairs={{0,3},{1,2},{2,1},{3,0},{4,7},{5,6},{6,5},{7,4},{8,11},{9,10},{10,... | collective-permute-start | bytes 393224 | tf_op jit(solution)/shard_map/ppermute | solution.py:626
  5.9 11.9 %collective-permute-start = (bf16[128,512]{1,0:T(8,128)(2,1)S(1)}, bf16[128,512]{1,0:T(8,128)(2,1)S(1)}, u32[]{:S(2)}, u32[]{:S(2)}) collective-permute-start(bf16[128,512]{1,0:T(8,128)(2,1)S(1)} %pick_piece.1.refs_7_), channel_id=1, source_target_pairs={{0,2},{1,3},{2,0},{3,1},{4,6},{5,7},{6,4},{7,5},{8,10},{9,11},{10,... | collective-permute-start | bytes 393224 | tf_op jit(solution)/shard_map/ppermute | solution.py:626
  12.6 6.6 %collective-permute-start.5 = (f32[4,1024]{1,0:T(4,128)S(1)}, f32[4,1024]{1,0:T(4,128)S(1)}, u32[]{:S(2)}, u32[]{:S(2)}) collective-permute-start(f32[4,1024]{1,0:T(4,128)S(1)} %get-tuple-element.102.refs_2_.refs_0_.refs_1_), channel_id=1, source_target_pairs={{0,3},{1,2},{2,1},{3,0},{4,7},{5,6},{6,5},{7,4},{8,11},{9,10},{10,... | collective-permute-start | bytes 49160 | tf_op jit(solution)/shard_map/ppermute | solution.py:626
  17.9 9.1 %collective-permute-start.2 = (bf16[256,512]{1,0:T(8,128)(2,1)S(1)}, bf16[256,512]{1,0:T(8,128)(2,1)S(1)}, u32[]{:S(2)}, u32[]{:S(2)}) collective-permute-start(bf16[256,512]{1,0:T(8,128)(2,1)S(1)} %join_depth.1.refs_0_.refs_2_), channel_id=1, source_target_pairs={{0,8},{4,20},{8,0},{12,28},{16,24},{20,4},{24,16},{28,12},{1,9},{5... | collective-permute-start | bytes 786440 | tf_op jit(solution)/shard_map/ppermute | solution.py:631
  20.3 8.4 %collective-permute-start.11 = (bf16[2,128,512]{2,1,0:T(8,128)(2,1)S(1)}, bf16[2,128,512]{2,1,0:T(8,128)(2,1)S(1)}, u32[]{:S(2)}, u32[]{:S(2)}) collective-permute-start(bf16[2,128,512]{2,1,0:T(8,128)(2,1)S(1)} %join_one.1.refs_0_), channel_id=1, source_target_pairs={{0,16},{4,12},{8,24},{12,4},{16,0},{20,28},{24,8},{28,20},{1,17},{... | collective-permute-start | bytes 786440 | tf_op jit(solution)/shard_map/ppermute | solution.py:631
  23.7 9.2 %collective-permute-start.12 = (bf16[2,128,512]{2,1,0:T(8,128)(2,1)S(1)}, bf16[2,128,512]{2,1,0:T(8,128)(2,1)S(1)}, u32[]{:S(2)}, u32[]{:S(2)}) collective-permute-start(bf16[2,128,512]{2,1,0:T(8,128)(2,1)S(1)} %join_one.1.refs_0_), channel_id=1, source_target_pairs={{0,4},{4,0},{8,12},{12,8},{16,20},{20,16},{24,28},{28,24},{1,5},{5... | collective-permute-start | bytes 786440 | tf_op jit(solution)/shard_map/ppermute | solution.py:626
  27.0 8.6 %collective-permute-start.6 = (bf16[2,256,512]{2,1,0:T(8,128)(2,1)S(1)}, bf16[2,256,512]{2,1,0:T(8,128)(2,1)S(1)}, u32[]{:S(2)}, u32[]{:S(2)}) collective-permute-start(bf16[2,256,512]{2,1,0:T(8,128)(2,1)S(1)} %join_two.1.refs_7_.refs_0_), channel_id=1, source_target_pairs={{0,16},{4,12},{8,24},{12,4},{16,0},{20,28},{24,8},{28,20},{1,17},{... | collective-permute-start | bytes 1572872 | tf_op jit(solution)/shard_map/ppermute | solution.py:631
  35.6 13.6 %collective-permute-start.19 = (bf16[4,128,512]{2,1,0:T(8,128)(2,1)S(1)}, bf16[4,128,512]{2,1,0:T(8,128)(2,1)S(1)}, u32[]{:S(2)}, u32[]{:S(2)}) collective-permute-start(bf16[4,128,512]{2,1,0:T(8,128)(2,1)S(1)} %get-tuple-element.135), channel_id=1, source_target_pairs={{0,4},{4,0},{8,12},{12,8},{16,20},{20,16},{24,28},{28,24},{1,5},{5... | collective-permute-start | bytes 1572872 | tf_op jit(solution)/shard_map/ppermute | solution.py:626
  38.5 13.6 %collective-permute-start.20 = (bf16[4,128,512]{2,1,0:T(8,128)(2,1)S(1)}, bf16[4,128,512]{2,1,0:T(8,128)(2,1)S(1)}, u32[]{:S(2)}, u32[]{:S(2)}) collective-permute-start(bf16[4,128,512]{2,1,0:T(8,128)(2,1)S(1)} %add_pair.1.refs_12_), channel_id=1, source_target_pairs={{0,1},{1,0},{2,3},{3,2},{4,5},{5,4},{6,7},{7,6},{8,9},{9,8},{10,11... | collective-permute-start | bytes 1572872 | tf_op jit(solution)/shard_map/ppermute | solution.py:626
  46.6 5.5 %collective-permute-start.21 = (bf16[4,128,512]{2,1,0:T(8,128)(2,1)S(1)}, bf16[4,128,512]{2,1,0:T(8,128)(2,1)S(1)}, u32[]{:S(2)}, u32[]{:S(2)}) collective-permute-start(bf16[4,128,512]{2,1,0:T(8,128)(2,1)S(1)} %get-tuple-element.138), channel_id=1, source_target_pairs={{0,4},{4,0},{8,12},{12,8},{16,20},{20,16},{24,28},{28,24},{1,5},{5... | collective-permute-start | bytes 1572872 | tf_op jit(solution)/shard_map/ppermute | solution.py:626
  46.8 6.3 %collective-permute-start.18 = (f32[2,1024]{1,0:T(2,128)S(1)}, f32[2,1024]{1,0:T(2,128)S(1)}, u32[]{:S(2)}, u32[]{:S(2)}) collective-permute-start(f32[2,1024]{1,0:T(2,128)S(1)} %gate.5.refs_0_), channel_id=1, source_target_pairs={{0,3},{1,2},{2,1},{3,0},{4,7},{5,6},{6,5},{7,4},{8,11},{9,10},{10,... | collective-permute-start | bytes 24584 | tf_op jit(solution)/shard_map/ppermute | solution.py:626
  54.8 6.7 %collective-permute-start.22 = (bf16[4,4,96,512]{3,2,1,0:T(8,128)(2,1)S(1)}, bf16[4,4,96,512]{3,2,1,0:T(8,128)(2,1)S(1)}, u32[]{:S(2)}, u32[]{:S(2)}) collective-permute-start(bf16[4,4,96,512]{3,2,1,0:T(8,128)(2,1)S(1)} %get-tuple-element.146), channel_id=1, source_target_pairs={{0,4},{4,0},{8,12},{12,8},{16,20},{20,16},{24,28},{28,24},{1,5},{5... | collective-permute-start | bytes 4718600 | tf_op jit(solution)/shard_map/ppermute | solution.py:626
  56.2 13.5 %collective-permute-start.24 = (bf16[2,256,512]{2,1,0:T(8,128)(2,1)S(1)}, bf16[2,256,512]{2,1,0:T(8,128)(2,1)S(1)}, u32[]{:S(2)}, u32[]{:S(2)}) collective-permute-start(bf16[2,256,512]{2,1,0:T(8,128)(2,1)S(1)} %get-tuple-element.155), channel_id=1, source_target_pairs={{0,8},{4,12},{8,0},{12,4},{16,24},{20,28},{24,16},{28,20},{1,9},{5... | collective-permute-start | bytes 1572872 | tf_op jit(solution)/shard_map/ppermute | solution.py:626
  57.4 13.2 %collective-permute-start.25 = (bf16[2,256,512]{2,1,0:T(8,128)(2,1)S(1)}, bf16[2,256,512]{2,1,0:T(8,128)(2,1)S(1)}, u32[]{:S(2)}, u32[]{:S(2)}) collective-permute-start(bf16[2,256,512]{2,1,0:T(8,128)(2,1)S(1)} %get-tuple-element.157), channel_id=1, source_target_pairs={{0,16},{4,20},{8,24},{12,28},{16,0},{20,4},{24,8},{28,12},{1,17},{... | collective-permute-start | bytes 1572872 | tf_op jit(solution)/shard_map/ppermute | solution.py:626
  61.9 19.2 %collective-permute-start.23 = (bf16[800,512]{1,0:T(8,128)(2,1)S(1)}, bf16[800,512]{1,0:T(8,128)(2,1)S(1)}, u32[]{:S(2)}, u32[]{:S(2)}) collective-permute-start(bf16[800,512]{1,0:T(8,128)(2,1)S(1)} %get-tuple-element.153), channel_id=1, source_target_pairs={{0,1},{1,0},{2,3},{3,2},{4,5},{5,4},{6,7},{7,6},{8,9},{9,8},{10,11... | collective-permute-start | bytes 2457608 | tf_op jit(solution)/shard_map/ppermute | solution.py:626
  70.8 6.7 %collective-permute-start.26 = (bf16[256,512]{1,0:T(8,128)(2,1)S(1)}, bf16[256,512]{1,0:T(8,128)(2,1)S(1)}, u32[]{:S(2)}, u32[]{:S(2)}) collective-permute-start(bf16[256,512]{1,0:T(8,128)(2,1)S(1)} %get-tuple-element.159), channel_id=1, source_target_pairs={{0,16},{4,20},{8,24},{12,28},{16,0},{20,4},{24,8},{28,12},{1,17},{... | collective-permute-start | bytes 786440 | tf_op jit(solution)/shard_map/ppermute | solution.py:626
  72.1 6.3 %collective-permute-start.27 = (bf16[256,512]{1,0:T(8,128)(2,1)S(1)}, bf16[256,512]{1,0:T(8,128)(2,1)S(1)}, u32[]{:S(2)}, u32[]{:S(2)}) collective-permute-start(bf16[256,512]{1,0:T(8,128)(2,1)S(1)} %get-tuple-element.161), channel_id=1, source_target_pairs={{0,8},{4,12},{8,0},{12,4},{16,24},{20,28},{24,16},{28,20},{1,9},{5... | collective-permute-start | bytes 786440 | tf_op jit(solution)/shard_map/ppermute | solution.py:626
  78.6 5.8 %collective-permute-start.30 = (bf16[192,512]{1,0:T(8,128)(2,1)S(1)}, bf16[192,512]{1,0:T(8,128)(2,1)S(1)}, u32[]{:S(2)}, u32[]{:S(2)}) collective-permute-start(bf16[192,512]{1,0:T(8,128)(2,1)S(1)} %get-tuple-element.170), channel_id=1, source_target_pairs={{0,1},{1,0},{2,3},{3,2},{4,5},{5,4},{6,7},{7,6},{8,9},{9,8},{10,11... | collective-permute-start | bytes 589832 | tf_op jit(solution)/shard_map/ppermute | solution.py:626
  81.3 4.9 %collective-permute-start.29 = (bf16[192,512]{1,0:T(8,128)(2,1)S(1)}, bf16[192,512]{1,0:T(8,128)(2,1)S(1)}, u32[]{:S(2)}, u32[]{:S(2)}) collective-permute-start(bf16[192,512]{1,0:T(8,128)(2,1)S(1)} %get-tuple-element.168), channel_id=1, source_target_pairs={{0,16},{4,20},{8,24},{12,28},{16,0},{20,4},{24,8},{28,12},{1,17},{... | collective-permute-start | bytes 589832 | tf_op jit(solution)/shard_map/ppermute | solution.py:626
  81.6 4.9 %collective-permute-start.28 = (bf16[224,512]{1,0:T(8,128)(2,1)S(1)}, bf16[224,512]{1,0:T(8,128)(2,1)S(1)}, u32[]{:S(2)}, u32[]{:S(2)}) collective-permute-start(bf16[224,512]{1,0:T(8,128)(2,1)S(1)} %get-tuple-element.166), channel_id=1, source_target_pairs={{0,8},{4,12},{8,0},{12,4},{16,24},{20,28},{24,16},{28,20},{1,9},{5... | collective-permute-start | bytes 688136 | tf_op jit(solution)/shard_map/ppermute | solution.py:626
  84.5 9.5 %collective-permute-start.34 = (bf16[160,512]{1,0:T(8,128)(2,1)S(1)}, bf16[160,512]{1,0:T(8,128)(2,1)S(1)}, u32[]{:S(2)}, u32[]{:S(2)}) collective-permute-start(bf16[160,512]{1,0:T(8,128)(2,1)S(1)} %get-tuple-element.180), channel_id=1, source_target_pairs={{0,2},{1,3},{2,0},{3,1},{4,6},{5,7},{6,4},{7,5},{8,10},{9,11},{10,... | collective-permute-start | bytes 491528 | tf_op jit(solution)/shard_map/ppermute | solution.py:626
  86.6 5.4 %collective-permute-start.31 = (bf16[128,512]{1,0:T(8,128)(2,1)S(1)}, bf16[128,512]{1,0:T(8,128)(2,1)S(1)}, u32[]{:S(2)}, u32[]{:S(2)}) collective-permute-start(bf16[128,512]{1,0:T(8,128)(2,1)S(1)} %get-tuple-element.173), channel_id=1, source_target_pairs={{0,16},{4,20},{8,24},{12,28},{16,0},{20,4},{24,8},{28,12},{1,17},{... | collective-permute-start | bytes 393224 | tf_op jit(solution)/shard_map/ppermute | solution.py:626
  92.0 5.8 %collective-permute-start.33 = (bf16[112,512]{1,0:T(8,128)(2,1)S(1)}, bf16[112,512]{1,0:T(8,128)(2,1)S(1)}, u32[]{:S(2)}, u32[]{:S(2)}) collective-permute-start(bf16[112,512]{1,0:T(8,128)(2,1)S(1)} %get-tuple-element.179), channel_id=1, source_target_pairs={{0,2},{1,3},{2,0},{3,1},{4,6},{5,7},{6,4},{7,5},{8,10},{9,11},{10,... | collective-permute-start | bytes 344072 | tf_op jit(solution)/shard_map/ppermute | solution.py:626
  94.0 5.4 %collective-permute-start.42 = (bf16[160,512]{1,0:T(8,128)(2,1)S(1)}, bf16[160,512]{1,0:T(8,128)(2,1)S(1)}, u32[]{:S(2)}, u32[]{:S(2)}) collective-permute-start(bf16[160,512]{1,0:T(8,128)(2,1)S(1)} %add_last.1.refs_3_.refs_0_), channel_id=1, source_target_pairs={{0,24},{4,28},{8,16},{12,20},{16,8},{20,12},{24,0},{28,4},{1,25},{... | collective-permute-start | bytes 491528 | tf_op jit(solution)/shard_map/ppermute | solution.py:626
  94.2 6.4 %collective-permute-start.41 = (bf16[160,512]{1,0:T(8,128)(2,1)S(1)}, bf16[160,512]{1,0:T(8,128)(2,1)S(1)}, u32[]{:S(2)}, u32[]{:S(2)}) collective-permute-start(bf16[160,512]{1,0:T(8,128)(2,1)S(1)} %add_last.1.refs_3_.refs_0_), channel_id=1, source_target_pairs={{0,16},{4,20},{8,24},{12,28},{16,0},{20,4},{24,8},{28,12},{1,17},{... | collective-permute-start | bytes 491528 | tf_op jit(solution)/shard_map/ppermute | solution.py:626
  95.4 11.8 %collective-permute-start.40 = (bf16[160,512]{1,0:T(8,128)(2,1)S(1)}, bf16[160,512]{1,0:T(8,128)(2,1)S(1)}, u32[]{:S(2)}, u32[]{:S(2)}) collective-permute-start(bf16[160,512]{1,0:T(8,128)(2,1)S(1)} %add_last.1.refs_3_.refs_0_), channel_id=1, source_target_pairs={{0,8},{4,12},{8,0},{12,4},{16,24},{20,28},{24,16},{28,20},{1,9},{5... | collective-permute-start | bytes 491528 | tf_op jit(solution)/shard_map/ppermute | solution.py:626
  97.9 9.4 %collective-permute-start.38 = (bf16[96,512]{1,0:T(8,128)(2,1)S(1)}, bf16[96,512]{1,0:T(8,128)(2,1)S(1)}, u32[]{:S(2)}, u32[]{:S(2)}) collective-permute-start(bf16[96,512]{1,0:T(8,128)(2,1)S(1)} %get-tuple-element.182.refs_0_.refs_4_), channel_id=1, source_target_pairs={{0,24},{4,28},{8,16},{12,20},{16,8},{20,12},{24,0},{28,4},{1,25},{... | collective-permute-start | bytes 294920 | tf_op jit(solution)/shard_map/ppermute | solution.py:626
  98.2 9.1 %collective-permute-start.37 = (bf16[96,512]{1,0:T(8,128)(2,1)S(1)}, bf16[96,512]{1,0:T(8,128)(2,1)S(1)}, u32[]{:S(2)}, u32[]{:S(2)}) collective-permute-start(bf16[96,512]{1,0:T(8,128)(2,1)S(1)} %get-tuple-element.182.refs_0_.refs_4_), channel_id=1, source_target_pairs={{0,16},{4,20},{8,24},{12,28},{16,0},{20,4},{24,8},{28,12},{1,17},{... | collective-permute-start | bytes 294920 | tf_op jit(solution)/shard_map/ppermute | solution.py:626
  99.4 8.0 %collective-permute-start.36 = (bf16[96,512]{1,0:T(8,128)(2,1)S(1)}, bf16[96,512]{1,0:T(8,128)(2,1)S(1)}, u32[]{:S(2)}, u32[]{:S(2)}) collective-permute-start(bf16[96,512]{1,0:T(8,128)(2,1)S(1)} %get-tuple-element.182.refs_0_.refs_4_), channel_id=1, source_target_pairs={{0,8},{4,12},{8,0},{12,4},{16,24},{20,28},{24,16},{28,20},{1,9},{5... | collective-permute-start | bytes 294920 | tf_op jit(solution)/shard_map/ppermute | solution.py:626
  100.6 11.7 %collective-permute-start.35 = (f32[8,512]{1,0:T(8,128)S(1)}, f32[8,512]{1,0:T(8,128)S(1)}, u32[]{:S(2)}, u32[]{:S(2)}) collective-permute-start(f32[8,512]{1,0:T(8,128)S(1)} %get-tuple-element.181.refs_0_), channel_id=1, source_target_pairs={{0,4},{4,0},{8,12},{12,8},{16,20},{20,16},{24,28},{28,24},{1,5},{5... | collective-permute-start | bytes 49160 | tf_op jit(solution)/shard_map/ppermute | solution.py:626
  107.4 5.0 %collective-permute-start.39 = (bf16[4,96,512]{2,1,0:T(8,128)(2,1)S(1)}, bf16[4,96,512]{2,1,0:T(8,128)(2,1)S(1)}, u32[]{:S(2)}, u32[]{:S(2)}) collective-permute-start(bf16[4,96,512]{2,1,0:T(8,128)(2,1)S(1)} %join_mix.1.refs_2_), channel_id=1, source_target_pairs={{0,4},{4,0},{8,12},{12,8},{16,20},{20,16},{24,28},{28,24},{1,5},{5... | collective-permute-start | bytes 1179656 | tf_op jit(solution)/shard_map/ppermute | solution.py:626
  (20 other events, 87.5 us)

commit v7 on v6

--- a/solution.py
+++ b/solution.py
@@ -18,10 +18,10 @@
 
 
 weight = {
-    "pick_piece": 4, "mixer_in": 32, "join_depth": 32, "join_one": 4, "mlp_one": 0, "join_two": 0, "mlp_two": 8, "mid_back": 8,
-    "add_core": 32, "mixer_back": 0, "mixer_out": 0, "add_core_small": 0, "add_cross": 16, "mixed_out": 0, "tokens_out": 2,
-    "add_cross_small": 16, "add_depth": 0, "add_near_small": 8, "add_far": 16, "add_far_small": 0, "add_last": 4,
-    "add_last_small": 4, "join_mlp": 2, "join_mix": 16, "spread_mlp": 8, "spread_mix": 0, "add_pair": 8, "mid_in": 8,
+    "pick_piece": 16, "mixer_in": 0, "join_depth": 0, "join_one": 4, "mlp_one": 4, "join_two": 2, "mlp_two": 8, "mid_back": 8,
+    "add_core": 0, "mixer_back": 0, "mixer_out": 0, "add_core_small": 0, "add_cross": 4, "mixed_out": 0, "tokens_out": 8,
+    "add_cross_small": 8, "add_depth": 0, "add_near_small": 32, "add_far": 16, "add_far_small": 0, "add_last": 4,
+    "add_last_small": 4, "join_mlp": 32, "join_mix": 16, "spread_mlp": 8, "spread_mix": 32, "add_pair": 32, "mid_in": 8,
     "mlp_own": 4,
 }
 

time: 114 us -> 113 us (level)
  starting transfers between devices: 54.4 us -> 51.4 us
  waiting for transfers between devices: 25.3 us -> 27.1 us
    ppermute x40, starting transfers between devices: 49.3 us -> 47.5 us  [swap(): return lax.ppermute(value, axis, [(i, i ^ bit) for i in range(size)])]
    ppermute x40, waiting for transfers between devices: 23.9 us -> 25.4 us  [swap(): return lax.ppermute(value, axis, [(i, i ^ bit) for i in range(size)])]
    ppermute x4, starting transfers between devices: 5.09 us -> 3.92 us  [across(): lax.ppermute(value, 'dp', [(i, i ^ 2 << (i & 1 ^ turn)) for i in range(si...]
  transfers between devices with their start and end apart: 44 -> 44, of which waited for: 17 -> 18; matrix products, arithmetic and copies ran while one was open for 0% -> 0% of each run, Pallas kernels for 26% -> 26%
where the time goes in v7:
time: 113 us; the launch traced here: 112 us
  starting transfers between devices  51.4 us (45%)
  Pallas kernels  32.9 us (29%)
  waiting for transfers between devices  27.1 us (24%)
    ppermute x40, starting transfers between devices, swap(): return lax.ppermute(value, axis, [(i, i ^ bit) for i in range(size)])  47.5 us
    pallas_call x29, Pallas kernels, call(): pl.pallas_call(run, out_shape=outs, in_specs=[HBM] * hbm + [VMEM] * (n -...  32.9 us
    ppermute x40, waiting for transfers between devices, swap(): return lax.ppermute(value, axis, [(i, i ^ bit) for i in range(size)])  25.4 us
    ppermute x4, starting transfers between devices, across(): lax.ppermute(value, 'dp', [(i, i ^ 2 << (i & 1 ^ turn)) for i in range(si...  3.92 us
  transfers between devices with their start and end apart: 44, of which 18 were waited for; matrix products, arithmetic and copies ran while one was open for 0% of the time, Pallas kernels for 26%

profile of v7, /device:TPU:1, one launch (start us, length us, event | category | flops | bytes accessed | tf_op | source)
XLA Modules:
  0.0 112.3 jit_solution(17198487930298747574)
XLA Ops:
  1.6 2.2 %collective-permute-start.9 = (bf16[128,512]{1,0:T(8,128)(2,1)S(1)}, bf16[128,512]{1,0:T(8,128)(2,1)S(1)}, u32[]{:S(2)}, u32[]{:S(2)}) collective-permute-start(bf16[128,512]{1,0:T(8,128)(2,1)S(1)} %pick_piece.1.refs_7_), channel_id=1, source_target_pairs={{0,1},{1,0},{2,3},{3,2},{4,5},{5,4},{6,7},{7,6},{8,9},{9,8},{10,11... | collective-permute-start | bytes 393224 | tf_op jit(solution)/shard_map/ppermute | solution.py:626
  3.7 2.2 %collective-permute-start.1 = (bf16[128,512]{1,0:T(8,128)(2,1)S(1)}, bf16[128,512]{1,0:T(8,128)(2,1)S(1)}, u32[]{:S(2)}, u32[]{:S(2)}) collective-permute-start(bf16[128,512]{1,0:T(8,128)(2,1)S(1)} %pick_piece.1.refs_7_), channel_id=1, source_target_pairs={{0,3},{1,2},{2,1},{3,0},{4,7},{5,6},{6,5},{7,4},{8,11},{9,10},{10,... | collective-permute-start | bytes 393224 | tf_op jit(solution)/shard_map/ppermute | solution.py:626
  6.1 6.5 %mixer_in.1 = (f32[512,1024]{1,0:T(8,128)S(1)}, f32[512,1024]{1,0:T(8,128)S(1)}, f32[512,1024]{1,0:T(8,128)S(1)}, f32[512,1024]{1,0:T(8,128)S(1)}, f32[512,1024]...) custom-call(s32[1,3]{1,0:T(1,128)} %refs_0_.4, ...), custom_call_target="tpu_custom_call" | custom-call | tf_op jit(solution)/shard_map/mixer_in/pallas_call | solution.py:55
  12.6 1.3 %collective-permute-start.10 = (bf16[128,512]{1,0:T(8,128)(2,1)S(1)}, bf16[128,512]{1,0:T(8,128)(2,1)S(1)}, u32[]{:S(2)}, u32[]{:S(2)}) collective-permute-start(bf16[128,512]{1,0:T(8,128)(2,1)S(1)} %gate.3.refs_0_), channel_id=1, source_target_pairs={{0,8},{4,20},{8,0},{12,28},{16,24},{20,4},{24,16},{28,12},{1,9},{5... | collective-permute-start | bytes 393224 | tf_op jit(solution)/shard_map/ppermute | solution.py:631
  13.9 2.4 %collective-permute-start.5 = (f32[4,1024]{1,0:T(4,128)S(1)}, f32[4,1024]{1,0:T(4,128)S(1)}, u32[]{:S(2)}, u32[]{:S(2)}) collective-permute-start(f32[4,1024]{1,0:T(4,128)S(1)} %get-tuple-element.102.refs_2_.refs_0_.refs_1_), channel_id=1, source_target_pairs={{0,3},{1,2},{2,1},{3,0},{4,7},{5,6},{6,5},{7,4},{8,11},{9,10},{10,... | collective-permute-start | bytes 49160 | tf_op jit(solution)/shard_map/ppermute | solution.py:626
  17.7 1.5 %collective-permute-start.2 = (bf16[256,512]{1,0:T(8,128)(2,1)S(1)}, bf16[256,512]{1,0:T(8,128)(2,1)S(1)}, u32[]{:S(2)}, u32[]{:S(2)}) collective-permute-start(bf16[256,512]{1,0:T(8,128)(2,1)S(1)} %join_depth.1.refs_0_.refs_2_), channel_id=1, source_target_pairs={{0,8},{4,20},{8,0},{12,28},{16,24},{20,4},{24,16},{28,12},{1,9},{5... | collective-permute-start | bytes 786440 | tf_op jit(solution)/shard_map/ppermute | solution.py:631
  21.1 2.0 %mid_in.1 = (f32[520,1024]{1,0:T(8,128)S(1)}, bf16[1024,512]{1,0:T(8,128)(2,1)S(1)}, f32[512,512]{1,0:T(8,128)S(1)}, bf16[512,512]{1,0:T(8,128)(2,1)S(1)}, bf16[...) custom-call(f32[4,1024]{1,0:T(4,128)S(1)} %get-tuple-element.102.refs_2_.refs_0_.refs_1_, ...), custom_call_target="tpu_custom_call" | custom-call | flops 8589934592 | bytes 33554432 | tf_op jit(solution)/shard_map/mid_in/pallas_call | solution.py:55
  23.2 3.6 %collective-permute-start.12 = (bf16[2,128,512]{2,1,0:T(8,128)(2,1)S(1)}, bf16[2,128,512]{2,1,0:T(8,128)(2,1)S(1)}, u32[]{:S(2)}, u32[]{:S(2)}) collective-permute-start(bf16[2,128,512]{2,1,0:T(8,128)(2,1)S(1)} %join_one.1.refs_0_), channel_id=1, source_target_pairs={{0,4},{4,0},{8,12},{12,8},{16,20},{20,16},{24,28},{28,24},{1,5},{5... | collective-permute-start | bytes 786440 | tf_op jit(solution)/shard_map/ppermute | solution.py:626
  27.1 1.6 %collective-permute-done.11.refs_0_ = bf16[2,128,512]{2,1,0:T(8,128)(2,1)S(1)} collective-permute-done((bf16[2,128,512]{2,1,0:T(8,128)(2,1)S(1)}, bf16[2,128,512]{2,1,0:T(8,128)(2,1)S(1)}, u32[]{:S(2)}, u32[]{:S(2)}) %collective-permute-start.11) | collective-permute-done | bytes 262176 | tf_op jit(solution)/shard_map/ppermute | solution.py:631
  29.8 2.1 %mlp_own.1 = (f32[512,512]{1,0:T(8,128)S(1)}, f32[512,512]{1,0:T(8,128)S(1)}, bf16[4,128,512]{2,1,0:T(8,128)(2,1)S(1)}, bf16[4,128,512]{2,1,0:T(8,128)(2,1)S(1)}, f32[16,512]{1,0:T(8,128)S(1)}) custom-call(bf16[512,512]{1,0:T(8,128)(2,1)S(1)} %copy-done.5, bf16[512,512]{1,0:T(8,128)(2,1)S(1)} %copy-done.6, f32[1,512]{1,0:T(1,128)S(1)} %bitcast.23, ...), custom_call_target="tpu_custom_call" | custom-call | flops 4294967296 | bytes 16777216 | tf_op jit(solution)/shard_map/mlp_own/pallas_call | solution.py:55
  31.9 2.2 %mlp_one.1 = (f32[512,512]{1,0:T(8,128)S(1)}, f32[512,512]{1,0:T(8,128)S(1)}, bf16[4,128,512]{2,1,0:T(8,128)(2,1)S(1)}, bf16[4,128,512]{2,1,0:T(8,128)(2,1)S(1)}, f32[16,512]{1,0:T(8,128)S(1)}) custom-call(bf16[2,128,512]{2,1,0:T(8,128)(2,1)S(1)} %join_one.1.refs_0_, bf16[2,128,512]{2,1,0:T(8,128)(2,1)S(1)} %gate.4.refs_1_, ...), custom_call_target="tpu_custom_call" | custom-call | flops 4294967296 | bytes 16777216 | tf_op jit(solution)/shard_map/mlp_one/pallas_call | solution.py:55
  35.2 3.2 %collective-permute-start.8 = (bf16[2,256,512]{2,1,0:T(8,128)(2,1)S(1)}, bf16[2,256,512]{2,1,0:T(8,128)(2,1)S(1)}, u32[]{:S(2)}, u32[]{:S(2)}) collective-permute-start(bf16[2,256,512]{2,1,0:T(8,128)(2,1)S(1)} %collective-permute-done.6.refs_1_), channel_id=1, source_target_pairs={{0,4},{4,0},{8,12},{12,8},{16,20},{20,16},{24,28},{28,24},{1,5},{5... | collective-permute-start | bytes 1572872 | tf_op jit(solution)/shard_map/ppermute | solution.py:626
  39.9 4.0 %mlp_two.1 = (f32[512,512]{1,0:T(8,128)S(1)}, f32[512,512]{1,0:T(8,128)S(1)}, bf16[4,256,512]{2,1,0:T(8,128)(2,1)S(1)}, bf16[4,256,512]{2,1,0:T(8,128)(2,1)S(1)}, f32[16,512]{1,0:T(8,128)S(1)}) custom-call(bf16[2,256,512]{2,1,0:T(8,128)(2,1)S(1)} %join_two.1.refs_7_.refs_0_, bf16[2,256,512]{2,1,0:T(8,128)(2,1)S(1)} %collective-permute-done.6.refs_1_, ...), custom_call_target="tpu_custom_call" | custom-call | flops 8589934592 | bytes 33554432 | tf_op jit(solution)/shard_map/mlp_two/pallas_call | solution.py:55
  44.3 2.2 %mid_back.1 = (bf16[4,128,512]{2,1,0:T(8,128)(2,1)S(1)}, bf16[4,128,512]{2,1,0:T(8,128)(2,1)S(1)}, f32[512,512]{1,0:T(8,128)S(1)}, f32[512,1024]{1,0:T(8,128)S(1...) custom-call(f32[512,512]{1,0:T(8,128)S(1)} %get-tuple-element.122.refs_0_, ...), custom_call_target="tpu_custom_call" | custom-call | flops 8589934592 | bytes 33554432 | tf_op jit(solution)/shard_map/mid_back/pallas_call | solution.py:55
  46.7 1.3 %collective-permute-start.18 = (f32[2,1024]{1,0:T(2,128)S(1)}, f32[2,1024]{1,0:T(2,128)S(1)}, u32[]{:S(2)}, u32[]{:S(2)}) collective-permute-start(f32[2,1024]{1,0:T(2,128)S(1)} %gate.5.refs_0_), channel_id=1, source_target_pairs={{0,3},{1,2},{2,1},{3,0},{4,7},{5,6},{6,5},{7,4},{8,11},{9,10},{10,... | collective-permute-start | bytes 24584 | tf_op jit(solution)/shard_map/ppermute | solution.py:626
  48.1 2.2 %collective-permute-start.16 = (f32[2,1024]{1,0:T(2,128)S(1)}, f32[2,1024]{1,0:T(2,128)S(1)}, u32[]{:S(2)}, u32[]{:S(2)}) collective-permute-start(f32[2,1024]{1,0:T(2,128)S(1)} %gate.5.refs_0_), channel_id=1, source_target_pairs={{0,1},{1,0},{2,3},{3,2},{4,5},{5,4},{6,7},{7,6},{8,9},{9,8},{10,11... | collective-permute-start | bytes 24584 | tf_op jit(solution)/shard_map/ppermute | solution.py:626
  50.3 1.9 %collective-permute-done.20.refs_2_ = bf16[4,128,512]{2,1,0:T(8,128)(2,1)S(1)} collective-permute-done((bf16[4,128,512]{2,1,0:T(8,128)(2,1)S(1)}, bf16[4,128,512]{2,1,0:T(8,128)(2,1)S(1)}, u32[]{:S(2)}, u32[]{:S(2)}) %collective-permute-start.20) | collective-permute-done | bytes 524320 | tf_op jit(solution)/shard_map/ppermute | solution.py:626
  52.8 1.7 %mixer_back.1 = (f32[512,1024]{1,0:T(8,128)S(1)}, bf16[4,4,96,512]{3,2,1,0:T(8,128)(2,1)S(1)}, bf16[3,512,512]{2,1,0:T(8,128)(2,1)S(1)}, f32[16,512]{1,0:T(8,128)S(1)}) custom-call(f32[2,1024]{1,0:T(2,128)S(1)} %gate.5.refs_0_, f32[2,1024]{1,0:T(2,128)S(1)} %collective-permute-done.16.refs_1_, f32[2,1024]{1,0:T(2,128)S(1)} %collective-permute-done.17.refs_2_, ...), custom_call_target="tpu_custom_call" | custom-call | tf_op jit(solution)/shard_map/mixer_back/pallas_call | solution.py:55
  57.6 2.8 %mixer_out.1 = (bf16[4,4,96,512]{3,2,1,0:T(8,128)(2,1)S(1)}, f32[512,512]{1,0:T(8,128)S(1)}, f32[16,512]{1,0:T(8,128)S(1)}) custom-call(f32[512,1024]{1,0:T(8,128)S(1)} %get-tuple-element.140.refs_0_, f32[512,1024]{1,0:T(8,128)S(1)} %get-tuple-element.106.refs_7_.refs_1_, f32[512,1024]{1,0:T(8,128)S(1)} %get-tuple-element.107.refs_8_.refs_2_, ...), custom_call_target="tpu_custom_call" | custom-call | tf_op jit(solution)/shard_map/mixer_out/pallas_call | solution.py:55
  62.0 7.2 %collective-permute-done.24.refs_1_ = bf16[2,256,512]{2,1,0:T(8,128)(2,1)S(1)} collective-permute-done((bf16[2,256,512]{2,1,0:T(8,128)(2,1)S(1)}, bf16[2,256,512]{2,1,0:T(8,128)(2,1)S(1)}, u32[]{:S(2)}, u32[]{:S(2)}) %collective-permute-start.24) | collective-permute-done | bytes 524320 | tf_op jit(solution)/shard_map/ppermute | solution.py:626
  71.4 2.2 %tokens_out.1 = (bf16[512,512]{1,0:T(8,128)(2,1)}, f32[8,128]{1,0:T(8,128)S(1)}) custom-call(f32[512,512]{1,0:T(8,128)S(1)} %get-tuple-element.150.refs_0_, f32[512,512]{1,0:T(8,128)S(1)} %get-tuple-element.108.refs_9_.refs_12_.refs_1_, f32[1,512]{1,0:T(1,128)S(1)} %bitcast.25, f32[512,512]{1,0:T(8,128)S(1)} %get-tuple-element.151.refs_3_, ...), custom_call_target="tpu_custom_call" | custom-call | flops 8589934592 | bytes 33554432 | tf_op jit(solution)/shard_map/tokens_out/pallas_call | solution.py:55
  73.6 1.5 %mixed_out.1 = (bf16[512,512]{1,0:T(8,128)(2,1)}, f32[8,128]{1,0:T(8,128)S(1)}) custom-call(f32[512,512]{1,0:T(8,128)S(1)} %get-tuple-element.121.refs_0_, f32[4,192,512]{2,1,0:T(8,128)S(1)} %get-tuple-element.148.refs_1_.refs_4_.refs_0_), custom_call_target="tpu_custom_call" | custom-call | tf_op jit(solution)/shard_map/mixed_out/pallas_call | solution.py:55
  75.1 1.4 %collective-permute-done.26.refs_1_ = bf16[256,512]{1,0:T(8,128)(2,1)S(1)} collective-permute-done((bf16[256,512]{1,0:T(8,128)(2,1)S(1)}, bf16[256,512]{1,0:T(8,128)(2,1)S(1)}, u32[]{:S(2)}, u32[]{:S(2)}) %collective-permute-start.26) | collective-permute-done | bytes 262176 | tf_op jit(solution)/shard_map/ppermute | solution.py:626
  78.6 1.4 %collective-permute-done.23.refs_1_ = bf16[800,512]{1,0:T(8,128)(2,1)S(1)} collective-permute-done((bf16[800,512]{1,0:T(8,128)(2,1)S(1)}, bf16[800,512]{1,0:T(8,128)(2,1)S(1)}, u32[]{:S(2)}, u32[]{:S(2)}) %collective-permute-start.23) | collective-permute-done | bytes 819232 | tf_op jit(solution)/shard_map/ppermute | solution.py:626
  81.4 2.0 %collective-permute-done.30.refs_1_ = bf16[192,512]{1,0:T(8,128)(2,1)S(1)} collective-permute-done((bf16[192,512]{1,0:T(8,128)(2,1)S(1)}, bf16[192,512]{1,0:T(8,128)(2,1)S(1)}, u32[]{:S(2)}, u32[]{:S(2)}) %collective-permute-start.30) | collective-permute-done | bytes 196640 | tf_op jit(solution)/shard_map/ppermute | solution.py:626
  85.6 1.5 %collective-permute-start.31 = (bf16[128,512]{1,0:T(8,128)(2,1)S(1)}, bf16[128,512]{1,0:T(8,128)(2,1)S(1)}, u32[]{:S(2)}, u32[]{:S(2)}) collective-permute-start(bf16[128,512]{1,0:T(8,128)(2,1)S(1)} %get-tuple-element.173), channel_id=1, source_target_pairs={{0,16},{4,20},{8,24},{12,28},{16,0},{20,4},{24,8},{28,12},{1,17},{... | collective-permute-start | bytes 393224 | tf_op jit(solution)/shard_map/ppermute | solution.py:626
  87.2 3.7 %collective-permute-done.32.refs_3_ = bf16[96,512]{1,0:T(8,128)(2,1)S(1)} collective-permute-done((bf16[96,512]{1,0:T(8,128)(2,1)S(1)}, bf16[96,512]{1,0:T(8,128)(2,1)S(1)}, u32[]{:S(2)}, u32[]{:S(2)}) %collective-permute-start.32) | collective-permute-done | bytes 98336 | tf_op jit(solution)/shard_map/ppermute | solution.py:626
  93.8 1.9 %collective-permute-start.40 = (bf16[160,512]{1,0:T(8,128)(2,1)S(1)}, bf16[160,512]{1,0:T(8,128)(2,1)S(1)}, u32[]{:S(2)}, u32[]{:S(2)}) collective-permute-start(bf16[160,512]{1,0:T(8,128)(2,1)S(1)} %add_last.1.refs_3_.refs_0_), channel_id=1, source_target_pairs={{0,8},{4,12},{8,0},{12,4},{16,24},{20,28},{24,16},{28,20},{1,9},{5... | collective-permute-start | bytes 491528 | tf_op jit(solution)/shard_map/ppermute | solution.py:626
  98.2 1.3 %collective-permute-start.36 = (bf16[96,512]{1,0:T(8,128)(2,1)S(1)}, bf16[96,512]{1,0:T(8,128)(2,1)S(1)}, u32[]{:S(2)}, u32[]{:S(2)}) collective-permute-start(bf16[96,512]{1,0:T(8,128)(2,1)S(1)} %get-tuple-element.182.refs_0_.refs_4_), channel_id=1, source_target_pairs={{0,8},{4,12},{8,0},{12,4},{16,24},{20,28},{24,16},{28,20},{1,9},{5... | collective-permute-start | bytes 294920 | tf_op jit(solution)/shard_map/ppermute | solution.py:626
  100.0 6.3 %collective-permute-start.35 = (f32[8,512]{1,0:T(8,128)S(1)}, f32[8,512]{1,0:T(8,128)S(1)}, u32[]{:S(2)}, u32[]{:S(2)}) collective-permute-start(f32[8,512]{1,0:T(8,128)S(1)} %get-tuple-element.181.refs_0_), channel_id=1, source_target_pairs={{0,4},{4,0},{8,12},{12,8},{16,20},{20,16},{24,28},{28,24},{1,5},{5... | collective-permute-start | bytes 49160 | tf_op jit(solution)/shard_map/ppermute | solution.py:626
  106.5 2.9 %collective-permute-start.39 = (bf16[4,96,512]{2,1,0:T(8,128)(2,1)S(1)}, bf16[4,96,512]{2,1,0:T(8,128)(2,1)S(1)}, u32[]{:S(2)}, u32[]{:S(2)}) collective-permute-start(bf16[4,96,512]{2,1,0:T(8,128)(2,1)S(1)} %join_mix.1.refs_2_), channel_id=1, source_target_pairs={{0,4},{4,0},{8,12},{12,8},{16,20},{20,16},{24,28},{28,24},{1,5},{5... | collective-permute-start | bytes 1179656 | tf_op jit(solution)/shard_map/ppermute | solution.py:626
  109.4 1.7 %spread_mlp.1 = (f32[512,512]{1,0:T(8,128)}, f32[512,512]{1,0:T(8,128)}, f32[256,512]{1,0:T(8,128)}, f32[8,128]{1,0:T(8,128)S(1)}) custom-call(bf16[4,160,512]{2,1,0:T(8,128)(2,1)S(1)} %join_mlp.1.refs_0_, bf16[4,160,512]{2,1,0:T(8,128)(2,1)S(1)} %collective-permute-done.43.refs_1_), custom_call_target="tpu_custom_call" | custom-call | flops 8589934592 | bytes 33554432 | tf_op jit(solution)/shard_map/spread_mlp/pallas_call | solution.py:55
  (104 shorter events, 29.6 us)
Async XLA Ops:
  1.6 11.0 %collective-permute-start.9 = (bf16[128,512]{1,0:T(8,128)(2,1)S(1)}, bf16[128,512]{1,0:T(8,128)(2,1)S(1)}, u32[]{:S(2)}, u32[]{:S(2)}) collective-permute-start(bf16[128,512]{1,0:T(8,128)(2,1)S(1)} %pick_piece.1.refs_7_), channel_id=1, source_target_pairs={{0,1},{1,0},{2,3},{3,2},{4,5},{5,4},{6,7},{7,6},{8,9},{9,8},{10,11... | collective-permute-start | bytes 393224 | tf_op jit(solution)/shard_map/ppermute | solution.py:626
  3.7 12.6 %collective-permute-start.1 = (bf16[128,512]{1,0:T(8,128)(2,1)S(1)}, bf16[128,512]{1,0:T(8,128)(2,1)S(1)}, u32[]{:S(2)}, u32[]{:S(2)}) collective-permute-start(bf16[128,512]{1,0:T(8,128)(2,1)S(1)} %pick_piece.1.refs_7_), channel_id=1, source_target_pairs={{0,3},{1,2},{2,1},{3,0},{4,7},{5,6},{6,5},{7,4},{8,11},{9,10},{10,... | collective-permute-start | bytes 393224 | tf_op jit(solution)/shard_map/ppermute | solution.py:626
  5.9 11.7 %collective-permute-start = (bf16[128,512]{1,0:T(8,128)(2,1)S(1)}, bf16[128,512]{1,0:T(8,128)(2,1)S(1)}, u32[]{:S(2)}, u32[]{:S(2)}) collective-permute-start(bf16[128,512]{1,0:T(8,128)(2,1)S(1)} %pick_piece.1.refs_7_), channel_id=1, source_target_pairs={{0,2},{1,3},{2,0},{3,1},{4,6},{5,7},{6,4},{7,5},{8,10},{9,11},{10,... | collective-permute-start | bytes 393224 | tf_op jit(solution)/shard_map/ppermute | solution.py:626
  12.6 7.7 %collective-permute-start.10 = (bf16[128,512]{1,0:T(8,128)(2,1)S(1)}, bf16[128,512]{1,0:T(8,128)(2,1)S(1)}, u32[]{:S(2)}, u32[]{:S(2)}) collective-permute-start(bf16[128,512]{1,0:T(8,128)(2,1)S(1)} %gate.3.refs_0_), channel_id=1, source_target_pairs={{0,8},{4,20},{8,0},{12,28},{16,24},{20,4},{24,16},{28,12},{1,9},{5... | collective-permute-start | bytes 393224 | tf_op jit(solution)/shard_map/ppermute | solution.py:631
  13.9 5.3 %collective-permute-start.5 = (f32[4,1024]{1,0:T(4,128)S(1)}, f32[4,1024]{1,0:T(4,128)S(1)}, u32[]{:S(2)}, u32[]{:S(2)}) collective-permute-start(f32[4,1024]{1,0:T(4,128)S(1)} %get-tuple-element.102.refs_2_.refs_0_.refs_1_), channel_id=1, source_target_pairs={{0,3},{1,2},{2,1},{3,0},{4,7},{5,6},{6,5},{7,4},{8,11},{9,10},{10,... | collective-permute-start | bytes 49160 | tf_op jit(solution)/shard_map/ppermute | solution.py:626
  17.7 9.0 %collective-permute-start.2 = (bf16[256,512]{1,0:T(8,128)(2,1)S(1)}, bf16[256,512]{1,0:T(8,128)(2,1)S(1)}, u32[]{:S(2)}, u32[]{:S(2)}) collective-permute-start(bf16[256,512]{1,0:T(8,128)(2,1)S(1)} %join_depth.1.refs_0_.refs_2_), channel_id=1, source_target_pairs={{0,8},{4,20},{8,0},{12,28},{16,24},{20,4},{24,16},{28,12},{1,9},{5... | collective-permute-start | bytes 786440 | tf_op jit(solution)/shard_map/ppermute | solution.py:631
  20.3 8.4 %collective-permute-start.11 = (bf16[2,128,512]{2,1,0:T(8,128)(2,1)S(1)}, bf16[2,128,512]{2,1,0:T(8,128)(2,1)S(1)}, u32[]{:S(2)}, u32[]{:S(2)}) collective-permute-start(bf16[2,128,512]{2,1,0:T(8,128)(2,1)S(1)} %join_one.1.refs_0_), channel_id=1, source_target_pairs={{0,16},{4,12},{8,24},{12,4},{16,0},{20,28},{24,8},{28,20},{1,17},{... | collective-permute-start | bytes 786440 | tf_op jit(solution)/shard_map/ppermute | solution.py:631
  23.2 8.7 %collective-permute-start.12 = (bf16[2,128,512]{2,1,0:T(8,128)(2,1)S(1)}, bf16[2,128,512]{2,1,0:T(8,128)(2,1)S(1)}, u32[]{:S(2)}, u32[]{:S(2)}) collective-permute-start(bf16[2,128,512]{2,1,0:T(8,128)(2,1)S(1)} %join_one.1.refs_0_), channel_id=1, source_target_pairs={{0,4},{4,0},{8,12},{12,8},{16,20},{20,16},{24,28},{28,24},{1,5},{5... | collective-permute-start | bytes 786440 | tf_op jit(solution)/shard_map/ppermute | solution.py:626
  26.8 8.4 %collective-permute-start.6 = (bf16[2,256,512]{2,1,0:T(8,128)(2,1)S(1)}, bf16[2,256,512]{2,1,0:T(8,128)(2,1)S(1)}, u32[]{:S(2)}, u32[]{:S(2)}) collective-permute-start(bf16[2,256,512]{2,1,0:T(8,128)(2,1)S(1)} %join_two.1.refs_7_.refs_0_), channel_id=1, source_target_pairs={{0,16},{4,12},{8,24},{12,4},{16,0},{20,28},{24,8},{28,20},{1,17},{... | collective-permute-start | bytes 1572872 | tf_op jit(solution)/shard_map/ppermute | solution.py:631
  34.7 13.4 %collective-permute-start.19 = (bf16[4,128,512]{2,1,0:T(8,128)(2,1)S(1)}, bf16[4,128,512]{2,1,0:T(8,128)(2,1)S(1)}, u32[]{:S(2)}, u32[]{:S(2)}) collective-permute-start(bf16[4,128,512]{2,1,0:T(8,128)(2,1)S(1)} %get-tuple-element.135), channel_id=1, source_target_pairs={{0,4},{4,0},{8,12},{12,8},{16,20},{20,16},{24,28},{28,24},{1,5},{5... | collective-permute-start | bytes 1572872 | tf_op jit(solution)/shard_map/ppermute | solution.py:626
  38.5 13.7 %collective-permute-start.20 = (bf16[4,128,512]{2,1,0:T(8,128)(2,1)S(1)}, bf16[4,128,512]{2,1,0:T(8,128)(2,1)S(1)}, u32[]{:S(2)}, u32[]{:S(2)}) collective-permute-start(bf16[4,128,512]{2,1,0:T(8,128)(2,1)S(1)} %add_pair.1.refs_12_), channel_id=1, source_target_pairs={{0,1},{1,0},{2,3},{3,2},{4,5},{5,4},{6,7},{7,6},{8,9},{9,8},{10,11... | collective-permute-start | bytes 1572872 | tf_op jit(solution)/shard_map/ppermute | solution.py:626
  46.5 5.7 %collective-permute-start.21 = (bf16[4,128,512]{2,1,0:T(8,128)(2,1)S(1)}, bf16[4,128,512]{2,1,0:T(8,128)(2,1)S(1)}, u32[]{:S(2)}, u32[]{:S(2)}) collective-permute-start(bf16[4,128,512]{2,1,0:T(8,128)(2,1)S(1)} %get-tuple-element.138), channel_id=1, source_target_pairs={{0,4},{4,0},{8,12},{12,8},{16,20},{20,16},{24,28},{28,24},{1,5},{5... | collective-permute-start | bytes 1572872 | tf_op jit(solution)/shard_map/ppermute | solution.py:626
  46.7 6.0 %collective-permute-start.18 = (f32[2,1024]{1,0:T(2,128)S(1)}, f32[2,1024]{1,0:T(2,128)S(1)}, u32[]{:S(2)}, u32[]{:S(2)}) collective-permute-start(f32[2,1024]{1,0:T(2,128)S(1)} %gate.5.refs_0_), channel_id=1, source_target_pairs={{0,3},{1,2},{2,1},{3,0},{4,7},{5,6},{6,5},{7,4},{8,11},{9,10},{10,... | collective-permute-start | bytes 24584 | tf_op jit(solution)/shard_map/ppermute | solution.py:626
  54.4 6.0 %collective-permute-start.22 = (bf16[4,4,96,512]{3,2,1,0:T(8,128)(2,1)S(1)}, bf16[4,4,96,512]{3,2,1,0:T(8,128)(2,1)S(1)}, u32[]{:S(2)}, u32[]{:S(2)}) collective-permute-start(bf16[4,4,96,512]{3,2,1,0:T(8,128)(2,1)S(1)} %get-tuple-element.146), channel_id=1, source_target_pairs={{0,4},{4,0},{8,12},{12,8},{16,20},{20,16},{24,28},{28,24},{1,5},{5... | collective-permute-start | bytes 4718600 | tf_op jit(solution)/shard_map/ppermute | solution.py:626
  55.7 13.5 %collective-permute-start.24 = (bf16[2,256,512]{2,1,0:T(8,128)(2,1)S(1)}, bf16[2,256,512]{2,1,0:T(8,128)(2,1)S(1)}, u32[]{:S(2)}, u32[]{:S(2)}) collective-permute-start(bf16[2,256,512]{2,1,0:T(8,128)(2,1)S(1)} %get-tuple-element.155), channel_id=1, source_target_pairs={{0,8},{4,12},{8,0},{12,4},{16,24},{20,28},{24,16},{28,20},{1,9},{5... | collective-permute-start | bytes 1572872 | tf_op jit(solution)/shard_map/ppermute | solution.py:626
  56.4 13.2 %collective-permute-start.25 = (bf16[2,256,512]{2,1,0:T(8,128)(2,1)S(1)}, bf16[2,256,512]{2,1,0:T(8,128)(2,1)S(1)}, u32[]{:S(2)}, u32[]{:S(2)}) collective-permute-start(bf16[2,256,512]{2,1,0:T(8,128)(2,1)S(1)} %get-tuple-element.157), channel_id=1, source_target_pairs={{0,16},{4,20},{8,24},{12,28},{16,0},{20,4},{24,8},{28,12},{1,17},{... | collective-permute-start | bytes 1572872 | tf_op jit(solution)/shard_map/ppermute | solution.py:626
  60.8 19.2 %collective-permute-start.23 = (bf16[800,512]{1,0:T(8,128)(2,1)S(1)}, bf16[800,512]{1,0:T(8,128)(2,1)S(1)}, u32[]{:S(2)}, u32[]{:S(2)}) collective-permute-start(bf16[800,512]{1,0:T(8,128)(2,1)S(1)} %get-tuple-element.153), channel_id=1, source_target_pairs={{0,1},{1,0},{2,3},{3,2},{4,5},{5,4},{6,7},{7,6},{8,9},{9,8},{10,11... | collective-permute-start | bytes 2457608 | tf_op jit(solution)/shard_map/ppermute | solution.py:626
  69.8 6.7 %collective-permute-start.26 = (bf16[256,512]{1,0:T(8,128)(2,1)S(1)}, bf16[256,512]{1,0:T(8,128)(2,1)S(1)}, u32[]{:S(2)}, u32[]{:S(2)}) collective-permute-start(bf16[256,512]{1,0:T(8,128)(2,1)S(1)} %get-tuple-element.159), channel_id=1, source_target_pairs={{0,16},{4,20},{8,24},{12,28},{16,0},{20,4},{24,8},{28,12},{1,17},{... | collective-permute-start | bytes 786440 | tf_op jit(solution)/shard_map/ppermute | solution.py:626
  71.0 6.3 %collective-permute-start.27 = (bf16[256,512]{1,0:T(8,128)(2,1)S(1)}, bf16[256,512]{1,0:T(8,128)(2,1)S(1)}, u32[]{:S(2)}, u32[]{:S(2)}) collective-permute-start(bf16[256,512]{1,0:T(8,128)(2,1)S(1)} %get-tuple-element.161), channel_id=1, source_target_pairs={{0,8},{4,12},{8,0},{12,4},{16,24},{20,28},{24,16},{28,20},{1,9},{5... | collective-permute-start | bytes 786440 | tf_op jit(solution)/shard_map/ppermute | solution.py:626
  77.5 5.9 %collective-permute-start.30 = (bf16[192,512]{1,0:T(8,128)(2,1)S(1)}, bf16[192,512]{1,0:T(8,128)(2,1)S(1)}, u32[]{:S(2)}, u32[]{:S(2)}) collective-permute-start(bf16[192,512]{1,0:T(8,128)(2,1)S(1)} %get-tuple-element.170), channel_id=1, source_target_pairs={{0,1},{1,0},{2,3},{3,2},{4,5},{5,4},{6,7},{7,6},{8,9},{9,8},{10,11... | collective-permute-start | bytes 589832 | tf_op jit(solution)/shard_map/ppermute | solution.py:626
  80.3 4.9 %collective-permute-start.29 = (bf16[192,512]{1,0:T(8,128)(2,1)S(1)}, bf16[192,512]{1,0:T(8,128)(2,1)S(1)}, u32[]{:S(2)}, u32[]{:S(2)}) collective-permute-start(bf16[192,512]{1,0:T(8,128)(2,1)S(1)} %get-tuple-element.168), channel_id=1, source_target_pairs={{0,16},{4,20},{8,24},{12,28},{16,0},{20,4},{24,8},{28,12},{1,17},{... | collective-permute-start | bytes 589832 | tf_op jit(solution)/shard_map/ppermute | solution.py:626
  80.6 4.9 %collective-permute-start.28 = (bf16[224,512]{1,0:T(8,128)(2,1)S(1)}, bf16[224,512]{1,0:T(8,128)(2,1)S(1)}, u32[]{:S(2)}, u32[]{:S(2)}) collective-permute-start(bf16[224,512]{1,0:T(8,128)(2,1)S(1)} %get-tuple-element.166), channel_id=1, source_target_pairs={{0,8},{4,12},{8,0},{12,4},{16,24},{20,28},{24,16},{28,20},{1,9},{5... | collective-permute-start | bytes 688136 | tf_op jit(solution)/shard_map/ppermute | solution.py:626
  83.4 9.5 %collective-permute-start.34 = (bf16[160,512]{1,0:T(8,128)(2,1)S(1)}, bf16[160,512]{1,0:T(8,128)(2,1)S(1)}, u32[]{:S(2)}, u32[]{:S(2)}) collective-permute-start(bf16[160,512]{1,0:T(8,128)(2,1)S(1)} %get-tuple-element.180), channel_id=1, source_target_pairs={{0,2},{1,3},{2,0},{3,1},{4,6},{5,7},{6,4},{7,5},{8,10},{9,11},{10,... | collective-permute-start | bytes 491528 | tf_op jit(solution)/shard_map/ppermute | solution.py:626
  85.6 5.3 %collective-permute-start.31 = (bf16[128,512]{1,0:T(8,128)(2,1)S(1)}, bf16[128,512]{1,0:T(8,128)(2,1)S(1)}, u32[]{:S(2)}, u32[]{:S(2)}) collective-permute-start(bf16[128,512]{1,0:T(8,128)(2,1)S(1)} %get-tuple-element.173), channel_id=1, source_target_pairs={{0,16},{4,20},{8,24},{12,28},{16,0},{20,4},{24,8},{28,12},{1,17},{... | collective-permute-start | bytes 393224 | tf_op jit(solution)/shard_map/ppermute | solution.py:626
  90.9 5.8 %collective-permute-start.33 = (bf16[112,512]{1,0:T(8,128)(2,1)S(1)}, bf16[112,512]{1,0:T(8,128)(2,1)S(1)}, u32[]{:S(2)}, u32[]{:S(2)}) collective-permute-start(bf16[112,512]{1,0:T(8,128)(2,1)S(1)} %get-tuple-element.179), channel_id=1, source_target_pairs={{0,2},{1,3},{2,0},{3,1},{4,6},{5,7},{6,4},{7,5},{8,10},{9,11},{10,... | collective-permute-start | bytes 344072 | tf_op jit(solution)/shard_map/ppermute | solution.py:626
  93.0 5.2 %collective-permute-start.42 = (bf16[160,512]{1,0:T(8,128)(2,1)S(1)}, bf16[160,512]{1,0:T(8,128)(2,1)S(1)}, u32[]{:S(2)}, u32[]{:S(2)}) collective-permute-start(bf16[160,512]{1,0:T(8,128)(2,1)S(1)} %add_last.1.refs_3_.refs_0_), channel_id=1, source_target_pairs={{0,24},{4,28},{8,16},{12,20},{16,8},{20,12},{24,0},{28,4},{1,25},{... | collective-permute-start | bytes 491528 | tf_op jit(solution)/shard_map/ppermute | solution.py:626
  93.8 6.2 %collective-permute-start.41 = (bf16[160,512]{1,0:T(8,128)(2,1)S(1)}, bf16[160,512]{1,0:T(8,128)(2,1)S(1)}, u32[]{:S(2)}, u32[]{:S(2)}) collective-permute-start(bf16[160,512]{1,0:T(8,128)(2,1)S(1)} %add_last.1.refs_3_.refs_0_), channel_id=1, source_target_pairs={{0,16},{4,20},{8,24},{12,28},{16,0},{20,4},{24,8},{28,12},{1,17},{... | collective-permute-start | bytes 491528 | tf_op jit(solution)/shard_map/ppermute | solution.py:626
  93.8 12.5 %collective-permute-start.40 = (bf16[160,512]{1,0:T(8,128)(2,1)S(1)}, bf16[160,512]{1,0:T(8,128)(2,1)S(1)}, u32[]{:S(2)}, u32[]{:S(2)}) collective-permute-start(bf16[160,512]{1,0:T(8,128)(2,1)S(1)} %add_last.1.refs_3_.refs_0_), channel_id=1, source_target_pairs={{0,8},{4,12},{8,0},{12,4},{16,24},{20,28},{24,16},{28,20},{1,9},{5... | collective-permute-start | bytes 491528 | tf_op jit(solution)/shard_map/ppermute | solution.py:626
  96.8 9.7 %collective-permute-start.38 = (bf16[96,512]{1,0:T(8,128)(2,1)S(1)}, bf16[96,512]{1,0:T(8,128)(2,1)S(1)}, u32[]{:S(2)}, u32[]{:S(2)}) collective-permute-start(bf16[96,512]{1,0:T(8,128)(2,1)S(1)} %get-tuple-element.182.refs_0_.refs_4_), channel_id=1, source_target_pairs={{0,24},{4,28},{8,16},{12,20},{16,8},{20,12},{24,0},{28,4},{1,25},{... | collective-permute-start | bytes 294920 | tf_op jit(solution)/shard_map/ppermute | solution.py:626
  97.6 8.9 %collective-permute-start.37 = (bf16[96,512]{1,0:T(8,128)(2,1)S(1)}, bf16[96,512]{1,0:T(8,128)(2,1)S(1)}, u32[]{:S(2)}, u32[]{:S(2)}) collective-permute-start(bf16[96,512]{1,0:T(8,128)(2,1)S(1)} %get-tuple-element.182.refs_0_.refs_4_), channel_id=1, source_target_pairs={{0,16},{4,20},{8,24},{12,28},{16,0},{20,4},{24,8},{28,12},{1,17},{... | collective-permute-start | bytes 294920 | tf_op jit(solution)/shard_map/ppermute | solution.py:626
  98.2 8.3 %collective-permute-start.36 = (bf16[96,512]{1,0:T(8,128)(2,1)S(1)}, bf16[96,512]{1,0:T(8,128)(2,1)S(1)}, u32[]{:S(2)}, u32[]{:S(2)}) collective-permute-start(bf16[96,512]{1,0:T(8,128)(2,1)S(1)} %get-tuple-element.182.refs_0_.refs_4_), channel_id=1, source_target_pairs={{0,8},{4,12},{8,0},{12,4},{16,24},{20,28},{24,16},{28,20},{1,9},{5... | collective-permute-start | bytes 294920 | tf_op jit(solution)/shard_map/ppermute | solution.py:626
  100.0 11.0 %collective-permute-start.35 = (f32[8,512]{1,0:T(8,128)S(1)}, f32[8,512]{1,0:T(8,128)S(1)}, u32[]{:S(2)}, u32[]{:S(2)}) collective-permute-start(f32[8,512]{1,0:T(8,128)S(1)} %get-tuple-element.181.refs_0_), channel_id=1, source_target_pairs={{0,4},{4,0},{8,12},{12,8},{16,20},{20,16},{24,28},{28,24},{1,5},{5... | collective-permute-start | bytes 49160 | tf_op jit(solution)/shard_map/ppermute | solution.py:626
  (20 other events, 73.8 us)

commit v8 on v7

--- a/solution.py
+++ b/solution.py
@@ -435,6 +435,10 @@
             out[k * rows : (k + 1) * rows, :] = ref[...]
 
 
+def stacked(*parts):
+    return jnp.concatenate([v.astype(f32) for v in parts], axis=0).astype(bf16)
+
+
 def two_terms(v):
     high = v.astype(bf16)
     return high, (v - high.astype(f32)).astype(bf16)
@@ -521,20 +525,22 @@
     for k in range(2):
         base = 8 * rows + 16 * k
         high, low = two_terms(slots[z ^ (2 * k + 1)])
-        send[base : base + 16, :] = jnp.concatenate([high, low], axis=0)
+        send[base : base + 16, :] = stacked(high, low)
         tiny[8 * k : 8 * k + 8, :] = slots[z ^ (2 * k)]
 
 
 def add_near_small(idx, own, got, tiny, send_x, send_y, own_x, own_y, tiny_out):
     x, y = idx[1] % 2, idx[1] // 2
     rows = own.shape[1] // 2
+    terms = []
     for k in range(2):
         base = 8 * rows + 16 * k
         other = got[base : base + 16, :].astype(f32)
-        high, low = two_terms(tiny[8 * k : 8 * k + 8, :] + (other[0:8] + other[8:16]))
-        for ref, top in ((tiny_out, 0), (send_x, 2 * rows)):
-            ref[top + 8 * k : top + 8 * k + 8, :] = high
-            ref[top + 16 + 8 * k : top + 24 + 8 * k, :] = low
+        terms.append(two_terms(tiny[8 * k : 8 * k + 8, :] + (other[0:8] + other[8:16])))
+    for i in range(2):
+        both = stacked(terms[0][i], terms[1][i])
+        tiny_out[16 * i : 16 * i + 16, :] = both
+        send_x[2 * rows + 16 * i : 2 * rows + 16 * i + 16, :] = both
 
     def total(p, slot):
         at = pl.ds(pl.multiple_of(p * 2 * rows + slot * rows, 16), rows)
@@ -580,7 +586,7 @@
     tiny_out[...] = total[0:8]
     send[0:rows, :] = (own_y[...] + got_y[...].astype(f32)).astype(bf16)
     high, low = two_terms(total[8:16])
-    send[rows:, :] = jnp.concatenate([high, low], axis=0)
+    send[rows:, :] = stacked(high, low)
 
 
 def add_last_small(own, tiny, got, out, tiny_out):

time: 113 us -> 113 us (level)
  no operation moved by 1% of the time
where the time goes in v8:
time: 113 us; the launch traced here: 112 us
  starting transfers between devices  51.4 us (45%)
  Pallas kernels  32.9 us (29%)
  waiting for transfers between devices  27.1 us (24%)
    ppermute x40, starting transfers between devices, swap(): return lax.ppermute(value, axis, [(i, i ^ bit) for i in range(size)])  47.5 us
    pallas_call x29, Pallas kernels, call(): pl.pallas_call(run, out_shape=outs, in_specs=[HBM] * hbm + [VMEM] * (n -...  32.9 us
    ppermute x40, waiting for transfers between devices, swap(): return lax.ppermute(value, axis, [(i, i ^ bit) for i in range(size)])  25.4 us
    ppermute x4, starting transfers between devices, across(): lax.ppermute(value, 'dp', [(i, i ^ 2 << (i & 1 ^ turn)) for i in range(si...  3.92 us
  transfers between devices with their start and end apart: 44, of which 18 were waited for; matrix products, arithmetic and copies ran while one was open for 0% of the time, Pallas kernels for 26%

profile of v8, /device:TPU:1, one launch (start us, length us, event | category | flops | bytes accessed | tf_op | source)
XLA Modules:
  0.0 112.3 jit_solution(2222964723635214432)
XLA Ops:
  1.6 2.2 %collective-permute-start.9 = (bf16[128,512]{1,0:T(8,128)(2,1)S(1)}, bf16[128,512]{1,0:T(8,128)(2,1)S(1)}, u32[]{:S(2)}, u32[]{:S(2)}) collective-permute-start(bf16[128,512]{1,0:T(8,128)(2,1)S(1)} %pick_piece.1.refs_7_), channel_id=1, source_target_pairs={{0,1},{1,0},{2,3},{3,2},{4,5},{5,4},{6,7},{7,6},{8,9},{9,8},{10,11... | collective-permute-start | bytes 393224 | tf_op jit(solution)/shard_map/ppermute | solution.py:632
  3.7 2.2 %collective-permute-start.1 = (bf16[128,512]{1,0:T(8,128)(2,1)S(1)}, bf16[128,512]{1,0:T(8,128)(2,1)S(1)}, u32[]{:S(2)}, u32[]{:S(2)}) collective-permute-start(bf16[128,512]{1,0:T(8,128)(2,1)S(1)} %pick_piece.1.refs_7_), channel_id=1, source_target_pairs={{0,3},{1,2},{2,1},{3,0},{4,7},{5,6},{6,5},{7,4},{8,11},{9,10},{10,... | collective-permute-start | bytes 393224 | tf_op jit(solution)/shard_map/ppermute | solution.py:632
  6.1 6.5 %mixer_in.1 = (f32[512,1024]{1,0:T(8,128)S(1)}, f32[512,1024]{1,0:T(8,128)S(1)}, f32[512,1024]{1,0:T(8,128)S(1)}, f32[512,1024]{1,0:T(8,128)S(1)}, f32[512,1024]...) custom-call(s32[1,3]{1,0:T(1,128)} %refs_0_.4, ...), custom_call_target="tpu_custom_call" | custom-call | tf_op jit(solution)/shard_map/mixer_in/pallas_call | solution.py:55
  12.6 1.3 %collective-permute-start.10 = (bf16[128,512]{1,0:T(8,128)(2,1)S(1)}, bf16[128,512]{1,0:T(8,128)(2,1)S(1)}, u32[]{:S(2)}, u32[]{:S(2)}) collective-permute-start(bf16[128,512]{1,0:T(8,128)(2,1)S(1)} %gate.3.refs_0_), channel_id=1, source_target_pairs={{0,8},{4,20},{8,0},{12,28},{16,24},{20,4},{24,16},{28,12},{1,9},{5... | collective-permute-start | bytes 393224 | tf_op jit(solution)/shard_map/ppermute | solution.py:637
  13.9 2.4 %collective-permute-start.5 = (f32[4,1024]{1,0:T(4,128)S(1)}, f32[4,1024]{1,0:T(4,128)S(1)}, u32[]{:S(2)}, u32[]{:S(2)}) collective-permute-start(f32[4,1024]{1,0:T(4,128)S(1)} %get-tuple-element.102.refs_2_.refs_0_.refs_1_), channel_id=1, source_target_pairs={{0,3},{1,2},{2,1},{3,0},{4,7},{5,6},{6,5},{7,4},{8,11},{9,10},{10,... | collective-permute-start | bytes 49160 | tf_op jit(solution)/shard_map/ppermute | solution.py:632
  17.7 1.5 %collective-permute-start.2 = (bf16[256,512]{1,0:T(8,128)(2,1)S(1)}, bf16[256,512]{1,0:T(8,128)(2,1)S(1)}, u32[]{:S(2)}, u32[]{:S(2)}) collective-permute-start(bf16[256,512]{1,0:T(8,128)(2,1)S(1)} %join_depth.1.refs_0_.refs_2_), channel_id=1, source_target_pairs={{0,8},{4,20},{8,0},{12,28},{16,24},{20,4},{24,16},{28,12},{1,9},{5... | collective-permute-start | bytes 786440 | tf_op jit(solution)/shard_map/ppermute | solution.py:637
  21.1 2.0 %mid_in.1 = (f32[520,1024]{1,0:T(8,128)S(1)}, bf16[1024,512]{1,0:T(8,128)(2,1)S(1)}, f32[512,512]{1,0:T(8,128)S(1)}, bf16[512,512]{1,0:T(8,128)(2,1)S(1)}, bf16[...) custom-call(f32[4,1024]{1,0:T(4,128)S(1)} %get-tuple-element.102.refs_2_.refs_0_.refs_1_, ...), custom_call_target="tpu_custom_call" | custom-call | flops 8589934592 | bytes 33554432 | tf_op jit(solution)/shard_map/mid_in/pallas_call | solution.py:55
  23.2 3.6 %collective-permute-start.12 = (bf16[2,128,512]{2,1,0:T(8,128)(2,1)S(1)}, bf16[2,128,512]{2,1,0:T(8,128)(2,1)S(1)}, u32[]{:S(2)}, u32[]{:S(2)}) collective-permute-start(bf16[2,128,512]{2,1,0:T(8,128)(2,1)S(1)} %join_one.1.refs_0_), channel_id=1, source_target_pairs={{0,4},{4,0},{8,12},{12,8},{16,20},{20,16},{24,28},{28,24},{1,5},{5... | collective-permute-start | bytes 786440 | tf_op jit(solution)/shard_map/ppermute | solution.py:632
  27.1 1.6 %collective-permute-done.11.refs_0_ = bf16[2,128,512]{2,1,0:T(8,128)(2,1)S(1)} collective-permute-done((bf16[2,128,512]{2,1,0:T(8,128)(2,1)S(1)}, bf16[2,128,512]{2,1,0:T(8,128)(2,1)S(1)}, u32[]{:S(2)}, u32[]{:S(2)}) %collective-permute-start.11) | collective-permute-done | bytes 262176 | tf_op jit(solution)/shard_map/ppermute | solution.py:637
  29.8 2.1 %mlp_own.1 = (f32[512,512]{1,0:T(8,128)S(1)}, f32[512,512]{1,0:T(8,128)S(1)}, bf16[4,128,512]{2,1,0:T(8,128)(2,1)S(1)}, bf16[4,128,512]{2,1,0:T(8,128)(2,1)S(1)}, f32[16,512]{1,0:T(8,128)S(1)}) custom-call(bf16[512,512]{1,0:T(8,128)(2,1)S(1)} %copy-done.5, bf16[512,512]{1,0:T(8,128)(2,1)S(1)} %copy-done.6, f32[1,512]{1,0:T(1,128)S(1)} %bitcast.23, ...), custom_call_target="tpu_custom_call" | custom-call | flops 4294967296 | bytes 16777216 | tf_op jit(solution)/shard_map/mlp_own/pallas_call | solution.py:55
  31.9 2.2 %mlp_one.1 = (f32[512,512]{1,0:T(8,128)S(1)}, f32[512,512]{1,0:T(8,128)S(1)}, bf16[4,128,512]{2,1,0:T(8,128)(2,1)S(1)}, bf16[4,128,512]{2,1,0:T(8,128)(2,1)S(1)}, f32[16,512]{1,0:T(8,128)S(1)}) custom-call(bf16[2,128,512]{2,1,0:T(8,128)(2,1)S(1)} %join_one.1.refs_0_, bf16[2,128,512]{2,1,0:T(8,128)(2,1)S(1)} %gate.4.refs_1_, ...), custom_call_target="tpu_custom_call" | custom-call | flops 4294967296 | bytes 16777216 | tf_op jit(solution)/shard_map/mlp_one/pallas_call | solution.py:55
  35.2 3.2 %collective-permute-start.8 = (bf16[2,256,512]{2,1,0:T(8,128)(2,1)S(1)}, bf16[2,256,512]{2,1,0:T(8,128)(2,1)S(1)}, u32[]{:S(2)}, u32[]{:S(2)}) collective-permute-start(bf16[2,256,512]{2,1,0:T(8,128)(2,1)S(1)} %collective-permute-done.6.refs_1_), channel_id=1, source_target_pairs={{0,4},{4,0},{8,12},{12,8},{16,20},{20,16},{24,28},{28,24},{1,5},{5... | collective-permute-start | bytes 1572872 | tf_op jit(solution)/shard_map/ppermute | solution.py:632
  39.9 4.0 %mlp_two.1 = (f32[512,512]{1,0:T(8,128)S(1)}, f32[512,512]{1,0:T(8,128)S(1)}, bf16[4,256,512]{2,1,0:T(8,128)(2,1)S(1)}, bf16[4,256,512]{2,1,0:T(8,128)(2,1)S(1)}, f32[16,512]{1,0:T(8,128)S(1)}) custom-call(bf16[2,256,512]{2,1,0:T(8,128)(2,1)S(1)} %join_two.1.refs_7_.refs_0_, bf16[2,256,512]{2,1,0:T(8,128)(2,1)S(1)} %collective-permute-done.6.refs_1_, ...), custom_call_target="tpu_custom_call" | custom-call | flops 8589934592 | bytes 33554432 | tf_op jit(solution)/shard_map/mlp_two/pallas_call | solution.py:55
  44.3 2.2 %mid_back.1 = (bf16[4,128,512]{2,1,0:T(8,128)(2,1)S(1)}, bf16[4,128,512]{2,1,0:T(8,128)(2,1)S(1)}, f32[512,512]{1,0:T(8,128)S(1)}, f32[512,1024]{1,0:T(8,128)S(1...) custom-call(f32[512,512]{1,0:T(8,128)S(1)} %get-tuple-element.122.refs_0_, ...), custom_call_target="tpu_custom_call" | custom-call | flops 8589934592 | bytes 33554432 | tf_op jit(solution)/shard_map/mid_back/pallas_call | solution.py:55
  46.7 1.3 %collective-permute-start.18 = (f32[2,1024]{1,0:T(2,128)S(1)}, f32[2,1024]{1,0:T(2,128)S(1)}, u32[]{:S(2)}, u32[]{:S(2)}) collective-permute-start(f32[2,1024]{1,0:T(2,128)S(1)} %gate.5.refs_0_), channel_id=1, source_target_pairs={{0,3},{1,2},{2,1},{3,0},{4,7},{5,6},{6,5},{7,4},{8,11},{9,10},{10,... | collective-permute-start | bytes 24584 | tf_op jit(solution)/shard_map/ppermute | solution.py:632
  48.1 2.2 %collective-permute-start.16 = (f32[2,1024]{1,0:T(2,128)S(1)}, f32[2,1024]{1,0:T(2,128)S(1)}, u32[]{:S(2)}, u32[]{:S(2)}) collective-permute-start(f32[2,1024]{1,0:T(2,128)S(1)} %gate.5.refs_0_), channel_id=1, source_target_pairs={{0,1},{1,0},{2,3},{3,2},{4,5},{5,4},{6,7},{7,6},{8,9},{9,8},{10,11... | collective-permute-start | bytes 24584 | tf_op jit(solution)/shard_map/ppermute | solution.py:632
  50.3 1.9 %collective-permute-done.20.refs_2_ = bf16[4,128,512]{2,1,0:T(8,128)(2,1)S(1)} collective-permute-done((bf16[4,128,512]{2,1,0:T(8,128)(2,1)S(1)}, bf16[4,128,512]{2,1,0:T(8,128)(2,1)S(1)}, u32[]{:S(2)}, u32[]{:S(2)}) %collective-permute-start.20) | collective-permute-done | bytes 524320 | tf_op jit(solution)/shard_map/ppermute | solution.py:632
  52.8 1.7 %mixer_back.1 = (f32[512,1024]{1,0:T(8,128)S(1)}, bf16[4,4,96,512]{3,2,1,0:T(8,128)(2,1)S(1)}, bf16[3,512,512]{2,1,0:T(8,128)(2,1)S(1)}, f32[16,512]{1,0:T(8,128)S(1)}) custom-call(f32[2,1024]{1,0:T(2,128)S(1)} %gate.5.refs_0_, f32[2,1024]{1,0:T(2,128)S(1)} %collective-permute-done.16.refs_1_, f32[2,1024]{1,0:T(2,128)S(1)} %collective-permute-done.17.refs_2_, ...), custom_call_target="tpu_custom_call" | custom-call | tf_op jit(solution)/shard_map/mixer_back/pallas_call | solution.py:55
  57.6 2.8 %mixer_out.1 = (bf16[4,4,96,512]{3,2,1,0:T(8,128)(2,1)S(1)}, f32[512,512]{1,0:T(8,128)S(1)}, f32[16,512]{1,0:T(8,128)S(1)}) custom-call(f32[512,1024]{1,0:T(8,128)S(1)} %get-tuple-element.140.refs_0_, f32[512,1024]{1,0:T(8,128)S(1)} %get-tuple-element.106.refs_7_.refs_1_, f32[512,1024]{1,0:T(8,128)S(1)} %get-tuple-element.107.refs_8_.refs_2_, ...), custom_call_target="tpu_custom_call" | custom-call | tf_op jit(solution)/shard_map/mixer_out/pallas_call | solution.py:55
  62.0 7.2 %collective-permute-done.24.refs_1_ = bf16[2,256,512]{2,1,0:T(8,128)(2,1)S(1)} collective-permute-done((bf16[2,256,512]{2,1,0:T(8,128)(2,1)S(1)}, bf16[2,256,512]{2,1,0:T(8,128)(2,1)S(1)}, u32[]{:S(2)}, u32[]{:S(2)}) %collective-permute-start.24) | collective-permute-done | bytes 524320 | tf_op jit(solution)/shard_map/ppermute | solution.py:632
  71.4 2.2 %tokens_out.1 = (bf16[512,512]{1,0:T(8,128)(2,1)}, f32[8,128]{1,0:T(8,128)S(1)}) custom-call(f32[512,512]{1,0:T(8,128)S(1)} %get-tuple-element.150.refs_0_, f32[512,512]{1,0:T(8,128)S(1)} %get-tuple-element.108.refs_9_.refs_12_.refs_1_, f32[1,512]{1,0:T(1,128)S(1)} %bitcast.25, f32[512,512]{1,0:T(8,128)S(1)} %get-tuple-element.151.refs_3_, ...), custom_call_target="tpu_custom_call" | custom-call | flops 8589934592 | bytes 33554432 | tf_op jit(solution)/shard_map/tokens_out/pallas_call | solution.py:55
  73.6 1.5 %mixed_out.1 = (bf16[512,512]{1,0:T(8,128)(2,1)}, f32[8,128]{1,0:T(8,128)S(1)}) custom-call(f32[512,512]{1,0:T(8,128)S(1)} %get-tuple-element.121.refs_0_, f32[4,192,512]{2,1,0:T(8,128)S(1)} %get-tuple-element.148.refs_1_.refs_4_.refs_0_), custom_call_target="tpu_custom_call" | custom-call | tf_op jit(solution)/shard_map/mixed_out/pallas_call | solution.py:55
  75.1 1.4 %collective-permute-done.26.refs_1_ = bf16[256,512]{1,0:T(8,128)(2,1)S(1)} collective-permute-done((bf16[256,512]{1,0:T(8,128)(2,1)S(1)}, bf16[256,512]{1,0:T(8,128)(2,1)S(1)}, u32[]{:S(2)}, u32[]{:S(2)}) %collective-permute-start.26) | collective-permute-done | bytes 262176 | tf_op jit(solution)/shard_map/ppermute | solution.py:632
  78.6 1.4 %collective-permute-done.23.refs_1_ = bf16[800,512]{1,0:T(8,128)(2,1)S(1)} collective-permute-done((bf16[800,512]{1,0:T(8,128)(2,1)S(1)}, bf16[800,512]{1,0:T(8,128)(2,1)S(1)}, u32[]{:S(2)}, u32[]{:S(2)}) %collective-permute-start.23) | collective-permute-done | bytes 819232 | tf_op jit(solution)/shard_map/ppermute | solution.py:632
  81.4 2.0 %collective-permute-done.30.refs_1_ = bf16[192,512]{1,0:T(8,128)(2,1)S(1)} collective-permute-done((bf16[192,512]{1,0:T(8,128)(2,1)S(1)}, bf16[192,512]{1,0:T(8,128)(2,1)S(1)}, u32[]{:S(2)}, u32[]{:S(2)}) %collective-permute-start.30) | collective-permute-done | bytes 196640 | tf_op jit(solution)/shard_map/ppermute | solution.py:632
  85.6 1.5 %collective-permute-start.31 = (bf16[128,512]{1,0:T(8,128)(2,1)S(1)}, bf16[128,512]{1,0:T(8,128)(2,1)S(1)}, u32[]{:S(2)}, u32[]{:S(2)}) collective-permute-start(bf16[128,512]{1,0:T(8,128)(2,1)S(1)} %get-tuple-element.173), channel_id=1, source_target_pairs={{0,16},{4,20},{8,24},{12,28},{16,0},{20,4},{24,8},{28,12},{1,17},{... | collective-permute-start | bytes 393224 | tf_op jit(solution)/shard_map/ppermute | solution.py:632
  87.2 3.7 %collective-permute-done.32.refs_3_ = bf16[96,512]{1,0:T(8,128)(2,1)S(1)} collective-permute-done((bf16[96,512]{1,0:T(8,128)(2,1)S(1)}, bf16[96,512]{1,0:T(8,128)(2,1)S(1)}, u32[]{:S(2)}, u32[]{:S(2)}) %collective-permute-start.32) | collective-permute-done | bytes 98336 | tf_op jit(solution)/shard_map/ppermute | solution.py:632
  93.8 1.9 %collective-permute-start.40 = (bf16[160,512]{1,0:T(8,128)(2,1)S(1)}, bf16[160,512]{1,0:T(8,128)(2,1)S(1)}, u32[]{:S(2)}, u32[]{:S(2)}) collective-permute-start(bf16[160,512]{1,0:T(8,128)(2,1)S(1)} %add_last.1.refs_3_.refs_0_), channel_id=1, source_target_pairs={{0,8},{4,12},{8,0},{12,4},{16,24},{20,28},{24,16},{28,20},{1,9},{5... | collective-permute-start | bytes 491528 | tf_op jit(solution)/shard_map/ppermute | solution.py:632
  98.2 1.3 %collective-permute-start.36 = (bf16[96,512]{1,0:T(8,128)(2,1)S(1)}, bf16[96,512]{1,0:T(8,128)(2,1)S(1)}, u32[]{:S(2)}, u32[]{:S(2)}) collective-permute-start(bf16[96,512]{1,0:T(8,128)(2,1)S(1)} %get-tuple-element.182.refs_0_.refs_4_), channel_id=1, source_target_pairs={{0,8},{4,12},{8,0},{12,4},{16,24},{20,28},{24,16},{28,20},{1,9},{5... | collective-permute-start | bytes 294920 | tf_op jit(solution)/shard_map/ppermute | solution.py:632
  100.0 6.3 %collective-permute-start.35 = (f32[8,512]{1,0:T(8,128)S(1)}, f32[8,512]{1,0:T(8,128)S(1)}, u32[]{:S(2)}, u32[]{:S(2)}) collective-permute-start(f32[8,512]{1,0:T(8,128)S(1)} %get-tuple-element.181.refs_0_), channel_id=1, source_target_pairs={{0,4},{4,0},{8,12},{12,8},{16,20},{20,16},{24,28},{28,24},{1,5},{5... | collective-permute-start | bytes 49160 | tf_op jit(solution)/shard_map/ppermute | solution.py:632
  106.5 2.9 %collective-permute-start.39 = (bf16[4,96,512]{2,1,0:T(8,128)(2,1)S(1)}, bf16[4,96,512]{2,1,0:T(8,128)(2,1)S(1)}, u32[]{:S(2)}, u32[]{:S(2)}) collective-permute-start(bf16[4,96,512]{2,1,0:T(8,128)(2,1)S(1)} %join_mix.1.refs_2_), channel_id=1, source_target_pairs={{0,4},{4,0},{8,12},{12,8},{16,20},{20,16},{24,28},{28,24},{1,5},{5... | collective-permute-start | bytes 1179656 | tf_op jit(solution)/shard_map/ppermute | solution.py:632
  109.4 1.7 %spread_mlp.1 = (f32[512,512]{1,0:T(8,128)}, f32[512,512]{1,0:T(8,128)}, f32[256,512]{1,0:T(8,128)}, f32[8,128]{1,0:T(8,128)S(1)}) custom-call(bf16[4,160,512]{2,1,0:T(8,128)(2,1)S(1)} %join_mlp.1.refs_0_, bf16[4,160,512]{2,1,0:T(8,128)(2,1)S(1)} %collective-permute-done.43.refs_1_), custom_call_target="tpu_custom_call" | custom-call | flops 8589934592 | bytes 33554432 | tf_op jit(solution)/shard_map/spread_mlp/pallas_call | solution.py:55
  (104 shorter events, 29.6 us)
Async XLA Ops:
  1.6 11.0 %collective-permute-start.9 = (bf16[128,512]{1,0:T(8,128)(2,1)S(1)}, bf16[128,512]{1,0:T(8,128)(2,1)S(1)}, u32[]{:S(2)}, u32[]{:S(2)}) collective-permute-start(bf16[128,512]{1,0:T(8,128)(2,1)S(1)} %pick_piece.1.refs_7_), channel_id=1, source_target_pairs={{0,1},{1,0},{2,3},{3,2},{4,5},{5,4},{6,7},{7,6},{8,9},{9,8},{10,11... | collective-permute-start | bytes 393224 | tf_op jit(solution)/shard_map/ppermute | solution.py:632
  3.7 12.6 %collective-permute-start.1 = (bf16[128,512]{1,0:T(8,128)(2,1)S(1)}, bf16[128,512]{1,0:T(8,128)(2,1)S(1)}, u32[]{:S(2)}, u32[]{:S(2)}) collective-permute-start(bf16[128,512]{1,0:T(8,128)(2,1)S(1)} %pick_piece.1.refs_7_), channel_id=1, source_target_pairs={{0,3},{1,2},{2,1},{3,0},{4,7},{5,6},{6,5},{7,4},{8,11},{9,10},{10,... | collective-permute-start | bytes 393224 | tf_op jit(solution)/shard_map/ppermute | solution.py:632
  5.9 11.7 %collective-permute-start = (bf16[128,512]{1,0:T(8,128)(2,1)S(1)}, bf16[128,512]{1,0:T(8,128)(2,1)S(1)}, u32[]{:S(2)}, u32[]{:S(2)}) collective-permute-start(bf16[128,512]{1,0:T(8,128)(2,1)S(1)} %pick_piece.1.refs_7_), channel_id=1, source_target_pairs={{0,2},{1,3},{2,0},{3,1},{4,6},{5,7},{6,4},{7,5},{8,10},{9,11},{10,... | collective-permute-start | bytes 393224 | tf_op jit(solution)/shard_map/ppermute | solution.py:632
  12.6 7.7 %collective-permute-start.10 = (bf16[128,512]{1,0:T(8,128)(2,1)S(1)}, bf16[128,512]{1,0:T(8,128)(2,1)S(1)}, u32[]{:S(2)}, u32[]{:S(2)}) collective-permute-start(bf16[128,512]{1,0:T(8,128)(2,1)S(1)} %gate.3.refs_0_), channel_id=1, source_target_pairs={{0,8},{4,20},{8,0},{12,28},{16,24},{20,4},{24,16},{28,12},{1,9},{5... | collective-permute-start | bytes 393224 | tf_op jit(solution)/shard_map/ppermute | solution.py:637
  13.9 5.3 %collective-permute-start.5 = (f32[4,1024]{1,0:T(4,128)S(1)}, f32[4,1024]{1,0:T(4,128)S(1)}, u32[]{:S(2)}, u32[]{:S(2)}) collective-permute-start(f32[4,1024]{1,0:T(4,128)S(1)} %get-tuple-element.102.refs_2_.refs_0_.refs_1_), channel_id=1, source_target_pairs={{0,3},{1,2},{2,1},{3,0},{4,7},{5,6},{6,5},{7,4},{8,11},{9,10},{10,... | collective-permute-start | bytes 49160 | tf_op jit(solution)/shard_map/ppermute | solution.py:632
  17.7 9.0 %collective-permute-start.2 = (bf16[256,512]{1,0:T(8,128)(2,1)S(1)}, bf16[256,512]{1,0:T(8,128)(2,1)S(1)}, u32[]{:S(2)}, u32[]{:S(2)}) collective-permute-start(bf16[256,512]{1,0:T(8,128)(2,1)S(1)} %join_depth.1.refs_0_.refs_2_), channel_id=1, source_target_pairs={{0,8},{4,20},{8,0},{12,28},{16,24},{20,4},{24,16},{28,12},{1,9},{5... | collective-permute-start | bytes 786440 | tf_op jit(solution)/shard_map/ppermute | solution.py:637
  20.3 8.4 %collective-permute-start.11 = (bf16[2,128,512]{2,1,0:T(8,128)(2,1)S(1)}, bf16[2,128,512]{2,1,0:T(8,128)(2,1)S(1)}, u32[]{:S(2)}, u32[]{:S(2)}) collective-permute-start(bf16[2,128,512]{2,1,0:T(8,128)(2,1)S(1)} %join_one.1.refs_0_), channel_id=1, source_target_pairs={{0,16},{4,12},{8,24},{12,4},{16,0},{20,28},{24,8},{28,20},{1,17},{... | collective-permute-start | bytes 786440 | tf_op jit(solution)/shard_map/ppermute | solution.py:637
  23.2 8.7 %collective-permute-start.12 = (bf16[2,128,512]{2,1,0:T(8,128)(2,1)S(1)}, bf16[2,128,512]{2,1,0:T(8,128)(2,1)S(1)}, u32[]{:S(2)}, u32[]{:S(2)}) collective-permute-start(bf16[2,128,512]{2,1,0:T(8,128)(2,1)S(1)} %join_one.1.refs_0_), channel_id=1, source_target_pairs={{0,4},{4,0},{8,12},{12,8},{16,20},{20,16},{24,28},{28,24},{1,5},{5... | collective-permute-start | bytes 786440 | tf_op jit(solution)/shard_map/ppermute | solution.py:632
  26.8 8.4 %collective-permute-start.6 = (bf16[2,256,512]{2,1,0:T(8,128)(2,1)S(1)}, bf16[2,256,512]{2,1,0:T(8,128)(2,1)S(1)}, u32[]{:S(2)}, u32[]{:S(2)}) collective-permute-start(bf16[2,256,512]{2,1,0:T(8,128)(2,1)S(1)} %join_two.1.refs_7_.refs_0_), channel_id=1, source_target_pairs={{0,16},{4,12},{8,24},{12,4},{16,0},{20,28},{24,8},{28,20},{1,17},{... | collective-permute-start | bytes 1572872 | tf_op jit(solution)/shard_map/ppermute | solution.py:637
  34.7 13.4 %collective-permute-start.19 = (bf16[4,128,512]{2,1,0:T(8,128)(2,1)S(1)}, bf16[4,128,512]{2,1,0:T(8,128)(2,1)S(1)}, u32[]{:S(2)}, u32[]{:S(2)}) collective-permute-start(bf16[4,128,512]{2,1,0:T(8,128)(2,1)S(1)} %get-tuple-element.135), channel_id=1, source_target_pairs={{0,4},{4,0},{8,12},{12,8},{16,20},{20,16},{24,28},{28,24},{1,5},{5... | collective-permute-start | bytes 1572872 | tf_op jit(solution)/shard_map/ppermute | solution.py:632
  38.5 13.7 %collective-permute-start.20 = (bf16[4,128,512]{2,1,0:T(8,128)(2,1)S(1)}, bf16[4,128,512]{2,1,0:T(8,128)(2,1)S(1)}, u32[]{:S(2)}, u32[]{:S(2)}) collective-permute-start(bf16[4,128,512]{2,1,0:T(8,128)(2,1)S(1)} %add_pair.1.refs_12_), channel_id=1, source_target_pairs={{0,1},{1,0},{2,3},{3,2},{4,5},{5,4},{6,7},{7,6},{8,9},{9,8},{10,11... | collective-permute-start | bytes 1572872 | tf_op jit(solution)/shard_map/ppermute | solution.py:632
  46.5 5.7 %collective-permute-start.21 = (bf16[4,128,512]{2,1,0:T(8,128)(2,1)S(1)}, bf16[4,128,512]{2,1,0:T(8,128)(2,1)S(1)}, u32[]{:S(2)}, u32[]{:S(2)}) collective-permute-start(bf16[4,128,512]{2,1,0:T(8,128)(2,1)S(1)} %get-tuple-element.138), channel_id=1, source_target_pairs={{0,4},{4,0},{8,12},{12,8},{16,20},{20,16},{24,28},{28,24},{1,5},{5... | collective-permute-start | bytes 1572872 | tf_op jit(solution)/shard_map/ppermute | solution.py:632
  46.7 6.0 %collective-permute-start.18 = (f32[2,1024]{1,0:T(2,128)S(1)}, f32[2,1024]{1,0:T(2,128)S(1)}, u32[]{:S(2)}, u32[]{:S(2)}) collective-permute-start(f32[2,1024]{1,0:T(2,128)S(1)} %gate.5.refs_0_), channel_id=1, source_target_pairs={{0,3},{1,2},{2,1},{3,0},{4,7},{5,6},{6,5},{7,4},{8,11},{9,10},{10,... | collective-permute-start | bytes 24584 | tf_op jit(solution)/shard_map/ppermute | solution.py:632
  54.4 6.0 %collective-permute-start.22 = (bf16[4,4,96,512]{3,2,1,0:T(8,128)(2,1)S(1)}, bf16[4,4,96,512]{3,2,1,0:T(8,128)(2,1)S(1)}, u32[]{:S(2)}, u32[]{:S(2)}) collective-permute-start(bf16[4,4,96,512]{3,2,1,0:T(8,128)(2,1)S(1)} %get-tuple-element.146), channel_id=1, source_target_pairs={{0,4},{4,0},{8,12},{12,8},{16,20},{20,16},{24,28},{28,24},{1,5},{5... | collective-permute-start | bytes 4718600 | tf_op jit(solution)/shard_map/ppermute | solution.py:632
  55.7 13.5 %collective-permute-start.24 = (bf16[2,256,512]{2,1,0:T(8,128)(2,1)S(1)}, bf16[2,256,512]{2,1,0:T(8,128)(2,1)S(1)}, u32[]{:S(2)}, u32[]{:S(2)}) collective-permute-start(bf16[2,256,512]{2,1,0:T(8,128)(2,1)S(1)} %get-tuple-element.155), channel_id=1, source_target_pairs={{0,8},{4,12},{8,0},{12,4},{16,24},{20,28},{24,16},{28,20},{1,9},{5... | collective-permute-start | bytes 1572872 | tf_op jit(solution)/shard_map/ppermute | solution.py:632
  56.4 13.2 %collective-permute-start.25 = (bf16[2,256,512]{2,1,0:T(8,128)(2,1)S(1)}, bf16[2,256,512]{2,1,0:T(8,128)(2,1)S(1)}, u32[]{:S(2)}, u32[]{:S(2)}) collective-permute-start(bf16[2,256,512]{2,1,0:T(8,128)(2,1)S(1)} %get-tuple-element.157), channel_id=1, source_target_pairs={{0,16},{4,20},{8,24},{12,28},{16,0},{20,4},{24,8},{28,12},{1,17},{... | collective-permute-start | bytes 1572872 | tf_op jit(solution)/shard_map/ppermute | solution.py:632
  60.8 19.2 %collective-permute-start.23 = (bf16[800,512]{1,0:T(8,128)(2,1)S(1)}, bf16[800,512]{1,0:T(8,128)(2,1)S(1)}, u32[]{:S(2)}, u32[]{:S(2)}) collective-permute-start(bf16[800,512]{1,0:T(8,128)(2,1)S(1)} %get-tuple-element.153), channel_id=1, source_target_pairs={{0,1},{1,0},{2,3},{3,2},{4,5},{5,4},{6,7},{7,6},{8,9},{9,8},{10,11... | collective-permute-start | bytes 2457608 | tf_op jit(solution)/shard_map/ppermute | solution.py:632
  69.8 6.7 %collective-permute-start.26 = (bf16[256,512]{1,0:T(8,128)(2,1)S(1)}, bf16[256,512]{1,0:T(8,128)(2,1)S(1)}, u32[]{:S(2)}, u32[]{:S(2)}) collective-permute-start(bf16[256,512]{1,0:T(8,128)(2,1)S(1)} %get-tuple-element.159), channel_id=1, source_target_pairs={{0,16},{4,20},{8,24},{12,28},{16,0},{20,4},{24,8},{28,12},{1,17},{... | collective-permute-start | bytes 786440 | tf_op jit(solution)/shard_map/ppermute | solution.py:632
  71.0 6.3 %collective-permute-start.27 = (bf16[256,512]{1,0:T(8,128)(2,1)S(1)}, bf16[256,512]{1,0:T(8,128)(2,1)S(1)}, u32[]{:S(2)}, u32[]{:S(2)}) collective-permute-start(bf16[256,512]{1,0:T(8,128)(2,1)S(1)} %get-tuple-element.161), channel_id=1, source_target_pairs={{0,8},{4,12},{8,0},{12,4},{16,24},{20,28},{24,16},{28,20},{1,9},{5... | collective-permute-start | bytes 786440 | tf_op jit(solution)/shard_map/ppermute | solution.py:632
  77.5 5.8 %collective-permute-start.30 = (bf16[192,512]{1,0:T(8,128)(2,1)S(1)}, bf16[192,512]{1,0:T(8,128)(2,1)S(1)}, u32[]{:S(2)}, u32[]{:S(2)}) collective-permute-start(bf16[192,512]{1,0:T(8,128)(2,1)S(1)} %get-tuple-element.170), channel_id=1, source_target_pairs={{0,1},{1,0},{2,3},{3,2},{4,5},{5,4},{6,7},{7,6},{8,9},{9,8},{10,11... | collective-permute-start | bytes 589832 | tf_op jit(solution)/shard_map/ppermute | solution.py:632
  80.3 4.9 %collective-permute-start.29 = (bf16[192,512]{1,0:T(8,128)(2,1)S(1)}, bf16[192,512]{1,0:T(8,128)(2,1)S(1)}, u32[]{:S(2)}, u32[]{:S(2)}) collective-permute-start(bf16[192,512]{1,0:T(8,128)(2,1)S(1)} %get-tuple-element.168), channel_id=1, source_target_pairs={{0,16},{4,20},{8,24},{12,28},{16,0},{20,4},{24,8},{28,12},{1,17},{... | collective-permute-start | bytes 589832 | tf_op jit(solution)/shard_map/ppermute | solution.py:632
  80.6 4.9 %collective-permute-start.28 = (bf16[224,512]{1,0:T(8,128)(2,1)S(1)}, bf16[224,512]{1,0:T(8,128)(2,1)S(1)}, u32[]{:S(2)}, u32[]{:S(2)}) collective-permute-start(bf16[224,512]{1,0:T(8,128)(2,1)S(1)} %get-tuple-element.166), channel_id=1, source_target_pairs={{0,8},{4,12},{8,0},{12,4},{16,24},{20,28},{24,16},{28,20},{1,9},{5... | collective-permute-start | bytes 688136 | tf_op jit(solution)/shard_map/ppermute | solution.py:632
  83.4 9.5 %collective-permute-start.34 = (bf16[160,512]{1,0:T(8,128)(2,1)S(1)}, bf16[160,512]{1,0:T(8,128)(2,1)S(1)}, u32[]{:S(2)}, u32[]{:S(2)}) collective-permute-start(bf16[160,512]{1,0:T(8,128)(2,1)S(1)} %get-tuple-element.180), channel_id=1, source_target_pairs={{0,2},{1,3},{2,0},{3,1},{4,6},{5,7},{6,4},{7,5},{8,10},{9,11},{10,... | collective-permute-start | bytes 491528 | tf_op jit(solution)/shard_map/ppermute | solution.py:632
  85.6 5.3 %collective-permute-start.31 = (bf16[128,512]{1,0:T(8,128)(2,1)S(1)}, bf16[128,512]{1,0:T(8,128)(2,1)S(1)}, u32[]{:S(2)}, u32[]{:S(2)}) collective-permute-start(bf16[128,512]{1,0:T(8,128)(2,1)S(1)} %get-tuple-element.173), channel_id=1, source_target_pairs={{0,16},{4,20},{8,24},{12,28},{16,0},{20,4},{24,8},{28,12},{1,17},{... | collective-permute-start | bytes 393224 | tf_op jit(solution)/shard_map/ppermute | solution.py:632
  90.9 5.8 %collective-permute-start.33 = (bf16[112,512]{1,0:T(8,128)(2,1)S(1)}, bf16[112,512]{1,0:T(8,128)(2,1)S(1)}, u32[]{:S(2)}, u32[]{:S(2)}) collective-permute-start(bf16[112,512]{1,0:T(8,128)(2,1)S(1)} %get-tuple-element.179), channel_id=1, source_target_pairs={{0,2},{1,3},{2,0},{3,1},{4,6},{5,7},{6,4},{7,5},{8,10},{9,11},{10,... | collective-permute-start | bytes 344072 | tf_op jit(solution)/shard_map/ppermute | solution.py:632
  92.9 5.2 %collective-permute-start.42 = (bf16[160,512]{1,0:T(8,128)(2,1)S(1)}, bf16[160,512]{1,0:T(8,128)(2,1)S(1)}, u32[]{:S(2)}, u32[]{:S(2)}) collective-permute-start(bf16[160,512]{1,0:T(8,128)(2,1)S(1)} %add_last.1.refs_3_.refs_0_), channel_id=1, source_target_pairs={{0,24},{4,28},{8,16},{12,20},{16,8},{20,12},{24,0},{28,4},{1,25},{... | collective-permute-start | bytes 491528 | tf_op jit(solution)/shard_map/ppermute | solution.py:632
  93.8 6.2 %collective-permute-start.41 = (bf16[160,512]{1,0:T(8,128)(2,1)S(1)}, bf16[160,512]{1,0:T(8,128)(2,1)S(1)}, u32[]{:S(2)}, u32[]{:S(2)}) collective-permute-start(bf16[160,512]{1,0:T(8,128)(2,1)S(1)} %add_last.1.refs_3_.refs_0_), channel_id=1, source_target_pairs={{0,16},{4,20},{8,24},{12,28},{16,0},{20,4},{24,8},{28,12},{1,17},{... | collective-permute-start | bytes 491528 | tf_op jit(solution)/shard_map/ppermute | solution.py:632
  93.8 12.6 %collective-permute-start.40 = (bf16[160,512]{1,0:T(8,128)(2,1)S(1)}, bf16[160,512]{1,0:T(8,128)(2,1)S(1)}, u32[]{:S(2)}, u32[]{:S(2)}) collective-permute-start(bf16[160,512]{1,0:T(8,128)(2,1)S(1)} %add_last.1.refs_3_.refs_0_), channel_id=1, source_target_pairs={{0,8},{4,12},{8,0},{12,4},{16,24},{20,28},{24,16},{28,20},{1,9},{5... | collective-permute-start | bytes 491528 | tf_op jit(solution)/shard_map/ppermute | solution.py:632
  96.8 9.7 %collective-permute-start.38 = (bf16[96,512]{1,0:T(8,128)(2,1)S(1)}, bf16[96,512]{1,0:T(8,128)(2,1)S(1)}, u32[]{:S(2)}, u32[]{:S(2)}) collective-permute-start(bf16[96,512]{1,0:T(8,128)(2,1)S(1)} %get-tuple-element.182.refs_0_.refs_4_), channel_id=1, source_target_pairs={{0,24},{4,28},{8,16},{12,20},{16,8},{20,12},{24,0},{28,4},{1,25},{... | collective-permute-start | bytes 294920 | tf_op jit(solution)/shard_map/ppermute | solution.py:632
  97.6 8.9 %collective-permute-start.37 = (bf16[96,512]{1,0:T(8,128)(2,1)S(1)}, bf16[96,512]{1,0:T(8,128)(2,1)S(1)}, u32[]{:S(2)}, u32[]{:S(2)}) collective-permute-start(bf16[96,512]{1,0:T(8,128)(2,1)S(1)} %get-tuple-element.182.refs_0_.refs_4_), channel_id=1, source_target_pairs={{0,16},{4,20},{8,24},{12,28},{16,0},{20,4},{24,8},{28,12},{1,17},{... | collective-permute-start | bytes 294920 | tf_op jit(solution)/shard_map/ppermute | solution.py:632
  98.2 8.3 %collective-permute-start.36 = (bf16[96,512]{1,0:T(8,128)(2,1)S(1)}, bf16[96,512]{1,0:T(8,128)(2,1)S(1)}, u32[]{:S(2)}, u32[]{:S(2)}) collective-permute-start(bf16[96,512]{1,0:T(8,128)(2,1)S(1)} %get-tuple-element.182.refs_0_.refs_4_), channel_id=1, source_target_pairs={{0,8},{4,12},{8,0},{12,4},{16,24},{20,28},{24,16},{28,20},{1,9},{5... | collective-permute-start | bytes 294920 | tf_op jit(solution)/shard_map/ppermute | solution.py:632
  100.0 11.0 %collective-permute-start.35 = (f32[8,512]{1,0:T(8,128)S(1)}, f32[8,512]{1,0:T(8,128)S(1)}, u32[]{:S(2)}, u32[]{:S(2)}) collective-permute-start(f32[8,512]{1,0:T(8,128)S(1)} %get-tuple-element.181.refs_0_), channel_id=1, source_target_pairs={{0,4},{4,0},{8,12},{12,8},{16,20},{20,16},{24,28},{28,24},{1,5},{5... | collective-permute-start | bytes 49160 | tf_op jit(solution)/shard_map/ppermute | solution.py:632
  (20 other events, 73.8 us)

commit v9 on v8

--- a/solution.py
+++ b/solution.py
@@ -707,7 +707,6 @@
         (idx, gn, cotp, middle, row(gain_mlp), stT, w_out, decay),
         [shape_of(bf16, 4, out_rows, width)] * 2 + [square, wide, shape_of(f32, 2, units), edge, edge, shape_of(f32, 1, width)],
     )
-    payload = gate(payload, got)
     behind = [swap(payload, "mp", j) for j in (1, 2, 3)]
 
     half = (3 * block + out_rows) // 2

time: 113 us -> 115 us (1.018)
  waiting for transfers between devices: 27.1 us -> 32.6 us
  starting transfers between devices: 51.4 us -> 48.5 us
    ppermute x40, waiting for transfers between devices: 25.4 us -> 31 us  [swap(): return lax.ppermute(value, axis, [(i, i ^ bit) for i in range(size)])]
    ppermute x40, starting transfers between devices: 47.5 us -> 44.6 us  [swap(): return lax.ppermute(value, axis, [(i, i ^ bit) for i in range(size)])]
  transfers between devices with their start and end apart: 44 -> 44, of which waited for: 18 -> 18; matrix products, arithmetic and copies ran while one was open for 0% -> 0% of each run, Pallas kernels for 26% -> 25%
where the time goes in v9:
time: 115 us
  starting transfers between devices  48.5 us (42%)
  Pallas kernels  32.9 us (29%)
  waiting for transfers between devices  32.6 us (28%)
    ppermute x40, starting transfers between devices, swap(): return lax.ppermute(value, axis, [(i, i ^ bit) for i in range(size)])  44.6 us
    pallas_call x29, Pallas kernels, call(): pl.pallas_call(run, out_shape=outs, in_specs=[HBM] * hbm + [VMEM] * (n -...  32.9 us
    ppermute x40, waiting for transfers between devices, swap(): return lax.ppermute(value, axis, [(i, i ^ bit) for i in range(size)])  31 us
    ppermute x4, starting transfers between devices, across(): lax.ppermute(value, 'dp', [(i, i ^ 2 << (i & 1 ^ turn)) for i in range(si...  3.92 us
  transfers between devices with their start and end apart: 44, of which 18 were waited for; matrix products, arithmetic and copies ran while one was open for 0% of the time, Pallas kernels for 25%

profile of v9, /device:TPU:1, one launch (start us, length us, event | category | flops | bytes accessed | tf_op | source)
XLA Modules:
  0.0 115.0 jit_solution(1371264792988581165)
XLA Ops:
  1.6 2.2 %collective-permute-start.9 = (bf16[128,512]{1,0:T(8,128)(2,1)S(1)}, bf16[128,512]{1,0:T(8,128)(2,1)S(1)}, u32[]{:S(2)}, u32[]{:S(2)}) collective-permute-start(bf16[128,512]{1,0:T(8,128)(2,1)S(1)} %pick_piece.1.refs_7_), channel_id=1, source_target_pairs={{0,1},{1,0},{2,3},{3,2},{4,5},{5,4},{6,7},{7,6},{8,9},{9,8},{10,11... | collective-permute-start | bytes 393224 | tf_op jit(solution)/shard_map/ppermute | solution.py:632
  3.7 2.2 %collective-permute-start.1 = (bf16[128,512]{1,0:T(8,128)(2,1)S(1)}, bf16[128,512]{1,0:T(8,128)(2,1)S(1)}, u32[]{:S(2)}, u32[]{:S(2)}) collective-permute-start(bf16[128,512]{1,0:T(8,128)(2,1)S(1)} %pick_piece.1.refs_7_), channel_id=1, source_target_pairs={{0,3},{1,2},{2,1},{3,0},{4,7},{5,6},{6,5},{7,4},{8,11},{9,10},{10,... | collective-permute-start | bytes 393224 | tf_op jit(solution)/shard_map/ppermute | solution.py:632
  6.1 6.5 %mixer_in.1 = (f32[512,1024]{1,0:T(8,128)S(1)}, f32[512,1024]{1,0:T(8,128)S(1)}, f32[512,1024]{1,0:T(8,128)S(1)}, f32[512,1024]{1,0:T(8,128)S(1)}, f32[512,1024]...) custom-call(s32[1,3]{1,0:T(1,128)} %refs_0_.4, ...), custom_call_target="tpu_custom_call" | custom-call | tf_op jit(solution)/shard_map/mixer_in/pallas_call | solution.py:55
  13.9 2.4 %collective-permute-start.5 = (f32[4,1024]{1,0:T(4,128)S(1)}, f32[4,1024]{1,0:T(4,128)S(1)}, u32[]{:S(2)}, u32[]{:S(2)}) collective-permute-start(f32[4,1024]{1,0:T(4,128)S(1)} %get-tuple-element.102.refs_2_.refs_0_.refs_1_), channel_id=1, source_target_pairs={{0,3},{1,2},{2,1},{3,0},{4,7},{5,6},{6,5},{7,4},{8,11},{9,10},{10,... | collective-permute-start | bytes 49160 | tf_op jit(solution)/shard_map/ppermute | solution.py:632
  17.7 1.5 %collective-permute-start.2 = (bf16[256,512]{1,0:T(8,128)(2,1)S(1)}, bf16[256,512]{1,0:T(8,128)(2,1)S(1)}, u32[]{:S(2)}, u32[]{:S(2)}) collective-permute-start(bf16[256,512]{1,0:T(8,128)(2,1)S(1)} %join_depth.1.refs_0_.refs_2_), channel_id=1, source_target_pairs={{0,8},{4,20},{8,0},{12,28},{16,24},{20,4},{24,16},{28,12},{1,9},{5... | collective-permute-start | bytes 786440 | tf_op jit(solution)/shard_map/ppermute | solution.py:637
  21.1 2.0 %mid_in.1 = (f32[520,1024]{1,0:T(8,128)S(1)}, bf16[1024,512]{1,0:T(8,128)(2,1)S(1)}, f32[512,512]{1,0:T(8,128)S(1)}, bf16[512,512]{1,0:T(8,128)(2,1)S(1)}, bf16[...) custom-call(f32[4,1024]{1,0:T(4,128)S(1)} %get-tuple-element.102.refs_2_.refs_0_.refs_1_, ...), custom_call_target="tpu_custom_call" | custom-call | flops 8589934592 | bytes 33554432 | tf_op jit(solution)/shard_map/mid_in/pallas_call | solution.py:55
  23.2 3.6 %collective-permute-start.12 = (bf16[2,128,512]{2,1,0:T(8,128)(2,1)S(1)}, bf16[2,128,512]{2,1,0:T(8,128)(2,1)S(1)}, u32[]{:S(2)}, u32[]{:S(2)}) collective-permute-start(bf16[2,128,512]{2,1,0:T(8,128)(2,1)S(1)} %join_one.1.refs_0_), channel_id=1, source_target_pairs={{0,4},{4,0},{8,12},{12,8},{16,20},{20,16},{24,28},{28,24},{1,5},{5... | collective-permute-start | bytes 786440 | tf_op jit(solution)/shard_map/ppermute | solution.py:632
  27.1 1.6 %collective-permute-done.11.refs_0_ = bf16[2,128,512]{2,1,0:T(8,128)(2,1)S(1)} collective-permute-done((bf16[2,128,512]{2,1,0:T(8,128)(2,1)S(1)}, bf16[2,128,512]{2,1,0:T(8,128)(2,1)S(1)}, u32[]{:S(2)}, u32[]{:S(2)}) %collective-permute-start.11) | collective-permute-done | bytes 262176 | tf_op jit(solution)/shard_map/ppermute | solution.py:637
  29.8 2.1 %mlp_own.1 = (f32[512,512]{1,0:T(8,128)S(1)}, f32[512,512]{1,0:T(8,128)S(1)}, bf16[4,128,512]{2,1,0:T(8,128)(2,1)S(1)}, bf16[4,128,512]{2,1,0:T(8,128)(2,1)S(1)}, f32[16,512]{1,0:T(8,128)S(1)}) custom-call(bf16[512,512]{1,0:T(8,128)(2,1)S(1)} %copy-done.5, bf16[512,512]{1,0:T(8,128)(2,1)S(1)} %copy-done.6, f32[1,512]{1,0:T(1,128)S(1)} %bitcast.23, ...), custom_call_target="tpu_custom_call" | custom-call | flops 4294967296 | bytes 16777216 | tf_op jit(solution)/shard_map/mlp_own/pallas_call | solution.py:55
  31.9 2.1 %mlp_one.1 = (f32[512,512]{1,0:T(8,128)S(1)}, f32[512,512]{1,0:T(8,128)S(1)}, bf16[4,128,512]{2,1,0:T(8,128)(2,1)S(1)}, bf16[4,128,512]{2,1,0:T(8,128)(2,1)S(1)}, f32[16,512]{1,0:T(8,128)S(1)}) custom-call(bf16[2,128,512]{2,1,0:T(8,128)(2,1)S(1)} %join_one.1.refs_0_, bf16[2,128,512]{2,1,0:T(8,128)(2,1)S(1)} %gate.3.refs_1_, ...), custom_call_target="tpu_custom_call" | custom-call | flops 4294967296 | bytes 16777216 | tf_op jit(solution)/shard_map/mlp_one/pallas_call | solution.py:55
  35.2 3.2 %collective-permute-start.8 = (bf16[2,256,512]{2,1,0:T(8,128)(2,1)S(1)}, bf16[2,256,512]{2,1,0:T(8,128)(2,1)S(1)}, u32[]{:S(2)}, u32[]{:S(2)}) collective-permute-start(bf16[2,256,512]{2,1,0:T(8,128)(2,1)S(1)} %collective-permute-done.6.refs_1_), channel_id=1, source_target_pairs={{0,4},{4,0},{8,12},{12,8},{16,20},{20,16},{24,28},{28,24},{1,5},{5... | collective-permute-start | bytes 1572872 | tf_op jit(solution)/shard_map/ppermute | solution.py:632
  39.9 4.0 %mlp_two.1 = (f32[512,512]{1,0:T(8,128)S(1)}, f32[512,512]{1,0:T(8,128)S(1)}, bf16[4,256,512]{2,1,0:T(8,128)(2,1)S(1)}, bf16[4,256,512]{2,1,0:T(8,128)(2,1)S(1)}, f32[16,512]{1,0:T(8,128)S(1)}) custom-call(bf16[2,256,512]{2,1,0:T(8,128)(2,1)S(1)} %join_two.1.refs_7_.refs_0_, bf16[2,256,512]{2,1,0:T(8,128)(2,1)S(1)} %collective-permute-done.6.refs_1_, ...), custom_call_target="tpu_custom_call" | custom-call | flops 8589934592 | bytes 33554432 | tf_op jit(solution)/shard_map/mlp_two/pallas_call | solution.py:55
  44.3 2.2 %mid_back.1 = (bf16[4,128,512]{2,1,0:T(8,128)(2,1)S(1)}, bf16[4,128,512]{2,1,0:T(8,128)(2,1)S(1)}, f32[512,512]{1,0:T(8,128)S(1)}, f32[512,1024]{1,0:T(8,128)S(1...) custom-call(f32[512,512]{1,0:T(8,128)S(1)} %get-tuple-element.122.refs_0_, ...), custom_call_target="tpu_custom_call" | custom-call | flops 8589934592 | bytes 33554432 | tf_op jit(solution)/shard_map/mid_back/pallas_call | solution.py:55
  46.7 1.3 %collective-permute-start.17 = (f32[2,1024]{1,0:T(2,128)S(1)}, f32[2,1024]{1,0:T(2,128)S(1)}, u32[]{:S(2)}, u32[]{:S(2)}) collective-permute-start(f32[2,1024]{1,0:T(2,128)S(1)} %get-tuple-element.124.refs_0_), channel_id=1, source_target_pairs={{0,3},{1,2},{2,1},{3,0},{4,7},{5,6},{6,5},{7,4},{8,11},{9,10},{10,... | collective-permute-start | bytes 24584 | tf_op jit(solution)/shard_map/ppermute | solution.py:632
  48.1 4.1 %collective-permute-done.19.refs_2_ = bf16[4,128,512]{2,1,0:T(8,128)(2,1)S(1)} collective-permute-done((bf16[4,128,512]{2,1,0:T(8,128)(2,1)S(1)}, bf16[4,128,512]{2,1,0:T(8,128)(2,1)S(1)}, u32[]{:S(2)}, u32[]{:S(2)}) %collective-permute-start.19) | collective-permute-done | bytes 524320 | tf_op jit(solution)/shard_map/ppermute | solution.py:632
  52.8 1.9 %collective-permute-done.15.refs_1_ = f32[2,1024]{1,0:T(2,128)S(1)} collective-permute-done((f32[2,1024]{1,0:T(2,128)S(1)}, f32[2,1024]{1,0:T(2,128)S(1)}, u32[]{:S(2)}, u32[]{:S(2)}) %collective-permute-start.15) | collective-permute-done | bytes 8224 | tf_op jit(solution)/shard_map/ppermute | solution.py:632
  54.7 1.7 %mixer_back.1 = (f32[512,1024]{1,0:T(8,128)S(1)}, bf16[4,4,96,512]{3,2,1,0:T(8,128)(2,1)S(1)}, bf16[3,512,512]{2,1,0:T(8,128)(2,1)S(1)}, f32[16,512]{1,0:T(8,128)S(1)}) custom-call(f32[2,1024]{1,0:T(2,128)S(1)} %get-tuple-element.124.refs_0_, f32[2,1024]{1,0:T(2,128)S(1)} %collective-permute-done.15.refs_1_, f32[2,1024]{1,0:T(2,128)S(1)} %collective-permute-done.16.refs_2_, ...), custom_call_target="tpu_custom_call" | custom-call | tf_op jit(solution)/shard_map/mixer_back/pallas_call | solution.py:55
  56.4 2.0 %collective-permute-start.22 = (bf16[4,4,96,512]{3,2,1,0:T(8,128)(2,1)S(1)}, bf16[4,4,96,512]{3,2,1,0:T(8,128)(2,1)S(1)}, u32[]{:S(2)}, u32[]{:S(2)}) collective-permute-start(bf16[4,4,96,512]{3,2,1,0:T(8,128)(2,1)S(1)} %get-tuple-element.146), channel_id=1, source_target_pairs={{0,4},{4,0},{8,12},{12,8},{16,20},{20,16},{24,28},{28,24},{1,5},{5... | collective-permute-start | bytes 4718600 | tf_op jit(solution)/shard_map/ppermute | solution.py:632
  59.1 1.5 %collective-permute-start.25 = (bf16[2,256,512]{2,1,0:T(8,128)(2,1)S(1)}, bf16[2,256,512]{2,1,0:T(8,128)(2,1)S(1)}, u32[]{:S(2)}, u32[]{:S(2)}) collective-permute-start(bf16[2,256,512]{2,1,0:T(8,128)(2,1)S(1)} %get-tuple-element.157), channel_id=1, source_target_pairs={{0,16},{4,20},{8,24},{12,28},{16,0},{20,4},{24,8},{28,12},{1,17},{... | collective-permute-start | bytes 1572872 | tf_op jit(solution)/shard_map/ppermute | solution.py:632
  60.6 2.8 %mixer_out.1 = (bf16[4,4,96,512]{3,2,1,0:T(8,128)(2,1)S(1)}, f32[512,512]{1,0:T(8,128)S(1)}, f32[16,512]{1,0:T(8,128)S(1)}) custom-call(f32[512,1024]{1,0:T(8,128)S(1)} %get-tuple-element.140.refs_0_, f32[512,1024]{1,0:T(8,128)S(1)} %get-tuple-element.106.refs_7_.refs_1_, f32[512,1024]{1,0:T(8,128)S(1)} %get-tuple-element.107.refs_8_.refs_2_, ...), custom_call_target="tpu_custom_call" | custom-call | tf_op jit(solution)/shard_map/mixer_out/pallas_call | solution.py:55
  63.9 8.0 %collective-permute-done.24.refs_1_ = bf16[2,256,512]{2,1,0:T(8,128)(2,1)S(1)} collective-permute-done((bf16[2,256,512]{2,1,0:T(8,128)(2,1)S(1)}, bf16[2,256,512]{2,1,0:T(8,128)(2,1)S(1)}, u32[]{:S(2)}, u32[]{:S(2)}) %collective-permute-start.24) | collective-permute-done | bytes 524320 | tf_op jit(solution)/shard_map/ppermute | solution.py:632
  72.6 1.4 %collective-permute-start.26 = (bf16[256,512]{1,0:T(8,128)(2,1)S(1)}, bf16[256,512]{1,0:T(8,128)(2,1)S(1)}, u32[]{:S(2)}, u32[]{:S(2)}) collective-permute-start(bf16[256,512]{1,0:T(8,128)(2,1)S(1)} %get-tuple-element.159), channel_id=1, source_target_pairs={{0,16},{4,20},{8,24},{12,28},{16,0},{20,4},{24,8},{28,12},{1,17},{... | collective-permute-start | bytes 786440 | tf_op jit(solution)/shard_map/ppermute | solution.py:632
  74.4 2.2 %tokens_out.1 = (bf16[512,512]{1,0:T(8,128)(2,1)}, f32[8,128]{1,0:T(8,128)S(1)}) custom-call(f32[512,512]{1,0:T(8,128)S(1)} %get-tuple-element.150.refs_0_, f32[512,512]{1,0:T(8,128)S(1)} %get-tuple-element.108.refs_9_.refs_12_.refs_1_, f32[1,512]{1,0:T(1,128)S(1)} %bitcast.25, f32[512,512]{1,0:T(8,128)S(1)} %get-tuple-element.151.refs_3_, ...), custom_call_target="tpu_custom_call" | custom-call | flops 8589934592 | bytes 33554432 | tf_op jit(solution)/shard_map/tokens_out/pallas_call | solution.py:55
  76.6 1.5 %mixed_out.1 = (bf16[512,512]{1,0:T(8,128)(2,1)}, f32[8,128]{1,0:T(8,128)S(1)}) custom-call(f32[512,512]{1,0:T(8,128)S(1)} %get-tuple-element.121.refs_0_, f32[4,192,512]{2,1,0:T(8,128)S(1)} %get-tuple-element.148.refs_1_.refs_4_.refs_0_), custom_call_target="tpu_custom_call" | custom-call | tf_op jit(solution)/shard_map/mixed_out/pallas_call | solution.py:55
  80.6 2.5 %collective-permute-done.23.refs_1_ = bf16[800,512]{1,0:T(8,128)(2,1)S(1)} collective-permute-done((bf16[800,512]{1,0:T(8,128)(2,1)S(1)}, bf16[800,512]{1,0:T(8,128)(2,1)S(1)}, u32[]{:S(2)}, u32[]{:S(2)}) %collective-permute-start.23) | collective-permute-done | bytes 819232 | tf_op jit(solution)/shard_map/ppermute | solution.py:632
  84.0 2.3 %collective-permute-done.30.refs_1_ = bf16[192,512]{1,0:T(8,128)(2,1)S(1)} collective-permute-done((bf16[192,512]{1,0:T(8,128)(2,1)S(1)}, bf16[192,512]{1,0:T(8,128)(2,1)S(1)}, u32[]{:S(2)}, u32[]{:S(2)}) %collective-permute-start.30) | collective-permute-done | bytes 196640 | tf_op jit(solution)/shard_map/ppermute | solution.py:632
  88.5 1.6 %collective-permute-start.31 = (bf16[128,512]{1,0:T(8,128)(2,1)S(1)}, bf16[128,512]{1,0:T(8,128)(2,1)S(1)}, u32[]{:S(2)}, u32[]{:S(2)}) collective-permute-start(bf16[128,512]{1,0:T(8,128)(2,1)S(1)} %get-tuple-element.173), channel_id=1, source_target_pairs={{0,16},{4,20},{8,24},{12,28},{16,0},{20,4},{24,8},{28,12},{1,17},{... | collective-permute-start | bytes 393224 | tf_op jit(solution)/shard_map/ppermute | solution.py:632
  90.3 3.3 %collective-permute-done.32.refs_3_ = bf16[96,512]{1,0:T(8,128)(2,1)S(1)} collective-permute-done((bf16[96,512]{1,0:T(8,128)(2,1)S(1)}, bf16[96,512]{1,0:T(8,128)(2,1)S(1)}, u32[]{:S(2)}, u32[]{:S(2)}) %collective-permute-start.32) | collective-permute-done | bytes 98336 | tf_op jit(solution)/shard_map/ppermute | solution.py:632
  96.2 2.2 %collective-permute-start.40 = (bf16[160,512]{1,0:T(8,128)(2,1)S(1)}, bf16[160,512]{1,0:T(8,128)(2,1)S(1)}, u32[]{:S(2)}, u32[]{:S(2)}) collective-permute-start(bf16[160,512]{1,0:T(8,128)(2,1)S(1)} %add_last.1.refs_3_.refs_0_), channel_id=1, source_target_pairs={{0,8},{4,12},{8,0},{12,4},{16,24},{20,28},{24,16},{28,20},{1,9},{5... | collective-permute-start | bytes 491528 | tf_op jit(solution)/shard_map/ppermute | solution.py:632
  102.2 6.6 %collective-permute-start.35 = (f32[8,512]{1,0:T(8,128)S(1)}, f32[8,512]{1,0:T(8,128)S(1)}, u32[]{:S(2)}, u32[]{:S(2)}) collective-permute-start(f32[8,512]{1,0:T(8,128)S(1)} %get-tuple-element.181.refs_0_), channel_id=1, source_target_pairs={{0,4},{4,0},{8,12},{12,8},{16,20},{20,16},{24,28},{28,24},{1,5},{5... | collective-permute-start | bytes 49160 | tf_op jit(solution)/shard_map/ppermute | solution.py:632
  109.0 3.1 %collective-permute-start.39 = (bf16[4,96,512]{2,1,0:T(8,128)(2,1)S(1)}, bf16[4,96,512]{2,1,0:T(8,128)(2,1)S(1)}, u32[]{:S(2)}, u32[]{:S(2)}) collective-permute-start(bf16[4,96,512]{2,1,0:T(8,128)(2,1)S(1)} %join_mix.1.refs_2_), channel_id=1, source_target_pairs={{0,4},{4,0},{8,12},{12,8},{16,20},{20,16},{24,28},{28,24},{1,5},{5... | collective-permute-start | bytes 1179656 | tf_op jit(solution)/shard_map/ppermute | solution.py:632
  112.1 1.7 %spread_mlp.1 = (f32[512,512]{1,0:T(8,128)}, f32[512,512]{1,0:T(8,128)}, f32[256,512]{1,0:T(8,128)}, f32[8,128]{1,0:T(8,128)S(1)}) custom-call(bf16[4,160,512]{2,1,0:T(8,128)(2,1)S(1)} %join_mlp.1.refs_0_, bf16[4,160,512]{2,1,0:T(8,128)(2,1)S(1)} %collective-permute-done.43.refs_1_), custom_call_target="tpu_custom_call" | custom-call | flops 8589934592 | bytes 33554432 | tf_op jit(solution)/shard_map/spread_mlp/pallas_call | solution.py:55
  (103 shorter events, 26.8 us)
Async XLA Ops:
  1.6 11.0 %collective-permute-start.9 = (bf16[128,512]{1,0:T(8,128)(2,1)S(1)}, bf16[128,512]{1,0:T(8,128)(2,1)S(1)}, u32[]{:S(2)}, u32[]{:S(2)}) collective-permute-start(bf16[128,512]{1,0:T(8,128)(2,1)S(1)} %pick_piece.1.refs_7_), channel_id=1, source_target_pairs={{0,1},{1,0},{2,3},{3,2},{4,5},{5,4},{6,7},{7,6},{8,9},{9,8},{10,11... | collective-permute-start | bytes 393224 | tf_op jit(solution)/shard_map/ppermute | solution.py:632
  3.7 12.6 %collective-permute-start.1 = (bf16[128,512]{1,0:T(8,128)(2,1)S(1)}, bf16[128,512]{1,0:T(8,128)(2,1)S(1)}, u32[]{:S(2)}, u32[]{:S(2)}) collective-permute-start(bf16[128,512]{1,0:T(8,128)(2,1)S(1)} %pick_piece.1.refs_7_), channel_id=1, source_target_pairs={{0,3},{1,2},{2,1},{3,0},{4,7},{5,6},{6,5},{7,4},{8,11},{9,10},{10,... | collective-permute-start | bytes 393224 | tf_op jit(solution)/shard_map/ppermute | solution.py:632
  5.9 11.7 %collective-permute-start = (bf16[128,512]{1,0:T(8,128)(2,1)S(1)}, bf16[128,512]{1,0:T(8,128)(2,1)S(1)}, u32[]{:S(2)}, u32[]{:S(2)}) collective-permute-start(bf16[128,512]{1,0:T(8,128)(2,1)S(1)} %pick_piece.1.refs_7_), channel_id=1, source_target_pairs={{0,2},{1,3},{2,0},{3,1},{4,6},{5,7},{6,4},{7,5},{8,10},{9,11},{10,... | collective-permute-start | bytes 393224 | tf_op jit(solution)/shard_map/ppermute | solution.py:632
  12.6 7.7 %collective-permute-start.10 = (bf16[128,512]{1,0:T(8,128)(2,1)S(1)}, bf16[128,512]{1,0:T(8,128)(2,1)S(1)}, u32[]{:S(2)}, u32[]{:S(2)}) collective-permute-start(bf16[128,512]{1,0:T(8,128)(2,1)S(1)} %gate.2.refs_0_), channel_id=1, source_target_pairs={{0,8},{4,20},{8,0},{12,28},{16,24},{20,4},{24,16},{28,12},{1,9},{5... | collective-permute-start | bytes 393224 | tf_op jit(solution)/shard_map/ppermute | solution.py:637
  13.9 5.3 %collective-permute-start.5 = (f32[4,1024]{1,0:T(4,128)S(1)}, f32[4,1024]{1,0:T(4,128)S(1)}, u32[]{:S(2)}, u32[]{:S(2)}) collective-permute-start(f32[4,1024]{1,0:T(4,128)S(1)} %get-tuple-element.102.refs_2_.refs_0_.refs_1_), channel_id=1, source_target_pairs={{0,3},{1,2},{2,1},{3,0},{4,7},{5,6},{6,5},{7,4},{8,11},{9,10},{10,... | collective-permute-start | bytes 49160 | tf_op jit(solution)/shard_map/ppermute | solution.py:632
  17.7 9.0 %collective-permute-start.2 = (bf16[256,512]{1,0:T(8,128)(2,1)S(1)}, bf16[256,512]{1,0:T(8,128)(2,1)S(1)}, u32[]{:S(2)}, u32[]{:S(2)}) collective-permute-start(bf16[256,512]{1,0:T(8,128)(2,1)S(1)} %join_depth.1.refs_0_.refs_2_), channel_id=1, source_target_pairs={{0,8},{4,20},{8,0},{12,28},{16,24},{20,4},{24,16},{28,12},{1,9},{5... | collective-permute-start | bytes 786440 | tf_op jit(solution)/shard_map/ppermute | solution.py:637
  20.3 8.4 %collective-permute-start.11 = (bf16[2,128,512]{2,1,0:T(8,128)(2,1)S(1)}, bf16[2,128,512]{2,1,0:T(8,128)(2,1)S(1)}, u32[]{:S(2)}, u32[]{:S(2)}) collective-permute-start(bf16[2,128,512]{2,1,0:T(8,128)(2,1)S(1)} %join_one.1.refs_0_), channel_id=1, source_target_pairs={{0,16},{4,12},{8,24},{12,4},{16,0},{20,28},{24,8},{28,20},{1,17},{... | collective-permute-start | bytes 786440 | tf_op jit(solution)/shard_map/ppermute | solution.py:637
  23.2 8.7 %collective-permute-start.12 = (bf16[2,128,512]{2,1,0:T(8,128)(2,1)S(1)}, bf16[2,128,512]{2,1,0:T(8,128)(2,1)S(1)}, u32[]{:S(2)}, u32[]{:S(2)}) collective-permute-start(bf16[2,128,512]{2,1,0:T(8,128)(2,1)S(1)} %join_one.1.refs_0_), channel_id=1, source_target_pairs={{0,4},{4,0},{8,12},{12,8},{16,20},{20,16},{24,28},{28,24},{1,5},{5... | collective-permute-start | bytes 786440 | tf_op jit(solution)/shard_map/ppermute | solution.py:632
  26.8 8.4 %collective-permute-start.6 = (bf16[2,256,512]{2,1,0:T(8,128)(2,1)S(1)}, bf16[2,256,512]{2,1,0:T(8,128)(2,1)S(1)}, u32[]{:S(2)}, u32[]{:S(2)}) collective-permute-start(bf16[2,256,512]{2,1,0:T(8,128)(2,1)S(1)} %join_two.1.refs_7_.refs_0_), channel_id=1, source_target_pairs={{0,16},{4,12},{8,24},{12,4},{16,0},{20,28},{24,8},{28,20},{1,17},{... | collective-permute-start | bytes 1572872 | tf_op jit(solution)/shard_map/ppermute | solution.py:637
  34.7 13.4 %collective-permute-start.18 = (bf16[4,128,512]{2,1,0:T(8,128)(2,1)S(1)}, bf16[4,128,512]{2,1,0:T(8,128)(2,1)S(1)}, u32[]{:S(2)}, u32[]{:S(2)}) collective-permute-start(bf16[4,128,512]{2,1,0:T(8,128)(2,1)S(1)} %get-tuple-element.134), channel_id=1, source_target_pairs={{0,4},{4,0},{8,12},{12,8},{16,20},{20,16},{24,28},{28,24},{1,5},{5... | collective-permute-start | bytes 1572872 | tf_op jit(solution)/shard_map/ppermute | solution.py:632
  38.5 13.7 %collective-permute-start.19 = (bf16[4,128,512]{2,1,0:T(8,128)(2,1)S(1)}, bf16[4,128,512]{2,1,0:T(8,128)(2,1)S(1)}, u32[]{:S(2)}, u32[]{:S(2)}) collective-permute-start(bf16[4,128,512]{2,1,0:T(8,128)(2,1)S(1)} %add_pair.1.refs_12_), channel_id=1, source_target_pairs={{0,1},{1,0},{2,3},{3,2},{4,5},{5,4},{6,7},{7,6},{8,9},{9,8},{10,11... | collective-permute-start | bytes 1572872 | tf_op jit(solution)/shard_map/ppermute | solution.py:632
  43.9 8.3 %collective-permute-start.20 = (bf16[4,256,512]{2,1,0:T(8,128)(2,1)S(1)}, bf16[4,256,512]{2,1,0:T(8,128)(2,1)S(1)}, u32[]{:S(2)}, u32[]{:S(2)}) collective-permute-start(bf16[4,256,512]{2,1,0:T(8,128)(2,1)S(1)} %get-tuple-element.136), channel_id=1, source_target_pairs={{0,4},{4,0},{8,12},{12,8},{16,20},{20,16},{24,28},{28,24},{1,5},{5... | collective-permute-start | bytes 3145736 | tf_op jit(solution)/shard_map/ppermute | solution.py:632
  46.5 5.7 %collective-permute-start.21 = (bf16[4,128,512]{2,1,0:T(8,128)(2,1)S(1)}, bf16[4,128,512]{2,1,0:T(8,128)(2,1)S(1)}, u32[]{:S(2)}, u32[]{:S(2)}) collective-permute-start(bf16[4,128,512]{2,1,0:T(8,128)(2,1)S(1)} %get-tuple-element.138), channel_id=1, source_target_pairs={{0,4},{4,0},{8,12},{12,8},{16,20},{20,16},{24,28},{28,24},{1,5},{5... | collective-permute-start | bytes 1572872 | tf_op jit(solution)/shard_map/ppermute | solution.py:632
  46.7 6.0 %collective-permute-start.17 = (f32[2,1024]{1,0:T(2,128)S(1)}, f32[2,1024]{1,0:T(2,128)S(1)}, u32[]{:S(2)}, u32[]{:S(2)}) collective-permute-start(f32[2,1024]{1,0:T(2,128)S(1)} %get-tuple-element.124.refs_0_), channel_id=1, source_target_pairs={{0,3},{1,2},{2,1},{3,0},{4,7},{5,6},{6,5},{7,4},{8,11},{9,10},{10,... | collective-permute-start | bytes 24584 | tf_op jit(solution)/shard_map/ppermute | solution.py:632
  56.4 7.1 %collective-permute-start.22 = (bf16[4,4,96,512]{3,2,1,0:T(8,128)(2,1)S(1)}, bf16[4,4,96,512]{3,2,1,0:T(8,128)(2,1)S(1)}, u32[]{:S(2)}, u32[]{:S(2)}) collective-permute-start(bf16[4,4,96,512]{3,2,1,0:T(8,128)(2,1)S(1)} %get-tuple-element.146), channel_id=1, source_target_pairs={{0,4},{4,0},{8,12},{12,8},{16,20},{20,16},{24,28},{28,24},{1,5},{5... | collective-permute-start | bytes 4718600 | tf_op jit(solution)/shard_map/ppermute | solution.py:632
  58.4 13.5 %collective-permute-start.24 = (bf16[2,256,512]{2,1,0:T(8,128)(2,1)S(1)}, bf16[2,256,512]{2,1,0:T(8,128)(2,1)S(1)}, u32[]{:S(2)}, u32[]{:S(2)}) collective-permute-start(bf16[2,256,512]{2,1,0:T(8,128)(2,1)S(1)} %get-tuple-element.155), channel_id=1, source_target_pairs={{0,8},{4,12},{8,0},{12,4},{16,24},{20,28},{24,16},{28,20},{1,9},{5... | collective-permute-start | bytes 1572872 | tf_op jit(solution)/shard_map/ppermute | solution.py:632
  59.1 13.3 %collective-permute-start.25 = (bf16[2,256,512]{2,1,0:T(8,128)(2,1)S(1)}, bf16[2,256,512]{2,1,0:T(8,128)(2,1)S(1)}, u32[]{:S(2)}, u32[]{:S(2)}) collective-permute-start(bf16[2,256,512]{2,1,0:T(8,128)(2,1)S(1)} %get-tuple-element.157), channel_id=1, source_target_pairs={{0,16},{4,20},{8,24},{12,28},{16,0},{20,4},{24,8},{28,12},{1,17},{... | collective-permute-start | bytes 1572872 | tf_op jit(solution)/shard_map/ppermute | solution.py:632
  63.8 19.2 %collective-permute-start.23 = (bf16[800,512]{1,0:T(8,128)(2,1)S(1)}, bf16[800,512]{1,0:T(8,128)(2,1)S(1)}, u32[]{:S(2)}, u32[]{:S(2)}) collective-permute-start(bf16[800,512]{1,0:T(8,128)(2,1)S(1)} %get-tuple-element.153), channel_id=1, source_target_pairs={{0,1},{1,0},{2,3},{3,2},{4,5},{5,4},{6,7},{7,6},{8,9},{9,8},{10,11... | collective-permute-start | bytes 2457608 | tf_op jit(solution)/shard_map/ppermute | solution.py:632
  72.6 6.8 %collective-permute-start.26 = (bf16[256,512]{1,0:T(8,128)(2,1)S(1)}, bf16[256,512]{1,0:T(8,128)(2,1)S(1)}, u32[]{:S(2)}, u32[]{:S(2)}) collective-permute-start(bf16[256,512]{1,0:T(8,128)(2,1)S(1)} %get-tuple-element.159), channel_id=1, source_target_pairs={{0,16},{4,20},{8,24},{12,28},{16,0},{20,4},{24,8},{28,12},{1,17},{... | collective-permute-start | bytes 786440 | tf_op jit(solution)/shard_map/ppermute | solution.py:632
  74.1 6.3 %collective-permute-start.27 = (bf16[256,512]{1,0:T(8,128)(2,1)S(1)}, bf16[256,512]{1,0:T(8,128)(2,1)S(1)}, u32[]{:S(2)}, u32[]{:S(2)}) collective-permute-start(bf16[256,512]{1,0:T(8,128)(2,1)S(1)} %get-tuple-element.161), channel_id=1, source_target_pairs={{0,8},{4,12},{8,0},{12,4},{16,24},{20,28},{24,16},{28,20},{1,9},{5... | collective-permute-start | bytes 786440 | tf_op jit(solution)/shard_map/ppermute | solution.py:632
  80.5 5.8 %collective-permute-start.30 = (bf16[192,512]{1,0:T(8,128)(2,1)S(1)}, bf16[192,512]{1,0:T(8,128)(2,1)S(1)}, u32[]{:S(2)}, u32[]{:S(2)}) collective-permute-start(bf16[192,512]{1,0:T(8,128)(2,1)S(1)} %get-tuple-element.170), channel_id=1, source_target_pairs={{0,1},{1,0},{2,3},{3,2},{4,5},{5,4},{6,7},{7,6},{8,9},{9,8},{10,11... | collective-permute-start | bytes 589832 | tf_op jit(solution)/shard_map/ppermute | solution.py:632
  83.4 5.0 %collective-permute-start.28 = (bf16[224,512]{1,0:T(8,128)(2,1)S(1)}, bf16[224,512]{1,0:T(8,128)(2,1)S(1)}, u32[]{:S(2)}, u32[]{:S(2)}) collective-permute-start(bf16[224,512]{1,0:T(8,128)(2,1)S(1)} %get-tuple-element.166), channel_id=1, source_target_pairs={{0,8},{4,12},{8,0},{12,4},{16,24},{20,28},{24,16},{28,20},{1,9},{5... | collective-permute-start | bytes 688136 | tf_op jit(solution)/shard_map/ppermute | solution.py:632
  86.4 9.3 %collective-permute-start.34 = (bf16[160,512]{1,0:T(8,128)(2,1)S(1)}, bf16[160,512]{1,0:T(8,128)(2,1)S(1)}, u32[]{:S(2)}, u32[]{:S(2)}) collective-permute-start(bf16[160,512]{1,0:T(8,128)(2,1)S(1)} %get-tuple-element.180), channel_id=1, source_target_pairs={{0,2},{1,3},{2,0},{3,1},{4,6},{5,7},{6,4},{7,5},{8,10},{9,11},{10,... | collective-permute-start | bytes 491528 | tf_op jit(solution)/shard_map/ppermute | solution.py:632
  88.5 5.1 %collective-permute-start.31 = (bf16[128,512]{1,0:T(8,128)(2,1)S(1)}, bf16[128,512]{1,0:T(8,128)(2,1)S(1)}, u32[]{:S(2)}, u32[]{:S(2)}) collective-permute-start(bf16[128,512]{1,0:T(8,128)(2,1)S(1)} %get-tuple-element.173), channel_id=1, source_target_pairs={{0,16},{4,20},{8,24},{12,28},{16,0},{20,4},{24,8},{28,12},{1,17},{... | collective-permute-start | bytes 393224 | tf_op jit(solution)/shard_map/ppermute | solution.py:632
  93.6 5.8 %collective-permute-start.33 = (bf16[112,512]{1,0:T(8,128)(2,1)S(1)}, bf16[112,512]{1,0:T(8,128)(2,1)S(1)}, u32[]{:S(2)}, u32[]{:S(2)}) collective-permute-start(bf16[112,512]{1,0:T(8,128)(2,1)S(1)} %get-tuple-element.179), channel_id=1, source_target_pairs={{0,2},{1,3},{2,0},{3,1},{4,6},{5,7},{6,4},{7,5},{8,10},{9,11},{10,... | collective-permute-start | bytes 344072 | tf_op jit(solution)/shard_map/ppermute | solution.py:632
  95.7 5.3 %collective-permute-start.42 = (bf16[160,512]{1,0:T(8,128)(2,1)S(1)}, bf16[160,512]{1,0:T(8,128)(2,1)S(1)}, u32[]{:S(2)}, u32[]{:S(2)}) collective-permute-start(bf16[160,512]{1,0:T(8,128)(2,1)S(1)} %add_last.1.refs_3_.refs_0_), channel_id=1, source_target_pairs={{0,24},{4,28},{8,16},{12,20},{16,8},{20,12},{24,0},{28,4},{1,25},{... | collective-permute-start | bytes 491528 | tf_op jit(solution)/shard_map/ppermute | solution.py:632
  96.2 6.0 %collective-permute-start.41 = (bf16[160,512]{1,0:T(8,128)(2,1)S(1)}, bf16[160,512]{1,0:T(8,128)(2,1)S(1)}, u32[]{:S(2)}, u32[]{:S(2)}) collective-permute-start(bf16[160,512]{1,0:T(8,128)(2,1)S(1)} %add_last.1.refs_3_.refs_0_), channel_id=1, source_target_pairs={{0,16},{4,20},{8,24},{12,28},{16,0},{20,4},{24,8},{28,12},{1,17},{... | collective-permute-start | bytes 491528 | tf_op jit(solution)/shard_map/ppermute | solution.py:632
  96.2 12.6 %collective-permute-start.40 = (bf16[160,512]{1,0:T(8,128)(2,1)S(1)}, bf16[160,512]{1,0:T(8,128)(2,1)S(1)}, u32[]{:S(2)}, u32[]{:S(2)}) collective-permute-start(bf16[160,512]{1,0:T(8,128)(2,1)S(1)} %add_last.1.refs_3_.refs_0_), channel_id=1, source_target_pairs={{0,8},{4,12},{8,0},{12,4},{16,24},{20,28},{24,16},{28,20},{1,9},{5... | collective-permute-start | bytes 491528 | tf_op jit(solution)/shard_map/ppermute | solution.py:632
  99.5 9.4 %collective-permute-start.38 = (bf16[96,512]{1,0:T(8,128)(2,1)S(1)}, bf16[96,512]{1,0:T(8,128)(2,1)S(1)}, u32[]{:S(2)}, u32[]{:S(2)}) collective-permute-start(bf16[96,512]{1,0:T(8,128)(2,1)S(1)} %get-tuple-element.182.refs_0_.refs_4_), channel_id=1, source_target_pairs={{0,24},{4,28},{8,16},{12,20},{16,8},{20,12},{24,0},{28,4},{1,25},{... | collective-permute-start | bytes 294920 | tf_op jit(solution)/shard_map/ppermute | solution.py:632
  100.0 8.9 %collective-permute-start.37 = (bf16[96,512]{1,0:T(8,128)(2,1)S(1)}, bf16[96,512]{1,0:T(8,128)(2,1)S(1)}, u32[]{:S(2)}, u32[]{:S(2)}) collective-permute-start(bf16[96,512]{1,0:T(8,128)(2,1)S(1)} %get-tuple-element.182.refs_0_.refs_4_), channel_id=1, source_target_pairs={{0,16},{4,20},{8,24},{12,28},{16,0},{20,4},{24,8},{28,12},{1,17},{... | collective-permute-start | bytes 294920 | tf_op jit(solution)/shard_map/ppermute | solution.py:632
  101.0 8.0 %collective-permute-start.36 = (bf16[96,512]{1,0:T(8,128)(2,1)S(1)}, bf16[96,512]{1,0:T(8,128)(2,1)S(1)}, u32[]{:S(2)}, u32[]{:S(2)}) collective-permute-start(bf16[96,512]{1,0:T(8,128)(2,1)S(1)} %get-tuple-element.182.refs_0_.refs_4_), channel_id=1, source_target_pairs={{0,8},{4,12},{8,0},{12,4},{16,24},{20,28},{24,16},{28,20},{1,9},{5... | collective-permute-start | bytes 294920 | tf_op jit(solution)/shard_map/ppermute | solution.py:632
  102.2 11.6 %collective-permute-start.35 = (f32[8,512]{1,0:T(8,128)S(1)}, f32[8,512]{1,0:T(8,128)S(1)}, u32[]{:S(2)}, u32[]{:S(2)}) collective-permute-start(f32[8,512]{1,0:T(8,128)S(1)} %get-tuple-element.181.refs_0_), channel_id=1, source_target_pairs={{0,4},{4,0},{8,12},{12,8},{16,20},{20,16},{24,28},{28,24},{1,5},{5... | collective-permute-start | bytes 49160 | tf_op jit(solution)/shard_map/ppermute | solution.py:632
  (20 other events, 75.3 us)
